TPU v7x, 256 devices: a whole 4x4x8 slice. The times are simulated.
256 devices in a mesh: view: 4 (over x_lo, core), tx: 2 (over x_hi), ty: 32 (over z, y).
Axes of the slice: x: 4 (x_hi: 2, x_lo: 2; x = x_hi * 2 + x_lo), y: 4, z: 8, core: 2. Of those that a mesh axis runs over, the one named last changes fastest.
Arguments:
- raw_views: float32 [4, 48, 1024, 256], P('view', None, 'ty', 'tx'), may hold values from 0.2 to 5
- psf_taps: float32 [4, 3, 31], replicated, may hold values from 0.05 to 1
- offsets: int32 [4, 2], replicated, may hold values from -8 to 8, as said below
- estimate: float32 [48, 1024, 256], P(None, 'ty', 'tx'), may hold values from 0.5 to 2
Outputs:
- deconvolved: float32 [48, 1024, 256], P(None, 'ty', 'tx')
Inputs may be any that keep to these rules, and one draw needn't show every extreme that they name: `offsets`: integer registration shifts; some entry equals 8 and some equals -8.
All inputs are finite; a program needn't handle non-finite values.
Results may differ from a plain program's by a relative error of at most 0.00011.
Values sent between devices are 32-bit elements; how exact they have to be, the bound alone decides.
No kernel may reach another device: no remote copies, remote signals or barrier semaphores. Data moves between devices by JAX's collectives and lax.ppermute only.
A program may use at most 128 MiB of HBM per device.

v0:
```python
import jax
import jax.numpy as jnp
from jax import lax
from jax.sharding import PartitionSpec as P

OMAX = 8
ITERS = 2


highest = lax.Precision.HIGHEST


def extended_2(cells, sides, width):
    for axis, dim in sides:
        count = lax.axis_size(axis)
        ends = count - 1
        head = lax.slice_in_dim(cells, 0, width, axis=dim)
        tail = lax.slice_in_dim(cells, cells.shape[dim] - width, cells.shape[dim], axis=dim)
        cells = jnp.concatenate(
            [
                lax.ppermute(tail, axis, [(i, (i + 1) % count) for i in range(ends)]),
                cells,
                lax.ppermute(head, axis, [((i + 1) % count, i) for i in range(ends)]),
            ],
            axis=dim,
        )
    return cells


def band_matrix(kernel, row_count, col_count, lead):
    offset_grid = (
        lax.broadcasted_iota(jnp.int32, (row_count, col_count), 1)
        - lax.broadcasted_iota(jnp.int32, (row_count, col_count), 0)
        + lead
    )
    one_hot = (
        offset_grid[:, :, None] == jnp.arange(kernel.shape[0], dtype=jnp.int32)[None, None, :]
    ).astype(jnp.float32)
    return jnp.dot(one_hot, kernel, precision=highest)


def build_matrices(kernels, depth, tile_x, tile_y, half):
    z_mat = band_matrix(kernels[0], depth, depth, half)
    x_mat = band_matrix(kernels[1], tile_x, tile_x + 2 * half, 0)
    y_mat = band_matrix(kernels[2], tile_y, tile_y + 2 * half, 0)
    return (z_mat, x_mat, y_mat)


def apply_blur(volume, matrices, half):
    z_mat, x_mat, y_mat = matrices
    along_z = jnp.einsum("ij,jxy->ixy", z_mat, volume, precision=highest)
    extended = extended_2(along_z, (("tx", 2), ("ty", 1)), half)
    along_x = jnp.einsum("ij,zjy->ziy", x_mat, extended, precision=highest)
    return jnp.einsum("zxj,ij->zxi", along_x, y_mat, precision=highest)


def shards(raw_views, psf_taps, offsets, estimate):
    depth, tile_x, tile_y = estimate.shape
    half = psf_taps.shape[-1] // 2
    view_index = lax.axis_index("view")
    kernels = lax.dynamic_index_in_dim(psf_taps, view_index, 0, keepdims=False)
    kernels = kernels / jnp.sum(kernels, axis=-1, keepdims=True)
    forward_mats = build_matrices(kernels, depth, tile_x, tile_y, half)
    mirror_mats = build_matrices(kernels[:, ::-1], depth, tile_x, tile_y, half)
    shifts = lax.dynamic_index_in_dim(offsets, view_index, 0, keepdims=False)
    shift_x = shifts[0]
    shift_y = shifts[1]
    widened = extended_2(raw_views[0], (("tx", 2), ("ty", 1)), OMAX)
    registered = lax.dynamic_slice(
        widened, (jnp.int32(0), OMAX + shift_x, OMAX + shift_y), (depth, tile_x, tile_y)
    )
    global_x = lax.axis_index("ty") * tile_x + jnp.arange(tile_x, dtype=jnp.int32)
    global_y = lax.axis_index("tx") * tile_y + jnp.arange(tile_y, dtype=jnp.int32)
    extent_x = tile_x * lax.axis_size("ty")
    extent_y = tile_y * lax.axis_size("tx")
    inside_x = ((global_x + shift_x >= 0) & (global_x + shift_x < extent_x)).astype(jnp.float32)
    inside_y = ((global_y + shift_y >= 0) & (global_y + shift_y < extent_y)).astype(jnp.float32)
    valid_mask = jnp.broadcast_to(
        inside_x[None, :, None] * inside_y[None, None, :], (depth, tile_x, tile_y)
    )
    weight_norm = lax.psum(apply_blur(valid_mask, mirror_mats, half), "view")
    current = estimate
    for iteration in range(ITERS):
        blurred = apply_blur(current, forward_mats, half)
        ratio_field = registered / blurred
        correction = apply_blur(ratio_field, mirror_mats, half)
        summed = lax.psum(correction, "view")
        current = current * summed / weight_norm
    return current


def solution(mesh):
    placed = (P("view", None, "ty", "tx"), P(), P(), P(None, "ty", "tx"))
    return jax.shard_map(
        shards, mesh=mesh, in_specs=placed, out_specs=P(None, "ty", "tx"), check_vma=False
    )
```

profile of v0, /device:TPU:121, one launch (start us, length us, event | category | flops | bytes accessed | tf_op | source)
XLA Modules:
  0.0 408.8 jit_solution(3972751183147534993)
XLA Ops:
  7.4 2.0 fusion.28
  10.1 2.4 fusion.42
  13.8 4.7 %collective-permute-start.4 = (f32[48,32,15]{0,1,2:T(8,128)}, f32[48,32,15]{0,1,2:T(8,128)S(1)}, u32[]{:S(2)}, u32[]{:S(2)}) collective-permute-start(f32[48,32,15]{0,1,2:T(8,128)} %copy.51), channel_id=1, source_target_pairs={{0,32},{1,33},{2,34},{3,35},{4,36},{5,37},{6,38},{7,39},{8,40},{9,... | collective-permute-start | bytes 276488 | tf_op jit(solution)/shard_map/ppermute | solution.py:21
  22.3 6.2 %collective-permute-start = (f32[48,32,8]{0,2,1:T(8,128)}, f32[48,32,8]{0,2,1:T(8,128)S(1)}, u32[]{:S(2)}, u32[]{:S(2)}) collective-permute-start(f32[48,32,8]{0,2,1:T(8,128)} %copy.46), channel_id=1, source_target_pairs={{0,32},{1,33},{2,34},{3,35},{4,36},{5,37},{6,38},{7,39},{8,40},{9,... | collective-permute-start | bytes 147464 | tf_op jit(solution)/shard_map/ppermute | solution.py:21
  32.3 2.7 fusion.29
  39.3 7.0 %collective-permute-start.12 = (f32[48,32,15]{0,1,2:T(8,128)}, f32[48,32,15]{0,1,2:T(8,128)}, u32[]{:S(2)}, u32[]{:S(2)}) collective-permute-start(f32[48,32,15]{0,1,2:T(8,128)} %copy.62), channel_id=1, source_target_pairs={{0,32},{1,33},{2,34},{3,35},{4,36},{5,37},{6,38},{7,39},{8,40},{9,... | collective-permute-start | bytes 276488 | tf_op jit(solution)/shard_map/ppermute | solution.py:21
  46.7 8.1 %fusion.21 = f32[1,128,158]{0,1,2:T(8,128)} fusion(pred[128,158,31]{0,1,2:T(8,128)(4,1)S(1)} %iota_compare_fusion, f32[3,31]{1,0:T(4,128)S(1)} %bitcast_divide_fusion), kind=kOutput, calls=%fused_computation.33 | convolution fusion | flops 8150272 | bytes 716288 | tf_op jit(solution)/shard_map/dot_general | solution.py:39
  54.9 7.9 %fusion.20 = f32[1,128,158]{0,1,2:T(8,128)} fusion(pred[128,158,31]{0,1,2:T(8,128)(4,1)S(1)} %iota_compare_fusion, f32[1,31]{1,0:T(1,128)S(1)} %slice.120), kind=kOutput, calls=%fused_computation.32 | convolution fusion | flops 8150272 | bytes 707964 | tf_op jit(solution)/shard_map/dot_general | solution.py:39
  62.8 2.0 fusion.31
  64.9 2.2 copy.63
  69.1 2.5 copy.49
  71.7 2.3 pad_maximum_fusion.20
  74.0 4.5 %collective-permute-start.2 = (f32[48,8,144]{2,1,0:T(8,128)}, f32[48,8,144]{2,1,0:T(8,128)}, u32[]{:S(2)}, u32[]{:S(2)}) collective-permute-start(f32[48,8,144]{2,1,0:T(8,128)} %get-tuple-element.18), channel_id=1, source_target_pairs={{0,1},{1,2},{2,3},{3,4},{4,5},{5,6},{6,7},{7,8},{8,9},{9,10},{10,1... | collective-permute-start | bytes 663560 | tf_op jit(solution)/shard_map/ppermute | solution.py:21
  78.5 1.9 collective-permute-start.3
  81.7 2.2 copy.54
  83.9 3.2 pad_maximum_fusion.19
  87.1 6.7 %collective-permute-start.6 = (f32[48,15,158]{2,0,1:T(8,128)}, f32[48,15,158]{2,0,1:T(8,128)}, u32[]{:S(2)}, u32[]{:S(2)}) collective-permute-start(f32[48,15,158]{2,0,1:T(8,128)} %get-tuple-element.15), channel_id=1, source_target_pairs={{0,1},{1,2},{2,3},{3,4},{4,5},{5,6},{6,7},{7,8},{8,9},{9,10},{10,1... | collective-permute-start | bytes 1365128 | tf_op jit(solution)/shard_map/ppermute | solution.py:21
  93.8 2.3 collective-permute-start.7
  100.0 6.0 %copy.83 = f32[1,128,158]{1,2,0:T(8,128)S(1)} copy(f32[1,128,158]{0,1,2:T(8,128)} %fusion.21) | data formatting | bytes 161792 | tf_op jit(solution)/shard_map/dot_general | solution.py:39
  106.0 6.0 %copy.85 = f32[1,128,158]{1,2,0:T(8,128)S(1)} copy(f32[1,128,158]{0,1,2:T(8,128)} %fusion.20) | data formatting | bytes 161792 | tf_op jit(solution)/shard_map/dot_general | solution.py:39
  113.3 2.4 copy.65
  115.7 3.1 pad_maximum_fusion.13
  118.8 6.7 %collective-permute-start.14 = (f32[48,15,158]{2,0,1:T(8,128)}, f32[48,15,158]{2,0,1:T(8,128)}, u32[]{:S(2)}, u32[]{:S(2)}) collective-permute-start(f32[48,15,158]{2,0,1:T(8,128)} %get-tuple-element.19), channel_id=1, source_target_pairs={{0,1},{1,2},{2,3},{3,4},{4,5},{5,6},{6,7},{7,8},{8,9},{9,10},{10,1... | collective-permute-start | bytes 1365128 | tf_op jit(solution)/shard_map/ppermute | solution.py:21
  125.5 1.9 collective-permute-start.15
  127.4 2.8 fusion.33
  130.3 2.1 pad_maximum_fusion
  132.4 3.9 fusion.8
  136.3 1.4 fusion.22
  140.4 2.2 copy.57
  142.5 7.0 %collective-permute-start.8 = (f32[48,32,15]{0,1,2:T(8,128)}, f32[48,32,15]{0,1,2:T(8,128)}, u32[]{:S(2)}, u32[]{:S(2)}) collective-permute-start(f32[48,32,15]{0,1,2:T(8,128)} %copy.57), channel_id=1, source_target_pairs={{0,32},{1,33},{2,34},{3,35},{4,36},{5,37},{6,38},{7,39},{8,40},{9,... | collective-permute-start | bytes 276488 | tf_op jit(solution)/shard_map/ppermute | solution.py:21
  149.6 2.2 copy.58
  153.1 3.9 pad_maximum_fusion.2
  158.3 2.2 collective-permute-done.9
  162.4 6.8 %collective-permute-start.10 = (f32[48,15,158]{2,0,1:T(8,128)S(1)}, f32[48,15,158]{2,0,1:T(8,128)S(1)}, u32[]{:S(2)}, u32[]{:S(2)}) collective-permute-start(f32[48,15,158]{2,0,1:T(8,128)S(1)} %get-tuple-element.13), channel_id=1, source_target_pairs={{0,1},{1,2},{2,3},{3,4},{4,5},{5,6},{6,7},{7,8},{8,9},{9,10},{10,1... | collective-permute-start | bytes 1365128 | tf_op jit(solution)/shard_map/ppermute | solution.py:21
  169.3 1.9 collective-permute-start.11
  171.2 3.9 fusion.4
  175.1 2.3 fusion.14
  177.4 2.0 collective-permute-done.10
  179.4 7.2 %collective-permute-done.11 = f32[48,15,158]{2,0,1:T(8,128)S(1)} collective-permute-done((f32[48,15,158]{2,0,1:T(8,128)S(1)}, f32[48,15,158]{2,0,1:T(8,128)S(1)}, u32[]{:S(2)}, u32[]{:S(2)}) %collective-permute-start.11) | collective-permute-done | bytes 455072 | tf_op jit(solution)/shard_map/ppermute | solution.py:23
  187.4 3.9 fusion.6
  191.3 2.3 fusion.16
  193.9 58.7 %all-reduce.6.cloned.1.call-done = (f32[48,32,128]{2,1,0:T(8,128)}, f32[48,32,128]{2,1,0:T(8,128)}) async-done(((f32[48,32,128]{2,1,0:T(8,128)}, f32[48,32,128]{2,1,0:T(8,128)}), (f32[48,32,128]{2,1,0:T(8,128)}, f32[48,32,128]{2,1,0:T(8,128)})) %all-reduce.6.cloned.1.call-update) | async-done | bytes 1572880 | tf_op jit(solution)/shard_map/psum | solution.py:81
  252.6 1.6 multiply_divide_fusion.1
  256.6 2.2 copy.68
  258.8 5.0 %collective-permute-start.16 = (f32[48,32,15]{0,1,2:T(8,128)}, f32[48,32,15]{0,1,2:T(8,128)}, u32[]{:S(2)}, u32[]{:S(2)}) collective-permute-start(f32[48,32,15]{0,1,2:T(8,128)} %copy.68), channel_id=1, source_target_pairs={{0,32},{1,33},{2,34},{3,35},{4,36},{5,37},{6,38},{7,39},{8,40},{9,... | collective-permute-start | bytes 276488 | tf_op jit(solution)/shard_map/ppermute | solution.py:21
  266.1 2.4 collective-permute-done.16
  269.8 5.7 %collective-permute-done.17 = f32[48,32,15]{0,1,2:T(8,128)} collective-permute-done((f32[48,32,15]{0,1,2:T(8,128)}, f32[48,32,15]{0,1,2:T(8,128)}, u32[]{:S(2)}, u32[]{:S(2)}) %collective-permute-start.17) | collective-permute-done | bytes 92192 | tf_op jit(solution)/shard_map/ppermute | solution.py:23
  275.5 2.2 copy.71
  277.7 1.9 pad_maximum_fusion.10
  279.5 4.3 %collective-permute-start.18 = (f32[48,15,158]{2,0,1:T(8,128)S(1)}, f32[48,15,158]{2,0,1:T(8,128)S(1)}, u32[]{:S(2)}, u32[]{:S(2)}) collective-permute-start(f32[48,15,158]{2,0,1:T(8,128)S(1)} %get-tuple-element.11), channel_id=1, source_target_pairs={{0,1},{1,2},{2,3},{3,4},{4,5},{5,6},{6,7},{7,8},{8,9},{9,10},{10,1... | collective-permute-start | bytes 1365128 | tf_op jit(solution)/shard_map/ppermute | solution.py:21
  283.9 1.9 collective-permute-start.19
  285.8 12.4 %collective-permute-done.18 = f32[48,15,158]{2,0,1:T(8,128)S(1)} collective-permute-done((f32[48,15,158]{2,0,1:T(8,128)S(1)}, f32[48,15,158]{2,0,1:T(8,128)S(1)}, u32[]{:S(2)}, u32[]{:S(2)}) %collective-permute-start.18) | collective-permute-done | bytes 455072 | tf_op jit(solution)/shard_map/ppermute | solution.py:21
  298.2 7.2 %collective-permute-done.19 = f32[48,15,158]{2,0,1:T(8,128)S(1)} collective-permute-done((f32[48,15,158]{2,0,1:T(8,128)S(1)}, f32[48,15,158]{2,0,1:T(8,128)S(1)}, u32[]{:S(2)}, u32[]{:S(2)}) %collective-permute-start.19) | collective-permute-done | bytes 455072 | tf_op jit(solution)/shard_map/ppermute | solution.py:23
  306.1 3.9 fusion.2
  315.1 1.5 collective-permute-start.21
  318.2 5.5 %collective-permute-done.21 = f32[48,32,15]{0,1,2:T(8,128)} collective-permute-done((f32[48,32,15]{0,1,2:T(8,128)S(1)}, f32[48,32,15]{0,1,2:T(8,128)}, u32[]{:S(2)}, u32[]{:S(2)}) %collective-permute-start.21) | collective-permute-done | bytes 92192 | tf_op jit(solution)/shard_map/ppermute | solution.py:23
  325.5 1.9 collective-permute-start.22
  327.5 3.4 collective-permute-start.23
  330.8 10.7 %collective-permute-done.22 = f32[48,15,158]{2,0,1:T(8,128)S(1)} collective-permute-done((f32[48,15,158]{2,0,1:T(8,128)S(1)}, f32[48,15,158]{2,0,1:T(8,128)S(1)}, u32[]{:S(2)}, u32[]{:S(2)}) %collective-permute-start.22) | collective-permute-done | bytes 455072 | tf_op jit(solution)/shard_map/ppermute | solution.py:21
  341.5 5.2 %collective-permute-done.23 = f32[48,15,158]{2,0,1:T(8,128)S(1)} collective-permute-done((f32[48,15,158]{2,0,1:T(8,128)S(1)}, f32[48,15,158]{2,0,1:T(8,128)S(1)}, u32[]{:S(2)}, u32[]{:S(2)}) %collective-permute-start.23) | collective-permute-done | bytes 455072 | tf_op jit(solution)/shard_map/ppermute | solution.py:23
  347.5 3.9 fusion
  351.4 2.3 fusion.10
  353.7 45.5 %all-reduce.4.cloned.1.call-done = f32[48,32,128]{2,1,0:T(8,128)} async-done(((f32[48,32,128]{2,1,0:T(8,128)}), f32[48,32,128]{2,1,0:T(8,128)}) %all-reduce.4.cloned.1.call-update) | async-done | bytes 786448 | tf_op jit(solution)/shard_map/psum | solution.py:87
  399.3 2.3 multiply_divide_fusion
  (112 shorter events, 45.2 us)
Async XLA Ops:
  6.5 25.0 %copy-start = (s32[4,2]{0,1:T(2,128)S(1)}, s32[4,2]{0,1:T(2,128)}, u32[]{:S(2)}) copy-start(s32[4,2]{0,1:T(2,128)} %param.6) | copy-start | bytes 100
  6.5 246.0 %all-reduce.6.cloned.1.call-start = ((), (), s32[]{:S(2)}) async-start(), calls=%async_computation.1 | async-start | bytes 3145728 | tf_op jit(solution)/shard_map/psum | solution.py:81
  6.5 2.9 copy-start.15
  9.5 0.6 copy-start.12
  10.1 10.7 %copy-start.3 = (f32[1,48,32,128]{3,2,1,0:T(8,128)S(1)}, f32[1,48,32,128]{3,2,1,0:T(8,128)}, u32[]{:S(2)}) copy-start(f32[1,48,32,128]{3,2,1,0:T(8,128)} %param.4) | copy-start | bytes 2359300
  13.8 64.7 %collective-permute-start.4 = (f32[48,32,15]{0,1,2:T(8,128)}, f32[48,32,15]{0,1,2:T(8,128)S(1)}, u32[]{:S(2)}, u32[]{:S(2)}) collective-permute-start(f32[48,32,15]{0,1,2:T(8,128)} %copy.51), channel_id=1, source_target_pairs={{0,32},{1,33},{2,34},{3,35},{4,36},{5,37},{6,38},{7,39},{8,40},{9,... | collective-permute-start | bytes 276488 | tf_op jit(solution)/shard_map/ppermute | solution.py:21
  19.6 62.1 %collective-permute-start.5 = (f32[48,32,15]{0,1,2:T(8,128)}, f32[48,32,15]{0,1,2:T(8,128)}, u32[]{:S(2)}, u32[]{:S(2)}) collective-permute-start(f32[48,32,15]{0,1,2:T(8,128)} %copy.52), channel_id=1, source_target_pairs={{32,0},{33,1},{34,2},{35,3},{36,4},{37,5},{38,6},{39,7},{40,8},{41... | collective-permute-start | bytes 276488 | tf_op jit(solution)/shard_map/ppermute | solution.py:23
  22.3 44.8 %collective-permute-start = (f32[48,32,8]{0,2,1:T(8,128)}, f32[48,32,8]{0,2,1:T(8,128)S(1)}, u32[]{:S(2)}, u32[]{:S(2)}) collective-permute-start(f32[48,32,8]{0,2,1:T(8,128)} %copy.46), channel_id=1, source_target_pairs={{0,32},{1,33},{2,34},{3,35},{4,36},{5,37},{6,38},{7,39},{8,40},{9,... | collective-permute-start | bytes 147464 | tf_op jit(solution)/shard_map/ppermute | solution.py:21
  29.7 39.4 %collective-permute-start.1 = (f32[48,32,8]{0,2,1:T(8,128)}, f32[48,32,8]{0,2,1:T(8,128)}, u32[]{:S(2)}, u32[]{:S(2)}) collective-permute-start(f32[48,32,8]{0,2,1:T(8,128)} %copy.47), channel_id=1, source_target_pairs={{32,0},{33,1},{34,2},{35,3},{36,4},{37,5},{38,6},{39,7},{40,8},{41... | collective-permute-start | bytes 147464 | tf_op jit(solution)/shard_map/ppermute | solution.py:23
  39.3 54.4 %collective-permute-start.12 = (f32[48,32,15]{0,1,2:T(8,128)}, f32[48,32,15]{0,1,2:T(8,128)}, u32[]{:S(2)}, u32[]{:S(2)}) collective-permute-start(f32[48,32,15]{0,1,2:T(8,128)} %copy.62), channel_id=1, source_target_pairs={{0,32},{1,33},{2,34},{3,35},{4,36},{5,37},{6,38},{7,39},{8,40},{9,... | collective-permute-start | bytes 276488 | tf_op jit(solution)/shard_map/ppermute | solution.py:21
  46.4 16.5 %copy-start.16 = (s32[32,62]{1,0:T(8,128)}, s32[32,62]{1,0:T(8,128)S(1)}, u32[]{:S(2)}) copy-start(s32[32,62]{1,0:T(8,128)S(1)} %iota_subtract_fusion.1) | copy-start | bytes 23812
  46.7 8.1 %copy-start.19 = (f32[1,31]{1,0:T(1,128)S(1)}, f32[1,31]{1,0:T(1,128)}, u32[]{:S(2)}) copy-start(f32[1,31]{1,0:T(1,128)} %get-tuple-element.33) | copy-start | bytes 376
  54.9 9.9 %copy-start.18 = (f32[1,31]{1,0:T(1,128)S(1)}, f32[1,31]{1,0:T(1,128)}, u32[]{:S(2)}) copy-start(f32[1,31]{1,0:T(1,128)} %get-tuple-element.34) | copy-start | bytes 376
  67.1 46.1 %collective-permute-start.13 = (f32[48,32,15]{0,1,2:T(8,128)}, f32[48,32,15]{0,1,2:T(8,128)}, u32[]{:S(2)}, u32[]{:S(2)}) collective-permute-start(f32[48,32,15]{0,1,2:T(8,128)} %copy.63), channel_id=1, source_target_pairs={{32,0},{33,1},{34,2},{35,3},{36,4},{37,5},{38,6},{39,7},{40,8},{41... | collective-permute-start | bytes 276488 | tf_op jit(solution)/shard_map/ppermute | solution.py:23
  69.1 14.8 %copy-start.4 = (f32[48,32,8]{2,1,0:T(8,128)}, f32[48,32,8]{2,1,0:T(8,128)S(1)}, u32[]{:S(2)}) copy-start(f32[48,32,8]{2,1,0:T(8,128)S(1)} %copy.48) | copy-start | bytes 147460
  74.0 22.1 %copy-start.17 = (s32[32,62]{1,0:T(8,128)S(1)}, s32[32,62]{1,0:T(8,128)}, u32[]{:S(2)}) copy-start(s32[32,62]{1,0:T(8,128)} %copy-done.16) | copy-start | bytes 23812
  74.0 51.5 %collective-permute-start.2 = (f32[48,8,144]{2,1,0:T(8,128)}, f32[48,8,144]{2,1,0:T(8,128)}, u32[]{:S(2)}, u32[]{:S(2)}) collective-permute-start(f32[48,8,144]{2,1,0:T(8,128)} %get-tuple-element.18), channel_id=1, source_target_pairs={{0,1},{1,2},{2,3},{3,4},{4,5},{5,6},{6,7},{7,8},{8,9},{9,10},{10,1... | collective-permute-start | bytes 663560 | tf_op jit(solution)/shard_map/ppermute | solution.py:21
  78.5 48.9 %collective-permute-start.3 = (f32[48,8,144]{2,1,0:T(8,128)}, f32[48,8,144]{2,1,0:T(8,128)}, u32[]{:S(2)}, u32[]{:S(2)}) collective-permute-start(f32[48,8,144]{2,1,0:T(8,128)} %get-tuple-element.17), channel_id=1, source_target_pairs={{1,0},{2,1},{3,2},{4,3},{5,4},{6,5},{7,6},{8,7},{9,8},{10,9},{11,1... | collective-permute-start | bytes 663560 | tf_op jit(solution)/shard_map/ppermute | solution.py:23
  87.1 43.1 %collective-permute-start.6 = (f32[48,15,158]{2,0,1:T(8,128)}, f32[48,15,158]{2,0,1:T(8,128)}, u32[]{:S(2)}, u32[]{:S(2)}) collective-permute-start(f32[48,15,158]{2,0,1:T(8,128)} %get-tuple-element.15), channel_id=1, source_target_pairs={{0,1},{1,2},{2,3},{3,4},{4,5},{5,6},{6,7},{7,8},{8,9},{9,10},{10,1... | collective-permute-start | bytes 1365128 | tf_op jit(solution)/shard_map/ppermute | solution.py:21
  93.8 36.5 %collective-permute-start.7 = (f32[48,15,158]{2,0,1:T(8,128)}, f32[48,15,158]{2,0,1:T(8,128)}, u32[]{:S(2)}, u32[]{:S(2)}) collective-permute-start(f32[48,15,158]{2,0,1:T(8,128)} %get-tuple-element.16), channel_id=1, source_target_pairs={{1,0},{2,1},{3,2},{4,3},{5,4},{6,5},{7,6},{8,7},{9,8},{10,9},{11,1... | collective-permute-start | bytes 1365128 | tf_op jit(solution)/shard_map/ppermute | solution.py:23
  113.2 14.2 %copy-start.7 = (f32[48,32,15]{2,0,1:T(8,128)}, f32[48,32,15]{2,0,1:T(8,128)S(1)}, u32[]{:S(2)}) copy-start(f32[48,32,15]{2,0,1:T(8,128)S(1)} %copy.64) | copy-start | bytes 276484
  115.7 14.5 %copy-start.5 = (f32[48,32,15]{2,0,1:T(8,128)S(1)}, f32[48,32,15]{2,0,1:T(8,128)}, u32[]{:S(2)}) copy-start(f32[48,32,15]{2,0,1:T(8,128)} %copy.53) | copy-start | bytes 276484
  115.7 14.6 %copy-start.6 = (f32[48,32,15]{2,0,1:T(8,128)S(1)}, f32[48,32,15]{2,0,1:T(8,128)}, u32[]{:S(2)}) copy-start(f32[48,32,15]{2,0,1:T(8,128)} %copy.54) | copy-start | bytes 276484
  118.8 34.2 %collective-permute-start.14 = (f32[48,15,158]{2,0,1:T(8,128)}, f32[48,15,158]{2,0,1:T(8,128)}, u32[]{:S(2)}, u32[]{:S(2)}) collective-permute-start(f32[48,15,158]{2,0,1:T(8,128)} %get-tuple-element.19), channel_id=1, source_target_pairs={{0,1},{1,2},{2,3},{3,4},{4,5},{5,6},{6,7},{7,8},{8,9},{9,10},{10,1... | collective-permute-start | bytes 1365128 | tf_op jit(solution)/shard_map/ppermute | solution.py:21
  125.5 27.6 %collective-permute-start.15 = (f32[48,15,158]{2,0,1:T(8,128)}, f32[48,15,158]{2,0,1:T(8,128)}, u32[]{:S(2)}, u32[]{:S(2)}) collective-permute-start(f32[48,15,158]{2,0,1:T(8,128)} %get-tuple-element.20), channel_id=1, source_target_pairs={{1,0},{2,1},{3,2},{4,3},{5,4},{6,5},{7,6},{8,7},{9,8},{10,9},{11,1... | collective-permute-start | bytes 1365128 | tf_op jit(solution)/shard_map/ppermute | solution.py:23
  130.2 2.1 copy-start.14
  137.7 15.4 %copy-start.8 = (f32[48,32,15]{2,0,1:T(8,128)S(1)}, f32[48,32,15]{2,0,1:T(8,128)}, u32[]{:S(2)}) copy-start(f32[48,32,15]{2,0,1:T(8,128)} %copy-done.7) | copy-start | bytes 276484
  142.5 14.5 %collective-permute-start.8 = (f32[48,32,15]{0,1,2:T(8,128)}, f32[48,32,15]{0,1,2:T(8,128)}, u32[]{:S(2)}, u32[]{:S(2)}) collective-permute-start(f32[48,32,15]{0,1,2:T(8,128)} %copy.57), channel_id=1, source_target_pairs={{0,32},{1,33},{2,34},{3,35},{4,36},{5,37},{6,38},{7,39},{8,40},{9,... | collective-permute-start | bytes 276488 | tf_op jit(solution)/shard_map/ppermute | solution.py:21
  151.8 8.8 %collective-permute-start.9 = (f32[48,32,15]{0,1,2:T(8,128)}, f32[48,32,15]{0,1,2:T(8,128)}, u32[]{:S(2)}, u32[]{:S(2)}) collective-permute-start(f32[48,32,15]{0,1,2:T(8,128)} %copy.58), channel_id=1, source_target_pairs={{32,0},{33,1},{34,2},{35,3},{36,4},{37,5},{38,6},{39,7},{40,8},{41... | collective-permute-start | bytes 276488 | tf_op jit(solution)/shard_map/ppermute | solution.py:23
  161.8 9.4 %copy-start.2 = (f32[48,62,158]{2,0,1:T(8,128)S(1)}, f32[48,62,158]{2,0,1:T(8,128)}, u32[]{:S(2)}) copy-start(f32[48,62,158]{2,0,1:T(8,128)} %pad_maximum_fusion.2) | copy-start | bytes 5642500
  162.4 17.0 %collective-permute-start.10 = (f32[48,15,158]{2,0,1:T(8,128)S(1)}, f32[48,15,158]{2,0,1:T(8,128)S(1)}, u32[]{:S(2)}, u32[]{:S(2)}) collective-permute-start(f32[48,15,158]{2,0,1:T(8,128)S(1)} %get-tuple-element.13), channel_id=1, source_target_pairs={{0,1},{1,2},{2,3},{3,4},{4,5},{5,6},{6,7},{7,8},{8,9},{9,10},{10,1... | collective-permute-start | bytes 1365128 | tf_op jit(solution)/shard_map/ppermute | solution.py:21
  169.3 17.3 %collective-permute-start.11 = (f32[48,15,158]{2,0,1:T(8,128)S(1)}, f32[48,15,158]{2,0,1:T(8,128)S(1)}, u32[]{:S(2)}, u32[]{:S(2)}) collective-permute-start(f32[48,15,158]{2,0,1:T(8,128)S(1)} %get-tuple-element.14), channel_id=1, source_target_pairs={{1,0},{2,1},{3,2},{4,3},{5,4},{6,5},{7,6},{8,7},{9,8},{10,9},{11,1... | collective-permute-start | bytes 1365128 | tf_op jit(solution)/shard_map/ppermute | solution.py:23
  191.3 61.3 %copy-start.10 = (f32[48,32,128]{2,1,0:T(8,128)S(1)}, f32[48,32,128]{2,1,0:T(8,128)}, u32[]{:S(2)}) copy-start(f32[48,32,128]{2,1,0:T(8,128)} %param.7) | copy-start | bytes 2359300
  191.3 62.9 %copy-start.13 = (f32[1,48,48]{2,0,1:T(1,128)S(1)}, f32[1,48,48]{2,0,1:T(1,128)}, u32[]{:S(2)}) copy-start(f32[1,48,48]{2,0,1:T(1,128)} %copy-done.12) | copy-start | bytes 27652
  193.6 205.7 %all-reduce.4.cloned.1.call-start = ((), (), s32[]{:S(2)}) async-start(), calls=%async_computation | async-start | bytes 1572864 | tf_op jit(solution)/shard_map/psum | solution.py:87
  258.8 9.7 %collective-permute-start.16 = (f32[48,32,15]{0,1,2:T(8,128)}, f32[48,32,15]{0,1,2:T(8,128)}, u32[]{:S(2)}, u32[]{:S(2)}) collective-permute-start(f32[48,32,15]{0,1,2:T(8,128)} %copy.68), channel_id=1, source_target_pairs={{0,32},{1,33},{2,34},{3,35},{4,36},{5,37},{6,38},{7,39},{8,40},{9,... | collective-permute-start | bytes 276488 | tf_op jit(solution)/shard_map/ppermute | solution.py:21
  264.8 10.7 %collective-permute-start.17 = (f32[48,32,15]{0,1,2:T(8,128)}, f32[48,32,15]{0,1,2:T(8,128)}, u32[]{:S(2)}, u32[]{:S(2)}) collective-permute-start(f32[48,32,15]{0,1,2:T(8,128)} %copy.69), channel_id=1, source_target_pairs={{32,0},{33,1},{34,2},{35,3},{36,4},{37,5},{38,6},{39,7},{40,8},{41... | collective-permute-start | bytes 276488 | tf_op jit(solution)/shard_map/ppermute | solution.py:23
  277.7 27.7 %copy-start.9 = (f32[48,32,15]{2,0,1:T(8,128)S(1)}, f32[48,32,15]{2,0,1:T(8,128)}, u32[]{:S(2)}) copy-start(f32[48,32,15]{2,0,1:T(8,128)} %copy.71) | copy-start | bytes 276484
  279.5 18.7 %collective-permute-start.18 = (f32[48,15,158]{2,0,1:T(8,128)S(1)}, f32[48,15,158]{2,0,1:T(8,128)S(1)}, u32[]{:S(2)}, u32[]{:S(2)}) collective-permute-start(f32[48,15,158]{2,0,1:T(8,128)S(1)} %get-tuple-element.11), channel_id=1, source_target_pairs={{0,1},{1,2},{2,3},{3,4},{4,5},{5,6},{6,7},{7,8},{8,9},{9,10},{10,1... | collective-permute-start | bytes 1365128 | tf_op jit(solution)/shard_map/ppermute | solution.py:21
  283.9 21.5 %collective-permute-start.19 = (f32[48,15,158]{2,0,1:T(8,128)S(1)}, f32[48,15,158]{2,0,1:T(8,128)S(1)}, u32[]{:S(2)}, u32[]{:S(2)}) collective-permute-start(f32[48,15,158]{2,0,1:T(8,128)S(1)} %get-tuple-element.12), channel_id=1, source_target_pairs={{1,0},{2,1},{3,2},{4,3},{5,4},{6,5},{7,6},{8,7},{9,8},{10,9},{11,1... | collective-permute-start | bytes 1365128 | tf_op jit(solution)/shard_map/ppermute | solution.py:23
  313.4 4.4 %collective-permute-start.20 = (f32[48,32,15]{0,1,2:T(8,128)S(1)}, f32[48,32,15]{0,1,2:T(8,128)S(1)}, u32[]{:S(2)}, u32[]{:S(2)}) collective-permute-start(f32[48,32,15]{0,1,2:T(8,128)S(1)} %copy.74), channel_id=1, source_target_pairs={{0,32},{1,33},{2,34},{3,35},{4,36},{5,37},{6,38},{7,39},{8,40},{9,... | collective-permute-start | bytes 276488 | tf_op jit(solution)/shard_map/ppermute | solution.py:21
  315.1 8.6 %collective-permute-start.21 = (f32[48,32,15]{0,1,2:T(8,128)S(1)}, f32[48,32,15]{0,1,2:T(8,128)}, u32[]{:S(2)}, u32[]{:S(2)}) collective-permute-start(f32[48,32,15]{0,1,2:T(8,128)S(1)} %copy.75), channel_id=1, source_target_pairs={{32,0},{33,1},{34,2},{35,3},{36,4},{37,5},{38,6},{39,7},{40,8},{41... | collective-permute-start | bytes 276488 | tf_op jit(solution)/shard_map/ppermute | solution.py:23
  325.5 16.0 %collective-permute-start.22 = (f32[48,15,158]{2,0,1:T(8,128)S(1)}, f32[48,15,158]{2,0,1:T(8,128)S(1)}, u32[]{:S(2)}, u32[]{:S(2)}) collective-permute-start(f32[48,15,158]{2,0,1:T(8,128)S(1)} %get-tuple-element.9), channel_id=1, source_target_pairs={{0,1},{1,2},{2,3},{3,4},{4,5},{5,6},{6,7},{7,8},{8,9},{9,10},{10,1... | collective-permute-start | bytes 1365128 | tf_op jit(solution)/shard_map/ppermute | solution.py:21
  327.5 19.3 %collective-permute-start.23 = (f32[48,15,158]{2,0,1:T(8,128)S(1)}, f32[48,15,158]{2,0,1:T(8,128)S(1)}, u32[]{:S(2)}, u32[]{:S(2)}) collective-permute-start(f32[48,15,158]{2,0,1:T(8,128)S(1)} %get-tuple-element.10), channel_id=1, source_target_pairs={{1,0},{2,1},{3,2},{4,3},{5,4},{6,5},{7,6},{8,7},{9,8},{10,9},{11,1... | collective-permute-start | bytes 1365128 | tf_op jit(solution)/shard_map/ppermute | solution.py:23
  347.5 51.8 %copy-start.11 = (f32[48,32,128]{2,1,0:T(8,128)S(1)}, f32[48,32,128]{2,1,0:T(8,128)}, u32[]{:S(2)}) copy-start(f32[48,32,128]{2,1,0:T(8,128)} %get-tuple-element.5) | copy-start | bytes 2359300
  347.5 54.1 %copy-start.1 = (s32[4,2]{0,1:T(2,128)S(1)}, s32[4,2]{0,1:T(2,128)}, u32[]{:S(2)}) copy-start(s32[4,2]{0,1:T(2,128)} %param.6) | copy-start | bytes 100
Sparse Core Ops, SparseCore 0:
  193.7 58.7 all-reduce.5
  353.9 45.3 all-reduce.3
where the time goes:
time: 417 us; the launch traced here: 409 us
  waiting for transfers between devices  166 us (40%)
  starting transfers between devices  83.7 us (20%)
  matrix products  60.3 us (14%)
  local copies, waits for them, and re-layouts  52.6 us (13%)
  other arithmetic  29.3 us (7%)
  between operations  17.1 us (4%)
    ppermute x12, starting transfers between devices, extended_2(): lax.ppermute(tail, axis, [(i, (i + 1) % count) for i in range(ends)])  62.1 us
    psum x1, waiting for transfers between devices, shards(): weight_norm = lax.psum(apply_blur(valid_mask, mirror_mats, half), 'view')  58.7 us
    psum x1, waiting for transfers between devices, shards(): summed = lax.psum(correction, 'view')  45.5 us
    ppermute x12, waiting for transfers between devices, extended_2(): lax.ppermute(head, axis, [((i + 1) % count, i) for i in range(ends)])  33 us
    ppermute x12, waiting for transfers between devices, extended_2(): lax.ppermute(tail, axis, [(i, (i + 1) % count) for i in range(ends)])  28.7 us
    dot_general x6, matrix products, band_matrix(): return jnp.dot(one_hot, kernel, precision=highest)  24.1 us
    ppermute x12, starting transfers between devices, extended_2(): lax.ppermute(head, axis, [((i + 1) % count, i) for i in range(ends)])  21.3 us
    dot_general x5, matrix products, apply_blur(): along_x = jnp.einsum('ij,zjy->ziy', x_mat, extended, precision=highest)  19.6 us
  transfers between devices with their start and end apart: 26, of which 13 were waited for; matrix products, arithmetic and copies ran while one was open for 24% of the time, Pallas kernels for 0%

commit v1 on v0

v1 whole, which is shorter than its diff:
```python
import jax
import jax.numpy as jnp
import numpy as np
from jax import lax
from jax.experimental import pallas as pl
from jax.experimental.pallas import tpu as pltpu
from jax.sharding import PartitionSpec as P

OMAX = 8
ITERS = 2
TAPS = 31
HALF = 15
EDGE = 16
F32 = jnp.float32
BF16 = jnp.bfloat16
highest = lax.Precision.HIGHEST

NN = (((1,), (0,)), ((), ()))
NT = (((1,), (1,)), ((), ()))


def split(value):
    high = value.astype(BF16)
    low = (value - high.astype(F32)).astype(BF16)
    return high, low


def dot3(a, b, dims):
    def one(p, q):
        return lax.dot_general(p, q, dims, preferred_element_type=F32)

    return one(a[0], b[0]) + (one(a[0], b[1]) + one(a[1], b[0]))


def call(body, outs, args, scratch=(), flops=0, name=None):
    specs = [
        pl.BlockSpec(memory_space=pltpu.SMEM) if a.dtype == jnp.int32 else pl.BlockSpec(memory_space=pltpu.VMEM)
        for a in args
    ]
    outs = [jax.ShapeDtypeStruct(*o) for o in outs]
    moved = sum(int(np.prod(a.shape)) * a.dtype.itemsize for a in list(args) + outs)
    return pl.pallas_call(
        body,
        out_shape=outs,
        in_specs=specs,
        out_specs=[pl.BlockSpec(memory_space=pltpu.VMEM)] * len(outs),
        scratch_shapes=list(scratch),
        compiler_params=pltpu.CompilerParams(vmem_limit_bytes=24 << 20),
        cost_estimate=pl.CostEstimate(flops=flops, bytes_accessed=moved, transcendentals=0),
        name=name,
    )(*args)


def toeplitz(row, rows, width, shift):
    wide = jnp.broadcast_to(row[:, :width], (rows, width))
    return pltpu.roll(wide, shift % width, 1, stride=1, stride_axis=0)


def bands_body(taps, kz_h, kz_l, bx_h, bx_l, bt_h, bt_l, yf_h, yf_l, ym_h, ym_l):
    nz = kz_h.shape[1]
    for m in range(2):
        kz_h[m], kz_l[m] = split(toeplitz(taps[m : m + 1], nz, 512, 0)[:, :nz])
    lane = lax.broadcasted_iota(jnp.int32, (64, 256), 1)
    for v in range(2):
        for p in range(4):
            h, l = split(toeplitz(taps[2 + v : 3 + v], 32, 256, 64 * p + 1))
            bx_h[v, 32 * p : 32 * p + 32], bx_l[v, 32 * p : 32 * p + 32] = h, l
        h, l = split(toeplitz(taps[6 + v : 7 + v], 128, 256, -HALF))
        yf_h[128 * v : 128 * v + 128], yf_l[128 * v : 128 * v + 128] = h, l
        ym_h[v], ym_l[v] = split(toeplitz(taps[8 + v : 9 + v], 128, 256, -HALF))
    for p in range(4):
        both = jnp.zeros((64, 256), F32)
        for v in range(2):
            at = 128 * v + 32 * p
            band = toeplitz(taps[4 + v : 5 + v], 64, 256, at - 2 * HALF - 1)
            both = jnp.where((lane >= at) & (lane < at + 32), band, both)
        bt_h[64 * p : 64 * p + 64], bt_l[64 * p : 64 * p + 64] = split(both)


def placing(width, step, start):
    place = np.zeros((TAPS, width), np.float32)
    for k in range(TAPS):
        place[k, (step * (k - start)) % width] = 1
    return place


def bands(own, other, planes):
    nz = 8 * planes
    z_rows = jnp.dot(jnp.stack([own[0], own[0, ::-1]]), placing(512, 8, HALF), precision=highest)
    rows = jnp.stack([own[1], other[1], own[1, ::-1], other[1, ::-1], own[2], other[2], own[2, ::-1], other[2, ::-1]])
    taps = jnp.concatenate([z_rows, jnp.pad(rows, ((0, 6), (0, 512 - TAPS)))])
    shapes = [(2, nz, nz), (2, 128, 256), (256, 256), (256, 256), (2, 128, 256)]
    return call(bands_body, [(s, BF16) for s in shapes for _ in range(2)], [taps], name="bands")


def pack_columns(value, at, width, scratch):
    flat = value.reshape(value.shape[0] * value.shape[1], 128)
    scratch[...] = flat.T
    return scratch[pl.ds(pl.multiple_of(at, 8), width), :]


def spread_columns(pack, at, width, scratch):
    for t, part in enumerate(pack):
        scratch[pl.ds(pl.multiple_of(at, 8), width), 128 * t : 128 * t + 128] = part
    return scratch[...].T


def begin_body(info, est, raw, cur_out, pack_out, turned):
    core, tx = info[0], info[1]
    cur_out[...] = est[pl.ds(24 * core, 24)]
    for xh in range(2):
        cols = pack_columns(cur_out[:, 16 * xh : 16 * xh + 16, :], 112 * (1 - tx), 16, turned)
        for t in range(3):
            pack_out[3 * xh + t] = cols[:, 128 * t : 128 * t + 128]
    for xb in range(4):
        cols = pack_columns(raw[:, 8 * xb : 8 * xb + 8, :], 120 * (1 - tx), 8, turned)
        for t in range(3):
            pack_out[6 + 3 * (xb // 2) + t, 8 * (xb % 2) : 8 * (xb % 2) + 8, :] = cols[:, 128 * t : 128 * t + 128]


def rims_body(cur, raw, pack, ext_out, up_out, dn_out, rup_out, rdn_out):
    ext_out[...] = pack[0:6]
    up_out[0:24] = cur[:, 0:16, :]
    up_out[24:27] = pack[0:3]
    dn_out[0:24] = cur[:, 16:32, :]
    dn_out[24:27] = pack[3:6]
    rup_out[0:48] = raw[:, 0:8, :]
    rup_out[48:51] = pack[6:9, 0:8, :]
    rdn_out[0:48] = raw[:, 24:32, :]
    rdn_out[48:51] = pack[9:12, 8:16, :]


def register_body(info, raw, pack, above, below, out, wide, turned):
    tx, sx, sy = info[1], info[2], info[3]
    wide[:, 0:8, 0:128] = above[0:48]
    wide[:, 8:40, 0:128] = raw[...]
    wide[:, 40:48, 0:128] = below[0:48]
    turned[...] = jnp.zeros_like(turned)
    for b in range(6):
        if b == 0:
            parts = [above[48 + t] for t in range(3)]
        elif b == 5:
            parts = [below[48 + t] for t in range(3)]
        else:
            xb = b - 1
            parts = [pack[6 + 3 * (xb // 2) + t, 8 * (xb % 2) : 8 * (xb % 2) + 8, :] for t in range(3)]
        wide[:, 8 * b : 8 * b + 8, 128:256] = spread_columns(parts, 120 * tx, 8, turned).reshape(48, 8, 128)
    for z in range(0, 48, 4):
        rows = pltpu.roll(wide[z : z + 4], lax.rem(40 - sx, 48), 1)[:, 0:32, :]
        out[z : z + 4] = pltpu.roll(rows, lax.rem(256 - sy, 256), 2)[:, :, 0:128]


def forward_body(info, cur, ext, above, below, yf_h, yf_l, bx_h, bx_l, own, other, x_h, x_l, turned):
    tx = info[1]
    turned[...] = jnp.zeros_like(turned)
    for b in range(4):
        main = (above[0:24], cur[:, 0:16, :], cur[:, 16:32, :], below[0:24])[b]
        rim = ([above[24 + t] for t in range(3)], [ext[t] for t in range(3)],
               [ext[3 + t] for t in range(3)], [below[24 + t] for t in range(3)])[b]
        at = slice(16 * b, 16 * b + 16)
        x_h[:, at, 0:128], x_l[:, at, 0:128] = split(main)
        side = spread_columns(rim, 112 * tx, 16, turned).reshape(24, 16, 128)
        x_h[:, at, 128:256], x_l[:, at, 128:256] = split(side)
    yf = (yf_h[...], yf_l[...])
    for g in range(6):
        z = slice(4 * g, 4 * g + 4)
        rows = (x_h[z].reshape(256, 256), x_l[z].reshape(256, 256))
        along_y = split(dot3(rows, yf, NT))
        for v, out in ((0, own), (1, other)):
            cols = slice(128 * v, 128 * v + 128)
            part = (along_y[0][:, cols], along_y[1][:, cols])
            out[z] = dot3((bx_h[v], bx_l[v]), part, NN).reshape(4, 32, 128)


def ratio_body(info, mine, theirs, seen, kz_h, kz_l, keep, send, side_keep, side_send, full, turned):
    core, tx = info[0], info[1]
    full[pl.ds(24 * core, 24)] = mine[...]
    full[pl.ds(24 * (1 - core), 24)] = theirs[...]
    for xp in range(2):
        def pair(ref):
            return jnp.concatenate(
                [ref[:, 16 * xp + 8 * i : 16 * xp + 8 * i + 8, :].reshape(384, 128) for i in range(2)], axis=1
            )
        blurred = dot3((kz_h[0], kz_l[0]), split(pair(full)), NN)
        ratio = pair(seen) / blurred
        turned_back = dot3((kz_h[1], kz_l[1]), split(ratio), NN)
        for i in range(2):
            at = slice(16 * xp + 8 * i, 16 * xp + 8 * i + 8)
            full[:, at, :] = turned_back[:, 128 * i : 128 * i + 128].reshape(48, 8, 128)
    for half, out, side in ((core, keep, side_keep), (1 - core, send, side_send)):
        out[...] = full[pl.ds(24 * half, 24)]
        for xh in range(2):
            cols = pack_columns(out[:, 16 * xh : 16 * xh + 16, :], 112 * (1 - tx), 16, turned)
            for t in range(3):
                side[3 * xh + t] = cols[:, 128 * t : 128 * t + 128]


def mirror_body(info, own, other, side_own, side_other, ym_h, ym_l, bt_h, bt_l, up, mid, dn, x_h, x_l, turned):
    tx = info[1]
    turned[...] = jnp.zeros_like(turned)
    for v, main, side in ((0, own, side_own), (1, other, side_other)):
        x_h[v, :, :, 0:128], x_l[v, :, :, 0:128] = split(main[...])
        for xh in range(2):
            at = slice(16 * xh, 16 * xh + 16)
            cols = spread_columns([side[3 * xh + t] for t in range(3)], 112 * tx, 16, turned).reshape(24, 16, 128)
            x_h[v, :, at, 128:256], x_l[v, :, at, 128:256] = split(cols)
    for g in range(6):
        z = slice(4 * g, 4 * g + 4)
        along_y = [
            split(dot3((x_h[v, z].reshape(128, 256), x_l[v, z].reshape(128, 256)), (ym_h[v], ym_l[v]), NT))
            for v in range(2)
        ]
        both = tuple(jnp.concatenate([along_y[0][i], along_y[1][i]], axis=0) for i in range(2))
        wide = dot3((bt_h[...], bt_l[...]), both, NN).reshape(4, 64, 128)
        up[z] = wide[:, 0:16, :]
        mid[z] = wide[:, 16:48, :]
        dn[z] = wide[:, 48:64, :]


def gather_body(info, mid, above, below, out, side, turned):
    tx = info[1]
    out[:, 0:16, :] = mid[:, 0:16, :] + above[...]
    out[:, 16:32, :] = mid[:, 16:32, :] + below[...]
    for xh in range(2):
        cols = pack_columns(out[:, 16 * xh : 16 * xh + 16, :], 112 * (1 - tx), 16, turned)
        for t in range(3):
            side[3 * xh + t] = cols[:, 128 * t : 128 * t + 128]


def update_body(mine, theirs, cur, norm, ext, side_a, side_b, norm_ext, cur_out, ext_out, up_out, dn_out):
    cur_out[...] = cur[...] * (mine[...] + theirs[...]) / norm[...]
    ext_out[...] = ext[...] * (side_a[...] + side_b[...]) / norm_ext[...]
    up_out[0:24] = cur_out[:, 0:16, :]
    up_out[24:27] = ext_out[0:3]
    dn_out[0:24] = cur_out[:, 16:32, :]
    dn_out[24:27] = ext_out[3:6]


def last_body(mine, theirs, cur, norm, cur_out):
    cur_out[...] = cur[...] * (mine[...] + theirs[...]) / norm[...]


def whole_body(info, mine, theirs, out):
    core = info[0]
    out[pl.ds(24 * core, 24)] = mine[...]
    out[pl.ds(24 * (1 - core), 24)] = theirs[...]


def window_sums(taps, first, count, shift, extent):
    place = first + lax.broadcasted_iota(jnp.int32, (1, count, TAPS), 1) + lax.broadcasted_iota(jnp.int32, (1, count, TAPS), 2) - HALF
    moved = place + shift[:, None, None]
    inside = (place >= 0) & (place < extent) & (moved >= 0) & (moved < extent)
    return jnp.sum(jnp.where(inside, taps[:, None, :], 0.0), axis=-1)


def norms(kernels, offsets, core, tx, ty, depth, tile_x, tile_y, nx, ny):
    mirrored = kernels[:, :, ::-1]
    zero = jnp.zeros_like(offsets[:, 0])
    part_z = window_sums(mirrored[:, 0], core * (depth // 2), depth // 2, zero, depth)
    part_x = window_sums(mirrored[:, 1], ty * tile_x, tile_x, offsets[:, 0], nx)
    part_y = window_sums(mirrored[:, 2], tx * tile_y, tile_y, offsets[:, 1], ny)
    part_e = window_sums(mirrored[:, 2], tile_y - EDGE * tx, EDGE, offsets[:, 1], ny)
    zx = part_z[:, :, None] * part_x[:, None, :]
    views = kernels.shape[0]
    norm = sum(zx[v][:, :, None] * part_y[v][None, None, :] for v in range(views))
    flat = jnp.stack([zx[:, :, :EDGE].reshape(views, 3, 128), zx[:, :, EDGE:].reshape(views, 3, 128)], axis=1)
    flat = flat.reshape(views, 6, 128)
    norm_ext = sum(flat[v][:, None, :] * part_e[v][None, :, None] for v in range(views))
    return norm, norm_ext


def swap(value, axis, by, sizes):
    count = int(np.prod(sizes))
    return lax.ppermute(value, axis, [(i, i ^ by) for i in range(count)])


def shards(raw_views, psf_taps, offsets, estimate):
    depth, tile_x, tile_y = estimate.shape
    half = depth // 2
    view, tx, ty = (lax.axis_index(a) for a in ("view", "tx", "ty"))
    core = view % 2
    rows = lax.axis_size("ty")
    lower = [(i, i + 1) for i in range(rows - 1)]
    upper = [(i + 1, i) for i in range(rows - 1)]
    raw = raw_views[0]

    shifts = lax.dynamic_index_in_dim(offsets, view, 0, keepdims=False)
    info = jnp.stack([core, tx, shifts[0], shifts[1]]).astype(jnp.int32)

    tile_half = (half, tile_x, tile_y)
    pack = (6, EDGE, 128)
    turned = pltpu.VMEM((128, 384), F32)

    cur, sides = call(begin_body, [(tile_half, F32), ((12, EDGE, 128), F32)], [info, estimate, raw], [turned], name="begin")
    sides = swap(sides, "tx", 1, (2,))

    kernels = psf_taps / jnp.sum(psf_taps, axis=-1, keepdims=True)
    own = lax.dynamic_index_in_dim(kernels, view, 0, keepdims=False)
    other = lax.dynamic_index_in_dim(kernels, view ^ 1, 0, keepdims=False)
    kz_h, kz_l, bx_h, bx_l, bt_h, bt_l, yf_h, yf_l, ym_h, ym_l = bands(own, other, depth)
    norm, norm_ext = norms(
        kernels, offsets, core, tx, ty, depth, tile_x, tile_y, tile_x * rows, tile_y * lax.axis_size("tx")
    )

    rim = (half + 3, EDGE, 128)
    raw_rim = (depth + 3, OMAX, 128)
    ext, up, dn, raw_up, raw_dn = call(
        rims_body, [(pack, F32), (rim, F32), (rim, F32), (raw_rim, F32), (raw_rim, F32)], [cur, raw, sides], name="rims"
    )
    above = lax.ppermute(dn, "ty", lower)
    below = lax.ppermute(up, "ty", upper)
    raw_above = lax.ppermute(raw_dn, "ty", lower)
    raw_below = lax.ppermute(raw_up, "ty", upper)
    seen = None

    for iteration in range(ITERS):
        mine, theirs = call(
            forward_body,
            [(tile_half, F32), (tile_half, F32)],
            [info, cur, ext, above, below, yf_h, yf_l, bx_h, bx_l],
            [pltpu.VMEM((half, 64, 256), BF16), pltpu.VMEM((half, 64, 256), BF16), turned],
            flops=3 * 2 * (1536 * 256 * 256 + 12 * 128 * 256 * 128),
            name="forward",
        )
        theirs = swap(theirs, "view", 1, (4,))
        if seen is None:
            (seen,) = call(
                register_body,
                [((depth, tile_x, tile_y), F32)],
                [info, raw, sides, raw_above, raw_below],
                [pltpu.VMEM((depth, tile_x + 2 * OMAX, 256), F32), turned],
                name="register",
            )
        keep, send, side_keep, side_send = call(
            ratio_body,
            [(tile_half, F32), (tile_half, F32), (pack, F32), (pack, F32)],
            [info, mine, theirs, seen, kz_h, kz_l],
            [pltpu.VMEM((depth, tile_x, tile_y), F32), turned],
            flops=3 * 2 * 2 * 384 * 384 * 512,
            name="ratio",
        )
        send = swap(send, "view", 1, (4,))
        side_keep = swap(side_keep, "tx", 1, (2,))
        side_send = swap(side_send, ("view", "tx"), 3, (4, 2))
        up_part, mid, dn_part = call(
            mirror_body,
            [((half, EDGE, tile_y), F32), (tile_half, F32), ((half, EDGE, tile_y), F32)],
            [info, keep, send, side_keep, side_send, ym_h, ym_l, bt_h, bt_l],
            [pltpu.VMEM((2, half, 32, 256), BF16), pltpu.VMEM((2, half, 32, 256), BF16), turned],
            flops=3 * 2 * (1536 * 256 * 128 + 6 * 256 * 256 * 128),
            name="mirror",
        )
        from_above = lax.ppermute(dn_part, "ty", lower)
        from_below = lax.ppermute(up_part, "ty", upper)
        summed, side = call(
            gather_body, [(tile_half, F32), (pack, F32)], [info, mid, from_above, from_below], [turned], name="gather"
        )
        partner = swap(summed, "view", 2, (4,))
        if iteration == ITERS - 1:
            (cur,) = call(last_body, [(tile_half, F32)], [summed, partner, cur, norm], name="last")
        else:
            side_a = swap(side, "tx", 1, (2,))
            side_b = swap(side, ("view", "tx"), 5, (4, 2))
            cur, ext, up, dn = call(
                update_body,
                [(tile_half, F32), (pack, F32), (rim, F32), (rim, F32)],
                [summed, partner, cur, norm, ext, side_a, side_b, norm_ext],
                name="update",
            )
            above = lax.ppermute(dn, "ty", lower)
            below = lax.ppermute(up, "ty", upper)
    far = swap(cur, "view", 1, (4,))
    (out,) = call(whole_body, [((depth, tile_x, tile_y), F32)], [info, cur, far], name="whole")
    return out


def solution(mesh):
    placed = (P("view", None, "ty", "tx"), P(), P(), P(None, "ty", "tx"))
    return jax.shard_map(
        shards, mesh=mesh, in_specs=placed, out_specs=P(None, "ty", "tx"), check_vma=False
    )
```

time: 417 us -> 160 us (0.38); the launches traced: 409 us -> 159 us
  waiting for transfers between devices: 166 us -> 60 us
  matrix products: 60.3 us -> 0.15 us
  local copies, waits for them, and re-layouts: 52.6 us -> 17.7 us
  starting transfers between devices: 83.7 us -> 50.9 us
  Pallas kernels: 0 us -> 25.5 us
  other arithmetic: 29.3 us -> 4.13 us
  between operations: 17.1 us -> 0.57 us
    psum x2 -> x0, waiting for transfers between devices: 104 us -> none  [the longest x1 58.7 us: shards(): weight_norm = lax.psum(apply_blur(valid_mask, mirror_mats, half), 'view')]
    dot_general x21 -> x1, matrix products: 60.3 us -> 0.15 us  [bands(): jnp.dot(jnp.stack([own[0], own[0, ::-1]]), placing(512, 8, HALF), precisi...]
    ppermute x24, starting transfers between devices: 83.4 us -> 50.9 us  [the longest x14 23.3 us: swap(): return lax.ppermute(value, axis, [(i, i ^ by) for i in range(count)])]
    pallas_call x0 -> x15, Pallas kernels: none -> 25.5 us  [call(): pl.pallas_call(body, out_shape=outs, in_specs=specs, out_specs=[pl.BlockS...]
    slice x23 -> x8, local copies, waits for them, and re-layouts: 21.9 us -> 1.56 us  [the longest x1 0.62 us: norms(): flat[v][:, None, :] * part_e[v][None, :, None]]
    ppermute x12 -> x0, local copies, waits for them, and re-layouts: 18 us -> none  [the longest x6 11.9 us: extended_2(): lax.ppermute(head, axis, [((i + 1) % count, i) for i in range(ends)])]
    concatenate x7 -> x1, other arithmetic: 13.4 us -> 0.01 us  [bands(): taps = jnp.concatenate([z_rows, jnp.pad(rows, ((0, 6), (0, 512 - TAPS)))])]
    dot_general x2 -> x0, local copies, waits for them, and re-layouts: 12 us -> none  [band_matrix(): return jnp.dot(one_hot, kernel, precision=highest)]
  transfers between devices with their start and end apart: 26 -> 24, of which waited for: 13 -> 18; matrix products, arithmetic and copies ran while one was open for 24% -> 5% of each run, Pallas kernels for 0% -> 1%
where the time goes in v1:
time: 160 us; the launch traced here: 159 us
  waiting for transfers between devices  60 us (38%)
  starting transfers between devices  50.9 us (32%)
  Pallas kernels  25.5 us (16%)
  local copies, waits for them, and re-layouts  17.7 us (11%)
  other arithmetic  4.13 us (3%)
    pallas_call x15, Pallas kernels, call(): pl.pallas_call(body, out_shape=outs, in_specs=specs, out_specs=[pl.BlockS...  25.5 us
    ppermute x14, starting transfers between devices, swap(): return lax.ppermute(value, axis, [(i, i ^ by) for i in range(count)])  23.3 us
    ppermute x14, waiting for transfers between devices, swap(): return lax.ppermute(value, axis, [(i, i ^ by) for i in range(count)])  23 us
    ppermute x2, waiting for transfers between devices, shards(): below = lax.ppermute(up, 'ty', upper)  12.4 us
    unnamed x95, local copies, waits for them, and re-layouts  11.9 us
    ppermute x2, waiting for transfers between devices, shards(): from_below = lax.ppermute(up_part, 'ty', upper)  10.5 us
    ppermute x2, starting transfers between devices, shards(): from_below = lax.ppermute(up_part, 'ty', upper)  6.9 us
    ppermute x2, starting transfers between devices, shards(): above = lax.ppermute(dn, 'ty', lower)  6.32 us
  transfers between devices with their start and end apart: 24, of which 18 were waited for; matrix products, arithmetic and copies ran while one was open for 5% of the time, Pallas kernels for 1%

profile of v1, /device:TPU:121, one launch (start us, length us, event | category | flops | bytes accessed | tf_op | source)
XLA Modules:
  0.0 158.9 jit_solution(8094122907572573462)
XLA Ops:
  0.0 0.7 copy-done.38
  1.3 1.3 pad_add_fusion.info
  2.7 1.1 copy-done
  3.8 1.1 copy-done.2
  4.9 0.9 begin.1
  5.9 2.8 %collective-permute-start = (f32[12,16,128]{2,1,0:T(8,128)S(1)}, f32[12,16,128]{2,1,0:T(8,128)S(1)}, u32[]{:S(2)}, u32[]{:S(2)}) collective-permute-start(f32[12,16,128]{2,1,0:T(8,128)S(1)} %get-tuple-element.48), channel_id=1, source_target_pairs={{0,32},{32,0},{1,33},{33,1},{2,34},{34,2},{3,35},{35,3},{4,36},{36... | collective-permute-start | bytes 294920 | tf_op jit(solution)/shard_map/ppermute | solution.py:274
  14.4 4.4 %collective-permute-start.1 = (f32[27,16,128]{2,1,0:T(8,128)S(1)}, f32[27,16,128]{2,1,0:T(8,128)S(1)}, u32[]{:S(2)}, u32[]{:S(2)}) collective-permute-start(f32[27,16,128]{2,1,0:T(8,128)S(1)} %get-tuple-element.50), channel_id=1, source_target_pairs={{0,1},{1,2},{2,3},{3,4},{4,5},{5,6},{6,7},{7,8},{8,9},{9,10},{10,1... | collective-permute-start | bytes 663560 | tf_op jit(solution)/shard_map/ppermute | solution.py:310
  18.8 1.9 %collective-permute-start.2 = (f32[27,16,128]{2,1,0:T(8,128)S(1)}, f32[27,16,128]{2,1,0:T(8,128)S(1)}, u32[]{:S(2)}, u32[]{:S(2)}) collective-permute-start(f32[27,16,128]{2,1,0:T(8,128)S(1)} %get-tuple-element.51), channel_id=1, source_target_pairs={{1,0},{2,1},{3,2},{4,3},{5,4},{6,5},{7,6},{8,7},{9,8},{10,9},{11,1... | collective-permute-start | bytes 663560 | tf_op jit(solution)/shard_map/ppermute | solution.py:311
  20.7 0.7 add_add_fusion.3
  21.4 1.1 collective-permute-done.1.above
  22.5 7.1 %collective-permute-done.2.below = f32[27,16,128]{2,1,0:T(8,128)S(1)} collective-permute-done((f32[27,16,128]{2,1,0:T(8,128)S(1)}, f32[27,16,128]{2,1,0:T(8,128)S(1)}, u32[]{:S(2)}, u32[]{:S(2)}) %collective-permute-start.2) | collective-permute-done | bytes 221216 | tf_op jit(solution)/shard_map/ppermute | solution.py:311
  29.7 3.5 %forward.2 = (f32[24,32,128]{2,1,0:T(8,128)S(1)}, f32[24,32,128]{2,1,0:T(8,128)}) custom-call(s32[4]{0:T(128)S(1)} %pad_add_fusion.info, f32[24,32,128]{2,1,0:T(8,128)S(1)} %get-tuple-element.47.cur, f32[6,16,128]{2,1,0:T(8,128)S(1)} %get-tuple-element.49.ext, f32[27,16,128]{2,1,0:T(8,128)S(1)} %collective-permute-done.1.above, ...), custom_call_target="tpu_custom_call" | custom-call | flops 905969664 | bytes 2195472 | tf_op jit(solution)/shard_map/forward/pallas_call | solution.py:42
  33.2 0.8 copy-done.21
  34.0 2.2 %collective-permute-start.3 = (f32[24,32,128]{2,1,0:T(8,128)}, f32[24,32,128]{2,1,0:T(8,128)}, u32[]{:S(2)}, u32[]{:S(2)}) collective-permute-start(f32[24,32,128]{2,1,0:T(8,128)} %get-tuple-element.57), channel_id=1, source_target_pairs={{0,64},{64,0},{128,192},{192,128},{1,65},{65,1},{129,193},{193,129... | collective-permute-start | bytes 1179656 | tf_op jit(solution)/shard_map/ppermute | solution.py:274
  36.8 0.7 copy-done.37
  37.6 1.9 %collective-permute-start.4 = (f32[51,8,128]{2,1,0:T(8,128)S(1)}, f32[51,8,128]{2,1,0:T(8,128)S(1)}, u32[]{:S(2)}, u32[]{:S(2)}) collective-permute-start(f32[51,8,128]{2,1,0:T(8,128)S(1)} %get-tuple-element.58), channel_id=1, source_target_pairs={{0,1},{1,2},{2,3},{3,4},{4,5},{5,6},{6,7},{7,8},{8,9},{9,10},{10,1... | collective-permute-start | bytes 626696 | tf_op jit(solution)/shard_map/ppermute | solution.py:312
  39.5 3.4 %collective-permute-start.5 = (f32[51,8,128]{2,1,0:T(8,128)S(1)}, f32[51,8,128]{2,1,0:T(8,128)S(1)}, u32[]{:S(2)}, u32[]{:S(2)}) collective-permute-start(f32[51,8,128]{2,1,0:T(8,128)S(1)} %get-tuple-element.59), channel_id=1, source_target_pairs={{1,0},{2,1},{3,2},{4,3},{5,4},{6,5},{7,6},{8,7},{9,8},{10,9},{11,1... | collective-permute-start | bytes 626696 | tf_op jit(solution)/shard_map/ppermute | solution.py:313
  43.5 2.2 %collective-permute-done.4.above = f32[51,8,128]{2,1,0:T(8,128)S(1)} collective-permute-done((f32[51,8,128]{2,1,0:T(8,128)S(1)}, f32[51,8,128]{2,1,0:T(8,128)S(1)}, u32[]{:S(2)}, u32[]{:S(2)}) %collective-permute-start.4) | collective-permute-done | bytes 208928 | tf_op jit(solution)/shard_map/ppermute | solution.py:312
  45.7 5.2 %collective-permute-done.5.below = f32[51,8,128]{2,1,0:T(8,128)S(1)} collective-permute-done((f32[51,8,128]{2,1,0:T(8,128)S(1)}, f32[51,8,128]{2,1,0:T(8,128)S(1)}, u32[]{:S(2)}, u32[]{:S(2)}) %collective-permute-start.5) | collective-permute-done | bytes 208928 | tf_op jit(solution)/shard_map/ppermute | solution.py:313
  50.9 1.4 register.1.seen
  52.4 3.4 %ratio.2 = (f32[24,32,128]{2,1,0:T(8,128)S(1)}, f32[24,32,128]{2,1,0:T(8,128)S(1)}, f32[6,16,128]{2,1,0:T(8,128)S(1)}, f32[6,16,128]{2,1,0:T(8,128)S(1)}) custom-call(s32[4]{0:T(128)S(1)} %pad_add_fusion.info, f32[24,32,128]{2,1,0:T(8,128)S(1)} %copy-done.22, f32[24,32,128]{2,1,0:T(8,128)} %collective-permute-done.3.theirs, ...), custom_call_target="tpu_custom_call" | custom-call | flops 905969664 | bytes 3637264 | tf_op jit(solution)/shard_map/ratio/pallas_call | solution.py:42
  55.8 0.7 copy-done.23
  56.5 1.4 collective-permute-start.6
  58.9 2.9 %collective-permute-start.8 = (f32[6,16,128]{2,1,0:T(8,128)S(1)}, f32[6,16,128]{2,1,0:T(8,128)S(1)}, u32[]{:S(2)}, u32[]{:S(2)}) collective-permute-start(f32[6,16,128]{2,1,0:T(8,128)S(1)} %get-tuple-element.65), channel_id=1, source_target_pairs={{0,96},{32,64},{64,32},{96,0},{128,224},{160,192},{192,160},{224,1... | collective-permute-start | bytes 147464 | tf_op jit(solution)/shard_map/ppermute | solution.py:274
  62.0 0.7 mul.184
  62.7 0.7 mul.199
  63.4 0.7 copy-done.35
  64.0 0.6 collective-permute-done.8.side_other
  64.7 0.9 copy-done.6
  65.6 0.9 copy-done.9
  66.5 0.9 copy-done.12
  67.4 1.0 copy-done.24
  68.4 3.1 %mirror.2 = (f32[24,16,128]{2,1,0:T(8,128)S(1)}, f32[24,32,128]{2,1,0:T(8,128)S(1)}, f32[24,16,128]{2,1,0:T(8,128)S(1)}) custom-call(s32[4]{0:T(128)S(1)} %pad_add_fusion.info, f32[24,32,128]{2,1,0:T(8,128)S(1)} %copy-done.24, f32[24,32,128]{2,1,0:T(8,128)S(1)} %collective-permute-done.6.other, f32[6,16,128]{2,1,0:T(8,128)S(1)} %collective-permute-done.7.side_own, ...), custom_call_target="tpu_custom_call" | custom-call | flops 603979776 | bytes 2195472 | tf_op jit(solution)/shard_map/mirror/pallas_call | solution.py:42
  71.5 1.9 %collective-permute-start.9 = (f32[24,16,128]{2,1,0:T(8,128)S(1)}, f32[24,16,128]{2,1,0:T(8,128)S(1)}, u32[]{:S(2)}, u32[]{:S(2)}) collective-permute-start(f32[24,16,128]{2,1,0:T(8,128)S(1)} %get-tuple-element.71), channel_id=1, source_target_pairs={{0,1},{1,2},{2,3},{3,4},{4,5},{5,6},{6,7},{7,8},{8,9},{9,10},{10,1... | collective-permute-start | bytes 589832 | tf_op jit(solution)/shard_map/ppermute | solution.py:353
  73.5 3.5 %collective-permute-start.10 = (f32[24,16,128]{2,1,0:T(8,128)S(1)}, f32[24,16,128]{2,1,0:T(8,128)S(1)}, u32[]{:S(2)}, u32[]{:S(2)}) collective-permute-start(f32[24,16,128]{2,1,0:T(8,128)S(1)} %get-tuple-element.72), channel_id=1, source_target_pairs={{1,0},{2,1},{3,2},{4,3},{5,4},{6,5},{7,6},{8,7},{9,8},{10,9},{11,1... | collective-permute-start | bytes 589832 | tf_op jit(solution)/shard_map/ppermute | solution.py:354
  78.2 1.4 collective-permute-done.9.above
  79.6 5.2 %collective-permute-done.10.below = f32[24,16,128]{2,1,0:T(8,128)S(1)} collective-permute-done((f32[24,16,128]{2,1,0:T(8,128)S(1)}, f32[24,16,128]{2,1,0:T(8,128)S(1)}, u32[]{:S(2)}, u32[]{:S(2)}) %collective-permute-start.10) | collective-permute-done | bytes 196640 | tf_op jit(solution)/shard_map/ppermute | solution.py:354
  84.9 0.7 gather.2
  86.2 1.8 %collective-permute-start.13 = (f32[6,16,128]{2,1,0:T(8,128)S(1)}, f32[6,16,128]{2,1,0:T(8,128)S(1)}, u32[]{:S(2)}, u32[]{:S(2)}) collective-permute-start(f32[6,16,128]{2,1,0:T(8,128)S(1)} %get-tuple-element.74), channel_id=1, source_target_pairs={{0,160},{32,128},{64,224},{96,192},{128,32},{160,0},{192,96},{224,... | collective-permute-start | bytes 147464 | tf_op jit(solution)/shard_map/ppermute | solution.py:274
  88.0 1.0 collective-permute-start.12
  89.1 1.2 collective-permute-done.13.side_b
  90.3 7.0 %collective-permute-done.12.side_a = f32[6,16,128]{2,1,0:T(8,128)S(1)} collective-permute-done((f32[6,16,128]{2,1,0:T(8,128)S(1)}, f32[6,16,128]{2,1,0:T(8,128)S(1)}, u32[]{:S(2)}, u32[]{:S(2)}) %collective-permute-start.12) | collective-permute-done | bytes 49184 | tf_op jit(solution)/shard_map/ppermute | solution.py:274
  97.4 1.9 %collective-permute-start.14 = (f32[27,16,128]{2,1,0:T(8,128)S(1)}, f32[27,16,128]{2,1,0:T(8,128)S(1)}, u32[]{:S(2)}, u32[]{:S(2)}) collective-permute-start(f32[27,16,128]{2,1,0:T(8,128)S(1)} %get-tuple-element.77), channel_id=1, source_target_pairs={{0,1},{1,2},{2,3},{3,4},{4,5},{5,6},{6,7},{7,8},{8,9},{9,10},{10,1... | collective-permute-start | bytes 663560 | tf_op jit(solution)/shard_map/ppermute | solution.py:370
  99.4 3.4 %collective-permute-start.15 = (f32[27,16,128]{2,1,0:T(8,128)S(1)}, f32[27,16,128]{2,1,0:T(8,128)S(1)}, u32[]{:S(2)}, u32[]{:S(2)}) collective-permute-start(f32[27,16,128]{2,1,0:T(8,128)S(1)} %get-tuple-element.78), channel_id=1, source_target_pairs={{1,0},{2,1},{3,2},{4,3},{5,4},{6,5},{7,6},{8,7},{9,8},{10,9},{11,1... | collective-permute-start | bytes 663560 | tf_op jit(solution)/shard_map/ppermute | solution.py:371
  102.7 1.4 collective-permute-done.14.above
  104.1 5.2 %collective-permute-done.15.below = f32[27,16,128]{2,1,0:T(8,128)S(1)} collective-permute-done((f32[27,16,128]{2,1,0:T(8,128)S(1)}, f32[27,16,128]{2,1,0:T(8,128)S(1)}, u32[]{:S(2)}, u32[]{:S(2)}) %collective-permute-start.15) | collective-permute-done | bytes 221216 | tf_op jit(solution)/shard_map/ppermute | solution.py:371
  109.4 2.7 %forward.3 = (f32[24,32,128]{2,1,0:T(8,128)S(1)}, f32[24,32,128]{2,1,0:T(8,128)S(1)}) custom-call(s32[4]{0:T(128)S(1)} %pad_add_fusion.info, f32[24,32,128]{2,1,0:T(8,128)S(1)} %get-tuple-element.75.cur, f32[6,16,128]{2,1,0:T(8,128)S(1)} %get-tuple-element.76.ext, f32[27,16,128]{2,1,0:T(8,128)S(1)} %collective-permute-done.14.above, ...), custom_call_target="tpu_custom_call" | custom-call | flops 905969664 | bytes 2195472 | tf_op jit(solution)/shard_map/forward/pallas_call | solution.py:42
  112.1 3.7 %collective-permute-start.16 = (f32[24,32,128]{2,1,0:T(8,128)S(1)}, f32[24,32,128]{2,1,0:T(8,128)S(1)}, u32[]{:S(2)}, u32[]{:S(2)}) collective-permute-start(f32[24,32,128]{2,1,0:T(8,128)S(1)} %get-tuple-element.80), channel_id=1, source_target_pairs={{0,64},{64,0},{128,192},{192,128},{1,65},{65,1},{129,193},{193,129... | collective-permute-start | bytes 1179656 | tf_op jit(solution)/shard_map/ppermute | solution.py:274
  115.8 1.3 collective-permute-done.16.theirs
  117.1 3.0 %ratio.3 = (f32[24,32,128]{2,1,0:T(8,128)S(1)}, f32[24,32,128]{2,1,0:T(8,128)S(1)}, f32[6,16,128]{2,1,0:T(8,128)S(1)}, f32[6,16,128]{2,1,0:T(8,128)S(1)}) custom-call(s32[4]{0:T(128)S(1)} %pad_add_fusion.info, f32[24,32,128]{2,1,0:T(8,128)S(1)} %get-tuple-element.79.mine, f32[24,32,128]{2,1,0:T(8,128)S(1)} %collective-permute-done.16.theirs, ...), custom_call_target="tpu_custom_call" | custom-call | flops 905969664 | bytes 3637264 | tf_op jit(solution)/shard_map/ratio/pallas_call | solution.py:42
  121.1 2.8 %collective-permute-start.19 = (f32[6,16,128]{2,1,0:T(8,128)S(1)}, f32[6,16,128]{2,1,0:T(8,128)S(1)}, u32[]{:S(2)}, u32[]{:S(2)}) collective-permute-start(f32[6,16,128]{2,1,0:T(8,128)S(1)} %get-tuple-element.84), channel_id=1, source_target_pairs={{0,96},{32,64},{64,32},{96,0},{128,224},{160,192},{192,160},{224,1... | collective-permute-start | bytes 147464 | tf_op jit(solution)/shard_map/ppermute | solution.py:274
  123.8 1.2 collective-permute-done.18.side_own
  125.0 1.7 %collective-permute-done.19.side_other = f32[6,16,128]{2,1,0:T(8,128)S(1)} collective-permute-done((f32[6,16,128]{2,1,0:T(8,128)S(1)}, f32[6,16,128]{2,1,0:T(8,128)S(1)}, u32[]{:S(2)}, u32[]{:S(2)}) %collective-permute-start.19) | collective-permute-done | bytes 49184 | tf_op jit(solution)/shard_map/ppermute | solution.py:274
  126.7 3.1 %mirror.3 = (f32[24,16,128]{2,1,0:T(8,128)S(1)}, f32[24,32,128]{2,1,0:T(8,128)S(1)}, f32[24,16,128]{2,1,0:T(8,128)S(1)}) custom-call(s32[4]{0:T(128)S(1)} %pad_add_fusion.info, f32[24,32,128]{2,1,0:T(8,128)S(1)} %get-tuple-element.81.own, f32[24,32,128]{2,1,0:T(8,128)S(1)} %collective-permute-done.17.other, ...), custom_call_target="tpu_custom_call" | custom-call | flops 603979776 | bytes 2195472 | tf_op jit(solution)/shard_map/mirror/pallas_call | solution.py:42
  129.8 1.9 %collective-permute-start.20 = (f32[24,16,128]{2,1,0:T(8,128)S(1)}, f32[24,16,128]{2,1,0:T(8,128)S(1)}, u32[]{:S(2)}, u32[]{:S(2)}) collective-permute-start(f32[24,16,128]{2,1,0:T(8,128)S(1)} %get-tuple-element.86), channel_id=1, source_target_pairs={{0,1},{1,2},{2,3},{3,4},{4,5},{5,6},{6,7},{7,8},{8,9},{9,10},{10,1... | collective-permute-start | bytes 589832 | tf_op jit(solution)/shard_map/ppermute | solution.py:353
  131.7 3.4 %collective-permute-start.21 = (f32[24,16,128]{2,1,0:T(8,128)S(1)}, f32[24,16,128]{2,1,0:T(8,128)S(1)}, u32[]{:S(2)}, u32[]{:S(2)}) collective-permute-start(f32[24,16,128]{2,1,0:T(8,128)S(1)} %get-tuple-element.87), channel_id=1, source_target_pairs={{1,0},{2,1},{3,2},{4,3},{5,4},{6,5},{7,6},{8,7},{9,8},{10,9},{11,1... | collective-permute-start | bytes 589832 | tf_op jit(solution)/shard_map/ppermute | solution.py:354
  135.1 2.7 %collective-permute-done.20.above = f32[24,16,128]{2,1,0:T(8,128)S(1)} collective-permute-done((f32[24,16,128]{2,1,0:T(8,128)S(1)}, f32[24,16,128]{2,1,0:T(8,128)S(1)}, u32[]{:S(2)}, u32[]{:S(2)}) %collective-permute-start.20) | collective-permute-done | bytes 196640 | tf_op jit(solution)/shard_map/ppermute | solution.py:353
  137.8 5.2 %collective-permute-done.21.below = f32[24,16,128]{2,1,0:T(8,128)S(1)} collective-permute-done((f32[24,16,128]{2,1,0:T(8,128)S(1)}, f32[24,16,128]{2,1,0:T(8,128)S(1)}, u32[]{:S(2)}, u32[]{:S(2)}) %collective-permute-start.21) | collective-permute-done | bytes 196640 | tf_op jit(solution)/shard_map/ppermute | solution.py:354
  143.0 1.3 gather.3
  144.4 0.7 collective-permute-start.22
  145.1 8.6 %collective-permute-done.22.theirs = f32[24,32,128]{2,1,0:T(8,128)S(1)} collective-permute-done((f32[24,32,128]{2,1,0:T(8,128)S(1)}, f32[24,32,128]{2,1,0:T(8,128)S(1)}, u32[]{:S(2)}, u32[]{:S(2)}) %collective-permute-start.22) | collective-permute-done | bytes 393248 | tf_op jit(solution)/shard_map/ppermute | solution.py:274
  153.8 2.2 %collective-permute-start.23 = (f32[24,32,128]{2,1,0:T(8,128)S(1)}, f32[24,32,128]{2,1,0:T(8,128)S(1)}, u32[]{:S(2)}, u32[]{:S(2)}) collective-permute-start(f32[24,32,128]{2,1,0:T(8,128)S(1)} %last.1.mine), channel_id=1, source_target_pairs={{0,64},{64,0},{128,192},{192,128},{1,65},{65,1},{129,193},{193,129... | collective-permute-start | bytes 1179656 | tf_op jit(solution)/shard_map/ppermute | solution.py:274
  156.1 1.3 collective-permute-done.23.theirs
  157.4 1.5 whole.1
  (145 shorter events, 11.7 us)
Async XLA Ops:
  0.0 0.7 copy-start.38
  2.7 1.1 copy-start
  3.8 1.1 copy-start.2
  4.9 4.5 %copy-start.32 = (f32[4,3,31]{2,0,1:T(4,128)S(1)}, f32[4,3,31]{2,0,1:T(4,128)}, u32[]{:S(2)}) copy-start(f32[4,3,31]{2,0,1:T(4,128)} %param.6) | copy-start | bytes 4468
  4.9 7.3 %copy-start.25 = (f32[31,512]{1,0:T(8,128)S(1)}, f32[31,512]{1,0:T(8,128)}, u32[]{:S(2)}) copy-start(f32[31,512]{1,0:T(8,128)} %constant.82.clone) | copy-start | bytes 190468
  5.9 7.8 %copy-start.1 = (f32[1,48,32,128]{3,2,1,0:T(8,128)S(1)}, f32[1,48,32,128]{3,2,1,0:T(8,128)}, u32[]{:S(2)}) copy-start(f32[1,48,32,128]{3,2,1,0:T(8,128)} %param.5) | copy-start | bytes 2359300
  5.9 7.8 %collective-permute-start = (f32[12,16,128]{2,1,0:T(8,128)S(1)}, f32[12,16,128]{2,1,0:T(8,128)S(1)}, u32[]{:S(2)}, u32[]{:S(2)}) collective-permute-start(f32[12,16,128]{2,1,0:T(8,128)S(1)} %get-tuple-element.48), channel_id=1, source_target_pairs={{0,32},{32,0},{1,33},{33,1},{2,34},{34,2},{3,35},{35,3},{4,36},{36... | collective-permute-start | bytes 294920 | tf_op jit(solution)/shard_map/ppermute | solution.py:274
  9.3 1.1 copy-start.43
  13.6 0.7 copy-start.5
  13.6 0.8 copy-start.8
  13.6 16.1 %copy-start.13 = (bf16[2,128,256]{2,1,0:T(8,128)(2,1)}, bf16[2,128,256]{2,1,0:T(8,128)(2,1)S(1)}, u32[]{:S(2)}) copy-start(bf16[2,128,256]{2,1,0:T(8,128)(2,1)S(1)} %get-tuple-element.54.bx_h) | copy-start | bytes 393220
  13.6 16.1 %copy-start.15 = (bf16[2,128,256]{2,1,0:T(8,128)(2,1)}, bf16[2,128,256]{2,1,0:T(8,128)(2,1)S(1)}, u32[]{:S(2)}) copy-start(bf16[2,128,256]{2,1,0:T(8,128)(2,1)S(1)} %get-tuple-element.55.bx_l) | copy-start | bytes 393220
  13.6 16.1 %copy-start.17 = (bf16[256,256]{1,0:T(8,128)(2,1)}, bf16[256,256]{1,0:T(8,128)(2,1)S(1)}, u32[]{:S(2)}) copy-start(bf16[256,256]{1,0:T(8,128)(2,1)S(1)} %get-tuple-element.52.yf_h) | copy-start | bytes 393220
  13.6 16.1 %copy-start.19 = (bf16[256,256]{1,0:T(8,128)(2,1)}, bf16[256,256]{1,0:T(8,128)(2,1)S(1)}, u32[]{:S(2)}) copy-start(bf16[256,256]{1,0:T(8,128)(2,1)S(1)} %get-tuple-element.53.yf_l) | copy-start | bytes 393220
  13.7 7.1 %copy-start.45 = (s32[16]{0:T(128)}, s32[16]{0:T(128)S(1)}, u32[]{:S(2)}) copy-start(s32[16]{0:T(128)S(1)} %iota_add_fusion) | copy-start | bytes 196
  14.4 8.2 %collective-permute-start.1 = (f32[27,16,128]{2,1,0:T(8,128)S(1)}, f32[27,16,128]{2,1,0:T(8,128)S(1)}, u32[]{:S(2)}, u32[]{:S(2)}) collective-permute-start(f32[27,16,128]{2,1,0:T(8,128)S(1)} %get-tuple-element.50), channel_id=1, source_target_pairs={{0,1},{1,2},{2,3},{3,4},{4,5},{5,6},{6,7},{7,8},{8,9},{9,10},{10,1... | collective-permute-start | bytes 663560 | tf_op jit(solution)/shard_map/ppermute | solution.py:310
  18.8 10.9 %collective-permute-start.2 = (f32[27,16,128]{2,1,0:T(8,128)S(1)}, f32[27,16,128]{2,1,0:T(8,128)S(1)}, u32[]{:S(2)}, u32[]{:S(2)}) collective-permute-start(f32[27,16,128]{2,1,0:T(8,128)S(1)} %get-tuple-element.51), channel_id=1, source_target_pairs={{1,0},{2,1},{3,2},{4,3},{5,4},{6,5},{7,6},{8,7},{9,8},{10,9},{11,1... | collective-permute-start | bytes 663560 | tf_op jit(solution)/shard_map/ppermute | solution.py:311
  33.2 0.8 copy-start.21
  34.0 2.2 %copy-start.44 = (s32[128]{0:T(128)S(1)}, s32[128]{0:T(128)}, u32[]{:S(2)}) copy-start(s32[128]{0:T(128)} %copy-done.43) | copy-start | bytes 1540
  34.0 2.9 %copy-start.26 = (s32[128,31]{0,1:T(8,128)S(1)}, s32[128,31]{0,1:T(8,128)}, u32[]{:S(2)}) copy-start(s32[128,31]{0,1:T(8,128)} %add_add_fusion) | copy-start | bytes 47620
  34.0 18.3 %collective-permute-start.3 = (f32[24,32,128]{2,1,0:T(8,128)}, f32[24,32,128]{2,1,0:T(8,128)}, u32[]{:S(2)}, u32[]{:S(2)}) collective-permute-start(f32[24,32,128]{2,1,0:T(8,128)} %get-tuple-element.57), channel_id=1, source_target_pairs={{0,64},{64,0},{128,192},{192,128},{1,65},{65,1},{129,193},{193,129... | collective-permute-start | bytes 1179656 | tf_op jit(solution)/shard_map/ppermute | solution.py:274
  37.6 8.0 %collective-permute-start.4 = (f32[51,8,128]{2,1,0:T(8,128)S(1)}, f32[51,8,128]{2,1,0:T(8,128)S(1)}, u32[]{:S(2)}, u32[]{:S(2)}) collective-permute-start(f32[51,8,128]{2,1,0:T(8,128)S(1)} %get-tuple-element.58), channel_id=1, source_target_pairs={{0,1},{1,2},{2,3},{3,4},{4,5},{5,6},{6,7},{7,8},{8,9},{9,10},{10,1... | collective-permute-start | bytes 626696 | tf_op jit(solution)/shard_map/ppermute | solution.py:312
  39.5 11.4 %collective-permute-start.5 = (f32[51,8,128]{2,1,0:T(8,128)S(1)}, f32[51,8,128]{2,1,0:T(8,128)S(1)}, u32[]{:S(2)}, u32[]{:S(2)}) collective-permute-start(f32[51,8,128]{2,1,0:T(8,128)S(1)} %get-tuple-element.59), channel_id=1, source_target_pairs={{1,0},{2,1},{3,2},{4,3},{5,4},{6,5},{7,6},{8,7},{9,8},{10,9},{11,1... | collective-permute-start | bytes 626696 | tf_op jit(solution)/shard_map/ppermute | solution.py:313
  43.5 8.8 %copy-start.22 = (f32[24,32,128]{2,1,0:T(8,128)S(1)}, f32[24,32,128]{2,1,0:T(8,128)}, u32[]{:S(2)}) copy-start(f32[24,32,128]{2,1,0:T(8,128)} %copy-done.21) | copy-start | bytes 1179652
  52.3 5.6 %copy-start.46 = (s32[16]{0:T(128)S(1)}, s32[16]{0:T(128)}, u32[]{:S(2)}) copy-start(s32[16]{0:T(128)} %copy-done.45) | copy-start | bytes 196
  52.3 9.5 %copy-start.31 = (s32[16,31]{1,0:T(8,128)S(1)}, s32[16,31]{1,0:T(8,128)}, u32[]{:S(2)}) copy-start(s32[16,31]{1,0:T(8,128)} %add_add_fusion.3) | copy-start | bytes 5956
  52.3 9.5 %copy-start.34 = (f32[4,1,31]{2,0,1:T(4,128)S(1)}, f32[4,1,31]{2,0,1:T(4,128)}, u32[]{:S(2)}) copy-start(f32[4,1,31]{2,0,1:T(4,128)} %copy-done.33) | copy-start | bytes 1492
  55.8 0.7 copy-start.23
  56.5 8.2 %copy-start.4 = (bf16[256,256]{1,0:T(8,128)(2,1)S(1)}, bf16[256,256]{1,0:T(8,128)(2,1)}, u32[]{:S(2)}) copy-start(bf16[256,256]{1,0:T(8,128)(2,1)} %copy-done.3) | copy-start | bytes 393220
  56.5 8.2 %collective-permute-start.6 = (f32[24,32,128]{2,1,0:T(8,128)S(1)}, f32[24,32,128]{2,1,0:T(8,128)S(1)}, u32[]{:S(2)}, u32[]{:S(2)}) collective-permute-start(f32[24,32,128]{2,1,0:T(8,128)S(1)} %get-tuple-element.63), channel_id=1, source_target_pairs={{0,64},{64,0},{128,192},{192,128},{1,65},{65,1},{129,193},{193,129... | collective-permute-start | bytes 1179656 | tf_op jit(solution)/shard_map/ppermute | solution.py:274
  58.7 5.4 %collective-permute-start.7 = (f32[6,16,128]{2,1,0:T(8,128)S(1)}, f32[6,16,128]{2,1,0:T(8,128)S(1)}, u32[]{:S(2)}, u32[]{:S(2)}) collective-permute-start(f32[6,16,128]{2,1,0:T(8,128)S(1)} %get-tuple-element.64), channel_id=1, source_target_pairs={{0,32},{32,0},{1,33},{33,1},{2,34},{34,2},{3,35},{35,3},{4,36},{36... | collective-permute-start | bytes 147464 | tf_op jit(solution)/shard_map/ppermute | solution.py:274
  58.9 5.8 %collective-permute-start.8 = (f32[6,16,128]{2,1,0:T(8,128)S(1)}, f32[6,16,128]{2,1,0:T(8,128)S(1)}, u32[]{:S(2)}, u32[]{:S(2)}) collective-permute-start(f32[6,16,128]{2,1,0:T(8,128)S(1)} %get-tuple-element.65), channel_id=1, source_target_pairs={{0,96},{32,64},{64,32},{96,0},{128,224},{160,192},{192,160},{224,1... | collective-permute-start | bytes 147464 | tf_op jit(solution)/shard_map/ppermute | solution.py:274
  62.7 0.7 copy-start.36
  63.4 0.7 copy-start.35
  64.7 0.9 copy-start.6
  65.6 0.9 copy-start.9
  66.5 0.9 copy-start.12
  67.4 1.0 copy-start.24
  68.4 8.7 %copy-start.28 = (f32[24,32]{1,0:T(8,128)S(1)}, f32[24,32]{1,0:T(8,128)}, u32[]{:S(2)}) copy-start(f32[24,32]{1,0:T(8,128)} %get-tuple-element.92) | copy-start | bytes 9220
  68.4 8.7 %copy-start.29 = (f32[24,32]{1,0:T(8,128)S(1)}, f32[24,32]{1,0:T(8,128)}, u32[]{:S(2)}) copy-start(f32[24,32]{1,0:T(8,128)} %get-tuple-element.93) | copy-start | bytes 9220
  68.4 8.7 %copy-start.30 = (f32[24,32]{1,0:T(8,128)S(1)}, f32[24,32]{1,0:T(8,128)}, u32[]{:S(2)}) copy-start(f32[24,32]{1,0:T(8,128)} %get-tuple-element.94) | copy-start | bytes 9220
  68.4 8.7 %copy-start.42 = (f32[128]{0:T(128)S(1)}, f32[128]{0:T(128)}, u32[]{:S(2)}) copy-start(f32[128]{0:T(128)} %get-tuple-element.114) | copy-start | bytes 1540
  71.5 5.6 %copy-start.27 = (f32[24,32]{1,0:T(8,128)S(1)}, f32[24,32]{1,0:T(8,128)}, u32[]{:S(2)}) copy-start(f32[24,32]{1,0:T(8,128)} %get-tuple-element.91) | copy-start | bytes 9220
  71.5 8.1 %collective-permute-start.9 = (f32[24,16,128]{2,1,0:T(8,128)S(1)}, f32[24,16,128]{2,1,0:T(8,128)S(1)}, u32[]{:S(2)}, u32[]{:S(2)}) collective-permute-start(f32[24,16,128]{2,1,0:T(8,128)S(1)} %get-tuple-element.71), channel_id=1, source_target_pairs={{0,1},{1,2},{2,3},{3,4},{4,5},{5,6},{6,7},{7,8},{8,9},{9,10},{10,1... | collective-permute-start | bytes 589832 | tf_op jit(solution)/shard_map/ppermute | solution.py:353
  73.5 11.4 %collective-permute-start.10 = (f32[24,16,128]{2,1,0:T(8,128)S(1)}, f32[24,16,128]{2,1,0:T(8,128)S(1)}, u32[]{:S(2)}, u32[]{:S(2)}) collective-permute-start(f32[24,16,128]{2,1,0:T(8,128)S(1)} %get-tuple-element.72), channel_id=1, source_target_pairs={{1,0},{2,1},{3,2},{4,3},{5,4},{6,5},{7,6},{8,7},{9,8},{10,9},{11,1... | collective-permute-start | bytes 589832 | tf_op jit(solution)/shard_map/ppermute | solution.py:354
  85.6 11.7 %collective-permute-start.11 = (f32[24,32,128]{2,1,0:T(8,128)S(1)}, f32[24,32,128]{2,1,0:T(8,128)S(1)}, u32[]{:S(2)}, u32[]{:S(2)}) collective-permute-start(f32[24,32,128]{2,1,0:T(8,128)S(1)} %get-tuple-element.73.mine), channel_id=1, source_target_pairs={{0,128},{64,192},{128,0},{192,64},{1,129},{65,193},{129,1},{193,65... | collective-permute-start | bytes 1179656 | tf_op jit(solution)/shard_map/ppermute | solution.py:274
  86.2 4.2 %collective-permute-start.13 = (f32[6,16,128]{2,1,0:T(8,128)S(1)}, f32[6,16,128]{2,1,0:T(8,128)S(1)}, u32[]{:S(2)}, u32[]{:S(2)}) collective-permute-start(f32[6,16,128]{2,1,0:T(8,128)S(1)} %get-tuple-element.74), channel_id=1, source_target_pairs={{0,160},{32,128},{64,224},{96,192},{128,32},{160,0},{192,96},{224,... | collective-permute-start | bytes 147464 | tf_op jit(solution)/shard_map/ppermute | solution.py:274
  88.0 9.3 %collective-permute-start.12 = (f32[6,16,128]{2,1,0:T(8,128)S(1)}, f32[6,16,128]{2,1,0:T(8,128)S(1)}, u32[]{:S(2)}, u32[]{:S(2)}) collective-permute-start(f32[6,16,128]{2,1,0:T(8,128)S(1)} %get-tuple-element.74), channel_id=1, source_target_pairs={{0,32},{32,0},{1,33},{33,1},{2,34},{34,2},{3,35},{35,3},{4,36},{36... | collective-permute-start | bytes 147464 | tf_op jit(solution)/shard_map/ppermute | solution.py:274
  89.0 20.3 %copy-start.14 = (bf16[2,128,256]{2,1,0:T(8,128)(2,1)S(1)}, bf16[2,128,256]{2,1,0:T(8,128)(2,1)}, u32[]{:S(2)}) copy-start(bf16[2,128,256]{2,1,0:T(8,128)(2,1)} %copy-done.13) | copy-start | bytes 393220
  89.0 20.3 %copy-start.16 = (bf16[2,128,256]{2,1,0:T(8,128)(2,1)S(1)}, bf16[2,128,256]{2,1,0:T(8,128)(2,1)}, u32[]{:S(2)}) copy-start(bf16[2,128,256]{2,1,0:T(8,128)(2,1)} %copy-done.15) | copy-start | bytes 393220
  89.1 20.3 %copy-start.18 = (bf16[256,256]{1,0:T(8,128)(2,1)S(1)}, bf16[256,256]{1,0:T(8,128)(2,1)}, u32[]{:S(2)}) copy-start(bf16[256,256]{1,0:T(8,128)(2,1)} %copy-done.17) | copy-start | bytes 393220
  89.1 20.3 %copy-start.20 = (bf16[256,256]{1,0:T(8,128)(2,1)S(1)}, bf16[256,256]{1,0:T(8,128)(2,1)}, u32[]{:S(2)}) copy-start(bf16[256,256]{1,0:T(8,128)(2,1)} %copy-done.19) | copy-start | bytes 393220
  97.4 6.7 %collective-permute-start.14 = (f32[27,16,128]{2,1,0:T(8,128)S(1)}, f32[27,16,128]{2,1,0:T(8,128)S(1)}, u32[]{:S(2)}, u32[]{:S(2)}) collective-permute-start(f32[27,16,128]{2,1,0:T(8,128)S(1)} %get-tuple-element.77), channel_id=1, source_target_pairs={{0,1},{1,2},{2,3},{3,4},{4,5},{5,6},{6,7},{7,8},{8,9},{9,10},{10,1... | collective-permute-start | bytes 663560 | tf_op jit(solution)/shard_map/ppermute | solution.py:370
  99.4 10.0 %collective-permute-start.15 = (f32[27,16,128]{2,1,0:T(8,128)S(1)}, f32[27,16,128]{2,1,0:T(8,128)S(1)}, u32[]{:S(2)}, u32[]{:S(2)}) collective-permute-start(f32[27,16,128]{2,1,0:T(8,128)S(1)} %get-tuple-element.78), channel_id=1, source_target_pairs={{1,0},{2,1},{3,2},{4,3},{5,4},{6,5},{7,6},{8,7},{9,8},{10,9},{11,1... | collective-permute-start | bytes 663560 | tf_op jit(solution)/shard_map/ppermute | solution.py:371
  112.1 5.0 %collective-permute-start.16 = (f32[24,32,128]{2,1,0:T(8,128)S(1)}, f32[24,32,128]{2,1,0:T(8,128)S(1)}, u32[]{:S(2)}, u32[]{:S(2)}) collective-permute-start(f32[24,32,128]{2,1,0:T(8,128)S(1)} %get-tuple-element.80), channel_id=1, source_target_pairs={{0,64},{64,0},{128,192},{192,128},{1,65},{65,1},{129,193},{193,129... | collective-permute-start | bytes 1179656 | tf_op jit(solution)/shard_map/ppermute | solution.py:274
  117.1 9.5 %copy-start.7 = (bf16[256,256]{1,0:T(8,128)(2,1)S(1)}, bf16[256,256]{1,0:T(8,128)(2,1)}, u32[]{:S(2)}) copy-start(bf16[256,256]{1,0:T(8,128)(2,1)} %copy-done.5) | copy-start | bytes 393220
  117.1 9.5 %copy-start.10 = (bf16[2,128,256]{2,1,0:T(8,128)(2,1)S(1)}, bf16[2,128,256]{2,1,0:T(8,128)(2,1)}, u32[]{:S(2)}) copy-start(bf16[2,128,256]{2,1,0:T(8,128)(2,1)} %copy-done.8) | copy-start | bytes 393220
  120.1 6.6 %collective-permute-start.17 = (f32[24,32,128]{2,1,0:T(8,128)S(1)}, f32[24,32,128]{2,1,0:T(8,128)S(1)}, u32[]{:S(2)}, u32[]{:S(2)}) collective-permute-start(f32[24,32,128]{2,1,0:T(8,128)S(1)} %get-tuple-element.82), channel_id=1, source_target_pairs={{0,64},{64,0},{128,192},{192,128},{1,65},{65,1},{129,193},{193,129... | collective-permute-start | bytes 1179656 | tf_op jit(solution)/shard_map/ppermute | solution.py:274
  120.5 4.4 %collective-permute-start.18 = (f32[6,16,128]{2,1,0:T(8,128)S(1)}, f32[6,16,128]{2,1,0:T(8,128)S(1)}, u32[]{:S(2)}, u32[]{:S(2)}) collective-permute-start(f32[6,16,128]{2,1,0:T(8,128)S(1)} %get-tuple-element.83), channel_id=1, source_target_pairs={{0,32},{32,0},{1,33},{33,1},{2,34},{34,2},{3,35},{35,3},{4,36},{36... | collective-permute-start | bytes 147464 | tf_op jit(solution)/shard_map/ppermute | solution.py:274
  121.1 5.6 %collective-permute-start.19 = (f32[6,16,128]{2,1,0:T(8,128)S(1)}, f32[6,16,128]{2,1,0:T(8,128)S(1)}, u32[]{:S(2)}, u32[]{:S(2)}) collective-permute-start(f32[6,16,128]{2,1,0:T(8,128)S(1)} %get-tuple-element.84), channel_id=1, source_target_pairs={{0,96},{32,64},{64,32},{96,0},{128,224},{160,192},{192,160},{224,1... | collective-permute-start | bytes 147464 | tf_op jit(solution)/shard_map/ppermute | solution.py:274
  129.8 8.0 %collective-permute-start.20 = (f32[24,16,128]{2,1,0:T(8,128)S(1)}, f32[24,16,128]{2,1,0:T(8,128)S(1)}, u32[]{:S(2)}, u32[]{:S(2)}) collective-permute-start(f32[24,16,128]{2,1,0:T(8,128)S(1)} %get-tuple-element.86), channel_id=1, source_target_pairs={{0,1},{1,2},{2,3},{3,4},{4,5},{5,6},{6,7},{7,8},{8,9},{9,10},{10,1... | collective-permute-start | bytes 589832 | tf_op jit(solution)/shard_map/ppermute | solution.py:353
  131.7 11.3 %collective-permute-start.21 = (f32[24,16,128]{2,1,0:T(8,128)S(1)}, f32[24,16,128]{2,1,0:T(8,128)S(1)}, u32[]{:S(2)}, u32[]{:S(2)}) collective-permute-start(f32[24,16,128]{2,1,0:T(8,128)S(1)} %get-tuple-element.87), channel_id=1, source_target_pairs={{1,0},{2,1},{3,2},{4,3},{5,4},{6,5},{7,6},{8,7},{9,8},{10,9},{11,1... | collective-permute-start | bytes 589832 | tf_op jit(solution)/shard_map/ppermute | solution.py:354
  144.4 9.4 %collective-permute-start.22 = (f32[24,32,128]{2,1,0:T(8,128)S(1)}, f32[24,32,128]{2,1,0:T(8,128)S(1)}, u32[]{:S(2)}, u32[]{:S(2)}) collective-permute-start(f32[24,32,128]{2,1,0:T(8,128)S(1)} %get-tuple-element.88.mine), channel_id=1, source_target_pairs={{0,128},{64,192},{128,0},{192,64},{1,129},{65,193},{129,1},{193,65... | collective-permute-start | bytes 1179656 | tf_op jit(solution)/shard_map/ppermute | solution.py:274
  153.8 3.6 %collective-permute-start.23 = (f32[24,32,128]{2,1,0:T(8,128)S(1)}, f32[24,32,128]{2,1,0:T(8,128)S(1)}, u32[]{:S(2)}, u32[]{:S(2)}) collective-permute-start(f32[24,32,128]{2,1,0:T(8,128)S(1)} %last.1.mine), channel_id=1, source_target_pairs={{0,64},{64,0},{128,192},{192,128},{1,65},{65,1},{129,193},{193,129... | collective-permute-start | bytes 1179656 | tf_op jit(solution)/shard_map/ppermute | solution.py:274
  (7 other events, 4.6 us)

commit v2 on v1

v2 whole, which is shorter than its diff:
```python
import functools

import jax
import jax.numpy as jnp
import numpy as np
from jax import lax
from jax.experimental import pallas as pl
from jax.experimental.pallas import tpu as pltpu
from jax.sharding import PartitionSpec as P

OMAX = 8
ITERS = 2
TAPS = 31
HALF = 15
EDGE = 16
F32 = jnp.float32
BF16 = jnp.bfloat16
highest = lax.Precision.HIGHEST

NN = (((1,), (0,)), ((), ()))
NT = (((1,), (1,)), ((), ()))


def split(value):
    high = value.astype(BF16)
    low = (value - high.astype(F32)).astype(BF16)
    return high, low


def dot3(a, b, dims):
    def one(p, q):
        return lax.dot_general(p, q, dims, preferred_element_type=F32)

    return one(a[0], b[0]) + (one(a[0], b[1]) + one(a[1], b[0]))


def call(body, outs, args, scratch=(), flops=0, name=None, place=pltpu.VMEM):
    specs = [
        pl.BlockSpec(memory_space=pltpu.SMEM if a.ndim == 1 or a.dtype == jnp.int32 else place) for a in args
    ]
    outs = [jax.ShapeDtypeStruct(*o) for o in outs]
    moved = sum(int(np.prod(a.shape)) * a.dtype.itemsize for a in list(args) + outs)
    return pl.pallas_call(
        body,
        out_shape=outs,
        in_specs=specs,
        out_specs=[pl.BlockSpec(memory_space=pltpu.VMEM)] * len(outs),
        scratch_shapes=list(scratch),
        compiler_params=pltpu.CompilerParams(vmem_limit_bytes=10 << 20),
        cost_estimate=pl.CostEstimate(flops=flops, bytes_accessed=moved, transcendentals=0),
        name=name,
    )(*args)


def toeplitz(row, rows, width, shift):
    wide = jnp.broadcast_to(row[:, :width], (rows, width))
    return pltpu.roll(wide, shift % width, 1, stride=1, stride_axis=0)


BX, BT, YF = 0, 2, 4


def bands_body(taps, kz, mats):
    nz = kz.shape[1]
    for m in range(2):
        kz[2 * m], kz[2 * m + 1] = split(toeplitz(taps[m : m + 1], nz, 512, 0)[:, :nz])
    lane = lax.broadcasted_iota(jnp.int32, (64, 256), 1)

    def put(m, at, band):
        rows = slice(at, at + band.shape[0])
        mats[m, rows], mats[m + 1, rows] = split(band)

    for v in range(2):
        for p in range(4):
            put(BX, 128 * v + 32 * p, toeplitz(taps[2 + v : 3 + v], 32, 256, 64 * p + 1))
        put(YF, 128 * v, toeplitz(taps[6 + v : 7 + v], 128, 256, -HALF))
    for p in range(4):
        both = jnp.zeros((64, 256), F32)
        for v in range(2):
            at = 128 * v + 32 * p
            band = toeplitz(taps[4 + v : 5 + v], 64, 256, at - 2 * HALF - 1)
            both = jnp.where((lane >= at) & (lane < at + 32), band, both)
        put(BT, 64 * p, both)


def placing(width, step, start):
    place = np.zeros((TAPS, width), np.float32)
    for k in range(TAPS):
        place[k, (step * (k - start)) % width] = 1
    return place


def bands(own, other, planes):
    nz = 8 * planes
    z_rows = jnp.dot(jnp.stack([own[0], own[0, ::-1]]), placing(512, 8, HALF), precision=highest)
    rows = jnp.stack([own[1], other[1], own[1, ::-1], other[1, ::-1], own[2], other[2]])
    taps = jnp.concatenate([z_rows, jnp.pad(rows, ((0, 0), (0, 512 - TAPS)))])
    return call(bands_body, [((4, nz, nz), BF16), ((6, 256, 256), BF16)], [taps], name="bands")


def pack_columns(value, at, width, scratch):
    flat = value.reshape(value.shape[0] * value.shape[1], 128)
    scratch[...] = flat.T
    return scratch[pl.ds(pl.multiple_of(at, 8), width), :]


def spread_columns(pack, at, width, scratch):
    for t, part in enumerate(pack):
        scratch[pl.ds(pl.multiple_of(at, 8), width), 128 * t : 128 * t + 128] = part
    return scratch[...].T


def norm_body(shape, psf, offsets, norm, norm_ext):
    nx, ny = shape
    views = offsets.shape[0]
    core = lax.axis_index("view") % 2
    x_first = 32 * lax.axis_index("ty")
    tx = lax.axis_index("tx")

    def window(view, dim, place, shift, extent):
        total = jnp.zeros(place.shape, F32)
        weight = 0.0
        for i in range(TAPS):
            tap = psf[(view * 3 + dim) * TAPS + TAPS - 1 - i]
            at = place + (i - HALF)
            moved = at + shift
            inside = (at >= 0) & (at < extent) & (moved >= 0) & (moved < extent)
            total = total + jnp.where(inside, tap, 0.0)
            weight = weight + tap
        return total / weight

    def iota(shape, dim):
        return lax.broadcasted_iota(jnp.int32, shape, dim)

    lane = iota((8, 128), 1)
    tile = jnp.minimum(iota((8, 128), 0), 2)
    flat_z = 24 * core + (128 * tile + lane) // EDGE
    flat_x = x_first + EDGE * (iota((8, 128), 0) % 2) + lane % EDGE
    acc = [jnp.zeros((32, 128), F32) for _ in range(24)]
    ext = [jnp.zeros((EDGE, 128), F32) for _ in range(6)]
    for v in range(views):
        sx, sy = offsets[v, 0], offsets[v, 1]
        in_z = window(v, 0, 24 * core + iota((24, 128), 0), 0, 48)
        in_x = window(v, 1, x_first + iota((32, 128), 0), sx, nx)
        in_y = window(v, 2, 128 * tx + lane, sy, ny)[0:1]
        in_e = window(v, 2, 128 - EDGE * tx + iota((EDGE, 128), 0), sy, ny)
        z_row = window(v, 0, flat_z, 0, 48)
        x_row = window(v, 1, flat_x, sx, nx)
        xy = in_x * in_y
        acc = [acc[z] + in_z[z : z + 1] * xy for z in range(24)]
        for k in range(6):
            ext[k] = ext[k] + in_e * (z_row[k % 3 : k % 3 + 1] * x_row[k // 3 : k // 3 + 1])
    for z in range(24):
        norm[z] = acc[z]
    for k in range(6):
        norm_ext[k] = ext[k]


def mesh_core():
    return lax.axis_index("view") % 2


def parity():
    return lax.axis_index("ty") % 2 == 1


def put_packs(value, at, width, turned, out, first):
    cols = pack_columns(value, at, width, turned)
    for t in range(3):
        out[first + t] = cols[:, 128 * t : 128 * t + 128]


def begin_body(est, raw, cur_out, pack_out, raw_here, turned, sems):
    tx = lax.axis_index("tx")
    half = est.at[pl.ds(24 * mesh_core(), 24)]
    copies = [pltpu.make_async_copy(half, cur_out, sems.at[0]), pltpu.make_async_copy(raw, raw_here, sems.at[1])]
    for copy in copies:
        copy.start()
    copies[0].wait()
    for xh in range(2):
        put_packs(cur_out[:, 16 * xh : 16 * xh + 16, :], 112 * (1 - tx), 16, turned, pack_out, 3 * xh)
    copies[1].wait()
    for xb in range(4):
        cols = pack_columns(raw_here[:, 8 * xb : 8 * xb + 8, :], 120 * (1 - tx), 8, turned)
        for t in range(3):
            pack_out[6 + 3 * (xb // 2) + t, 8 * (xb % 2) : 8 * (xb % 2) + 8, :] = cols[:, 128 * t : 128 * t + 128]


def raw_part(pack, xb, t):
    at = 8 * (xb % 2)
    return pack[6 + 3 * (xb // 2) + t, at : at + 8, :]


def put_rims(top, bottom, even_out, odd_out, planes):
    odd = parity()
    even_out[planes] = jnp.where(odd, top, bottom)
    odd_out[planes] = jnp.where(odd, bottom, top)


def rims_body(cur, raw, pack, ext_out, even_out, odd_out):
    ext_out[...] = pack[0:6]
    put_rims(cur[:, 0:16, :], cur[:, 16:32, :], even_out, odd_out, slice(0, 24))
    put_rims(pack[0:3], pack[3:6], even_out, odd_out, slice(24, 27))
    top = raw[:, 0:8, :].reshape(24, 16, 128)
    bottom = raw[:, 24:32, :].reshape(24, 16, 128)
    put_rims(top, bottom, even_out, odd_out, slice(27, 51))
    for p in range(2):
        tops, bottoms = (
            jnp.concatenate([raw_part(pack, xb, 2 * p), raw_part(pack, xb, min(2 * p + 1, 2))])[None] for xb in (0, 3)
        )
        put_rims(tops, bottoms, even_out, odd_out, slice(51 + p, 52 + p))


def register_body(offsets, raw, pack, from_even, from_odd, out, wide, turned):
    view, tx = lax.axis_index("view"), lax.axis_index("tx")
    sx, sy = offsets[view, 0], offsets[view, 1]
    odd = parity()
    above = jnp.where(odd, from_even[27:53], from_odd[27:53])
    below = jnp.where(odd, from_odd[27:53], from_even[27:53])
    wide[:, 0:8, 0:128] = above[0:24].reshape(48, 8, 128)
    wide[:, 8:40, 0:128] = raw[...]
    wide[:, 40:48, 0:128] = below[0:24].reshape(48, 8, 128)
    turned[...] = jnp.zeros_like(turned)
    for b in range(6):
        if b in (0, 5):
            rim = above if b == 0 else below
            parts = [rim[24, 0:8], rim[24, 8:16], rim[25, 0:8]]
        else:
            parts = [raw_part(pack, b - 1, t) for t in range(3)]
        wide[:, 8 * b : 8 * b + 8, 128:256] = spread_columns(parts, 120 * tx, 8, turned).reshape(48, 8, 128)
    for z in range(0, 48, 4):
        rows = pltpu.roll(wide[z : z + 4], lax.rem(40 - sx, 48), 1)[:, 0:32, :]
        out[z : z + 4] = pltpu.roll(rows, lax.rem(256 - sy, 256), 2)[:, :, 0:128]


def forward_body(cur, ext, from_even, from_odd, mats, own, other, x_h, x_l, turned):
    tx = lax.axis_index("tx")
    odd = parity()
    above = jnp.where(odd, from_even[0:27], from_odd[0:27])
    below = jnp.where(odd, from_odd[0:27], from_even[0:27])
    turned[...] = jnp.zeros_like(turned)
    for b in range(4):
        main = (above[0:24], cur[:, 0:16, :], cur[:, 16:32, :], below[0:24])[b]
        rim = ([above[24 + t] for t in range(3)], [ext[t] for t in range(3)],
               [ext[3 + t] for t in range(3)], [below[24 + t] for t in range(3)])[b]
        at = slice(16 * b, 16 * b + 16)
        x_h[:, at, 0:128], x_l[:, at, 0:128] = split(main)
        side = spread_columns(rim, 112 * tx, 16, turned).reshape(24, 16, 128)
        x_h[:, at, 128:256], x_l[:, at, 128:256] = split(side)
    yf = (mats[YF], mats[YF + 1])
    for g in range(6):
        z = slice(4 * g, 4 * g + 4)
        rows = (x_h[z].reshape(256, 256), x_l[z].reshape(256, 256))
        along_y = split(dot3(rows, yf, NT))
        for v, out in ((0, own), (1, other)):
            cols = slice(128 * v, 128 * v + 128)
            part = (along_y[0][:, cols], along_y[1][:, cols])
            out[z] = dot3((mats[BX, cols], mats[BX + 1, cols]), part, NN).reshape(4, 32, 128)


def ratio_body(mine, theirs, seen, kz, keep, send, full):
    core = mesh_core()
    full[pl.ds(24 * core, 24)] = mine[...]
    full[pl.ds(24 * (1 - core), 24)] = theirs[...]
    for xp in range(2):
        def pair(ref):
            return jnp.concatenate(
                [ref[:, 16 * xp + 8 * i : 16 * xp + 8 * i + 8, :].reshape(384, 128) for i in range(2)], axis=1
            )
        blurred = dot3((kz[0], kz[1]), split(pair(full)), NN)
        ratio = pair(seen) / blurred
        back = dot3((kz[2], kz[3]), split(ratio), NN)
        for i in range(2):
            at = slice(16 * xp + 8 * i, 16 * xp + 8 * i + 8)
            full[:, at, :] = back[:, 128 * i : 128 * i + 128].reshape(48, 8, 128)
    keep[...] = full[pl.ds(24 * core, 24)]
    send[...] = full[pl.ds(24 * (1 - core), 24)]


def mirror_body(own, other, mats, even_out, odd_out, mid, mid_ext, sides, turned):
    tx = lax.axis_index("tx")
    for g in range(6):
        z = slice(4 * g, 4 * g + 4)
        along_y = [
            split(dot3(split(ref[z].reshape(128, 128)), (mats[YF, at : at + 128], mats[YF + 1, at : at + 128]), NN))
            for ref, at in ((own, 0), (other, 128))
        ]
        both = tuple(jnp.concatenate([along_y[0][i], along_y[1][i]], axis=0) for i in range(2))
        wide = dot3((mats[BT], mats[BT + 1]), both, NN).reshape(4, 64, 256)
        put_rims(wide[:, 0:16, 0:128], wide[:, 48:64, 0:128], even_out, odd_out, z)
        mid[z] = wide[:, 16:48, 0:128]
        sides[z] = wide[:, :, 128:256]
    cols = []
    for b in range(4):
        cols.append(pack_columns(sides[:, 16 * b : 16 * b + 16, :], 112 * tx, 16, turned))
    parts = [[c[:, 128 * t : 128 * t + 128] for t in range(3)] for c in cols]
    for t in range(3):
        put_rims(parts[0][t][None], parts[3][t][None], even_out, odd_out, slice(24 + t, 25 + t))
        mid_ext[t] = parts[1][t]
        mid_ext[3 + t] = parts[2][t]


def gather_body(mid, mid_ext, from_even, from_odd, low_out, high_out, sides_out, turned):
    tx = lax.axis_index("tx")
    odd = parity()
    above = jnp.where(odd, from_even[...], from_odd[...])
    below = jnp.where(odd, from_odd[...], from_even[...])
    for out, z in ((low_out, slice(0, 12)), (high_out, slice(12, 24))):
        out[0:12, 0:16, :] = mid[z, 0:16, :] + above[z]
        out[0:12, 16:32, :] = mid[z, 16:32, :] + below[z]
    sides_out[0:3] = mid_ext[0:3] + above[24:27]
    sides_out[3:6] = mid_ext[3:6] + below[24:27]
    low_out[12:13] = sides_out[0:2].reshape(1, 32, 128)
    high_out[12:14] = sides_out[2:6].reshape(2, 32, 128)
    for xh in range(2):
        at = slice(16 * xh, 16 * xh + 16)
        both = jnp.concatenate([low_out[0:12, at, :], high_out[0:12, at, :]])
        put_packs(both, 112 * (1 - tx), 16, turned, sides_out, 6 + 3 * xh)


def new_estimate(low, high, p_low, p_high, side_a, side_b, cur, norm, cur_out, turned):
    tx = lax.axis_index("tx")
    turned[...] = jnp.zeros_like(turned)
    for xh in range(2):
        at = slice(16 * xh, 16 * xh + 16)
        parts = [side_a[3 * xh + t] + side_b[3 * xh + t] for t in range(3)]
        edge = spread_columns(parts, 112 * (1 - tx), 16, turned).reshape(24, 16, 128)
        for mine, theirs, z in ((low, p_low, slice(0, 12)), (high, p_high, slice(12, 24))):
            total = mine[0:12, at, :] + theirs[0:12, at, :] + edge[z]
            cur_out[z, at, :] = cur[z, at, :] * total / norm[z, at, :]


def update_body(
    low, high, p_low, p_high, side_a, side_b, cur, norm, ext, norm_ext, cur_out, ext_out, even_out, odd_out, turned
):
    new_estimate(low, high, p_low, p_high, side_a, side_b, cur, norm, cur_out, turned)
    total = side_a[6:12] + side_b[6:12]
    total_low = total[0:2] + low[12:13].reshape(2, 16, 128) + p_low[12:13].reshape(2, 16, 128)
    total_high = total[2:6] + high[12:14].reshape(4, 16, 128) + p_high[12:14].reshape(4, 16, 128)
    ext_out[0:2] = ext[0:2] * total_low / norm_ext[0:2]
    ext_out[2:6] = ext[2:6] * total_high / norm_ext[2:6]
    put_rims(cur_out[:, 0:16, :], cur_out[:, 16:32, :], even_out, odd_out, slice(0, 24))
    put_rims(ext_out[0:3], ext_out[3:6], even_out, odd_out, slice(24, 27))


def whole_body(mine, theirs, out):
    core = mesh_core()
    out[pl.ds(24 * core, 24)] = mine[...]
    out[pl.ds(24 * (1 - core), 24)] = theirs[...]


def swap(value, axis, by, sizes):
    count = int(np.prod(sizes))
    return lax.ppermute(value, axis, [(i, i ^ by) for i in range(count)])


def rim_swap(even, odd):
    rows = lax.axis_size("ty")
    odd_pairs = [(i, i + 1) for i in range(1, rows - 1, 2)]
    odd_pairs += [(b, a) for a, b in odd_pairs]
    from_odd = lax.ppermute(odd, "ty", odd_pairs)
    from_even = lax.ppermute(even, "ty", [(i, i ^ 1) for i in range(rows)])
    return from_even, from_odd


def shards(raw_views, psf_taps, offsets, estimate):
    depth, tile_x, tile_y = estimate.shape
    half = depth // 2
    view = lax.axis_index("view")
    raw = raw_views[0]

    tile_half = ((half, tile_x, tile_y), F32)
    pack = ((6, EDGE, 128), F32)
    rim = ((half + 3, EDGE, 128), F32)
    turned = pltpu.VMEM((128, 384), F32)

    cur, sides = call(
        begin_body,
        [tile_half, ((12, EDGE, 128), F32)],
        [estimate, raw],
        [pltpu.VMEM(raw.shape, F32), turned, pltpu.SemaphoreType.DMA((2,))],
        name="begin",
        place=pl.ANY,
    )
    sides = swap(sides, "tx", 1, (2,))

    kernels = psf_taps / jnp.sum(psf_taps, axis=-1, keepdims=True)
    own = lax.dynamic_index_in_dim(kernels, view, 0, keepdims=False)
    other = lax.dynamic_index_in_dim(kernels, view ^ 1, 0, keepdims=False)
    kz, mats = bands(own, other, depth)
    extents = (tile_x * lax.axis_size("ty"), tile_y * lax.axis_size("tx"))
    norm, norm_ext = call(
        functools.partial(norm_body, extents), [tile_half, pack], [psf_taps.reshape(-1), offsets], name="norm"
    )

    first_rim = ((half + 3 + half + 2, EDGE, 128), F32)
    ext, even, odd = call(rims_body, [pack, first_rim, first_rim], [cur, raw, sides], name="rims")
    from_even, from_odd = rim_swap(even, odd)
    seen = None

    for iteration in range(ITERS):
        mine, theirs = call(
            forward_body,
            [tile_half, tile_half],
            [cur, ext, from_even, from_odd, mats],
            [pltpu.VMEM((half, 64, 256), BF16), pltpu.VMEM((half, 64, 256), BF16), turned],
            flops=3 * 2 * (1536 * 256 * 256 + 12 * 128 * 256 * 128),
            name="forward",
        )
        theirs = swap(theirs, "view", 1, (4,))
        if seen is None:
            (seen,) = call(
                register_body,
                [((depth, tile_x, tile_y), F32)],
                [offsets, raw, sides, from_even, from_odd],
                [pltpu.VMEM((depth, tile_x + 2 * OMAX, 256), F32), turned],
                name="register",
            )
        keep, send = call(
            ratio_body,
            [tile_half, tile_half],
            [mine, theirs, seen, kz],
            [pltpu.VMEM((depth, tile_x, tile_y), F32)],
            flops=3 * 2 * 2 * 384 * 384 * 512,
            name="ratio",
        )
        send = swap(send, "view", 1, (4,))
        even, odd, mid, mid_ext = call(
            mirror_body,
            [rim, rim, tile_half, pack],
            [keep, send, mats],
            [pltpu.VMEM((half, 64, 128), F32), turned],
            flops=3 * 2 * (1536 * 128 * 256 + 6 * 256 * 256 * 256),
            name="mirror",
        )
        from_even, from_odd = rim_swap(even, odd)
        low, high, sides_now = call(
            gather_body,
            [((13, tile_x, tile_y), F32), ((14, tile_x, tile_y), F32), ((12, EDGE, 128), F32)],
            [mid, mid_ext, from_even, from_odd],
            [turned],
            name="gather",
        )
        last = iteration == ITERS - 1
        if last:
            low, high, sides_now = low[0:12], high[0:12], sides_now[0:6]
        p_low = swap(low, "view", 2, (4,))
        p_high = swap(high, "view", 2, (4,))
        side_a = swap(sides_now, "tx", 1, (2,))
        side_b = swap(sides_now, ("view", "tx"), 5, (4, 2))
        parts = [low, high, p_low, p_high, side_a, side_b, cur, norm]
        if last:
            (cur,) = call(new_estimate, [tile_half], parts, [turned], name="last")
        else:
            cur, ext, even, odd = call(
                update_body, [tile_half, pack, rim, rim], parts + [ext, norm_ext], [turned], name="update"
            )
            from_even, from_odd = rim_swap(even, odd)
    far = swap(cur, "view", 1, (4,))
    (out,) = call(whole_body, [((depth, tile_x, tile_y), F32)], [cur, far], name="whole")
    return out


def solution(mesh):
    placed = (P("view", None, "ty", "tx"), P(), P(), P(None, "ty", "tx"))
    return jax.shard_map(
        shards, mesh=mesh, in_specs=placed, out_specs=P(None, "ty", "tx"), check_vma=False
    )
```

time: 160 us -> 117 us (0.73)
  waiting for transfers between devices: 60 us -> 47.1 us
  local copies, waits for them, and re-layouts: 17.7 us -> 5.76 us
  starting transfers between devices: 50.9 us -> 42.7 us
  Pallas kernels: 25.5 us -> 20.2 us
  other arithmetic: 4.13 us -> 0.18 us
    ppermute x10 -> x8, waiting for transfers between devices: 36.9 us -> 25.2 us  [the longest x4 20.6 us: rim_swap(): from_odd = lax.ppermute(odd, 'ty', odd_pairs)]
    unnamed x95 -> x32, local copies, waits for them, and re-layouts: 11.9 us -> 5.31 us
    ppermute x10 -> x8, starting transfers between devices: 27.6 us -> 21.8 us  [the longest x4 21 us: rim_swap(): from_odd = lax.ppermute(odd, 'ty', odd_pairs)]
    pallas_call x15 -> x16, Pallas kernels: 25.5 us -> 20.2 us  [call(): pl.pallas_call(body, out_shape=outs, in_specs=specs, out_specs=[pl.BlockS...]
    mul x7 -> x0, local copies, waits for them, and re-layouts: 2.61 us -> none  [the longest x5 1.39 us: norms(): flat[v][:, None, :] * part_e[v][None, :, None]]
    ppermute x14, starting transfers between devices: 23.3 us -> 20.9 us  [swap(): return lax.ppermute(value, axis, [(i, i ^ by) for i in range(count)])]
  transfers between devices with their start and end apart: 24 -> 22, of which waited for: 18 -> 16; matrix products, arithmetic and copies ran while one was open for 5% -> 1% of each run, Pallas kernels for 1% -> 4%
where the time goes in v2:
time: 117 us; the launch traced here: 116 us
  waiting for transfers between devices  47.1 us (40%)
  starting transfers between devices  42.7 us (36%)
  Pallas kernels  20.2 us (17%)
  local copies, waits for them, and re-layouts  5.76 us (5%)
    ppermute x14, waiting for transfers between devices, swap(): return lax.ppermute(value, axis, [(i, i ^ by) for i in range(count)])  21.9 us
    ppermute x4, starting transfers between devices, rim_swap(): from_odd = lax.ppermute(odd, 'ty', odd_pairs)  21 us
    ppermute x14, starting transfers between devices, swap(): return lax.ppermute(value, axis, [(i, i ^ by) for i in range(count)])  20.9 us
    ppermute x4, waiting for transfers between devices, rim_swap(): from_odd = lax.ppermute(odd, 'ty', odd_pairs)  20.6 us
    pallas_call x16, Pallas kernels, call(): pl.pallas_call(body, out_shape=outs, in_specs=specs, out_specs=[pl.BlockS...  20.2 us
    unnamed x32, local copies, waits for them, and re-layouts  5.31 us
    ppermute x4, waiting for transfers between devices, rim_swap(): from_even = lax.ppermute(even, 'ty', [(i, i ^ 1) for i in range(rows)])  4.65 us
  transfers between devices with their start and end apart: 22, of which 16 were waited for; matrix products, arithmetic and copies ran while one was open for 1% of the time, Pallas kernels for 4%

profile of v2, /device:TPU:121, one launch (start us, length us, event | category | flops | bytes accessed | tf_op | source)
XLA Modules:
  0.0 116.3 jit_solution(2689722371991776303)
XLA Ops:
  0.0 1.1 copy-done
  1.1 1.1 copy-done.2
  2.3 0.7 begin.1
  3.0 2.8 %collective-permute-start = (f32[12,16,128]{2,1,0:T(8,128)S(1)}, f32[12,16,128]{2,1,0:T(8,128)S(1)}, u32[]{:S(2)}, u32[]{:S(2)}) collective-permute-start(f32[12,16,128]{2,1,0:T(8,128)S(1)} %get-tuple-element.41), channel_id=1, source_target_pairs={{0,32},{32,0},{1,33},{33,1},{2,34},{34,2},{3,35},{35,3},{4,36},{36... | collective-permute-start | bytes 294920 | tf_op jit(solution)/shard_map/ppermute | solution.py:354
  5.8 0.1 reduce_sum.9
  6.0 2.1 %collective-permute-done.pack = f32[12,16,128]{2,1,0:T(8,128)S(1)} collective-permute-done((f32[12,16,128]{2,1,0:T(8,128)S(1)}, f32[12,16,128]{2,1,0:T(8,128)S(1)}, u32[]{:S(2)}, u32[]{:S(2)}) %collective-permute-start) | collective-permute-done | bytes 98336 | tf_op jit(solution)/shard_map/ppermute | solution.py:354
  8.0 0.1 rims.1
  8.1 0.5 collective-permute-start.1
  8.7 5.2 %collective-permute-start.2 = (f32[53,16,128]{2,1,0:T(8,128)S(1)}, f32[53,16,128]{2,1,0:T(8,128)S(1)}, u32[]{:S(2)}, u32[]{:S(2)}) collective-permute-start(f32[53,16,128]{2,1,0:T(8,128)S(1)} %get-tuple-element.44), channel_id=1, source_target_pairs={{1,2},{3,4},{5,6},{7,8},{9,10},{11,12},{13,14},{15,16},{17,18},{19... | collective-permute-start | bytes 1302536 | tf_op jit(solution)/shard_map/ppermute | solution.py:361
  14.0 0.1 rev.9
  14.1 0.1 rev.11
  14.2 0.1 rev.10
  14.3 0.2 fusion
  14.5 0.5 bands.1
  14.9 1.0 copy-done.3
  16.0 1.9 %collective-permute-done.1.from_even = f32[53,16,128]{2,1,0:T(8,128)S(1)} collective-permute-done((f32[53,16,128]{2,1,0:T(8,128)S(1)}, f32[53,16,128]{2,1,0:T(8,128)S(1)}, u32[]{:S(2)}, u32[]{:S(2)}) %collective-permute-start.1) | collective-permute-done | bytes 434208 | tf_op jit(solution)/shard_map/ppermute | solution.py:362
  17.9 5.4 %collective-permute-done.2.from_odd = f32[53,16,128]{2,1,0:T(8,128)S(1)} collective-permute-done((f32[53,16,128]{2,1,0:T(8,128)S(1)}, f32[53,16,128]{2,1,0:T(8,128)S(1)}, u32[]{:S(2)}, u32[]{:S(2)}) %collective-permute-start.2) | collective-permute-done | bytes 434208 | tf_op jit(solution)/shard_map/ppermute | solution.py:361
  23.3 3.0 %forward.2 = (f32[24,32,128]{2,1,0:T(8,128)S(1)}, f32[24,32,128]{2,1,0:T(8,128)}) custom-call(f32[24,32,128]{2,1,0:T(8,128)S(1)} %get-tuple-element.40.cur, f32[6,16,128]{2,1,0:T(8,128)S(1)} %get-tuple-element.42.ext, f32[53,16,128]{2,1,0:T(8,128)S(1)} %collective-permute-done.1.from_even, f32[53,16,128]{2,1,0:T(8,128)S(1)} %collective-permute-done.2.from_odd, ...), custom_call_target="tpu_custom_call" | custom-call | flops 905969664 | bytes 2883584 | tf_op jit(solution)/shard_map/forward/pallas_call | solution.py:43
  26.2 0.7 copy-done.10
  27.0 3.0 %collective-permute-start.3 = (f32[24,32,128]{2,1,0:T(8,128)}, f32[24,32,128]{2,1,0:T(8,128)S(1)}, u32[]{:S(2)}, u32[]{:S(2)}) collective-permute-start(f32[24,32,128]{2,1,0:T(8,128)} %get-tuple-element.47), channel_id=1, source_target_pairs={{0,64},{64,0},{128,192},{192,128},{1,65},{65,1},{129,193},{193,129... | collective-permute-start | bytes 1179656 | tf_op jit(solution)/shard_map/ppermute | solution.py:354
  30.0 0.1 copy.8.offsets
  30.1 1.4 %register.1.seen = f32[48,32,128]{2,1,0:T(8,128)S(1)} custom-call(s32[4,2]{1,0:T(4,128)S(1)} %copy.8.offsets, f32[48,32,128]{2,1,0:T(8,128)S(1)} %bitcast.14, f32[12,16,128]{2,1,0:T(8,128)S(1)} %collective-permute-done.pack, f32[53,16,128]{2,1,0:T(8,128)S(1)} %collective-permute-done.1.from_even, f32[53,16,128]{2,1,0:T(8,128)S(1)} %collective-permute-done.2.from_odd), custom_call_target="tpu_custom_call" | custom-call | bytes 2539552 | tf_op jit(solution)/shard_map/register/pallas_call | solution.py:43
  31.6 2.2 %ratio.2 = (f32[24,32,128]{2,1,0:T(8,128)S(1)}, f32[24,32,128]{2,1,0:T(8,128)S(1)}) custom-call(f32[24,32,128]{2,1,0:T(8,128)S(1)} %copy-done.11, f32[24,32,128]{2,1,0:T(8,128)S(1)} %collective-permute-done.3.theirs, f32[48,32,128]{2,1,0:T(8,128)S(1)} %register.1.seen, bf16[4,384,384]{2,1,0:T(8,128)(2,1)S(1)} %copy-done.4), custom_call_target="tpu_custom_call" | custom-call | flops 905969664 | bytes 3538944 | tf_op jit(solution)/shard_map/ratio/pallas_call | solution.py:43
  33.8 0.5 collective-permute-start.4
  34.3 1.4 %collective-permute-done.4.other = f32[24,32,128]{2,1,0:T(8,128)S(1)} collective-permute-done((f32[24,32,128]{2,1,0:T(8,128)S(1)}, f32[24,32,128]{2,1,0:T(8,128)S(1)}, u32[]{:S(2)}, u32[]{:S(2)}) %collective-permute-start.4) | collective-permute-done | bytes 393248 | tf_op jit(solution)/shard_map/ppermute | solution.py:354
  35.6 1.9 %mirror.2 = (f32[27,16,128]{2,1,0:T(8,128)S(1)}, f32[27,16,128]{2,1,0:T(8,128)S(1)}, f32[24,32,128]{2,1,0:T(8,128)S(1)}, f32[6,16,128]{2,1,0:T(8,128)S(1)}) custom-call(f32[24,32,128]{2,1,0:T(8,128)S(1)} %get-tuple-element.49.own, f32[24,32,128]{2,1,0:T(8,128)S(1)} %collective-permute-done.4.other, bf16[6,256,256]{2,1,0:T(8,128)(2,1)S(1)} %copy-done.7), custom_call_target="tpu_custom_call" | custom-call | flops 905969664 | bytes 2457600 | tf_op jit(solution)/shard_map/mirror/pallas_call | solution.py:43
  37.6 0.1 collective-permute-start.5
  37.7 5.2 %collective-permute-start.6 = (f32[27,16,128]{2,1,0:T(8,128)S(1)}, f32[27,16,128]{2,1,0:T(8,128)S(1)}, u32[]{:S(2)}, u32[]{:S(2)}) collective-permute-start(f32[27,16,128]{2,1,0:T(8,128)S(1)} %get-tuple-element.54), channel_id=1, source_target_pairs={{1,2},{3,4},{5,6},{7,8},{9,10},{11,12},{13,14},{15,16},{17,18},{19... | collective-permute-start | bytes 663560 | tf_op jit(solution)/shard_map/ppermute | solution.py:361
  42.9 1.4 %collective-permute-done.5.from_even = f32[27,16,128]{2,1,0:T(8,128)S(1)} collective-permute-done((f32[27,16,128]{2,1,0:T(8,128)S(1)}, f32[27,16,128]{2,1,0:T(8,128)S(1)}, u32[]{:S(2)}, u32[]{:S(2)}) %collective-permute-start.5) | collective-permute-done | bytes 221216 | tf_op jit(solution)/shard_map/ppermute | solution.py:362
  44.3 5.2 %collective-permute-done.6.from_odd = f32[27,16,128]{2,1,0:T(8,128)S(1)} collective-permute-done((f32[27,16,128]{2,1,0:T(8,128)S(1)}, f32[27,16,128]{2,1,0:T(8,128)S(1)}, u32[]{:S(2)}, u32[]{:S(2)}) %collective-permute-start.6) | collective-permute-done | bytes 221216 | tf_op jit(solution)/shard_map/ppermute | solution.py:361
  49.6 0.2 gather.2
  49.8 1.3 %collective-permute-start.8 = (f32[14,32,128]{2,1,0:T(8,128)S(1)}, f32[14,32,128]{2,1,0:T(8,128)S(1)}, u32[]{:S(2)}, u32[]{:S(2)}) collective-permute-start(f32[14,32,128]{2,1,0:T(8,128)S(1)} %get-tuple-element.56.high), channel_id=1, source_target_pairs={{0,128},{64,192},{128,0},{192,64},{1,129},{65,193},{129,1},{193,65... | collective-permute-start | bytes 688136 | tf_op jit(solution)/shard_map/ppermute | solution.py:354
  51.1 0.3 collective-permute-start.7
  51.3 2.5 %collective-permute-start.10 = (f32[12,16,128]{2,1,0:T(8,128)S(1)}, f32[12,16,128]{2,1,0:T(8,128)S(1)}, u32[]{:S(2)}, u32[]{:S(2)}) collective-permute-start(f32[12,16,128]{2,1,0:T(8,128)S(1)} %get-tuple-element.57), channel_id=1, source_target_pairs={{0,160},{32,128},{64,224},{96,192},{128,32},{160,0},{192,96},{224,... | collective-permute-start | bytes 294920 | tf_op jit(solution)/shard_map/ppermute | solution.py:354
  53.8 0.5 collective-permute-start.9
  54.4 2.3 %norm.1 = (f32[24,32,128]{2,1,0:T(8,128)S(1)}, f32[6,16,128]{2,1,0:T(8,128)S(1)}) custom-call(f32[372]{0:T(512)S(1)} %reshape.9.psf, s32[4,2]{1,0:T(4,128)S(1)} %copy.8.offsets), custom_call_target="tpu_custom_call" | custom-call | bytes 443888 | tf_op jit(solution)/shard_map/norm/pallas_call | solution.py:43
  56.7 7.6 %collective-permute-done.9.side_a = f32[12,16,128]{2,1,0:T(8,128)S(1)} collective-permute-done((f32[12,16,128]{2,1,0:T(8,128)S(1)}, f32[12,16,128]{2,1,0:T(8,128)S(1)}, u32[]{:S(2)}, u32[]{:S(2)}) %collective-permute-start.9) | collective-permute-done | bytes 98336 | tf_op jit(solution)/shard_map/ppermute | solution.py:354
  64.3 0.2 update.1
  64.5 0.1 collective-permute-start.11
  64.6 5.3 %collective-permute-start.12 = (f32[27,16,128]{2,1,0:T(8,128)S(1)}, f32[27,16,128]{2,1,0:T(8,128)S(1)}, u32[]{:S(2)}, u32[]{:S(2)}) collective-permute-start(f32[27,16,128]{2,1,0:T(8,128)S(1)} %get-tuple-element.63), channel_id=1, source_target_pairs={{1,2},{3,4},{5,6},{7,8},{9,10},{11,12},{13,14},{15,16},{17,18},{19... | collective-permute-start | bytes 663560 | tf_op jit(solution)/shard_map/ppermute | solution.py:361
  69.9 4.7 %collective-permute-done.12.from_odd = f32[27,16,128]{2,1,0:T(8,128)S(1)} collective-permute-done((f32[27,16,128]{2,1,0:T(8,128)S(1)}, f32[27,16,128]{2,1,0:T(8,128)S(1)}, u32[]{:S(2)}, u32[]{:S(2)}) %collective-permute-start.12) | collective-permute-done | bytes 221216 | tf_op jit(solution)/shard_map/ppermute | solution.py:361
  74.6 1.1 copy-done.8
  75.8 2.2 %forward.3 = (f32[24,32,128]{2,1,0:T(8,128)S(1)}, f32[24,32,128]{2,1,0:T(8,128)S(1)}) custom-call(f32[24,32,128]{2,1,0:T(8,128)S(1)} %get-tuple-element.60.cur, f32[6,16,128]{2,1,0:T(8,128)S(1)} %get-tuple-element.61.ext, f32[27,16,128]{2,1,0:T(8,128)S(1)} %collective-permute-done.11.from_even, f32[27,16,128]{2,1,0:T(8,128)S(1)} %collective-permute-done.12.from_odd, ...), custom_call_target="tpu_custom_call" | custom-call | flops 905969664 | bytes 2457600 | tf_op jit(solution)/shard_map/forward/pallas_call | solution.py:43
  77.9 3.6 %collective-permute-start.13 = (f32[24,32,128]{2,1,0:T(8,128)S(1)}, f32[24,32,128]{2,1,0:T(8,128)S(1)}, u32[]{:S(2)}, u32[]{:S(2)}) collective-permute-start(f32[24,32,128]{2,1,0:T(8,128)S(1)} %get-tuple-element.65), channel_id=1, source_target_pairs={{0,64},{64,0},{128,192},{192,128},{1,65},{65,1},{129,193},{193,129... | collective-permute-start | bytes 1179656 | tf_op jit(solution)/shard_map/ppermute | solution.py:354
  81.6 1.3 %collective-permute-done.13.theirs = f32[24,32,128]{2,1,0:T(8,128)S(1)} collective-permute-done((f32[24,32,128]{2,1,0:T(8,128)S(1)}, f32[24,32,128]{2,1,0:T(8,128)S(1)}, u32[]{:S(2)}, u32[]{:S(2)}) %collective-permute-start.13) | collective-permute-done | bytes 393248 | tf_op jit(solution)/shard_map/ppermute | solution.py:354
  82.9 2.2 %ratio.3 = (f32[24,32,128]{2,1,0:T(8,128)S(1)}, f32[24,32,128]{2,1,0:T(8,128)S(1)}) custom-call(f32[24,32,128]{2,1,0:T(8,128)S(1)} %get-tuple-element.64.mine, f32[24,32,128]{2,1,0:T(8,128)S(1)} %collective-permute-done.13.theirs, f32[48,32,128]{2,1,0:T(8,128)S(1)} %register.1.seen, bf16[4,384,384]{2,1,0:T(8,128)(2,1)S(1)} %copy-done.5), custom_call_target="tpu_custom_call" | custom-call | flops 905969664 | bytes 3538944 | tf_op jit(solution)/shard_map/ratio/pallas_call | solution.py:43
  85.2 0.5 collective-permute-start.14
  85.6 1.4 %collective-permute-done.14.other = f32[24,32,128]{2,1,0:T(8,128)S(1)} collective-permute-done((f32[24,32,128]{2,1,0:T(8,128)S(1)}, f32[24,32,128]{2,1,0:T(8,128)S(1)}, u32[]{:S(2)}, u32[]{:S(2)}) %collective-permute-start.14) | collective-permute-done | bytes 393248 | tf_op jit(solution)/shard_map/ppermute | solution.py:354
  87.0 2.0 %mirror.3 = (f32[27,16,128]{2,1,0:T(8,128)S(1)}, f32[27,16,128]{2,1,0:T(8,128)S(1)}, f32[24,32,128]{2,1,0:T(8,128)S(1)}, f32[6,16,128]{2,1,0:T(8,128)S(1)}) custom-call(f32[24,32,128]{2,1,0:T(8,128)S(1)} %get-tuple-element.66.own, f32[24,32,128]{2,1,0:T(8,128)S(1)} %collective-permute-done.14.other, bf16[6,256,256]{2,1,0:T(8,128)(2,1)S(1)} %copy-done.9), custom_call_target="tpu_custom_call" | custom-call | flops 905969664 | bytes 2457600 | tf_op jit(solution)/shard_map/mirror/pallas_call | solution.py:43
  88.9 0.1 collective-permute-start.15
  89.0 5.3 %collective-permute-start.16 = (f32[27,16,128]{2,1,0:T(8,128)S(1)}, f32[27,16,128]{2,1,0:T(8,128)S(1)}, u32[]{:S(2)}, u32[]{:S(2)}) collective-permute-start(f32[27,16,128]{2,1,0:T(8,128)S(1)} %get-tuple-element.71), channel_id=1, source_target_pairs={{1,2},{3,4},{5,6},{7,8},{9,10},{11,12},{13,14},{15,16},{17,18},{19... | collective-permute-start | bytes 663560 | tf_op jit(solution)/shard_map/ppermute | solution.py:361
  94.3 1.4 %collective-permute-done.15.from_even = f32[27,16,128]{2,1,0:T(8,128)S(1)} collective-permute-done((f32[27,16,128]{2,1,0:T(8,128)S(1)}, f32[27,16,128]{2,1,0:T(8,128)S(1)}, u32[]{:S(2)}, u32[]{:S(2)}) %collective-permute-start.15) | collective-permute-done | bytes 221216 | tf_op jit(solution)/shard_map/ppermute | solution.py:362
  95.7 5.2 %collective-permute-done.16.from_odd = f32[27,16,128]{2,1,0:T(8,128)S(1)} collective-permute-done((f32[27,16,128]{2,1,0:T(8,128)S(1)}, f32[27,16,128]{2,1,0:T(8,128)S(1)}, u32[]{:S(2)}, u32[]{:S(2)}) %collective-permute-start.16) | collective-permute-done | bytes 221216 | tf_op jit(solution)/shard_map/ppermute | solution.py:361
  100.9 0.2 gather.3
  101.1 0.1 collective-permute-start.18
  101.2 1.5 %collective-permute-start.17 = (f32[12,32,128]{2,1,0:T(8,128)S(1)}, f32[12,32,128]{2,1,0:T(8,128)S(1)}, u32[]{:S(2)}, u32[]{:S(2)}) collective-permute-start(f32[12,32,128]{2,1,0:T(8,128)S(1)} %slice.52.low), channel_id=1, source_target_pairs={{0,128},{64,192},{128,0},{192,64},{1,129},{65,193},{129,1},{193,65... | collective-permute-start | bytes 589832 | tf_op jit(solution)/shard_map/ppermute | solution.py:354
  102.7 0.2 collective-permute-start.20
  102.9 1.7 %collective-permute-start.19 = (f32[6,16,128]{2,1,0:T(8,128)S(1)}, f32[6,16,128]{2,1,0:T(8,128)S(1)}, u32[]{:S(2)}, u32[]{:S(2)}) collective-permute-start(f32[6,16,128]{2,1,0:T(8,128)S(1)} %slice.54), channel_id=1, source_target_pairs={{0,32},{32,0},{1,33},{33,1},{2,34},{34,2},{3,35},{35,3},{4,36},{36... | collective-permute-start | bytes 147464 | tf_op jit(solution)/shard_map/ppermute | solution.py:354
  104.6 2.3 %collective-permute-done.20.side_b = f32[6,16,128]{2,1,0:T(8,128)S(1)} collective-permute-done((f32[6,16,128]{2,1,0:T(8,128)S(1)}, f32[6,16,128]{2,1,0:T(8,128)S(1)}, u32[]{:S(2)}, u32[]{:S(2)}) %collective-permute-start.20) | collective-permute-done | bytes 49184 | tf_op jit(solution)/shard_map/ppermute | solution.py:354
  106.9 4.5 %collective-permute-done.19.side_a = f32[6,16,128]{2,1,0:T(8,128)S(1)} collective-permute-done((f32[6,16,128]{2,1,0:T(8,128)S(1)}, f32[6,16,128]{2,1,0:T(8,128)S(1)}, u32[]{:S(2)}, u32[]{:S(2)}) %collective-permute-start.19) | collective-permute-done | bytes 49184 | tf_op jit(solution)/shard_map/ppermute | solution.py:354
  111.3 0.2 last.1.mine
  111.5 2.5 %collective-permute-start.21 = (f32[24,32,128]{2,1,0:T(8,128)S(1)}, f32[24,32,128]{2,1,0:T(8,128)S(1)}, u32[]{:S(2)}, u32[]{:S(2)}) collective-permute-start(f32[24,32,128]{2,1,0:T(8,128)S(1)} %last.1.mine), channel_id=1, source_target_pairs={{0,64},{64,0},{128,192},{192,128},{1,65},{65,1},{129,193},{193,129... | collective-permute-start | bytes 1179656 | tf_op jit(solution)/shard_map/ppermute | solution.py:354
  114.0 1.3 %collective-permute-done.21.theirs = f32[24,32,128]{2,1,0:T(8,128)S(1)} collective-permute-done((f32[24,32,128]{2,1,0:T(8,128)S(1)}, f32[24,32,128]{2,1,0:T(8,128)S(1)}, u32[]{:S(2)}, u32[]{:S(2)}) %collective-permute-start.21) | collective-permute-done | bytes 393248 | tf_op jit(solution)/shard_map/ppermute | solution.py:354
  115.4 0.9 whole.1
  (41 shorter events, 0.4 us)
Async XLA Ops:
  0.0 1.1 copy-start
  1.1 1.1 copy-start.2
  2.3 3.5 %copy-start.13 = (f32[4,3,31]{2,0,1:T(4,128)S(1)}, f32[4,3,31]{2,0,1:T(4,128)}, u32[]{:S(2)}) copy-start(f32[4,3,31]{2,0,1:T(4,128)} %param.6) | copy-start | bytes 4468
  2.3 5.8 %copy-start.1 = (f32[1,48,32,128]{3,2,1,0:T(8,128)S(1)}, f32[1,48,32,128]{3,2,1,0:T(8,128)}, u32[]{:S(2)}) copy-start(f32[1,48,32,128]{3,2,1,0:T(8,128)} %param.5) | copy-start | bytes 2359300
  2.3 12.0 %copy-start.12 = (f32[31,512]{1,0:T(8,128)S(1)}, f32[31,512]{1,0:T(8,128)}, u32[]{:S(2)}) copy-start(f32[31,512]{1,0:T(8,128)} %constant.22.clone) | copy-start | bytes 190468
  3.0 5.1 %collective-permute-start = (f32[12,16,128]{2,1,0:T(8,128)S(1)}, f32[12,16,128]{2,1,0:T(8,128)S(1)}, u32[]{:S(2)}, u32[]{:S(2)}) collective-permute-start(f32[12,16,128]{2,1,0:T(8,128)S(1)} %get-tuple-element.41), channel_id=1, source_target_pairs={{0,32},{32,0},{1,33},{33,1},{2,34},{34,2},{3,35},{35,3},{4,36},{36... | collective-permute-start | bytes 294920 | tf_op jit(solution)/shard_map/ppermute | solution.py:354
  8.1 9.7 %collective-permute-start.1 = (f32[53,16,128]{2,1,0:T(8,128)S(1)}, f32[53,16,128]{2,1,0:T(8,128)S(1)}, u32[]{:S(2)}, u32[]{:S(2)}) collective-permute-start(f32[53,16,128]{2,1,0:T(8,128)S(1)} %get-tuple-element.43), channel_id=1, source_target_pairs={{0,1},{1,0},{2,3},{3,2},{4,5},{5,4},{6,7},{7,6},{8,9},{9,8},{10,11... | collective-permute-start | bytes 1302536 | tf_op jit(solution)/shard_map/ppermute | solution.py:362
  8.7 14.6 %collective-permute-start.2 = (f32[53,16,128]{2,1,0:T(8,128)S(1)}, f32[53,16,128]{2,1,0:T(8,128)S(1)}, u32[]{:S(2)}, u32[]{:S(2)}) collective-permute-start(f32[53,16,128]{2,1,0:T(8,128)S(1)} %get-tuple-element.44), channel_id=1, source_target_pairs={{1,2},{3,4},{5,6},{7,8},{9,10},{11,12},{13,14},{15,16},{17,18},{19... | collective-permute-start | bytes 1302536 | tf_op jit(solution)/shard_map/ppermute | solution.py:361
  14.9 1.0 copy-start.3
  16.0 10.3 %copy-start.6 = (bf16[6,256,256]{2,1,0:T(8,128)(2,1)}, bf16[6,256,256]{2,1,0:T(8,128)(2,1)S(1)}, u32[]{:S(2)}) copy-start(bf16[6,256,256]{2,1,0:T(8,128)(2,1)S(1)} %get-tuple-element.45.mats) | copy-start | bytes 2359300
  23.3 6.8 %copy-start.14 = (s32[4,2]{0,1:T(2,128)S(1)}, s32[4,2]{0,1:T(2,128)}, u32[]{:S(2)}) copy-start(s32[4,2]{0,1:T(2,128)} %param.7) | copy-start | bytes 100
  26.2 0.7 copy-start.10
  27.0 4.6 %collective-permute-start.3 = (f32[24,32,128]{2,1,0:T(8,128)}, f32[24,32,128]{2,1,0:T(8,128)S(1)}, u32[]{:S(2)}, u32[]{:S(2)}) collective-permute-start(f32[24,32,128]{2,1,0:T(8,128)} %get-tuple-element.47), channel_id=1, source_target_pairs={{0,64},{64,0},{128,192},{192,128},{1,65},{65,1},{129,193},{193,129... | collective-permute-start | bytes 1179656 | tf_op jit(solution)/shard_map/ppermute | solution.py:354
  30.1 1.5 %copy-start.4 = (bf16[4,384,384]{2,1,0:T(8,128)(2,1)S(1)}, bf16[4,384,384]{2,1,0:T(8,128)(2,1)}, u32[]{:S(2)}) copy-start(bf16[4,384,384]{2,1,0:T(8,128)(2,1)} %copy-done.3) | copy-start | bytes 3538948
  30.1 1.5 %copy-start.11 = (f32[24,32,128]{2,1,0:T(8,128)S(1)}, f32[24,32,128]{2,1,0:T(8,128)}, u32[]{:S(2)}) copy-start(f32[24,32,128]{2,1,0:T(8,128)} %copy-done.10) | copy-start | bytes 1179652
  31.6 4.0 %copy-start.7 = (bf16[6,256,256]{2,1,0:T(8,128)(2,1)S(1)}, bf16[6,256,256]{2,1,0:T(8,128)(2,1)}, u32[]{:S(2)}) copy-start(bf16[6,256,256]{2,1,0:T(8,128)(2,1)} %copy-done.6) | copy-start | bytes 2359300
  33.8 1.8 %collective-permute-start.4 = (f32[24,32,128]{2,1,0:T(8,128)S(1)}, f32[24,32,128]{2,1,0:T(8,128)S(1)}, u32[]{:S(2)}, u32[]{:S(2)}) collective-permute-start(f32[24,32,128]{2,1,0:T(8,128)S(1)} %get-tuple-element.50), channel_id=1, source_target_pairs={{0,64},{64,0},{128,192},{192,128},{1,65},{65,1},{129,193},{193,129... | collective-permute-start | bytes 1179656 | tf_op jit(solution)/shard_map/ppermute | solution.py:354
  37.6 6.7 %collective-permute-start.5 = (f32[27,16,128]{2,1,0:T(8,128)S(1)}, f32[27,16,128]{2,1,0:T(8,128)S(1)}, u32[]{:S(2)}, u32[]{:S(2)}) collective-permute-start(f32[27,16,128]{2,1,0:T(8,128)S(1)} %get-tuple-element.53), channel_id=1, source_target_pairs={{0,1},{1,0},{2,3},{3,2},{4,5},{5,4},{6,7},{7,6},{8,9},{9,8},{10,11... | collective-permute-start | bytes 663560 | tf_op jit(solution)/shard_map/ppermute | solution.py:362
  37.7 11.9 %collective-permute-start.6 = (f32[27,16,128]{2,1,0:T(8,128)S(1)}, f32[27,16,128]{2,1,0:T(8,128)S(1)}, u32[]{:S(2)}, u32[]{:S(2)}) collective-permute-start(f32[27,16,128]{2,1,0:T(8,128)S(1)} %get-tuple-element.54), channel_id=1, source_target_pairs={{1,2},{3,4},{5,6},{7,8},{9,10},{11,12},{13,14},{15,16},{17,18},{19... | collective-permute-start | bytes 663560 | tf_op jit(solution)/shard_map/ppermute | solution.py:361
  49.8 14.6 %collective-permute-start.8 = (f32[14,32,128]{2,1,0:T(8,128)S(1)}, f32[14,32,128]{2,1,0:T(8,128)S(1)}, u32[]{:S(2)}, u32[]{:S(2)}) collective-permute-start(f32[14,32,128]{2,1,0:T(8,128)S(1)} %get-tuple-element.56.high), channel_id=1, source_target_pairs={{0,128},{64,192},{128,0},{192,64},{1,129},{65,193},{129,1},{193,65... | collective-permute-start | bytes 688136 | tf_op jit(solution)/shard_map/ppermute | solution.py:354
  51.1 13.3 %collective-permute-start.7 = (f32[13,32,128]{2,1,0:T(8,128)S(1)}, f32[13,32,128]{2,1,0:T(8,128)S(1)}, u32[]{:S(2)}, u32[]{:S(2)}) collective-permute-start(f32[13,32,128]{2,1,0:T(8,128)S(1)} %get-tuple-element.55.low), channel_id=1, source_target_pairs={{0,128},{64,192},{128,0},{192,64},{1,129},{65,193},{129,1},{193,65... | collective-permute-start | bytes 638984 | tf_op jit(solution)/shard_map/ppermute | solution.py:354
  51.3 5.4 %collective-permute-start.10 = (f32[12,16,128]{2,1,0:T(8,128)S(1)}, f32[12,16,128]{2,1,0:T(8,128)S(1)}, u32[]{:S(2)}, u32[]{:S(2)}) collective-permute-start(f32[12,16,128]{2,1,0:T(8,128)S(1)} %get-tuple-element.57), channel_id=1, source_target_pairs={{0,160},{32,128},{64,224},{96,192},{128,32},{160,0},{192,96},{224,... | collective-permute-start | bytes 294920 | tf_op jit(solution)/shard_map/ppermute | solution.py:354
  53.8 10.5 %collective-permute-start.9 = (f32[12,16,128]{2,1,0:T(8,128)S(1)}, f32[12,16,128]{2,1,0:T(8,128)S(1)}, u32[]{:S(2)}, u32[]{:S(2)}) collective-permute-start(f32[12,16,128]{2,1,0:T(8,128)S(1)} %get-tuple-element.57), channel_id=1, source_target_pairs={{0,32},{32,0},{1,33},{33,1},{2,34},{34,2},{3,35},{35,3},{4,36},{36... | collective-permute-start | bytes 294920 | tf_op jit(solution)/shard_map/ppermute | solution.py:354
  64.5 5.4 %collective-permute-start.11 = (f32[27,16,128]{2,1,0:T(8,128)S(1)}, f32[27,16,128]{2,1,0:T(8,128)S(1)}, u32[]{:S(2)}, u32[]{:S(2)}) collective-permute-start(f32[27,16,128]{2,1,0:T(8,128)S(1)} %get-tuple-element.62), channel_id=1, source_target_pairs={{0,1},{1,0},{2,3},{3,2},{4,5},{5,4},{6,7},{7,6},{8,9},{9,8},{10,11... | collective-permute-start | bytes 663560 | tf_op jit(solution)/shard_map/ppermute | solution.py:362
  64.6 10.0 %collective-permute-start.12 = (f32[27,16,128]{2,1,0:T(8,128)S(1)}, f32[27,16,128]{2,1,0:T(8,128)S(1)}, u32[]{:S(2)}, u32[]{:S(2)}) collective-permute-start(f32[27,16,128]{2,1,0:T(8,128)S(1)} %get-tuple-element.63), channel_id=1, source_target_pairs={{1,2},{3,4},{5,6},{7,8},{9,10},{11,12},{13,14},{15,16},{17,18},{19... | collective-permute-start | bytes 663560 | tf_op jit(solution)/shard_map/ppermute | solution.py:361
  74.6 1.1 copy-start.8
  75.8 7.2 %copy-start.5 = (bf16[4,384,384]{2,1,0:T(8,128)(2,1)S(1)}, bf16[4,384,384]{2,1,0:T(8,128)(2,1)}, u32[]{:S(2)}) copy-start(bf16[4,384,384]{2,1,0:T(8,128)(2,1)} %copy-done.3) | copy-start | bytes 3538948
  77.9 5.0 %collective-permute-start.13 = (f32[24,32,128]{2,1,0:T(8,128)S(1)}, f32[24,32,128]{2,1,0:T(8,128)S(1)}, u32[]{:S(2)}, u32[]{:S(2)}) collective-permute-start(f32[24,32,128]{2,1,0:T(8,128)S(1)} %get-tuple-element.65), channel_id=1, source_target_pairs={{0,64},{64,0},{128,192},{192,128},{1,65},{65,1},{129,193},{193,129... | collective-permute-start | bytes 1179656 | tf_op jit(solution)/shard_map/ppermute | solution.py:354
  82.9 4.0 %copy-start.9 = (bf16[6,256,256]{2,1,0:T(8,128)(2,1)S(1)}, bf16[6,256,256]{2,1,0:T(8,128)(2,1)}, u32[]{:S(2)}) copy-start(bf16[6,256,256]{2,1,0:T(8,128)(2,1)} %copy-done.6) | copy-start | bytes 2359300
  85.2 1.8 %collective-permute-start.14 = (f32[24,32,128]{2,1,0:T(8,128)S(1)}, f32[24,32,128]{2,1,0:T(8,128)S(1)}, u32[]{:S(2)}, u32[]{:S(2)}) collective-permute-start(f32[24,32,128]{2,1,0:T(8,128)S(1)} %get-tuple-element.67), channel_id=1, source_target_pairs={{0,64},{64,0},{128,192},{192,128},{1,65},{65,1},{129,193},{193,129... | collective-permute-start | bytes 1179656 | tf_op jit(solution)/shard_map/ppermute | solution.py:354
  88.9 6.7 %collective-permute-start.15 = (f32[27,16,128]{2,1,0:T(8,128)S(1)}, f32[27,16,128]{2,1,0:T(8,128)S(1)}, u32[]{:S(2)}, u32[]{:S(2)}) collective-permute-start(f32[27,16,128]{2,1,0:T(8,128)S(1)} %get-tuple-element.70), channel_id=1, source_target_pairs={{0,1},{1,0},{2,3},{3,2},{4,5},{5,4},{6,7},{7,6},{8,9},{9,8},{10,11... | collective-permute-start | bytes 663560 | tf_op jit(solution)/shard_map/ppermute | solution.py:362
  89.0 11.9 %collective-permute-start.16 = (f32[27,16,128]{2,1,0:T(8,128)S(1)}, f32[27,16,128]{2,1,0:T(8,128)S(1)}, u32[]{:S(2)}, u32[]{:S(2)}) collective-permute-start(f32[27,16,128]{2,1,0:T(8,128)S(1)} %get-tuple-element.71), channel_id=1, source_target_pairs={{1,2},{3,4},{5,6},{7,8},{9,10},{11,12},{13,14},{15,16},{17,18},{19... | collective-permute-start | bytes 663560 | tf_op jit(solution)/shard_map/ppermute | solution.py:361
  101.1 10.2 %collective-permute-start.18 = (f32[12,32,128]{2,1,0:T(8,128)S(1)}, f32[12,32,128]{2,1,0:T(8,128)S(1)}, u32[]{:S(2)}, u32[]{:S(2)}) collective-permute-start(f32[12,32,128]{2,1,0:T(8,128)S(1)} %slice.53.high), channel_id=1, source_target_pairs={{0,128},{64,192},{128,0},{192,64},{1,129},{65,193},{129,1},{193,65... | collective-permute-start | bytes 589832 | tf_op jit(solution)/shard_map/ppermute | solution.py:354
  101.2 10.1 %collective-permute-start.17 = (f32[12,32,128]{2,1,0:T(8,128)S(1)}, f32[12,32,128]{2,1,0:T(8,128)S(1)}, u32[]{:S(2)}, u32[]{:S(2)}) collective-permute-start(f32[12,32,128]{2,1,0:T(8,128)S(1)} %slice.52.low), channel_id=1, source_target_pairs={{0,128},{64,192},{128,0},{192,64},{1,129},{65,193},{129,1},{193,65... | collective-permute-start | bytes 589832 | tf_op jit(solution)/shard_map/ppermute | solution.py:354
  102.7 4.2 %collective-permute-start.20 = (f32[6,16,128]{2,1,0:T(8,128)S(1)}, f32[6,16,128]{2,1,0:T(8,128)S(1)}, u32[]{:S(2)}, u32[]{:S(2)}) collective-permute-start(f32[6,16,128]{2,1,0:T(8,128)S(1)} %slice.54), channel_id=1, source_target_pairs={{0,160},{32,128},{64,224},{96,192},{128,32},{160,0},{192,96},{224,... | collective-permute-start | bytes 147464 | tf_op jit(solution)/shard_map/ppermute | solution.py:354
  102.9 8.4 %collective-permute-start.19 = (f32[6,16,128]{2,1,0:T(8,128)S(1)}, f32[6,16,128]{2,1,0:T(8,128)S(1)}, u32[]{:S(2)}, u32[]{:S(2)}) collective-permute-start(f32[6,16,128]{2,1,0:T(8,128)S(1)} %slice.54), channel_id=1, source_target_pairs={{0,32},{32,0},{1,33},{33,1},{2,34},{34,2},{3,35},{35,3},{4,36},{36... | collective-permute-start | bytes 147464 | tf_op jit(solution)/shard_map/ppermute | solution.py:354
  111.5 3.9 %collective-permute-start.21 = (f32[24,32,128]{2,1,0:T(8,128)S(1)}, f32[24,32,128]{2,1,0:T(8,128)S(1)}, u32[]{:S(2)}, u32[]{:S(2)}) collective-permute-start(f32[24,32,128]{2,1,0:T(8,128)S(1)} %last.1.mine), channel_id=1, source_target_pairs={{0,64},{64,0},{128,192},{192,128},{1,65},{65,1},{129,193},{193,129... | collective-permute-start | bytes 1179656 | tf_op jit(solution)/shard_map/ppermute | solution.py:354

commit v3 on v2

v3 whole, which is shorter than its diff:
```python
import functools

import jax
import jax.numpy as jnp
import numpy as np
from jax import lax
from jax.experimental import pallas as pl
from jax.experimental.pallas import tpu as pltpu
from jax.sharding import PartitionSpec as P

OMAX = 8
ITERS = 2
TAPS = 31
HALF = 15
EDGE = 16
F32 = jnp.float32
BUSY = 6000000000
BF16 = jnp.bfloat16
highest = lax.Precision.HIGHEST

NN = (((1,), (0,)), ((), ()))


def split(value):
    high = value.astype(BF16)
    low = (value - high.astype(F32)).astype(BF16)
    return high, low


def dot(a, b, dims):
    return lax.dot_general(a, b, dims, preferred_element_type=F32)


def rows3(a, b):
    n = a.shape[0] // 2
    both = dot(a, b[0], NN)
    return both[:n] + (dot(a[:n], b[1], NN) + both[n:])


def call(body, outs, args, scratch=(), flops=0, name=None, hbm=(), limit=8, aliases=None, out_place=pltpu.VMEM):
    def place(i, a):
        if i in hbm:
            return pltpu.HBM
        return pltpu.SMEM if a.ndim == 1 or a.dtype == jnp.int32 else pltpu.VMEM

    specs = [pl.BlockSpec(memory_space=place(i, a)) for i, a in enumerate(args)]
    outs = [jax.ShapeDtypeStruct(*o) for o in outs]
    moved = sum(int(np.prod(a.shape)) * a.dtype.itemsize for a in list(args) + outs)
    return pl.pallas_call(
        body,
        out_shape=outs,
        in_specs=specs,
        out_specs=[pl.BlockSpec(memory_space=out_place)] * len(outs),
        scratch_shapes=list(scratch),
        input_output_aliases=aliases or {},
        compiler_params=pltpu.CompilerParams(vmem_limit_bytes=limit << 20),
        cost_estimate=pl.CostEstimate(flops=flops, bytes_accessed=moved, transcendentals=0),
        name=name,
    )(*args)


def toeplitz(row, rows, width, shift):
    wide = jnp.broadcast_to(row[:, :width], (rows, width))
    return pltpu.roll(wide, shift % width, 1, stride=1, stride_axis=0)


MATS = 10
YF, IN, OUT, BT, YT = 0, 2, 4, 6, 8


def bands_body(taps, psf, offsets, kz, mats):
    for m in range(2):
        high, low = split(toeplitz(taps[m : m + 1], 384, 512, 0)[:, :384])
        for third in range(3):
            rows = slice(128 * third, 128 * third + 128)
            kz[m, 256 * third : 256 * third + 128] = high[rows]
            kz[m, 256 * third + 128 : 256 * third + 256] = low[rows]
    lane = lax.broadcasted_iota(jnp.int32, (64, 256), 1)

    def between(band, first, count, rest):
        at = lane[: band.shape[0]]
        return jnp.where((at >= first) & (at < first + count), band, rest)

    for v in range(2):
        row = taps[2 + v : 3 + v]
        for p in range(4):
            at = 32 * p
            none = jnp.zeros((32, 256), F32)
            inner = between(toeplitz(row, 32, 256, at - HALF), at, 32, none)
            outer = between(toeplitz(row, 32, 256, at + 1), at, 16, none)
            outer = between(toeplitz(row, 32, 256, at - 2 * HALF - 1), at + 16, 16, outer)
            for m, band in ((IN + v, inner), (OUT + v, outer)):
                mats[m, at : at + 32], mats[m, 128 + at : 160 + at] = split(band)
        rows = slice(128 * v, 128 * v + 128)
        mats[0, rows], mats[1, rows] = split(toeplitz(taps[6 + v : 7 + v], 128, 256, -HALF))
        mats[YT, :, rows], mats[YT + 1, :, rows] = split(toeplitz(taps[8 + v : 9 + v], 256, 256, -HALF)[:, :128])
    for p in range(4):
        both = jnp.zeros((64, 256), F32)
        for v in range(2):
            at = 128 * v + 32 * p
            both = between(toeplitz(taps[4 + v : 5 + v], 64, 256, at - 2 * HALF - 1), at, 32, both)
        rows = slice(64 * p, 64 * p + 64)
        mats[BT, rows], mats[BT + 1, rows] = split(both)


def placing(width, step, start):
    place = np.zeros((TAPS, width), np.float32)
    for k in range(TAPS):
        place[k, (step * (k - start)) % width] = 1
    return place


def bands(own, other, planes, psf, offsets):
    nz = 8 * planes
    z_rows = jnp.dot(jnp.stack([own[0], own[0, ::-1]]), placing(512, 8, HALF), precision=highest)
    rows = jnp.stack([own[1], other[1], own[1, ::-1], other[1, ::-1], own[2], other[2], own[2, ::-1], other[2, ::-1]])
    taps = jnp.concatenate([z_rows, jnp.pad(rows, ((0, 0), (0, 512 - TAPS)))])
    return call(bands_body, [((2, 2 * nz, nz), BF16), ((MATS, 256, 256), BF16)], [taps, psf, offsets], name="bands")


def pack_columns(value, at, width, scratch):
    flat = value.reshape(value.shape[0] * value.shape[1], 128)
    scratch[...] = flat.T
    return scratch[pl.ds(pl.multiple_of(at, 8), width), :]


def spread_columns(pack, at, width, scratch):
    for t, part in enumerate(pack):
        scratch[pl.ds(pl.multiple_of(at, 8), width), 128 * t : 128 * t + 128] = part
    return scratch[...].T


def norm_body(shape, psf, offsets, norm, norm_ext):
    nx, ny = shape
    views = offsets.shape[0]
    core = lax.axis_index("view") % 2
    x_first = 32 * lax.axis_index("ty")
    tx = lax.axis_index("tx")

    def window(view, dim, place, shift, extent):
        total = jnp.zeros(place.shape, F32)
        weight = 0.0
        for i in range(TAPS):
            tap = psf[(view * 3 + dim) * TAPS + TAPS - 1 - i]
            at = place + (i - HALF)
            moved = at + shift
            inside = (at >= 0) & (at < extent) & (moved >= 0) & (moved < extent)
            total = total + jnp.where(inside, tap, 0.0)
            weight = weight + tap
        return total / weight

    def iota(shape, dim):
        return lax.broadcasted_iota(jnp.int32, shape, dim)

    lane = iota((8, 128), 1)
    tile = jnp.minimum(iota((8, 128), 0), 2)
    flat_z = 24 * core + (128 * tile + lane) // EDGE
    flat_x = x_first + EDGE * (iota((8, 128), 0) % 2) + lane % EDGE
    acc = [jnp.zeros((32, 128), F32) for _ in range(24)]
    ext = [jnp.zeros((EDGE, 128), F32) for _ in range(6)]
    for v in range(views):
        sx, sy = offsets[v, 0], offsets[v, 1]
        in_z = window(v, 0, 24 * core + iota((24, 128), 0), 0, 48)
        in_x = window(v, 1, x_first + iota((32, 128), 0), sx, nx)
        in_y = window(v, 2, 128 * tx + lane, sy, ny)[0:1]
        in_e = window(v, 2, 128 - EDGE * tx + iota((EDGE, 128), 0), sy, ny)
        z_row = window(v, 0, flat_z, 0, 48)
        x_row = window(v, 1, flat_x, sx, nx)
        xy = in_x * in_y
        acc = [acc[z] + in_z[z : z + 1] * xy for z in range(24)]
        for k in range(6):
            ext[k] = ext[k] + in_e * (z_row[k % 3 : k % 3 + 1] * x_row[k // 3 : k // 3 + 1])
    for z in range(24):
        norm[z] = acc[z]
    for k in range(6):
        norm_ext[k] = ext[k]


def mesh_core():
    return lax.axis_index("view") % 2


def parity():
    return lax.axis_index("ty") % 2 == 1


def put_packs(value, at, width, turned, out, first):
    cols = pack_columns(value, at, width, turned)
    for t in range(3):
        out[first + t] = cols[:, 128 * t : 128 * t + 128]


def begin_body(est, pack_out, cur, turned, sem):
    tx = lax.axis_index("tx")
    copy = pltpu.make_async_copy(est.at[pl.ds(24 * mesh_core(), 24)], cur, sem)
    copy.start()
    copy.wait()
    for xh in range(2):
        put_packs(cur[:, 16 * xh : 16 * xh + 16, :], 112 * (1 - tx), 16, turned, pack_out, 3 * xh)


def raw_sides_body(raw, pack_out, turned):
    tx = lax.axis_index("tx")
    for xb in range(4):
        put_packs(raw[:, 8 * xb : 8 * xb + 8, :], 120 * (1 - tx), 8, turned, pack_out, 3 * xb)


def put_rims(top, bottom, even_out, odd_out, planes):
    odd = parity()
    even_out[planes] = jnp.where(odd, top, bottom)
    odd_out[planes] = jnp.where(odd, bottom, top)


def rims_body(est, cur_out, odd_out, even_out):
    cur_out[...] = est[pl.ds(24 * mesh_core(), 24)]
    put_rims(cur_out[:, 0:16, :], cur_out[:, 16:32, :], even_out, odd_out, slice(0, 24))
    odd_out[24:27] = jnp.zeros((3, 16, 128), F32)
    even_out[24:27] = jnp.zeros((3, 16, 128), F32)


def corners_body(pack, odd_in, even_in, odd_out, even_out):
    put_rims(pack[0:3], pack[3:6], even_out, odd_out, slice(24, 27))


def raw_rims_body(raw, pack, odd_out, even_out):
    put_rims(raw[:, 0:8, :], raw[:, 24:32, :], even_out, odd_out, slice(0, 48))
    for t in range(3):
        put_rims(pack[t][None], pack[9 + t][None], even_out, odd_out, slice(48 + t, 49 + t))


def register_body(offsets, raw, pack, from_odd, from_even, out, wide, turned):
    view, tx = lax.axis_index("view"), lax.axis_index("tx")
    sx, sy = offsets[view, 0], offsets[view, 1]
    odd = parity()
    above = jnp.where(odd, from_even[...], from_odd[...])
    below = jnp.where(odd, from_odd[...], from_even[...])
    wide[:, 0:8, 0:128] = above[0:48]
    wide[:, 8:40, 0:128] = raw[...]
    wide[:, 40:48, 0:128] = below[0:48]
    turned[...] = jnp.zeros_like(turned)
    for b in range(6):
        if b in (0, 5):
            parts = [(above if b == 0 else below)[48 + t] for t in range(3)]
        else:
            parts = [pack[3 * (b - 1) + t] for t in range(3)]
        wide[:, 8 * b : 8 * b + 8, 128:256] = spread_columns(parts, 120 * tx, 8, turned).reshape(48, 8, 128)
    for z in range(0, 48, 4):
        rows = pltpu.roll(wide[z : z + 4], lax.rem(40 - sx, 48), 1)[:, 0:32, :]
        out[z : z + 4] = pltpu.roll(rows, lax.rem(256 - sy, 256), 2)[:, :, 0:128]


def put_columns(rows, main, rim, tx, x_h, x_l, turned):
    x_h[:, rows, 0:128], x_l[:, rows, 0:128] = split(main)
    side = spread_columns(rim, 112 * tx, 16, turned).reshape(24, 16, 128)
    x_h[:, rows, 128:256], x_l[:, rows, 128:256] = split(side)


def blur_rows(x_h, x_l, yf, bx, g):
    z = slice(4 * g, 4 * g + 4)
    high, low = x_h[z].reshape(128, 256), x_l[z].reshape(128, 256)
    along_y = split(dot(high, yf[0], NN) + (dot(high, yf[1], NN) + dot(low, yf[0], NN)))
    for v in range(2):
        cols = slice(128 * v, 128 * v + 128)
        yield v, z, rows3(bx[v][:, 0:128], (along_y[0][:, cols], along_y[1][:, cols])).reshape(4, 32, 128)


def inner_body(cur, ext, mats, own, other, x_h, x_l, turned):
    tx = lax.axis_index("tx")
    turned[...] = jnp.zeros_like(turned)
    for xh in range(2):
        rows = slice(16 * xh, 16 * xh + 16)
        put_columns(rows, cur[:, rows, :], [ext[3 * xh + t] for t in range(3)], tx, x_h, x_l, turned)
    for g in range(6):
        for v, z, part in blur_rows(x_h, x_l, (mats[YT], mats[YT + 1]), (mats[IN], mats[IN + 1]), g):
            (own, other)[v][z] = part


def outer_body(from_odd, from_even, mats, in_own, in_other, own, other, x_h, x_l, turned):
    tx = lax.axis_index("tx")
    odd = parity()
    above = jnp.where(odd, from_even[...], from_odd[...])
    below = jnp.where(odd, from_odd[...], from_even[...])
    turned[...] = jnp.zeros_like(turned)
    for xh, rim in ((0, above), (1, below)):
        rows = slice(16 * xh, 16 * xh + 16)
        put_columns(rows, rim[0:24], [rim[24 + t] for t in range(3)], tx, x_h, x_l, turned)
    for g in range(6):
        for v, z, part in blur_rows(x_h, x_l, (mats[YT], mats[YT + 1]), (mats[OUT], mats[OUT + 1]), g):
            (own, other)[v][z] = (in_own, in_other)[v][z] + part


def along_z(kz, m, high, low):
    parts = []
    for third, reach in ((0, slice(0, 256)), (1, slice(0, 384)), (2, slice(128, 384))):
        parts.append(rows3(kz[m, 256 * third : 256 * third + 256, reach], (high[reach], low[reach])))
    return jnp.concatenate(parts)


def ratio_body(mine, theirs, seen, kz, keep, send, full):
    core = mesh_core()
    full[pl.ds(24 * core, 24)] = mine[...]
    full[pl.ds(24 * (1 - core), 24)] = theirs[...]
    for xp in range(2):
        def pair(ref):
            return jnp.concatenate(
                [ref[:, 16 * xp + 8 * i : 16 * xp + 8 * i + 8, :].reshape(384, 128) for i in range(2)], axis=1
            )
        blurred = along_z(kz, 0, *split(pair(full)))
        ratio = pair(seen) / blurred
        back = along_z(kz, 1, *split(ratio))
        for i in range(2):
            at = slice(16 * xp + 8 * i, 16 * xp + 8 * i + 8)
            full[:, at, :] = back[:, 128 * i : 128 * i + 128].reshape(48, 8, 128)
    keep[...] = full[pl.ds(24 * core, 24)]
    send[...] = full[pl.ds(24 * (1 - core), 24)]


def mirror_body(own, other, mats, odd_out, even_out, mid, mid_ext, sides, turned):
    tx = lax.axis_index("tx")
    parts = [split(ref[...].reshape(768, 128)) for ref in (own, other)]
    along_y = []
    for v in range(2):
        rows = slice(128 * v, 128 * v + 128)
        high = mats[YF, rows]
        along_y.append(
            split(
                dot(jnp.concatenate(parts[v], axis=1), jnp.concatenate([high, high]), NN)
                + dot(parts[v][0], mats[YF + 1, rows], NN)
            )
        )
    both_rows = mats[BT : BT + 2].reshape(512, 256)
    for g in range(6):
        z = slice(4 * g, 4 * g + 4)
        rows = slice(128 * g, 128 * g + 128)
        both = tuple(jnp.concatenate([along_y[0][i][rows], along_y[1][i][rows]], axis=0) for i in range(2))
        wide = rows3(both_rows, both).reshape(4, 64, 256)
        put_rims(wide[:, 0:16, 0:128], wide[:, 48:64, 0:128], even_out, odd_out, z)
        mid[z] = wide[:, 16:48, 0:128]
        sides[z] = wide[:, :, 128:256]
    cols = []
    for b in range(4):
        cols.append(pack_columns(sides[:, 16 * b : 16 * b + 16, :], 112 * tx, 16, turned))
    parts = [[c[:, 128 * t : 128 * t + 128] for t in range(3)] for c in cols]
    for t in range(3):
        put_rims(parts[0][t][None], parts[3][t][None], even_out, odd_out, slice(24 + t, 25 + t))
        mid_ext[t] = parts[1][t]
        mid_ext[3 + t] = parts[2][t]


def gather_body(mid, mid_ext, from_odd, from_even, sides_out, low_out, high_out, turned):
    tx = lax.axis_index("tx")
    odd = parity()
    above = jnp.where(odd, from_even[...], from_odd[...])
    below = jnp.where(odd, from_odd[...], from_even[...])
    for out, z in ((low_out, slice(0, 12)), (high_out, slice(12, 24))):
        out[:, 0:16, :] = mid[z, 0:16, :] + above[z]
        out[:, 16:32, :] = mid[z, 16:32, :] + below[z]
    sides_out[0:3] = mid_ext[0:3] + above[24:27]
    sides_out[3:6] = mid_ext[3:6] + below[24:27]
    if sides_out.shape[0] == 12:
        for xh in range(2):
            at = slice(16 * xh, 16 * xh + 16)
            both = jnp.concatenate([low_out[:, at, :], high_out[:, at, :]])
            put_packs(both, 112 * (1 - tx), 16, turned, sides_out, 6 + 3 * xh)


def join_body(mine, theirs, out):
    out[...] = mine[...] + theirs[...]


def new_estimate(side, low, high, p_low, p_high, cur, norm, cur_out, turned):
    tx = lax.axis_index("tx")
    turned[...] = jnp.zeros_like(turned)
    for xh in range(2):
        at = slice(16 * xh, 16 * xh + 16)
        parts = [side[3 * xh + t] for t in range(3)]
        edge = spread_columns(parts, 112 * (1 - tx), 16, turned).reshape(24, 16, 128)
        for mine, theirs, z in ((low, p_low, slice(0, 12)), (high, p_high, slice(12, 24))):
            total = mine[:, at, :] + theirs[:, at, :] + edge[z]
            cur_out[z, at, :] = cur[z, at, :] * total / norm[z, at, :]


def update_body(
    side, low, high, p_low, p_high, cur, norm, joined, ext, norm_ext, cur_out, ext_out, odd_out, even_out, turned
):
    new_estimate(side, low, high, p_low, p_high, cur, norm, cur_out, turned)
    ext_out[...] = ext[0:6] * (side[6:12] + joined[0:6]) / norm_ext[...]
    put_rims(cur_out[:, 0:16, :], cur_out[:, 16:32, :], even_out, odd_out, slice(0, 24))
    put_rims(ext_out[0:3], ext_out[3:6], even_out, odd_out, slice(24, 27))


def whole_body(mine, theirs, out, sems):
    core = mesh_core()
    copies = [
        pltpu.make_async_copy(part, out.at[pl.ds(24 * half, 24)], sems.at[i])
        for i, (part, half) in enumerate(((mine, core), (theirs, 1 - core)))
    ]
    for copy in copies:
        copy.start()
    for copy in copies:
        copy.wait()


def swap(value, axis, by, sizes):
    count = int(np.prod(sizes))
    return lax.ppermute(value, axis, [(i, i ^ by) for i in range(count)])


def rim_swap(odd, even):
    rows = lax.axis_size("ty")
    odd_pairs = [(i, i + 1) for i in range(1, rows - 1, 2)]
    odd_pairs += [(b, a) for a, b in odd_pairs]
    from_odd = lax.ppermute(odd, "ty", odd_pairs)
    from_even = lax.ppermute(even, "ty", [(i, i ^ 1) for i in range(rows)])
    return from_odd, from_even


def shards(raw_views, psf_taps, offsets, estimate):
    depth, tile_x, tile_y = estimate.shape
    half = depth // 2
    view = lax.axis_index("view")
    raw = raw_views[0]

    tile_half = ((half, tile_x, tile_y), F32)
    tile_quarter = ((half // 2, tile_x, tile_y), F32)
    pack = ((6, EDGE, 128), F32)
    rim = ((half + 3, EDGE, 128), F32)
    turned = pltpu.VMEM((128, 384), F32)
    two_sems = pltpu.SemaphoreType.DMA((2,))

    (ext,) = call(
        begin_body,
        [pack],
        [estimate],
        [pltpu.VMEM((half, tile_x, tile_y), F32), turned, pltpu.SemaphoreType.DMA],
        name="begin",
        hbm=(0,),
        limit=62,
    )
    ext = swap(ext, ("view", "tx"), 5, (4, 2))
    (sides,) = call(raw_sides_body, [((12, OMAX, 128), F32)], [raw], [turned], flops=BUSY, name="raw_sides")
    sides = swap(sides, "tx", 1, (2,))
    cur, odd, even = call(rims_body, [tile_half, rim, rim], [estimate], name="rims")

    kernels = psf_taps / jnp.sum(psf_taps, axis=-1, keepdims=True)
    own = lax.dynamic_index_in_dim(kernels, view, 0, keepdims=False)
    other = lax.dynamic_index_in_dim(kernels, view ^ 1, 0, keepdims=False)
    flat_psf = psf_taps.reshape(-1)
    kz, mats = bands(own, other, depth, flat_psf, offsets)
    extents = (tile_x * lax.axis_size("ty"), tile_y * lax.axis_size("tx"))
    norm, norm_ext = call(
        functools.partial(norm_body, extents), [tile_half, pack], [flat_psf, offsets], name="norm"
    )

    odd, even = call(corners_body, [rim, rim], [ext, odd, even], name="corners", aliases={1: 0, 2: 1})
    from_odd, from_even = rim_swap(odd, even)
    raw_rim = ((depth + 3, OMAX, 128), F32)
    raw_odd, raw_even = call(raw_rims_body, [raw_rim, raw_rim], [raw, sides], name="raw_rims")
    raw_from = rim_swap(raw_odd, raw_even)
    columns = [pltpu.VMEM((half, 32, 256), BF16), pltpu.VMEM((half, 32, 256), BF16), turned]
    seen = None

    for iteration in range(ITERS):
        inner = call(
            inner_body, [tile_half, tile_half], [cur, ext, mats], columns, flops=BUSY, name="inner"
        )
        mine, theirs = call(
            outer_body,
            [tile_half, tile_half],
            [from_odd, from_even, mats, *inner],
            columns,
            flops=BUSY,
            name="outer",
        )
        theirs = swap(theirs, "view", 1, (4,))
        if seen is None:
            (seen,) = call(
                register_body,
                [((depth, tile_x, tile_y), F32)],
                [offsets, raw, sides, *raw_from],
                [pltpu.VMEM((depth, tile_x + 2 * OMAX, 256), F32), turned],
                flops=BUSY,
                name="register",
            )
        keep, send = call(
            ratio_body,
            [tile_half, tile_half],
            [mine, theirs, seen, kz],
            [pltpu.VMEM((depth, tile_x, tile_y), F32)],
            flops=3 * 2 * 2 * 384 * 384 * 512,
            name="ratio",
        )
        send = swap(send, "view", 1, (4,))
        odd, even, mid, mid_ext = call(
            mirror_body,
            [rim, rim, tile_half, pack],
            [keep, send, mats],
            [pltpu.VMEM((half, 64, 128), F32), turned],
            flops=3 * 2 * (1536 * 128 * 256 + 6 * 256 * 256 * 256),
            name="mirror",
        )
        from_odd, from_even = rim_swap(odd, even)
        last = iteration == ITERS - 1
        sides, low, high = call(
            gather_body,
            [pack if last else ((12, EDGE, 128), F32), tile_quarter, tile_quarter],
            [mid, mid_ext, from_odd, from_even],
            [turned],
            name="gather",
        )
        theirs = swap(sides, "view", 2, (4,))
        p_low = swap(low, "view", 2, (4,))
        p_high = swap(high, "view", 2, (4,))
        (joined,) = call(join_body, [(sides.shape, F32)], [sides, theirs], flops=BUSY, name="join")
        side = swap(joined, ("view", "tx"), 5, (4, 2))
        if last:
            (cur,) = call(new_estimate, [tile_half], [side, low, high, p_low, p_high, cur, norm], [turned], name="last")
            break
        cur, ext, odd, even = call(
            update_body,
            [tile_half, pack, rim, rim],
            [side, low, high, p_low, p_high, cur, norm, joined, ext, norm_ext],
            [turned],
            name="update",
        )
        from_odd, from_even = rim_swap(odd, even)
    far = swap(cur, "view", 1, (4,))
    (out,) = call(whole_body, [((depth, tile_x, tile_y), F32)], [cur, far], [two_sems], name="whole", out_place=pl.ANY)
    return out


def solution(mesh):
    placed = (P("view", None, "ty", "tx"), P(), P(), P(None, "ty", "tx"))
    return jax.shard_map(
        shards, mesh=mesh, in_specs=placed, out_specs=P(None, "ty", "tx"), check_vma=False
    )
```

time: 117 us -> 104 us (0.89)
  waiting for transfers between devices: 47.1 us -> 38 us
  local copies, waits for them, and re-layouts: 5.76 us -> 1.85 us
  Pallas kernels: 20.2 us -> 18.3 us
  starting transfers between devices: 42.7 us -> 44.4 us
    ppermute x4 -> x5, waiting for transfers between devices: 4.65 us -> 0.01 us  [rim_swap(): from_even = lax.ppermute(even, 'ty', [(i, i ^ 1) for i in range(rows)])]
    ppermute x14 -> x15, waiting for transfers between devices: 21.9 us -> 17.4 us  [swap(): return lax.ppermute(value, axis, [(i, i ^ by) for i in range(count)])]
    unnamed x32 -> x14, local copies, waits for them, and re-layouts: 5.31 us -> 1.25 us
    pallas_call x16 -> x23, Pallas kernels: 20.2 us -> 18.3 us  [call(): pl.pallas_call(body, out_shape=outs, in_specs=specs, out_specs=[pl.BlockS...]
    ppermute x4 -> x5, starting transfers between devices: 21 us -> 22.1 us  [rim_swap(): from_odd = lax.ppermute(odd, 'ty', odd_pairs)]
    ppermute x14 -> x15, starting transfers between devices: 20.9 us -> 21.8 us  [swap(): return lax.ppermute(value, axis, [(i, i ^ by) for i in range(count)])]
    ppermute x4 -> x5, waiting for transfers between devices: 20.6 us -> 20.6 us  [rim_swap(): from_odd = lax.ppermute(odd, 'ty', odd_pairs)]
  transfers between devices with their start and end apart: 22 -> 25, of which waited for: 16 -> 14; matrix products, arithmetic and copies ran while one was open for 1% -> 1% of each run, Pallas kernels for 4% -> 8%
where the time goes in v3:
time: 104 us; the launch traced here: 103 us
  starting transfers between devices  44.4 us (43%)
  waiting for transfers between devices  38 us (37%)
  Pallas kernels  18.3 us (18%)
  local copies, waits for them, and re-layouts  1.85 us (2%)
    ppermute x5, starting transfers between devices, rim_swap(): from_odd = lax.ppermute(odd, 'ty', odd_pairs)  22.1 us
    ppermute x15, starting transfers between devices, swap(): return lax.ppermute(value, axis, [(i, i ^ by) for i in range(count)])  21.8 us
    ppermute x5, waiting for transfers between devices, rim_swap(): from_odd = lax.ppermute(odd, 'ty', odd_pairs)  20.6 us
    pallas_call x23, Pallas kernels, call(): pl.pallas_call(body, out_shape=outs, in_specs=specs, out_specs=[pl.BlockS...  18.3 us
    ppermute x15, waiting for transfers between devices, swap(): return lax.ppermute(value, axis, [(i, i ^ by) for i in range(count)])  17.4 us
  transfers between devices with their start and end apart: 25, of which 14 were waited for; matrix products, arithmetic and copies ran while one was open for 1% of the time, Pallas kernels for 8%

profile of v3, /device:TPU:121, one launch (start us, length us, event | category | flops | bytes accessed | tf_op | source)
XLA Modules:
  0.0 103.4 jit_solution(745648197348091109)
XLA Ops:
  0.0 1.8 %begin.1 = f32[6,16,128]{2,1,0:T(8,128)} custom-call(f32[48,32,128]{2,1,0:T(8,128)} %est.3), custom_call_target="tpu_custom_call" | custom-call | bytes 835584 | tf_op jit(solution)/shard_map/begin/pallas_call | solution.py:49
  1.8 2.6 %collective-permute-start = (f32[6,16,128]{2,1,0:T(8,128)}, f32[6,16,128]{2,1,0:T(8,128)S(1)}, u32[]{:S(2)}, u32[]{:S(2)}) collective-permute-start(f32[6,16,128]{2,1,0:T(8,128)} %begin.1), channel_id=1, source_target_pairs={{0,160},{32,128},{64,224},{96,192},{128,32},{160,0},{192,96},{224,... | collective-permute-start | bytes 147464 | tf_op jit(solution)/shard_map/ppermute | solution.py:406
  4.4 1.1 %copy-done.1 = f32[1,48,32,128]{3,2,1,0:T(8,128)S(1)} copy-done((f32[1,48,32,128]{3,2,1,0:T(8,128)S(1)}, f32[1,48,32,128]{3,2,1,0:T(8,128)}, u32[]{:S(2)}) %copy-start.1) | copy-done | bytes 786456
  5.5 0.3 raw_sides.1
  5.8 0.6 collective-permute-start.4
  6.6 0.1 rev.16
  6.7 0.1 rev.17
  6.8 0.1 rev.18
  6.9 0.1 rev.19
  7.0 0.1 rev.15
  7.1 0.1 fusion
  7.4 0.1 copy.12.offsets
  7.6 1.1 %bands.1 = (bf16[2,768,384]{2,1,0:T(8,128)(2,1)S(1)}, bf16[10,256,256]{2,1,0:T(8,128)(2,1)S(1)}) custom-call(f32[10,512]{1,0:T(8,128)S(1)} %select_maximum_fusion.taps, f32[372]{0:T(512)S(1)} %reshape.9.psf, s32[4,2]{1,0:T(4,128)S(1)} %copy.12.offsets), custom_call_target="tpu_custom_call" | custom-call | bytes 2512368 | tf_op jit(solution)/shard_map/bands/pallas_call | solution.py:49
  8.7 4.4 %collective-permute-start.1 = (f32[27,16,128]{2,1,0:T(8,128)S(1)}, f32[27,16,128]{2,1,0:T(8,128)S(1)}, u32[]{:S(2)}, u32[]{:S(2)}) collective-permute-start(f32[27,16,128]{2,1,0:T(8,128)S(1)} %get-tuple-element.48), channel_id=1, source_target_pairs={{1,2},{3,4},{5,6},{7,8},{9,10},{11,12},{13,14},{15,16},{17,18},{19... | collective-permute-start | bytes 663560 | tf_op jit(solution)/shard_map/ppermute | solution.py:413
  13.2 0.1 collective-permute-start.2
  13.3 4.5 %collective-permute-start.5 = (f32[51,8,128]{2,1,0:T(8,128)S(1)}, f32[51,8,128]{2,1,0:T(8,128)S(1)}, u32[]{:S(2)}, u32[]{:S(2)}) collective-permute-start(f32[51,8,128]{2,1,0:T(8,128)S(1)} %get-tuple-element.56), channel_id=1, source_target_pairs={{1,2},{3,4},{5,6},{7,8},{9,10},{11,12},{13,14},{15,16},{17,18},{19... | collective-permute-start | bytes 626696 | tf_op jit(solution)/shard_map/ppermute | solution.py:413
  17.8 0.1 collective-permute-start.6
  17.9 1.1 %inner.2 = (f32[24,32,128]{2,1,0:T(8,128)S(1)}, f32[24,32,128]{2,1,0:T(8,128)S(1)}) custom-call(f32[24,32,128]{2,1,0:T(8,128)S(1)} %get-tuple-element.51.cur, f32[6,16,128]{2,1,0:T(8,128)S(1)} %collective-permute-done.pack.ext, bf16[10,256,256]{2,1,0:T(8,128)(2,1)S(1)} %get-tuple-element.50.mats), custom_call_target="tpu_custom_call" | custom-call | flops 6000000000 | bytes 2539520 | tf_op jit(solution)/shard_map/inner/pallas_call | solution.py:49
  19.0 0.7 collective-permute-done.1.from_odd
  19.6 1.1 %outer.2 = (f32[24,32,128]{2,1,0:T(8,128)S(1)}, f32[24,32,128]{2,1,0:T(8,128)S(1)}) custom-call(f32[27,16,128]{2,1,0:T(8,128)S(1)} %collective-permute-done.1.from_odd, f32[27,16,128]{2,1,0:T(8,128)S(1)} %collective-permute-done.2.from_even, bf16[10,256,256]{2,1,0:T(8,128)(2,1)S(1)} %get-tuple-element.50.mats, f32[24,32,128]{2,1,0:T(8,128)S(1)} %get-tuple-element.52.in_own, ...), custom_call_target="tpu_custom_call" | custom-call | flops 6000000000 | bytes 3325952 | tf_op jit(solution)/shard_map/outer/pallas_call | solution.py:49
  20.7 2.3 %collective-permute-start.3 = (f32[24,32,128]{2,1,0:T(8,128)S(1)}, f32[24,32,128]{2,1,0:T(8,128)S(1)}, u32[]{:S(2)}, u32[]{:S(2)}) collective-permute-start(f32[24,32,128]{2,1,0:T(8,128)S(1)} %get-tuple-element.55), channel_id=1, source_target_pairs={{0,64},{64,0},{128,192},{192,128},{1,65},{65,1},{129,193},{193,129... | collective-permute-start | bytes 1179656 | tf_op jit(solution)/shard_map/ppermute | solution.py:406
  23.0 0.9 collective-permute-done.5.from_odd
  24.0 1.4 %register.1.seen = f32[48,32,128]{2,1,0:T(8,128)S(1)} custom-call(s32[4,2]{1,0:T(4,128)S(1)} %copy.12.offsets, f32[48,32,128]{2,1,0:T(8,128)S(1)} %bitcast.14, f32[12,8,128]{2,1,0:T(8,128)S(1)} %collective-permute-done.4.pack, f32[51,8,128]{2,1,0:T(8,128)S(1)} %collective-permute-done.5.from_odd, f32[51,8,128]{2,1,0:T(8,128)S(1)} %collective-permute-done.6.from_even), custom_call_target="tpu_custom_call" | custom-call | flops 6000000000 | bytes 2039840 | tf_op jit(solution)/shard_map/register/pallas_call | solution.py:49
  25.4 1.4 %ratio.2 = (f32[24,32,128]{2,1,0:T(8,128)S(1)}, f32[24,32,128]{2,1,0:T(8,128)S(1)}) custom-call(f32[24,32,128]{2,1,0:T(8,128)S(1)} %get-tuple-element.54.mine, f32[24,32,128]{2,1,0:T(8,128)S(1)} %collective-permute-done.3.theirs, f32[48,32,128]{2,1,0:T(8,128)S(1)} %register.1.seen, bf16[2,768,384]{2,1,0:T(8,128)(2,1)S(1)} %get-tuple-element.58.kz), custom_call_target="tpu_custom_call" | custom-call | flops 905969664 | bytes 3538944 | tf_op jit(solution)/shard_map/ratio/pallas_call | solution.py:49
  26.8 2.4 %collective-permute-start.7 = (f32[24,32,128]{2,1,0:T(8,128)S(1)}, f32[24,32,128]{2,1,0:T(8,128)S(1)}, u32[]{:S(2)}, u32[]{:S(2)}) collective-permute-start(f32[24,32,128]{2,1,0:T(8,128)S(1)} %get-tuple-element.60), channel_id=1, source_target_pairs={{0,64},{64,0},{128,192},{192,128},{1,65},{65,1},{129,193},{193,129... | collective-permute-start | bytes 1179656 | tf_op jit(solution)/shard_map/ppermute | solution.py:406
  29.2 1.3 %collective-permute-done.7.other = f32[24,32,128]{2,1,0:T(8,128)S(1)} collective-permute-done((f32[24,32,128]{2,1,0:T(8,128)S(1)}, f32[24,32,128]{2,1,0:T(8,128)S(1)}, u32[]{:S(2)}, u32[]{:S(2)}) %collective-permute-start.7) | collective-permute-done | bytes 393248 | tf_op jit(solution)/shard_map/ppermute | solution.py:406
  30.6 1.3 %mirror.2 = (f32[27,16,128]{2,1,0:T(8,128)S(1)}, f32[27,16,128]{2,1,0:T(8,128)S(1)}, f32[24,32,128]{2,1,0:T(8,128)S(1)}, f32[6,16,128]{2,1,0:T(8,128)S(1)}) custom-call(f32[24,32,128]{2,1,0:T(8,128)S(1)} %get-tuple-element.59.own, f32[24,32,128]{2,1,0:T(8,128)S(1)} %collective-permute-done.7.other, bf16[10,256,256]{2,1,0:T(8,128)(2,1)S(1)} %get-tuple-element.50.mats), custom_call_target="tpu_custom_call" | custom-call | flops 905969664 | bytes 2981888 | tf_op jit(solution)/shard_map/mirror/pallas_call | solution.py:49
  31.9 4.4 %collective-permute-start.8 = (f32[27,16,128]{2,1,0:T(8,128)S(1)}, f32[27,16,128]{2,1,0:T(8,128)S(1)}, u32[]{:S(2)}, u32[]{:S(2)}) collective-permute-start(f32[27,16,128]{2,1,0:T(8,128)S(1)} %get-tuple-element.63), channel_id=1, source_target_pairs={{1,2},{3,4},{5,6},{7,8},{9,10},{11,12},{13,14},{15,16},{17,18},{19... | collective-permute-start | bytes 663560 | tf_op jit(solution)/shard_map/ppermute | solution.py:413
  36.3 0.1 collective-permute-start.9
  36.4 7.3 %collective-permute-done.8.from_odd = f32[27,16,128]{2,1,0:T(8,128)S(1)} collective-permute-done((f32[27,16,128]{2,1,0:T(8,128)S(1)}, f32[27,16,128]{2,1,0:T(8,128)S(1)}, u32[]{:S(2)}, u32[]{:S(2)}) %collective-permute-start.8) | collective-permute-done | bytes 221216 | tf_op jit(solution)/shard_map/ppermute | solution.py:413
  43.7 0.2 gather.2
  44.0 0.3 collective-permute-start.10
  44.3 1.2 %collective-permute-start.12 = (f32[12,32,128]{2,1,0:T(8,128)S(1)}, f32[12,32,128]{2,1,0:T(8,128)S(1)}, u32[]{:S(2)}, u32[]{:S(2)}) collective-permute-start(f32[12,32,128]{2,1,0:T(8,128)S(1)} %get-tuple-element.66.low), channel_id=1, source_target_pairs={{0,128},{64,192},{128,0},{192,64},{1,129},{65,193},{129,1},{193,65... | collective-permute-start | bytes 589832 | tf_op jit(solution)/shard_map/ppermute | solution.py:406
  45.5 0.3 collective-permute-start.13
  45.8 1.7 %collective-permute-done.10.theirs = f32[12,16,128]{2,1,0:T(8,128)S(1)} collective-permute-done((f32[12,16,128]{2,1,0:T(8,128)S(1)}, f32[12,16,128]{2,1,0:T(8,128)S(1)}, u32[]{:S(2)}, u32[]{:S(2)}) %collective-permute-start.10) | collective-permute-done | bytes 98336 | tf_op jit(solution)/shard_map/ppermute | solution.py:406
  47.5 2.1 %collective-permute-start.11 = (f32[12,16,128]{2,1,0:T(8,128)S(1)}, f32[12,16,128]{2,1,0:T(8,128)S(1)}, u32[]{:S(2)}, u32[]{:S(2)}) collective-permute-start(f32[12,16,128]{2,1,0:T(8,128)S(1)} %join.2.joined), channel_id=1, source_target_pairs={{0,160},{32,128},{64,224},{96,192},{128,32},{160,0},{192,96},{224,... | collective-permute-start | bytes 294920 | tf_op jit(solution)/shard_map/ppermute | solution.py:406
  49.6 2.3 %norm.1 = (f32[24,32,128]{2,1,0:T(8,128)S(1)}, f32[6,16,128]{2,1,0:T(8,128)S(1)}) custom-call(f32[372]{0:T(512)S(1)} %reshape.9.psf, s32[4,2]{1,0:T(4,128)S(1)} %copy.12.offsets), custom_call_target="tpu_custom_call" | custom-call | bytes 443888 | tf_op jit(solution)/shard_map/norm/pallas_call | solution.py:49
  51.9 3.6 %collective-permute-done.13.p_high = f32[12,32,128]{2,1,0:T(8,128)S(1)} collective-permute-done((f32[12,32,128]{2,1,0:T(8,128)S(1)}, f32[12,32,128]{2,1,0:T(8,128)S(1)}, u32[]{:S(2)}, u32[]{:S(2)}) %collective-permute-start.13) | collective-permute-done | bytes 196640 | tf_op jit(solution)/shard_map/ppermute | solution.py:406
  55.6 0.2 update.1
  55.8 4.4 %collective-permute-start.14 = (f32[27,16,128]{2,1,0:T(8,128)S(1)}, f32[27,16,128]{2,1,0:T(8,128)S(1)}, u32[]{:S(2)}, u32[]{:S(2)}) collective-permute-start(f32[27,16,128]{2,1,0:T(8,128)S(1)} %get-tuple-element.70), channel_id=1, source_target_pairs={{1,2},{3,4},{5,6},{7,8},{9,10},{11,12},{13,14},{15,16},{17,18},{19... | collective-permute-start | bytes 663560 | tf_op jit(solution)/shard_map/ppermute | solution.py:413
  60.2 0.1 collective-permute-start.15
  60.3 1.1 %inner.3 = (f32[24,32,128]{2,1,0:T(8,128)S(1)}, f32[24,32,128]{2,1,0:T(8,128)S(1)}) custom-call(f32[24,32,128]{2,1,0:T(8,128)S(1)} %get-tuple-element.72.cur, f32[6,16,128]{2,1,0:T(8,128)S(1)} %get-tuple-element.73.ext, bf16[10,256,256]{2,1,0:T(8,128)(2,1)S(1)} %get-tuple-element.50.mats), custom_call_target="tpu_custom_call" | custom-call | flops 6000000000 | bytes 2539520 | tf_op jit(solution)/shard_map/inner/pallas_call | solution.py:49
  61.3 4.4 %collective-permute-done.14.from_odd = f32[27,16,128]{2,1,0:T(8,128)S(1)} collective-permute-done((f32[27,16,128]{2,1,0:T(8,128)S(1)}, f32[27,16,128]{2,1,0:T(8,128)S(1)}, u32[]{:S(2)}, u32[]{:S(2)}) %collective-permute-start.14) | collective-permute-done | bytes 221216 | tf_op jit(solution)/shard_map/ppermute | solution.py:413
  65.8 1.1 %outer.3 = (f32[24,32,128]{2,1,0:T(8,128)S(1)}, f32[24,32,128]{2,1,0:T(8,128)S(1)}) custom-call(f32[27,16,128]{2,1,0:T(8,128)S(1)} %collective-permute-done.14.from_odd, f32[27,16,128]{2,1,0:T(8,128)S(1)} %collective-permute-done.15.from_even, bf16[10,256,256]{2,1,0:T(8,128)(2,1)S(1)} %get-tuple-element.50.mats, ...), custom_call_target="tpu_custom_call" | custom-call | flops 6000000000 | bytes 3325952 | tf_op jit(solution)/shard_map/outer/pallas_call | solution.py:49
  66.8 3.4 %collective-permute-start.16 = (f32[24,32,128]{2,1,0:T(8,128)S(1)}, f32[24,32,128]{2,1,0:T(8,128)S(1)}, u32[]{:S(2)}, u32[]{:S(2)}) collective-permute-start(f32[24,32,128]{2,1,0:T(8,128)S(1)} %get-tuple-element.77), channel_id=1, source_target_pairs={{0,64},{64,0},{128,192},{192,128},{1,65},{65,1},{129,193},{193,129... | collective-permute-start | bytes 1179656 | tf_op jit(solution)/shard_map/ppermute | solution.py:406
  70.2 1.3 %collective-permute-done.16.theirs = f32[24,32,128]{2,1,0:T(8,128)S(1)} collective-permute-done((f32[24,32,128]{2,1,0:T(8,128)S(1)}, f32[24,32,128]{2,1,0:T(8,128)S(1)}, u32[]{:S(2)}, u32[]{:S(2)}) %collective-permute-start.16) | collective-permute-done | bytes 393248 | tf_op jit(solution)/shard_map/ppermute | solution.py:406
  71.5 1.4 %ratio.3 = (f32[24,32,128]{2,1,0:T(8,128)S(1)}, f32[24,32,128]{2,1,0:T(8,128)S(1)}) custom-call(f32[24,32,128]{2,1,0:T(8,128)S(1)} %get-tuple-element.76.mine, f32[24,32,128]{2,1,0:T(8,128)S(1)} %collective-permute-done.16.theirs, f32[48,32,128]{2,1,0:T(8,128)S(1)} %register.1.seen, bf16[2,768,384]{2,1,0:T(8,128)(2,1)S(1)} %get-tuple-element.58.kz), custom_call_target="tpu_custom_call" | custom-call | flops 905969664 | bytes 3538944 | tf_op jit(solution)/shard_map/ratio/pallas_call | solution.py:49
  73.0 0.5 collective-permute-start.17
  73.4 1.4 %collective-permute-done.17.other = f32[24,32,128]{2,1,0:T(8,128)S(1)} collective-permute-done((f32[24,32,128]{2,1,0:T(8,128)S(1)}, f32[24,32,128]{2,1,0:T(8,128)S(1)}, u32[]{:S(2)}, u32[]{:S(2)}) %collective-permute-start.17) | collective-permute-done | bytes 393248 | tf_op jit(solution)/shard_map/ppermute | solution.py:406
  74.8 1.3 %mirror.3 = (f32[27,16,128]{2,1,0:T(8,128)S(1)}, f32[27,16,128]{2,1,0:T(8,128)S(1)}, f32[24,32,128]{2,1,0:T(8,128)S(1)}, f32[6,16,128]{2,1,0:T(8,128)S(1)}) custom-call(f32[24,32,128]{2,1,0:T(8,128)S(1)} %get-tuple-element.78.own, f32[24,32,128]{2,1,0:T(8,128)S(1)} %collective-permute-done.17.other, bf16[10,256,256]{2,1,0:T(8,128)(2,1)S(1)} %get-tuple-element.50.mats), custom_call_target="tpu_custom_call" | custom-call | flops 905969664 | bytes 2981888 | tf_op jit(solution)/shard_map/mirror/pallas_call | solution.py:49
  76.1 4.4 %collective-permute-start.18 = (f32[27,16,128]{2,1,0:T(8,128)S(1)}, f32[27,16,128]{2,1,0:T(8,128)S(1)}, u32[]{:S(2)}, u32[]{:S(2)}) collective-permute-start(f32[27,16,128]{2,1,0:T(8,128)S(1)} %get-tuple-element.82), channel_id=1, source_target_pairs={{1,2},{3,4},{5,6},{7,8},{9,10},{11,12},{13,14},{15,16},{17,18},{19... | collective-permute-start | bytes 663560 | tf_op jit(solution)/shard_map/ppermute | solution.py:413
  80.5 0.1 collective-permute-start.19
  80.6 7.3 %collective-permute-done.18.from_odd = f32[27,16,128]{2,1,0:T(8,128)S(1)} collective-permute-done((f32[27,16,128]{2,1,0:T(8,128)S(1)}, f32[27,16,128]{2,1,0:T(8,128)S(1)}, u32[]{:S(2)}, u32[]{:S(2)}) %collective-permute-start.18) | collective-permute-done | bytes 221216 | tf_op jit(solution)/shard_map/ppermute | solution.py:413
  88.0 0.6 collective-permute-start.20
  88.6 1.0 collective-permute-start.22
  89.6 0.5 collective-permute-start.23
  90.1 1.0 collective-permute-done.20.theirs
  91.1 1.9 %collective-permute-start.21 = (f32[6,16,128]{2,1,0:T(8,128)S(1)}, f32[6,16,128]{2,1,0:T(8,128)S(1)}, u32[]{:S(2)}, u32[]{:S(2)}) collective-permute-start(f32[6,16,128]{2,1,0:T(8,128)S(1)} %join.3), channel_id=1, source_target_pairs={{0,160},{32,128},{64,224},{96,192},{128,32},{160,0},{192,96},{224,... | collective-permute-start | bytes 147464 | tf_op jit(solution)/shard_map/ppermute | solution.py:406
  93.0 2.3 %collective-permute-done.21.side = f32[6,16,128]{2,1,0:T(8,128)S(1)} collective-permute-done((f32[6,16,128]{2,1,0:T(8,128)S(1)}, f32[6,16,128]{2,1,0:T(8,128)S(1)}, u32[]{:S(2)}, u32[]{:S(2)}) %collective-permute-start.21) | collective-permute-done | bytes 49184 | tf_op jit(solution)/shard_map/ppermute | solution.py:406
  95.3 3.3 %collective-permute-done.23.p_high = f32[12,32,128]{2,1,0:T(8,128)S(1)} collective-permute-done((f32[12,32,128]{2,1,0:T(8,128)S(1)}, f32[12,32,128]{2,1,0:T(8,128)S(1)}, u32[]{:S(2)}, u32[]{:S(2)}) %collective-permute-start.23) | collective-permute-done | bytes 196640 | tf_op jit(solution)/shard_map/ppermute | solution.py:406
  98.6 0.2 last.1.mine
  98.8 2.2 %collective-permute-start.24 = (f32[24,32,128]{2,1,0:T(8,128)S(1)}, f32[24,32,128]{2,1,0:T(8,128)S(1)}, u32[]{:S(2)}, u32[]{:S(2)}) collective-permute-start(f32[24,32,128]{2,1,0:T(8,128)S(1)} %last.1.mine), channel_id=1, source_target_pairs={{0,64},{64,0},{128,192},{192,128},{1,65},{65,1},{129,193},{193,129... | collective-permute-start | bytes 1179656 | tf_op jit(solution)/shard_map/ppermute | solution.py:406
  101.0 1.3 %collective-permute-done.24.theirs = f32[24,32,128]{2,1,0:T(8,128)S(1)} collective-permute-done((f32[24,32,128]{2,1,0:T(8,128)S(1)}, f32[24,32,128]{2,1,0:T(8,128)S(1)}, u32[]{:S(2)}, u32[]{:S(2)}) %collective-permute-start.24) | collective-permute-done | bytes 393248 | tf_op jit(solution)/shard_map/ppermute | solution.py:406
  102.3 0.9 whole.1
  (35 shorter events, 0.6 us)
Async XLA Ops:
  1.8 6.9 %collective-permute-start = (f32[6,16,128]{2,1,0:T(8,128)}, f32[6,16,128]{2,1,0:T(8,128)S(1)}, u32[]{:S(2)}, u32[]{:S(2)}) collective-permute-start(f32[6,16,128]{2,1,0:T(8,128)} %begin.1), channel_id=1, source_target_pairs={{0,160},{32,128},{64,224},{96,192},{128,32},{160,0},{192,96},{224,... | collective-permute-start | bytes 147464 | tf_op jit(solution)/shard_map/ppermute | solution.py:406
  4.4 1.1 %copy-start.1 = (f32[1,48,32,128]{3,2,1,0:T(8,128)S(1)}, f32[1,48,32,128]{3,2,1,0:T(8,128)}, u32[]{:S(2)}) copy-start(f32[1,48,32,128]{3,2,1,0:T(8,128)} %param.5) | copy-start | bytes 2359300
  5.5 0.9 copy-start.4
  5.5 1.6 %copy-start.3 = (f32[31,512]{1,0:T(8,128)S(1)}, f32[31,512]{1,0:T(8,128)}, u32[]{:S(2)}) copy-start(f32[31,512]{1,0:T(8,128)} %constant.22.clone) | copy-start | bytes 190468
  5.5 1.8 %copy-start = (f32[48,32,128]{2,1,0:T(8,128)S(1)}, f32[48,32,128]{2,1,0:T(8,128)}, u32[]{:S(2)}) copy-start(f32[48,32,128]{2,1,0:T(8,128)} %est.3) | copy-start | bytes 2359300
  5.5 1.9 %copy-start.5 = (s32[4,2]{0,1:T(2,128)S(1)}, s32[4,2]{0,1:T(2,128)}, u32[]{:S(2)}) copy-start(s32[4,2]{0,1:T(2,128)} %param.7) | copy-start | bytes 100
  5.8 7.5 %copy-start.2 = (f32[1,48,32,128]{3,2,1,0:T(8,128)S(1)}, f32[1,48,32,128]{3,2,1,0:T(8,128)}, u32[]{:S(2)}) copy-start(f32[1,48,32,128]{3,2,1,0:T(8,128)} %param.5) | copy-start | bytes 2359300
  5.8 7.5 %collective-permute-start.4 = (f32[12,8,128]{2,1,0:T(8,128)S(1)}, f32[12,8,128]{2,1,0:T(8,128)S(1)}, u32[]{:S(2)}, u32[]{:S(2)}) collective-permute-start(f32[12,8,128]{2,1,0:T(8,128)S(1)} %raw_sides.1), channel_id=1, source_target_pairs={{0,32},{32,0},{1,33},{33,1},{2,34},{34,2},{3,35},{35,3},{4,36},{36... | collective-permute-start | bytes 147464 | tf_op jit(solution)/shard_map/ppermute | solution.py:406
  8.7 10.9 %collective-permute-start.1 = (f32[27,16,128]{2,1,0:T(8,128)S(1)}, f32[27,16,128]{2,1,0:T(8,128)S(1)}, u32[]{:S(2)}, u32[]{:S(2)}) collective-permute-start(f32[27,16,128]{2,1,0:T(8,128)S(1)} %get-tuple-element.48), channel_id=1, source_target_pairs={{1,2},{3,4},{5,6},{7,8},{9,10},{11,12},{13,14},{15,16},{17,18},{19... | collective-permute-start | bytes 663560 | tf_op jit(solution)/shard_map/ppermute | solution.py:413
  13.2 6.5 %collective-permute-start.2 = (f32[27,16,128]{2,1,0:T(8,128)S(1)}, f32[27,16,128]{2,1,0:T(8,128)S(1)}, u32[]{:S(2)}, u32[]{:S(2)}) collective-permute-start(f32[27,16,128]{2,1,0:T(8,128)S(1)} %get-tuple-element.49), channel_id=1, source_target_pairs={{0,1},{1,0},{2,3},{3,2},{4,5},{5,4},{6,7},{7,6},{8,9},{9,8},{10,11... | collective-permute-start | bytes 663560 | tf_op jit(solution)/shard_map/ppermute | solution.py:414
  13.3 10.6 %collective-permute-start.5 = (f32[51,8,128]{2,1,0:T(8,128)S(1)}, f32[51,8,128]{2,1,0:T(8,128)S(1)}, u32[]{:S(2)}, u32[]{:S(2)}) collective-permute-start(f32[51,8,128]{2,1,0:T(8,128)S(1)} %get-tuple-element.56), channel_id=1, source_target_pairs={{1,2},{3,4},{5,6},{7,8},{9,10},{11,12},{13,14},{15,16},{17,18},{19... | collective-permute-start | bytes 626696 | tf_op jit(solution)/shard_map/ppermute | solution.py:413
  17.8 6.2 %collective-permute-start.6 = (f32[51,8,128]{2,1,0:T(8,128)S(1)}, f32[51,8,128]{2,1,0:T(8,128)S(1)}, u32[]{:S(2)}, u32[]{:S(2)}) collective-permute-start(f32[51,8,128]{2,1,0:T(8,128)S(1)} %get-tuple-element.57), channel_id=1, source_target_pairs={{0,1},{1,0},{2,3},{3,2},{4,5},{5,4},{6,7},{7,6},{8,9},{9,8},{10,11... | collective-permute-start | bytes 626696 | tf_op jit(solution)/shard_map/ppermute | solution.py:414
  20.7 4.7 %collective-permute-start.3 = (f32[24,32,128]{2,1,0:T(8,128)S(1)}, f32[24,32,128]{2,1,0:T(8,128)S(1)}, u32[]{:S(2)}, u32[]{:S(2)}) collective-permute-start(f32[24,32,128]{2,1,0:T(8,128)S(1)} %get-tuple-element.55), channel_id=1, source_target_pairs={{0,64},{64,0},{128,192},{192,128},{1,65},{65,1},{129,193},{193,129... | collective-permute-start | bytes 1179656 | tf_op jit(solution)/shard_map/ppermute | solution.py:406
  26.8 3.7 %collective-permute-start.7 = (f32[24,32,128]{2,1,0:T(8,128)S(1)}, f32[24,32,128]{2,1,0:T(8,128)S(1)}, u32[]{:S(2)}, u32[]{:S(2)}) collective-permute-start(f32[24,32,128]{2,1,0:T(8,128)S(1)} %get-tuple-element.60), channel_id=1, source_target_pairs={{0,64},{64,0},{128,192},{192,128},{1,65},{65,1},{129,193},{193,129... | collective-permute-start | bytes 1179656 | tf_op jit(solution)/shard_map/ppermute | solution.py:406
  31.9 11.9 %collective-permute-start.8 = (f32[27,16,128]{2,1,0:T(8,128)S(1)}, f32[27,16,128]{2,1,0:T(8,128)S(1)}, u32[]{:S(2)}, u32[]{:S(2)}) collective-permute-start(f32[27,16,128]{2,1,0:T(8,128)S(1)} %get-tuple-element.63), channel_id=1, source_target_pairs={{1,2},{3,4},{5,6},{7,8},{9,10},{11,12},{13,14},{15,16},{17,18},{19... | collective-permute-start | bytes 663560 | tf_op jit(solution)/shard_map/ppermute | solution.py:413
  36.3 7.4 %collective-permute-start.9 = (f32[27,16,128]{2,1,0:T(8,128)S(1)}, f32[27,16,128]{2,1,0:T(8,128)S(1)}, u32[]{:S(2)}, u32[]{:S(2)}) collective-permute-start(f32[27,16,128]{2,1,0:T(8,128)S(1)} %get-tuple-element.64), channel_id=1, source_target_pairs={{0,1},{1,0},{2,3},{3,2},{4,5},{5,4},{6,7},{7,6},{8,9},{9,8},{10,11... | collective-permute-start | bytes 663560 | tf_op jit(solution)/shard_map/ppermute | solution.py:414
  44.0 3.6 %collective-permute-start.10 = (f32[12,16,128]{2,1,0:T(8,128)S(1)}, f32[12,16,128]{2,1,0:T(8,128)S(1)}, u32[]{:S(2)}, u32[]{:S(2)}) collective-permute-start(f32[12,16,128]{2,1,0:T(8,128)S(1)} %get-tuple-element.65.mine), channel_id=1, source_target_pairs={{0,128},{64,192},{128,0},{192,64},{1,129},{65,193},{129,1},{193,65... | collective-permute-start | bytes 294920 | tf_op jit(solution)/shard_map/ppermute | solution.py:406
  44.3 7.6 %collective-permute-start.12 = (f32[12,32,128]{2,1,0:T(8,128)S(1)}, f32[12,32,128]{2,1,0:T(8,128)S(1)}, u32[]{:S(2)}, u32[]{:S(2)}) collective-permute-start(f32[12,32,128]{2,1,0:T(8,128)S(1)} %get-tuple-element.66.low), channel_id=1, source_target_pairs={{0,128},{64,192},{128,0},{192,64},{1,129},{65,193},{129,1},{193,65... | collective-permute-start | bytes 589832 | tf_op jit(solution)/shard_map/ppermute | solution.py:406
  45.5 10.0 %collective-permute-start.13 = (f32[12,32,128]{2,1,0:T(8,128)S(1)}, f32[12,32,128]{2,1,0:T(8,128)S(1)}, u32[]{:S(2)}, u32[]{:S(2)}) collective-permute-start(f32[12,32,128]{2,1,0:T(8,128)S(1)} %get-tuple-element.67.high), channel_id=1, source_target_pairs={{0,128},{64,192},{128,0},{192,64},{1,129},{65,193},{129,1},{193,65... | collective-permute-start | bytes 589832 | tf_op jit(solution)/shard_map/ppermute | solution.py:406
  47.5 8.0 %collective-permute-start.11 = (f32[12,16,128]{2,1,0:T(8,128)S(1)}, f32[12,16,128]{2,1,0:T(8,128)S(1)}, u32[]{:S(2)}, u32[]{:S(2)}) collective-permute-start(f32[12,16,128]{2,1,0:T(8,128)S(1)} %join.2.joined), channel_id=1, source_target_pairs={{0,160},{32,128},{64,224},{96,192},{128,32},{160,0},{192,96},{224,... | collective-permute-start | bytes 294920 | tf_op jit(solution)/shard_map/ppermute | solution.py:406
  55.8 10.0 %collective-permute-start.14 = (f32[27,16,128]{2,1,0:T(8,128)S(1)}, f32[27,16,128]{2,1,0:T(8,128)S(1)}, u32[]{:S(2)}, u32[]{:S(2)}) collective-permute-start(f32[27,16,128]{2,1,0:T(8,128)S(1)} %get-tuple-element.70), channel_id=1, source_target_pairs={{1,2},{3,4},{5,6},{7,8},{9,10},{11,12},{13,14},{15,16},{17,18},{19... | collective-permute-start | bytes 663560 | tf_op jit(solution)/shard_map/ppermute | solution.py:413
  60.2 5.6 %collective-permute-start.15 = (f32[27,16,128]{2,1,0:T(8,128)S(1)}, f32[27,16,128]{2,1,0:T(8,128)S(1)}, u32[]{:S(2)}, u32[]{:S(2)}) collective-permute-start(f32[27,16,128]{2,1,0:T(8,128)S(1)} %get-tuple-element.71), channel_id=1, source_target_pairs={{0,1},{1,0},{2,3},{3,2},{4,5},{5,4},{6,7},{7,6},{8,9},{9,8},{10,11... | collective-permute-start | bytes 663560 | tf_op jit(solution)/shard_map/ppermute | solution.py:414
  66.8 4.7 %collective-permute-start.16 = (f32[24,32,128]{2,1,0:T(8,128)S(1)}, f32[24,32,128]{2,1,0:T(8,128)S(1)}, u32[]{:S(2)}, u32[]{:S(2)}) collective-permute-start(f32[24,32,128]{2,1,0:T(8,128)S(1)} %get-tuple-element.77), channel_id=1, source_target_pairs={{0,64},{64,0},{128,192},{192,128},{1,65},{65,1},{129,193},{193,129... | collective-permute-start | bytes 1179656 | tf_op jit(solution)/shard_map/ppermute | solution.py:406
  73.0 1.8 %collective-permute-start.17 = (f32[24,32,128]{2,1,0:T(8,128)S(1)}, f32[24,32,128]{2,1,0:T(8,128)S(1)}, u32[]{:S(2)}, u32[]{:S(2)}) collective-permute-start(f32[24,32,128]{2,1,0:T(8,128)S(1)} %get-tuple-element.79), channel_id=1, source_target_pairs={{0,64},{64,0},{128,192},{192,128},{1,65},{65,1},{129,193},{193,129... | collective-permute-start | bytes 1179656 | tf_op jit(solution)/shard_map/ppermute | solution.py:406
  76.1 11.9 %collective-permute-start.18 = (f32[27,16,128]{2,1,0:T(8,128)S(1)}, f32[27,16,128]{2,1,0:T(8,128)S(1)}, u32[]{:S(2)}, u32[]{:S(2)}) collective-permute-start(f32[27,16,128]{2,1,0:T(8,128)S(1)} %get-tuple-element.82), channel_id=1, source_target_pairs={{1,2},{3,4},{5,6},{7,8},{9,10},{11,12},{13,14},{15,16},{17,18},{19... | collective-permute-start | bytes 663560 | tf_op jit(solution)/shard_map/ppermute | solution.py:413
  80.5 7.4 %collective-permute-start.19 = (f32[27,16,128]{2,1,0:T(8,128)S(1)}, f32[27,16,128]{2,1,0:T(8,128)S(1)}, u32[]{:S(2)}, u32[]{:S(2)}) collective-permute-start(f32[27,16,128]{2,1,0:T(8,128)S(1)} %get-tuple-element.83), channel_id=1, source_target_pairs={{0,1},{1,0},{2,3},{3,2},{4,5},{5,4},{6,7},{7,6},{8,9},{9,8},{10,11... | collective-permute-start | bytes 663560 | tf_op jit(solution)/shard_map/ppermute | solution.py:414
  88.0 3.0 %collective-permute-start.20 = (f32[6,16,128]{2,1,0:T(8,128)S(1)}, f32[6,16,128]{2,1,0:T(8,128)S(1)}, u32[]{:S(2)}, u32[]{:S(2)}) collective-permute-start(f32[6,16,128]{2,1,0:T(8,128)S(1)} %get-tuple-element.84.mine), channel_id=1, source_target_pairs={{0,128},{64,192},{128,0},{192,64},{1,129},{65,193},{129,1},{193,65... | collective-permute-start | bytes 147464 | tf_op jit(solution)/shard_map/ppermute | solution.py:406
  88.6 6.7 %collective-permute-start.22 = (f32[12,32,128]{2,1,0:T(8,128)S(1)}, f32[12,32,128]{2,1,0:T(8,128)S(1)}, u32[]{:S(2)}, u32[]{:S(2)}) collective-permute-start(f32[12,32,128]{2,1,0:T(8,128)S(1)} %get-tuple-element.85.low), channel_id=1, source_target_pairs={{0,128},{64,192},{128,0},{192,64},{1,129},{65,193},{129,1},{193,65... | collective-permute-start | bytes 589832 | tf_op jit(solution)/shard_map/ppermute | solution.py:406
  89.6 9.0 %collective-permute-start.23 = (f32[12,32,128]{2,1,0:T(8,128)S(1)}, f32[12,32,128]{2,1,0:T(8,128)S(1)}, u32[]{:S(2)}, u32[]{:S(2)}) collective-permute-start(f32[12,32,128]{2,1,0:T(8,128)S(1)} %get-tuple-element.86.high), channel_id=1, source_target_pairs={{0,128},{64,192},{128,0},{192,64},{1,129},{65,193},{129,1},{193,65... | collective-permute-start | bytes 589832 | tf_op jit(solution)/shard_map/ppermute | solution.py:406
  91.1 4.2 %collective-permute-start.21 = (f32[6,16,128]{2,1,0:T(8,128)S(1)}, f32[6,16,128]{2,1,0:T(8,128)S(1)}, u32[]{:S(2)}, u32[]{:S(2)}) collective-permute-start(f32[6,16,128]{2,1,0:T(8,128)S(1)} %join.3), channel_id=1, source_target_pairs={{0,160},{32,128},{64,224},{96,192},{128,32},{160,0},{192,96},{224,... | collective-permute-start | bytes 147464 | tf_op jit(solution)/shard_map/ppermute | solution.py:406
  98.8 3.6 %collective-permute-start.24 = (f32[24,32,128]{2,1,0:T(8,128)S(1)}, f32[24,32,128]{2,1,0:T(8,128)S(1)}, u32[]{:S(2)}, u32[]{:S(2)}) collective-permute-start(f32[24,32,128]{2,1,0:T(8,128)S(1)} %last.1.mine), channel_id=1, source_target_pairs={{0,64},{64,0},{128,192},{192,128},{1,65},{65,1},{129,193},{193,129... | collective-permute-start | bytes 1179656 | tf_op jit(solution)/shard_map/ppermute | solution.py:406

commit v4 on v3

--- a/solution.py
+++ b/solution.py
@@ -99,8 +99,9 @@
         for v in range(2):
             at = 128 * v + 32 * p
             both = between(toeplitz(taps[4 + v : 5 + v], 64, 256, at - 2 * HALF - 1), at, 32, both)
-        rows = slice(64 * p, 64 * p + 64)
-        mats[BT, rows], mats[BT + 1, rows] = split(both)
+        rims, at = jnp.concatenate([both[0:16], both[48:64]]), 32 * p
+        mats[BT, at : at + 32], mats[BT, 128 + at : 160 + at] = split(rims)
+        mats[BT + 1, at : at + 32], mats[BT + 1, 128 + at : 160 + at] = split(both[16:48])
 
 
 def placing(width, step, start):
@@ -137,43 +138,48 @@
     x_first = 32 * lax.axis_index("ty")
     tx = lax.axis_index("tx")
 
-    def window(view, dim, place, shift, extent):
-        total = jnp.zeros(place.shape, F32)
-        weight = 0.0
-        for i in range(TAPS):
-            tap = psf[(view * 3 + dim) * TAPS + TAPS - 1 - i]
-            at = place + (i - HALF)
-            moved = at + shift
-            inside = (at >= 0) & (at < extent) & (moved >= 0) & (moved < extent)
-            total = total + jnp.where(inside, tap, 0.0)
-            weight = weight + tap
-        return total / weight
-
     def iota(shape, dim):
         return lax.broadcasted_iota(jnp.int32, shape, dim)
 
     lane = iota((8, 128), 1)
     tile = jnp.minimum(iota((8, 128), 0), 2)
-    flat_z = 24 * core + (128 * tile + lane) // EDGE
-    flat_x = x_first + EDGE * (iota((8, 128), 0) % 2) + lane % EDGE
-    acc = [jnp.zeros((32, 128), F32) for _ in range(24)]
-    ext = [jnp.zeros((EDGE, 128), F32) for _ in range(6)]
-    for v in range(views):
-        sx, sy = offsets[v, 0], offsets[v, 1]
-        in_z = window(v, 0, 24 * core + iota((24, 128), 0), 0, 48)
-        in_x = window(v, 1, x_first + iota((32, 128), 0), sx, nx)
-        in_y = window(v, 2, 128 * tx + lane, sy, ny)[0:1]
-        in_e = window(v, 2, 128 - EDGE * tx + iota((EDGE, 128), 0), sy, ny)
-        z_row = window(v, 0, flat_z, 0, 48)
-        x_row = window(v, 1, flat_x, sx, nx)
-        xy = in_x * in_y
-        acc = [acc[z] + in_z[z : z + 1] * xy for z in range(24)]
+    places = (
+        (0, 24 * core + iota((24, 128), 0)),
+        (0, 24 * core + (128 * tile + lane) // EDGE),
+        (1, x_first + iota((32, 128), 0)),
+        (1, x_first + EDGE * (iota((8, 128), 0) % 2) + lane % EDGE),
+        (2, 128 * tx + lane),
+        (2, 128 - EDGE * tx + iota((EDGE, 128), 0)),
+    )
+    extents = (48, nx, ny)
+    norm[...] = jnp.zeros_like(norm)
+    norm_ext[...] = jnp.zeros_like(norm_ext)
+
+    def one_view(v, _):
+        shifts = (0, offsets[v, 0], offsets[v, 1])
+
+        def one_tap(i, carry):
+            totals, weights = carry
+            taps = [psf[(v * 3 + dim) * TAPS + TAPS - 1 - i] for dim in range(3)]
+            new = []
+            for (dim, place), total in zip(places, totals):
+                at = place + (i - HALF)
+                moved = at + shifts[dim]
+                inside = (at >= 0) & (at < extents[dim]) & (moved >= 0) & (moved < extents[dim])
+                new.append(total + jnp.where(inside, taps[dim], 0.0))
+            return tuple(new), tuple(w + t for w, t in zip(weights, taps))
+
+        none = tuple(jnp.zeros(place.shape, F32) for _, place in places)
+        totals, weights = lax.fori_loop(0, TAPS, one_tap, (none, (0.0, 0.0, 0.0)))
+        in_z, z_row, in_x, x_row, in_y, in_e = (t / weights[dim] for t, (dim, _) in zip(totals, places))
+        xy = in_x * in_y[0:1]
+        for z in range(24):
+            norm[z] += in_z[z : z + 1] * xy
         for k in range(6):
-            ext[k] = ext[k] + in_e * (z_row[k % 3 : k % 3 + 1] * x_row[k // 3 : k // 3 + 1])
-    for z in range(24):
-        norm[z] = acc[z]
-    for k in range(6):
-        norm_ext[k] = ext[k]
+            norm_ext[k] += in_e * (z_row[k % 3 : k % 3 + 1] * x_row[k // 3 : k // 3 + 1])
+        return 0
+
+    lax.fori_loop(0, offsets.shape[0], one_view, 0)
 
 
 def mesh_core():
@@ -228,25 +234,32 @@
         put_rims(pack[t][None], pack[9 + t][None], even_out, odd_out, slice(48 + t, 49 + t))
 
 
-def register_body(offsets, raw, pack, from_odd, from_even, out, wide, turned):
+def register_columns_body(offsets, raw, pack, after, out, wide, turned):
+    view, tx = lax.axis_index("view"), lax.axis_index("tx")
+    sy = offsets[view, 1]
+    wide[:, :, 0:128] = raw[...]
+    turned[...] = jnp.zeros_like(turned)
+    for b in range(4):
+        parts = [pack[3 * b + t] for t in range(3)]
+        wide[:, 8 * b : 8 * b + 8, 128:256] = spread_columns(parts, 120 * tx, 8, turned).reshape(48, 8, 128)
+    for z in range(0, 48, 4):
+        out[z : z + 4] = pltpu.roll(wide[z : z + 4], lax.rem(256 - sy, 256), 2)[:, :, 0:128]
+
+
+def register_body(offsets, moved, from_odd, from_even, out, wide, turned):
     view, tx = lax.axis_index("view"), lax.axis_index("tx")
     sx, sy = offsets[view, 0], offsets[view, 1]
     odd = parity()
     above = jnp.where(odd, from_even[...], from_odd[...])
     below = jnp.where(odd, from_odd[...], from_even[...])
-    wide[:, 0:8, 0:128] = above[0:48]
-    wide[:, 8:40, 0:128] = raw[...]
-    wide[:, 40:48, 0:128] = below[0:48]
     turned[...] = jnp.zeros_like(turned)
-    for b in range(6):
-        if b in (0, 5):
-            parts = [(above if b == 0 else below)[48 + t] for t in range(3)]
-        else:
-            parts = [pack[3 * (b - 1) + t] for t in range(3)]
-        wide[:, 8 * b : 8 * b + 8, 128:256] = spread_columns(parts, 120 * tx, 8, turned).reshape(48, 8, 128)
-    for z in range(0, 48, 4):
-        rows = pltpu.roll(wide[z : z + 4], lax.rem(40 - sx, 48), 1)[:, 0:32, :]
-        out[z : z + 4] = pltpu.roll(rows, lax.rem(256 - sy, 256), 2)[:, :, 0:128]
+    wide[:, 8:40, :] = moved[...]
+    for rim, rows in ((above, slice(0, 8)), (below, slice(40, 48))):
+        side = spread_columns([rim[48 + t] for t in range(3)], 120 * tx, 8, turned).reshape(48, 8, 128)
+        both = jnp.concatenate([rim[0:48], side], axis=2)
+        wide[:, rows, :] = pltpu.roll(both, lax.rem(256 - sy, 256), 2)[:, :, 0:128]
+    for z in range(0, 48, 8):
+        out[z : z + 8] = pltpu.roll(wide[z : z + 8], lax.rem(40 - sx, 48), 1)[:, 0:32, :]
 
 
 def put_columns(rows, main, rim, tx, x_h, x_l, turned):
@@ -315,36 +328,51 @@
     send[...] = full[pl.ds(24 * (1 - core), 24)]
 
 
-def mirror_body(own, other, mats, odd_out, even_out, mid, mid_ext, sides, turned):
-    tx = lax.axis_index("tx")
-    parts = [split(ref[...].reshape(768, 128)) for ref in (own, other)]
-    along_y = []
-    for v in range(2):
+def put_sides(sides, tx, turned, put):
+    for xh in range(2):
+        cols = pack_columns(sides[:, 16 * xh : 16 * xh + 16, :], 112 * tx, 16, turned)
+        for t in range(3):
+            put(xh, t, cols[:, 128 * t : 128 * t + 128])
+
+
+def spread_rows(band, y_h, y_l, g):
+    rows = slice(128 * g, 128 * g + 128)
+    both = tuple(jnp.concatenate([y[0, rows], y[1, rows]], axis=0) for y in (y_h, y_l))
+    return rows3(band, both).reshape(4, 32, 256)
+
+
+def mirror_rims_body(own, other, mats, odd_out, even_out, y_h, y_l, sides, turned):
+    tx = lax.axis_index("tx")
+    for v, ref in ((0, own), (1, other)):
+        high, low = split(ref[...].reshape(768, 128))
         rows = slice(128 * v, 128 * v + 128)
-        high = mats[YF, rows]
-        along_y.append(
-            split(
-                dot(jnp.concatenate(parts[v], axis=1), jnp.concatenate([high, high]), NN)
-                + dot(parts[v][0], mats[YF + 1, rows], NN)
-            )
-        )
-    both_rows = mats[BT : BT + 2].reshape(512, 256)
+        band = mats[YF, rows]
+        y_h[v], y_l[v] = split(
+            dot(jnp.concatenate([high, low], axis=1), jnp.concatenate([band, band]), NN)
+            + dot(high, mats[YF + 1, rows], NN)
+        )
     for g in range(6):
         z = slice(4 * g, 4 * g + 4)
-        rows = slice(128 * g, 128 * g + 128)
-        both = tuple(jnp.concatenate([along_y[0][i][rows], along_y[1][i][rows]], axis=0) for i in range(2))
-        wide = rows3(both_rows, both).reshape(4, 64, 256)
-        put_rims(wide[:, 0:16, 0:128], wide[:, 48:64, 0:128], even_out, odd_out, z)
-        mid[z] = wide[:, 16:48, 0:128]
+        wide = spread_rows(mats[BT], y_h, y_l, g)
+        put_rims(wide[:, 0:16, 0:128], wide[:, 16:32, 0:128], even_out, odd_out, z)
         sides[z] = wide[:, :, 128:256]
-    cols = []
-    for b in range(4):
-        cols.append(pack_columns(sides[:, 16 * b : 16 * b + 16, :], 112 * tx, 16, turned))
-    parts = [[c[:, 128 * t : 128 * t + 128] for t in range(3)] for c in cols]
+    parts = {}
+    put_sides(sides, tx, turned, lambda xh, t, cols: parts.update({(xh, t): cols}))
     for t in range(3):
-        put_rims(parts[0][t][None], parts[3][t][None], even_out, odd_out, slice(24 + t, 25 + t))
-        mid_ext[t] = parts[1][t]
-        mid_ext[3 + t] = parts[2][t]
+        put_rims(parts[0, t][None], parts[1, t][None], even_out, odd_out, slice(24 + t, 25 + t))
+
+
+def mirror_body(y_h, y_l, mats, mid, mid_ext, sides, turned):
+    for g in range(6):
+        z = slice(4 * g, 4 * g + 4)
+        wide = spread_rows(mats[BT + 1], y_h, y_l, g)
+        mid[z] = wide[:, :, 0:128]
+        sides[z] = wide[:, :, 128:256]
+
+    def put(xh, t, cols):
+        mid_ext[3 * xh + t] = cols
+
+    put_sides(sides, lax.axis_index("tx"), turned, put)
 
 
 def gather_body(mid, mid_ext, from_odd, from_even, sides_out, low_out, high_out, turned):
@@ -442,17 +470,18 @@
     sides = swap(sides, "tx", 1, (2,))
     cur, odd, even = call(rims_body, [tile_half, rim, rim], [estimate], name="rims")
 
-    kernels = psf_taps / jnp.sum(psf_taps, axis=-1, keepdims=True)
+    odd, even = call(corners_body, [rim, rim], [ext, odd, even], name="corners", aliases={1: 0, 2: 1})
+    late_taps, late_offsets, _ = lax.optimization_barrier((psf_taps, offsets, odd))
+    kernels = late_taps / jnp.sum(late_taps, axis=-1, keepdims=True)
     own = lax.dynamic_index_in_dim(kernels, view, 0, keepdims=False)
     other = lax.dynamic_index_in_dim(kernels, view ^ 1, 0, keepdims=False)
-    flat_psf = psf_taps.reshape(-1)
-    kz, mats = bands(own, other, depth, flat_psf, offsets)
+    flat_psf = late_taps.reshape(-1)
+    kz, mats = bands(own, other, depth, flat_psf, late_offsets)
     extents = (tile_x * lax.axis_size("ty"), tile_y * lax.axis_size("tx"))
     norm, norm_ext = call(
-        functools.partial(norm_body, extents), [tile_half, pack], [flat_psf, offsets], name="norm"
+        functools.partial(norm_body, extents), [tile_half, pack], [flat_psf, late_offsets], name="norm"
     )
 
-    odd, even = call(corners_body, [rim, rim], [ext, odd, even], name="corners", aliases={1: 0, 2: 1})
     from_odd, from_even = rim_swap(odd, even)
     raw_rim = ((depth + 3, OMAX, 128), F32)
     raw_odd, raw_even = call(raw_rims_body, [raw_rim, raw_rim], [raw, sides], name="raw_rims")
@@ -474,11 +503,20 @@
         )
         theirs = swap(theirs, "view", 1, (4,))
         if seen is None:
+            whole = ((depth, tile_x, tile_y), F32)
+            (moved,) = call(
+                register_columns_body,
+                [whole],
+                [late_offsets, raw, sides, mine],
+                [pltpu.VMEM((depth, tile_x, 256), F32), turned],
+                flops=BUSY,
+                name="register_columns",
+            )
             (seen,) = call(
                 register_body,
-                [((depth, tile_x, tile_y), F32)],
-                [offsets, raw, sides, *raw_from],
-                [pltpu.VMEM((depth, tile_x + 2 * OMAX, 256), F32), turned],
+                [whole],
+                [late_offsets, moved, *raw_from],
+                [pltpu.VMEM((depth, tile_x + 2 * OMAX, 128), F32), turned],
                 flops=BUSY,
                 name="register",
             )
@@ -491,12 +529,20 @@
             name="ratio",
         )
         send = swap(send, "view", 1, (4,))
-        odd, even, mid, mid_ext = call(
+        along_y = ((2, 768, 256), BF16)
+        odd, even, y_h, y_l = call(
+            mirror_rims_body,
+            [rim, rim, along_y, along_y],
+            [keep, send, mats],
+            [pltpu.VMEM((half, 32, 128), F32), turned],
+            name="mirror_rims",
+        )
+        mid, mid_ext = call(
             mirror_body,
-            [rim, rim, tile_half, pack],
-            [keep, send, mats],
-            [pltpu.VMEM((half, 64, 128), F32), turned],
-            flops=3 * 2 * (1536 * 128 * 256 + 6 * 256 * 256 * 256),
+            [tile_half, pack],
+            [y_h, y_l, mats],
+            [pltpu.VMEM((half, 32, 128), F32), turned],
+            flops=BUSY,
             name="mirror",
         )
         from_odd, from_even = rim_swap(odd, even)

time: 104 us -> 102 us (0.981)
  waiting for transfers between devices: 38 us -> 32.8 us
  Pallas kernels: 18.3 us -> 21 us
    ppermute x5, waiting for transfers between devices: 20.6 us -> 17.3 us  [rim_swap(): from_odd = lax.ppermute(odd, 'ty', odd_pairs)]
    pallas_call x23 -> x26, Pallas kernels: 18.3 us -> 21 us  [call(): pl.pallas_call(body, out_shape=outs, in_specs=specs, out_specs=[pl.BlockS...]
    ppermute x15, waiting for transfers between devices: 17.4 us -> 15.6 us  [swap(): return lax.ppermute(value, axis, [(i, i ^ by) for i in range(count)])]
  transfers between devices with their start and end apart: 25 -> 25, of which waited for: 14 -> 12; matrix products, arithmetic and copies ran while one was open for 1% -> 1% of each run, Pallas kernels for 8% -> 12%
where the time goes in v4:
time: 102 us; the launch traced here: 101 us
  starting transfers between devices  44.4 us (44%)
  waiting for transfers between devices  32.8 us (32%)
  Pallas kernels  21 us (21%)
  local copies, waits for them, and re-layouts  2.05 us (2%)
    ppermute x5, starting transfers between devices, rim_swap(): from_odd = lax.ppermute(odd, 'ty', odd_pairs)  22.8 us
    ppermute x15, starting transfers between devices, swap(): return lax.ppermute(value, axis, [(i, i ^ by) for i in range(count)])  21.2 us
    pallas_call x26, Pallas kernels, call(): pl.pallas_call(body, out_shape=outs, in_specs=specs, out_specs=[pl.BlockS...  21 us
    ppermute x5, waiting for transfers between devices, rim_swap(): from_odd = lax.ppermute(odd, 'ty', odd_pairs)  17.3 us
    ppermute x15, waiting for transfers between devices, swap(): return lax.ppermute(value, axis, [(i, i ^ by) for i in range(count)])  15.6 us
  transfers between devices with their start and end apart: 25, of which 12 were waited for; matrix products, arithmetic and copies ran while one was open for 1% of the time, Pallas kernels for 12%

profile of v4, /device:TPU:121, one launch (start us, length us, event | category | flops | bytes accessed | tf_op | source)
XLA Modules:
  0.0 101.2 jit_solution(16357159584022635051)
XLA Ops:
  0.0 1.8 %begin.1 = f32[6,16,128]{2,1,0:T(8,128)} custom-call(f32[48,32,128]{2,1,0:T(8,128)} %est.3), custom_call_target="tpu_custom_call" | custom-call | bytes 835584 | tf_op jit(solution)/shard_map/begin/pallas_call | solution.py:49
  1.8 2.6 %collective-permute-start = (f32[6,16,128]{2,1,0:T(8,128)}, f32[6,16,128]{2,1,0:T(8,128)S(1)}, u32[]{:S(2)}, u32[]{:S(2)}) collective-permute-start(f32[6,16,128]{2,1,0:T(8,128)} %begin.1), channel_id=1, source_target_pairs={{0,160},{32,128},{64,224},{96,192},{128,32},{160,0},{192,96},{224,... | collective-permute-start | bytes 147464 | tf_op jit(solution)/shard_map/ppermute | solution.py:434
  4.4 1.1 %copy-done.1 = f32[1,48,32,128]{3,2,1,0:T(8,128)S(1)} copy-done((f32[1,48,32,128]{3,2,1,0:T(8,128)S(1)}, f32[1,48,32,128]{3,2,1,0:T(8,128)}, u32[]{:S(2)}) %copy-start.1) | copy-done | bytes 786456
  5.5 0.3 raw_sides.1
  5.8 0.6 collective-permute-start.4
  6.4 0.2 copy-done
  6.7 4.4 %collective-permute-start.1 = (f32[27,16,128]{2,1,0:T(8,128)S(1)}, f32[27,16,128]{2,1,0:T(8,128)S(1)}, u32[]{:S(2)}, u32[]{:S(2)}) collective-permute-start(f32[27,16,128]{2,1,0:T(8,128)S(1)} %get-tuple-element.54), channel_id=1, source_target_pairs={{1,2},{3,4},{5,6},{7,8},{9,10},{11,12},{13,14},{15,16},{17,18},{19... | collective-permute-start | bytes 663560 | tf_op jit(solution)/shard_map/ppermute | solution.py:441
  11.4 0.1 rev.16
  11.5 0.1 rev.17
  11.6 0.1 rev.18
  11.7 0.1 rev.19
  11.8 0.1 rev.15
  11.9 0.1 copy.13.offsets
  12.1 4.5 %collective-permute-start.5 = (f32[51,8,128]{2,1,0:T(8,128)S(1)}, f32[51,8,128]{2,1,0:T(8,128)S(1)}, u32[]{:S(2)}, u32[]{:S(2)}) collective-permute-start(f32[51,8,128]{2,1,0:T(8,128)S(1)} %get-tuple-element.64), channel_id=1, source_target_pairs={{1,2},{3,4},{5,6},{7,8},{9,10},{11,12},{13,14},{15,16},{17,18},{19... | collective-permute-start | bytes 626696 | tf_op jit(solution)/shard_map/ppermute | solution.py:441
  16.6 0.1 collective-permute-start.6
  16.7 0.2 fusion
  16.9 1.1 %bands.1 = (bf16[2,768,384]{2,1,0:T(8,128)(2,1)S(1)}, bf16[10,256,256]{2,1,0:T(8,128)(2,1)S(1)}) custom-call(f32[10,512]{1,0:T(8,128)S(1)} %select_maximum_fusion.taps, f32[372]{0:T(512)S(1)} %reshape.9.psf, s32[4,2]{1,0:T(4,128)S(1)} %copy.13.offsets), custom_call_target="tpu_custom_call" | custom-call | bytes 2512368 | tf_op jit(solution)/shard_map/bands/pallas_call | solution.py:49
  18.1 1.1 %inner.2 = (f32[24,32,128]{2,1,0:T(8,128)S(1)}, f32[24,32,128]{2,1,0:T(8,128)S(1)}) custom-call(f32[24,32,128]{2,1,0:T(8,128)S(1)} %get-tuple-element.59.cur, f32[6,16,128]{2,1,0:T(8,128)S(1)} %collective-permute-done.pack.ext, bf16[10,256,256]{2,1,0:T(8,128)(2,1)S(1)} %get-tuple-element.58.mats), custom_call_target="tpu_custom_call" | custom-call | flops 6000000000 | bytes 2539520 | tf_op jit(solution)/shard_map/inner/pallas_call | solution.py:49
  19.1 1.1 %outer.2 = (f32[24,32,128]{2,1,0:T(8,128)S(1)}, f32[24,32,128]{2,1,0:T(8,128)S(1)}) custom-call(f32[27,16,128]{2,1,0:T(8,128)S(1)} %collective-permute-done.1.from_odd, f32[27,16,128]{2,1,0:T(8,128)S(1)} %collective-permute-done.2.from_even, bf16[10,256,256]{2,1,0:T(8,128)(2,1)S(1)} %get-tuple-element.58.mats, f32[24,32,128]{2,1,0:T(8,128)S(1)} %get-tuple-element.60.in_own, ...), custom_call_target="tpu_custom_call" | custom-call | flops 6000000000 | bytes 3325952 | tf_op jit(solution)/shard_map/outer/pallas_call | solution.py:49
  20.2 2.3 %collective-permute-start.3 = (f32[24,32,128]{2,1,0:T(8,128)S(1)}, f32[24,32,128]{2,1,0:T(8,128)S(1)}, u32[]{:S(2)}, u32[]{:S(2)}) collective-permute-start(f32[24,32,128]{2,1,0:T(8,128)S(1)} %get-tuple-element.63), channel_id=1, source_target_pairs={{0,64},{64,0},{128,192},{192,128},{1,65},{65,1},{129,193},{193,129... | collective-permute-start | bytes 1179656 | tf_op jit(solution)/shard_map/ppermute | solution.py:434
  22.5 1.3 %register_columns.1.moved = f32[48,32,128]{2,1,0:T(8,128)S(1)} custom-call(s32[4,2]{1,0:T(4,128)S(1)} %copy.13.offsets, f32[48,32,128]{2,1,0:T(8,128)S(1)} %bitcast.14, f32[12,8,128]{2,1,0:T(8,128)S(1)} %collective-permute-done.4.pack, f32[24,32,128]{2,1,0:T(8,128)S(1)} %get-tuple-element.62.after.mine), custom_call_target="tpu_custom_call" | custom-call | flops 6000000000 | bytes 2015264 | tf_op jit(solution)/shard_map/register_columns/pallas_call | solution.py:49
  23.8 1.1 %register.1.seen = f32[48,32,128]{2,1,0:T(8,128)S(1)} custom-call(s32[4,2]{1,0:T(4,128)S(1)} %copy.13.offsets, f32[48,32,128]{2,1,0:T(8,128)S(1)} %register_columns.1.moved, f32[51,8,128]{2,1,0:T(8,128)S(1)} %collective-permute-done.5.from_odd, f32[51,8,128]{2,1,0:T(8,128)S(1)} %collective-permute-done.6.from_even), custom_call_target="tpu_custom_call" | custom-call | flops 6000000000 | bytes 1990688 | tf_op jit(solution)/shard_map/register/pallas_call | solution.py:49
  24.9 1.4 %ratio.2 = (f32[24,32,128]{2,1,0:T(8,128)S(1)}, f32[24,32,128]{2,1,0:T(8,128)S(1)}) custom-call(f32[24,32,128]{2,1,0:T(8,128)S(1)} %get-tuple-element.62.after.mine, f32[24,32,128]{2,1,0:T(8,128)S(1)} %collective-permute-done.3.theirs, f32[48,32,128]{2,1,0:T(8,128)S(1)} %register.1.seen, bf16[2,768,384]{2,1,0:T(8,128)(2,1)S(1)} %get-tuple-element.66.kz), custom_call_target="tpu_custom_call" | custom-call | flops 905969664 | bytes 3538944 | tf_op jit(solution)/shard_map/ratio/pallas_call | solution.py:49
  26.4 1.2 %collective-permute-start.7 = (f32[24,32,128]{2,1,0:T(8,128)S(1)}, f32[24,32,128]{2,1,0:T(8,128)S(1)}, u32[]{:S(2)}, u32[]{:S(2)}) collective-permute-start(f32[24,32,128]{2,1,0:T(8,128)S(1)} %get-tuple-element.68), channel_id=1, source_target_pairs={{0,64},{64,0},{128,192},{192,128},{1,65},{65,1},{129,193},{193,129... | collective-permute-start | bytes 1179656 | tf_op jit(solution)/shard_map/ppermute | solution.py:434
  27.6 1.3 %collective-permute-done.7.other = f32[24,32,128]{2,1,0:T(8,128)S(1)} collective-permute-done((f32[24,32,128]{2,1,0:T(8,128)S(1)}, f32[24,32,128]{2,1,0:T(8,128)S(1)}, u32[]{:S(2)}, u32[]{:S(2)}) %collective-permute-start.7) | collective-permute-done | bytes 393248 | tf_op jit(solution)/shard_map/ppermute | solution.py:434
  28.9 1.0 mirror_rims.2
  29.9 4.6 %collective-permute-start.8 = (f32[27,16,128]{2,1,0:T(8,128)S(1)}, f32[27,16,128]{2,1,0:T(8,128)S(1)}, u32[]{:S(2)}, u32[]{:S(2)}) collective-permute-start(f32[27,16,128]{2,1,0:T(8,128)S(1)} %get-tuple-element.73), channel_id=1, source_target_pairs={{1,2},{3,4},{5,6},{7,8},{9,10},{11,12},{13,14},{15,16},{17,18},{19... | collective-permute-start | bytes 663560 | tf_op jit(solution)/shard_map/ppermute | solution.py:441
  34.5 0.1 collective-permute-start.9
  34.6 0.6 mirror.2
  35.2 6.5 %collective-permute-done.8.from_odd = f32[27,16,128]{2,1,0:T(8,128)S(1)} collective-permute-done((f32[27,16,128]{2,1,0:T(8,128)S(1)}, f32[27,16,128]{2,1,0:T(8,128)S(1)}, u32[]{:S(2)}, u32[]{:S(2)}) %collective-permute-start.8) | collective-permute-done | bytes 221216 | tf_op jit(solution)/shard_map/ppermute | solution.py:441
  41.8 0.2 gather.2
  42.0 0.2 collective-permute-start.10
  42.2 1.4 %collective-permute-start.12 = (f32[12,32,128]{2,1,0:T(8,128)S(1)}, f32[12,32,128]{2,1,0:T(8,128)S(1)}, u32[]{:S(2)}, u32[]{:S(2)}) collective-permute-start(f32[12,32,128]{2,1,0:T(8,128)S(1)} %get-tuple-element.76.low), channel_id=1, source_target_pairs={{0,128},{64,192},{128,0},{192,64},{1,129},{65,193},{129,1},{193,65... | collective-permute-start | bytes 589832 | tf_op jit(solution)/shard_map/ppermute | solution.py:434
  43.5 0.1 collective-permute-start.13
  43.6 1.9 %collective-permute-done.10.theirs = f32[12,16,128]{2,1,0:T(8,128)S(1)} collective-permute-done((f32[12,16,128]{2,1,0:T(8,128)S(1)}, f32[12,16,128]{2,1,0:T(8,128)S(1)}, u32[]{:S(2)}, u32[]{:S(2)}) %collective-permute-start.10) | collective-permute-done | bytes 98336 | tf_op jit(solution)/shard_map/ppermute | solution.py:434
  45.5 2.4 %collective-permute-start.11 = (f32[12,16,128]{2,1,0:T(8,128)S(1)}, f32[12,16,128]{2,1,0:T(8,128)S(1)}, u32[]{:S(2)}, u32[]{:S(2)}) collective-permute-start(f32[12,16,128]{2,1,0:T(8,128)S(1)} %join.2.joined), channel_id=1, source_target_pairs={{0,160},{32,128},{64,224},{96,192},{128,32},{160,0},{192,96},{224,... | collective-permute-start | bytes 294920 | tf_op jit(solution)/shard_map/ppermute | solution.py:434
  48.0 3.5 %norm.1 = (f32[24,32,128]{2,1,0:T(8,128)S(1)}, f32[6,16,128]{2,1,0:T(8,128)S(1)}) custom-call(f32[372]{0:T(512)S(1)} %reshape.9.psf, s32[4,2]{1,0:T(4,128)S(1)} %copy.13.offsets), custom_call_target="tpu_custom_call" | custom-call | bytes 443888 | tf_op jit(solution)/shard_map/norm/pallas_call | solution.py:49
  51.5 2.1 %collective-permute-done.13.p_high = f32[12,32,128]{2,1,0:T(8,128)S(1)} collective-permute-done((f32[12,32,128]{2,1,0:T(8,128)S(1)}, f32[12,32,128]{2,1,0:T(8,128)S(1)}, u32[]{:S(2)}, u32[]{:S(2)}) %collective-permute-start.13) | collective-permute-done | bytes 196640 | tf_op jit(solution)/shard_map/ppermute | solution.py:434
  53.6 0.2 update.1
  53.8 4.6 %collective-permute-start.14 = (f32[27,16,128]{2,1,0:T(8,128)S(1)}, f32[27,16,128]{2,1,0:T(8,128)S(1)}, u32[]{:S(2)}, u32[]{:S(2)}) collective-permute-start(f32[27,16,128]{2,1,0:T(8,128)S(1)} %get-tuple-element.80), channel_id=1, source_target_pairs={{1,2},{3,4},{5,6},{7,8},{9,10},{11,12},{13,14},{15,16},{17,18},{19... | collective-permute-start | bytes 663560 | tf_op jit(solution)/shard_map/ppermute | solution.py:441
  58.4 0.1 collective-permute-start.15
  58.5 1.1 %inner.3 = (f32[24,32,128]{2,1,0:T(8,128)S(1)}, f32[24,32,128]{2,1,0:T(8,128)S(1)}) custom-call(f32[24,32,128]{2,1,0:T(8,128)S(1)} %get-tuple-element.82.cur, f32[6,16,128]{2,1,0:T(8,128)S(1)} %get-tuple-element.83.ext, bf16[10,256,256]{2,1,0:T(8,128)(2,1)S(1)} %get-tuple-element.58.mats), custom_call_target="tpu_custom_call" | custom-call | flops 6000000000 | bytes 2539520 | tf_op jit(solution)/shard_map/inner/pallas_call | solution.py:49
  59.6 4.2 %collective-permute-done.14.from_odd = f32[27,16,128]{2,1,0:T(8,128)S(1)} collective-permute-done((f32[27,16,128]{2,1,0:T(8,128)S(1)}, f32[27,16,128]{2,1,0:T(8,128)S(1)}, u32[]{:S(2)}, u32[]{:S(2)}) %collective-permute-start.14) | collective-permute-done | bytes 221216 | tf_op jit(solution)/shard_map/ppermute | solution.py:441
  63.8 1.1 %outer.3 = (f32[24,32,128]{2,1,0:T(8,128)S(1)}, f32[24,32,128]{2,1,0:T(8,128)S(1)}) custom-call(f32[27,16,128]{2,1,0:T(8,128)S(1)} %collective-permute-done.14.from_odd, f32[27,16,128]{2,1,0:T(8,128)S(1)} %collective-permute-done.15.from_even, bf16[10,256,256]{2,1,0:T(8,128)(2,1)S(1)} %get-tuple-element.58.mats, ...), custom_call_target="tpu_custom_call" | custom-call | flops 6000000000 | bytes 3325952 | tf_op jit(solution)/shard_map/outer/pallas_call | solution.py:49
  64.8 3.4 %collective-permute-start.16 = (f32[24,32,128]{2,1,0:T(8,128)S(1)}, f32[24,32,128]{2,1,0:T(8,128)S(1)}, u32[]{:S(2)}, u32[]{:S(2)}) collective-permute-start(f32[24,32,128]{2,1,0:T(8,128)S(1)} %get-tuple-element.87), channel_id=1, source_target_pairs={{0,64},{64,0},{128,192},{192,128},{1,65},{65,1},{129,193},{193,129... | collective-permute-start | bytes 1179656 | tf_op jit(solution)/shard_map/ppermute | solution.py:434
  68.2 1.3 %collective-permute-done.16.theirs = f32[24,32,128]{2,1,0:T(8,128)S(1)} collective-permute-done((f32[24,32,128]{2,1,0:T(8,128)S(1)}, f32[24,32,128]{2,1,0:T(8,128)S(1)}, u32[]{:S(2)}, u32[]{:S(2)}) %collective-permute-start.16) | collective-permute-done | bytes 393248 | tf_op jit(solution)/shard_map/ppermute | solution.py:434
  69.6 1.4 %ratio.3 = (f32[24,32,128]{2,1,0:T(8,128)S(1)}, f32[24,32,128]{2,1,0:T(8,128)S(1)}) custom-call(f32[24,32,128]{2,1,0:T(8,128)S(1)} %get-tuple-element.86.mine, f32[24,32,128]{2,1,0:T(8,128)S(1)} %collective-permute-done.16.theirs, f32[48,32,128]{2,1,0:T(8,128)S(1)} %register.1.seen, bf16[2,768,384]{2,1,0:T(8,128)(2,1)S(1)} %get-tuple-element.66.kz), custom_call_target="tpu_custom_call" | custom-call | flops 905969664 | bytes 3538944 | tf_op jit(solution)/shard_map/ratio/pallas_call | solution.py:49
  71.0 0.5 collective-permute-start.17
  71.5 1.4 %collective-permute-done.17.other = f32[24,32,128]{2,1,0:T(8,128)S(1)} collective-permute-done((f32[24,32,128]{2,1,0:T(8,128)S(1)}, f32[24,32,128]{2,1,0:T(8,128)S(1)}, u32[]{:S(2)}, u32[]{:S(2)}) %collective-permute-start.17) | collective-permute-done | bytes 393248 | tf_op jit(solution)/shard_map/ppermute | solution.py:434
  72.8 1.0 mirror_rims.3
  73.8 4.6 %collective-permute-start.18 = (f32[27,16,128]{2,1,0:T(8,128)S(1)}, f32[27,16,128]{2,1,0:T(8,128)S(1)}, u32[]{:S(2)}, u32[]{:S(2)}) collective-permute-start(f32[27,16,128]{2,1,0:T(8,128)S(1)} %get-tuple-element.94), channel_id=1, source_target_pairs={{1,2},{3,4},{5,6},{7,8},{9,10},{11,12},{13,14},{15,16},{17,18},{19... | collective-permute-start | bytes 663560 | tf_op jit(solution)/shard_map/ppermute | solution.py:441
  78.5 0.6 mirror.3
  79.1 6.5 %collective-permute-done.18.from_odd = f32[27,16,128]{2,1,0:T(8,128)S(1)} collective-permute-done((f32[27,16,128]{2,1,0:T(8,128)S(1)}, f32[27,16,128]{2,1,0:T(8,128)S(1)}, u32[]{:S(2)}, u32[]{:S(2)}) %collective-permute-start.18) | collective-permute-done | bytes 221216 | tf_op jit(solution)/shard_map/ppermute | solution.py:441
  85.7 0.7 collective-permute-start.20
  86.4 0.9 collective-permute-start.22
  87.3 0.6 collective-permute-start.23
  87.9 0.9 collective-permute-done.20.theirs
  88.8 2.4 %collective-permute-start.21 = (f32[6,16,128]{2,1,0:T(8,128)S(1)}, f32[6,16,128]{2,1,0:T(8,128)S(1)}, u32[]{:S(2)}, u32[]{:S(2)}) collective-permute-start(f32[6,16,128]{2,1,0:T(8,128)S(1)} %join.3), channel_id=1, source_target_pairs={{0,160},{32,128},{64,224},{96,192},{128,32},{160,0},{192,96},{224,... | collective-permute-start | bytes 147464 | tf_op jit(solution)/shard_map/ppermute | solution.py:434
  91.2 1.8 %collective-permute-done.21.side = f32[6,16,128]{2,1,0:T(8,128)S(1)} collective-permute-done((f32[6,16,128]{2,1,0:T(8,128)S(1)}, f32[6,16,128]{2,1,0:T(8,128)S(1)}, u32[]{:S(2)}, u32[]{:S(2)}) %collective-permute-start.21) | collective-permute-done | bytes 49184 | tf_op jit(solution)/shard_map/ppermute | solution.py:434
  93.0 3.5 %collective-permute-done.23.p_high = f32[12,32,128]{2,1,0:T(8,128)S(1)} collective-permute-done((f32[12,32,128]{2,1,0:T(8,128)S(1)}, f32[12,32,128]{2,1,0:T(8,128)S(1)}, u32[]{:S(2)}, u32[]{:S(2)}) %collective-permute-start.23) | collective-permute-done | bytes 196640 | tf_op jit(solution)/shard_map/ppermute | solution.py:434
  96.5 0.2 last.1.mine
  96.7 2.1 %collective-permute-start.24 = (f32[24,32,128]{2,1,0:T(8,128)S(1)}, f32[24,32,128]{2,1,0:T(8,128)S(1)}, u32[]{:S(2)}, u32[]{:S(2)}) collective-permute-start(f32[24,32,128]{2,1,0:T(8,128)S(1)} %last.1.mine), channel_id=1, source_target_pairs={{0,64},{64,0},{128,192},{192,128},{1,65},{65,1},{129,193},{193,129... | collective-permute-start | bytes 1179656 | tf_op jit(solution)/shard_map/ppermute | solution.py:434
  98.8 1.3 %collective-permute-done.24.theirs = f32[24,32,128]{2,1,0:T(8,128)S(1)} collective-permute-done((f32[24,32,128]{2,1,0:T(8,128)S(1)}, f32[24,32,128]{2,1,0:T(8,128)S(1)}, u32[]{:S(2)}, u32[]{:S(2)}) %collective-permute-start.24) | collective-permute-done | bytes 393248 | tf_op jit(solution)/shard_map/ppermute | solution.py:434
  100.1 0.9 whole.1
  (38 shorter events, 0.7 us)
Async XLA Ops:
  1.8 4.9 %collective-permute-start = (f32[6,16,128]{2,1,0:T(8,128)}, f32[6,16,128]{2,1,0:T(8,128)S(1)}, u32[]{:S(2)}, u32[]{:S(2)}) collective-permute-start(f32[6,16,128]{2,1,0:T(8,128)} %begin.1), channel_id=1, source_target_pairs={{0,160},{32,128},{64,224},{96,192},{128,32},{160,0},{192,96},{224,... | collective-permute-start | bytes 147464 | tf_op jit(solution)/shard_map/ppermute | solution.py:434
  4.4 1.1 %copy-start.1 = (f32[1,48,32,128]{3,2,1,0:T(8,128)S(1)}, f32[1,48,32,128]{3,2,1,0:T(8,128)}, u32[]{:S(2)}) copy-start(f32[1,48,32,128]{3,2,1,0:T(8,128)} %param.5) | copy-start | bytes 2359300
  5.5 1.1 %copy-start = (f32[48,32,128]{2,1,0:T(8,128)S(1)}, f32[48,32,128]{2,1,0:T(8,128)}, u32[]{:S(2)}) copy-start(f32[48,32,128]{2,1,0:T(8,128)} %est.3) | copy-start | bytes 2359300
  5.8 5.4 %copy-start.4 = (f32[4,3,31]{2,0,1:T(4,128)S(1)}, f32[4,3,31]{2,0,1:T(4,128)}, u32[]{:S(2)}) copy-start(f32[4,3,31]{2,0,1:T(4,128)} %param.6) | copy-start | bytes 4468
  5.8 6.2 %copy-start.5 = (s32[4,2]{0,1:T(2,128)S(1)}, s32[4,2]{0,1:T(2,128)}, u32[]{:S(2)}) copy-start(s32[4,2]{0,1:T(2,128)} %param.7) | copy-start | bytes 100
  5.8 6.3 %copy-start.2 = (f32[1,48,32,128]{3,2,1,0:T(8,128)S(1)}, f32[1,48,32,128]{3,2,1,0:T(8,128)}, u32[]{:S(2)}) copy-start(f32[1,48,32,128]{3,2,1,0:T(8,128)} %param.5) | copy-start | bytes 2359300
  5.8 10.9 %copy-start.3 = (f32[31,512]{1,0:T(8,128)S(1)}, f32[31,512]{1,0:T(8,128)}, u32[]{:S(2)}) copy-start(f32[31,512]{1,0:T(8,128)} %constant.22.clone) | copy-start | bytes 190468
  5.8 6.2 %collective-permute-start.4 = (f32[12,8,128]{2,1,0:T(8,128)S(1)}, f32[12,8,128]{2,1,0:T(8,128)S(1)}, u32[]{:S(2)}, u32[]{:S(2)}) collective-permute-start(f32[12,8,128]{2,1,0:T(8,128)S(1)} %raw_sides.1), channel_id=1, source_target_pairs={{0,32},{32,0},{1,33},{33,1},{2,34},{34,2},{3,35},{35,3},{4,36},{36... | collective-permute-start | bytes 147464 | tf_op jit(solution)/shard_map/ppermute | solution.py:434
  6.7 12.4 %collective-permute-start.1 = (f32[27,16,128]{2,1,0:T(8,128)S(1)}, f32[27,16,128]{2,1,0:T(8,128)S(1)}, u32[]{:S(2)}, u32[]{:S(2)}) collective-permute-start(f32[27,16,128]{2,1,0:T(8,128)S(1)} %get-tuple-element.54), channel_id=1, source_target_pairs={{1,2},{3,4},{5,6},{7,8},{9,10},{11,12},{13,14},{15,16},{17,18},{19... | collective-permute-start | bytes 663560 | tf_op jit(solution)/shard_map/ppermute | solution.py:441
  12.0 7.1 %collective-permute-start.2 = (f32[27,16,128]{2,1,0:T(8,128)S(1)}, f32[27,16,128]{2,1,0:T(8,128)S(1)}, u32[]{:S(2)}, u32[]{:S(2)}) collective-permute-start(f32[27,16,128]{2,1,0:T(8,128)S(1)} %get-tuple-element.55), channel_id=1, source_target_pairs={{0,1},{1,0},{2,3},{3,2},{4,5},{5,4},{6,7},{7,6},{8,9},{9,8},{10,11... | collective-permute-start | bytes 663560 | tf_op jit(solution)/shard_map/ppermute | solution.py:442
  12.1 11.6 %collective-permute-start.5 = (f32[51,8,128]{2,1,0:T(8,128)S(1)}, f32[51,8,128]{2,1,0:T(8,128)S(1)}, u32[]{:S(2)}, u32[]{:S(2)}) collective-permute-start(f32[51,8,128]{2,1,0:T(8,128)S(1)} %get-tuple-element.64), channel_id=1, source_target_pairs={{1,2},{3,4},{5,6},{7,8},{9,10},{11,12},{13,14},{15,16},{17,18},{19... | collective-permute-start | bytes 626696 | tf_op jit(solution)/shard_map/ppermute | solution.py:441
  16.6 7.2 %collective-permute-start.6 = (f32[51,8,128]{2,1,0:T(8,128)S(1)}, f32[51,8,128]{2,1,0:T(8,128)S(1)}, u32[]{:S(2)}, u32[]{:S(2)}) collective-permute-start(f32[51,8,128]{2,1,0:T(8,128)S(1)} %get-tuple-element.65), channel_id=1, source_target_pairs={{0,1},{1,0},{2,3},{3,2},{4,5},{5,4},{6,7},{7,6},{8,9},{9,8},{10,11... | collective-permute-start | bytes 626696 | tf_op jit(solution)/shard_map/ppermute | solution.py:442
  20.2 4.7 %collective-permute-start.3 = (f32[24,32,128]{2,1,0:T(8,128)S(1)}, f32[24,32,128]{2,1,0:T(8,128)S(1)}, u32[]{:S(2)}, u32[]{:S(2)}) collective-permute-start(f32[24,32,128]{2,1,0:T(8,128)S(1)} %get-tuple-element.63), channel_id=1, source_target_pairs={{0,64},{64,0},{128,192},{192,128},{1,65},{65,1},{129,193},{193,129... | collective-permute-start | bytes 1179656 | tf_op jit(solution)/shard_map/ppermute | solution.py:434
  26.4 2.6 %collective-permute-start.7 = (f32[24,32,128]{2,1,0:T(8,128)S(1)}, f32[24,32,128]{2,1,0:T(8,128)S(1)}, u32[]{:S(2)}, u32[]{:S(2)}) collective-permute-start(f32[24,32,128]{2,1,0:T(8,128)S(1)} %get-tuple-element.68), channel_id=1, source_target_pairs={{0,64},{64,0},{128,192},{192,128},{1,65},{65,1},{129,193},{193,129... | collective-permute-start | bytes 1179656 | tf_op jit(solution)/shard_map/ppermute | solution.py:434
  29.9 11.8 %collective-permute-start.8 = (f32[27,16,128]{2,1,0:T(8,128)S(1)}, f32[27,16,128]{2,1,0:T(8,128)S(1)}, u32[]{:S(2)}, u32[]{:S(2)}) collective-permute-start(f32[27,16,128]{2,1,0:T(8,128)S(1)} %get-tuple-element.73), channel_id=1, source_target_pairs={{1,2},{3,4},{5,6},{7,8},{9,10},{11,12},{13,14},{15,16},{17,18},{19... | collective-permute-start | bytes 663560 | tf_op jit(solution)/shard_map/ppermute | solution.py:441
  34.5 7.2 %collective-permute-start.9 = (f32[27,16,128]{2,1,0:T(8,128)S(1)}, f32[27,16,128]{2,1,0:T(8,128)S(1)}, u32[]{:S(2)}, u32[]{:S(2)}) collective-permute-start(f32[27,16,128]{2,1,0:T(8,128)S(1)} %get-tuple-element.74), channel_id=1, source_target_pairs={{0,1},{1,0},{2,3},{3,2},{4,5},{5,4},{6,7},{7,6},{8,9},{9,8},{10,11... | collective-permute-start | bytes 663560 | tf_op jit(solution)/shard_map/ppermute | solution.py:442
  42.0 3.6 %collective-permute-start.10 = (f32[12,16,128]{2,1,0:T(8,128)S(1)}, f32[12,16,128]{2,1,0:T(8,128)S(1)}, u32[]{:S(2)}, u32[]{:S(2)}) collective-permute-start(f32[12,16,128]{2,1,0:T(8,128)S(1)} %get-tuple-element.75.mine), channel_id=1, source_target_pairs={{0,128},{64,192},{128,0},{192,64},{1,129},{65,193},{129,1},{193,65... | collective-permute-start | bytes 294920 | tf_op jit(solution)/shard_map/ppermute | solution.py:434
  42.2 9.3 %collective-permute-start.12 = (f32[12,32,128]{2,1,0:T(8,128)S(1)}, f32[12,32,128]{2,1,0:T(8,128)S(1)}, u32[]{:S(2)}, u32[]{:S(2)}) collective-permute-start(f32[12,32,128]{2,1,0:T(8,128)S(1)} %get-tuple-element.76.low), channel_id=1, source_target_pairs={{0,128},{64,192},{128,0},{192,64},{1,129},{65,193},{129,1},{193,65... | collective-permute-start | bytes 589832 | tf_op jit(solution)/shard_map/ppermute | solution.py:434
  43.5 10.0 %collective-permute-start.13 = (f32[12,32,128]{2,1,0:T(8,128)S(1)}, f32[12,32,128]{2,1,0:T(8,128)S(1)}, u32[]{:S(2)}, u32[]{:S(2)}) collective-permute-start(f32[12,32,128]{2,1,0:T(8,128)S(1)} %get-tuple-element.77.high), channel_id=1, source_target_pairs={{0,128},{64,192},{128,0},{192,64},{1,129},{65,193},{129,1},{193,65... | collective-permute-start | bytes 589832 | tf_op jit(solution)/shard_map/ppermute | solution.py:434
  45.5 8.0 %collective-permute-start.11 = (f32[12,16,128]{2,1,0:T(8,128)S(1)}, f32[12,16,128]{2,1,0:T(8,128)S(1)}, u32[]{:S(2)}, u32[]{:S(2)}) collective-permute-start(f32[12,16,128]{2,1,0:T(8,128)S(1)} %join.2.joined), channel_id=1, source_target_pairs={{0,160},{32,128},{64,224},{96,192},{128,32},{160,0},{192,96},{224,... | collective-permute-start | bytes 294920 | tf_op jit(solution)/shard_map/ppermute | solution.py:434
  53.8 10.0 %collective-permute-start.14 = (f32[27,16,128]{2,1,0:T(8,128)S(1)}, f32[27,16,128]{2,1,0:T(8,128)S(1)}, u32[]{:S(2)}, u32[]{:S(2)}) collective-permute-start(f32[27,16,128]{2,1,0:T(8,128)S(1)} %get-tuple-element.80), channel_id=1, source_target_pairs={{1,2},{3,4},{5,6},{7,8},{9,10},{11,12},{13,14},{15,16},{17,18},{19... | collective-permute-start | bytes 663560 | tf_op jit(solution)/shard_map/ppermute | solution.py:441
  58.4 5.4 %collective-permute-start.15 = (f32[27,16,128]{2,1,0:T(8,128)S(1)}, f32[27,16,128]{2,1,0:T(8,128)S(1)}, u32[]{:S(2)}, u32[]{:S(2)}) collective-permute-start(f32[27,16,128]{2,1,0:T(8,128)S(1)} %get-tuple-element.81), channel_id=1, source_target_pairs={{0,1},{1,0},{2,3},{3,2},{4,5},{5,4},{6,7},{7,6},{8,9},{9,8},{10,11... | collective-permute-start | bytes 663560 | tf_op jit(solution)/shard_map/ppermute | solution.py:442
  64.8 4.7 %collective-permute-start.16 = (f32[24,32,128]{2,1,0:T(8,128)S(1)}, f32[24,32,128]{2,1,0:T(8,128)S(1)}, u32[]{:S(2)}, u32[]{:S(2)}) collective-permute-start(f32[24,32,128]{2,1,0:T(8,128)S(1)} %get-tuple-element.87), channel_id=1, source_target_pairs={{0,64},{64,0},{128,192},{192,128},{1,65},{65,1},{129,193},{193,129... | collective-permute-start | bytes 1179656 | tf_op jit(solution)/shard_map/ppermute | solution.py:434
  71.0 1.8 %collective-permute-start.17 = (f32[24,32,128]{2,1,0:T(8,128)S(1)}, f32[24,32,128]{2,1,0:T(8,128)S(1)}, u32[]{:S(2)}, u32[]{:S(2)}) collective-permute-start(f32[24,32,128]{2,1,0:T(8,128)S(1)} %get-tuple-element.89), channel_id=1, source_target_pairs={{0,64},{64,0},{128,192},{192,128},{1,65},{65,1},{129,193},{193,129... | collective-permute-start | bytes 1179656 | tf_op jit(solution)/shard_map/ppermute | solution.py:434
  73.8 11.9 %collective-permute-start.18 = (f32[27,16,128]{2,1,0:T(8,128)S(1)}, f32[27,16,128]{2,1,0:T(8,128)S(1)}, u32[]{:S(2)}, u32[]{:S(2)}) collective-permute-start(f32[27,16,128]{2,1,0:T(8,128)S(1)} %get-tuple-element.94), channel_id=1, source_target_pairs={{1,2},{3,4},{5,6},{7,8},{9,10},{11,12},{13,14},{15,16},{17,18},{19... | collective-permute-start | bytes 663560 | tf_op jit(solution)/shard_map/ppermute | solution.py:441
  78.4 7.2 %collective-permute-start.19 = (f32[27,16,128]{2,1,0:T(8,128)S(1)}, f32[27,16,128]{2,1,0:T(8,128)S(1)}, u32[]{:S(2)}, u32[]{:S(2)}) collective-permute-start(f32[27,16,128]{2,1,0:T(8,128)S(1)} %get-tuple-element.95), channel_id=1, source_target_pairs={{0,1},{1,0},{2,3},{3,2},{4,5},{5,4},{6,7},{7,6},{8,9},{9,8},{10,11... | collective-permute-start | bytes 663560 | tf_op jit(solution)/shard_map/ppermute | solution.py:442
  85.7 3.0 %collective-permute-start.20 = (f32[6,16,128]{2,1,0:T(8,128)S(1)}, f32[6,16,128]{2,1,0:T(8,128)S(1)}, u32[]{:S(2)}, u32[]{:S(2)}) collective-permute-start(f32[6,16,128]{2,1,0:T(8,128)S(1)} %get-tuple-element.96.mine), channel_id=1, source_target_pairs={{0,128},{64,192},{128,0},{192,64},{1,129},{65,193},{129,1},{193,65... | collective-permute-start | bytes 147464 | tf_op jit(solution)/shard_map/ppermute | solution.py:434
  86.4 6.6 %collective-permute-start.22 = (f32[12,32,128]{2,1,0:T(8,128)S(1)}, f32[12,32,128]{2,1,0:T(8,128)S(1)}, u32[]{:S(2)}, u32[]{:S(2)}) collective-permute-start(f32[12,32,128]{2,1,0:T(8,128)S(1)} %get-tuple-element.97.low), channel_id=1, source_target_pairs={{0,128},{64,192},{128,0},{192,64},{1,129},{65,193},{129,1},{193,65... | collective-permute-start | bytes 589832 | tf_op jit(solution)/shard_map/ppermute | solution.py:434
  87.3 9.2 %collective-permute-start.23 = (f32[12,32,128]{2,1,0:T(8,128)S(1)}, f32[12,32,128]{2,1,0:T(8,128)S(1)}, u32[]{:S(2)}, u32[]{:S(2)}) collective-permute-start(f32[12,32,128]{2,1,0:T(8,128)S(1)} %get-tuple-element.98.high), channel_id=1, source_target_pairs={{0,128},{64,192},{128,0},{192,64},{1,129},{65,193},{129,1},{193,65... | collective-permute-start | bytes 589832 | tf_op jit(solution)/shard_map/ppermute | solution.py:434
  88.8 4.2 %collective-permute-start.21 = (f32[6,16,128]{2,1,0:T(8,128)S(1)}, f32[6,16,128]{2,1,0:T(8,128)S(1)}, u32[]{:S(2)}, u32[]{:S(2)}) collective-permute-start(f32[6,16,128]{2,1,0:T(8,128)S(1)} %join.3), channel_id=1, source_target_pairs={{0,160},{32,128},{64,224},{96,192},{128,32},{160,0},{192,96},{224,... | collective-permute-start | bytes 147464 | tf_op jit(solution)/shard_map/ppermute | solution.py:434
  96.7 3.4 %collective-permute-start.24 = (f32[24,32,128]{2,1,0:T(8,128)S(1)}, f32[24,32,128]{2,1,0:T(8,128)S(1)}, u32[]{:S(2)}, u32[]{:S(2)}) collective-permute-start(f32[24,32,128]{2,1,0:T(8,128)S(1)} %last.1.mine), channel_id=1, source_target_pairs={{0,64},{64,0},{128,192},{192,128},{1,65},{65,1},{129,193},{193,129... | collective-permute-start | bytes 1179656 | tf_op jit(solution)/shard_map/ppermute | solution.py:434

commit v5 on v4

--- a/solution.py
+++ b/solution.py
@@ -68,9 +68,22 @@
 YF, IN, OUT, BT, YT = 0, 2, 4, 6, 8
 
 
-def bands_body(taps, psf, offsets, kz, mats):
+def bands_body(taps, place, psf, offsets, kz, mats, placed):
+    view = lax.axis_index("view")
+    views = (view, view + 1 - 2 * (view % 2))
+    total = jnp.sum(taps[...], axis=1, keepdims=True)
+    rest = taps[...] / jnp.where(total > 0, total, 1.0)
+    placed[...] = jnp.zeros_like(placed)
+    for _ in range(3):
+        part = rest.astype(BF16)
+        placed[...] += dot(part, place[...], NN)
+        rest = rest - part.astype(F32)
+
+    def row(v, dim, kind):
+        return placed[pl.ds(3 * views[v] + dim, 1), 512 * kind : 512 * kind + 512]
+
     for m in range(2):
-        high, low = split(toeplitz(taps[m : m + 1], 384, 512, 0)[:, :384])
+        high, low = split(toeplitz(row(0, 0, m), 384, 512, 0)[:, :384])
         for third in range(3):
             rows = slice(128 * third, 128 * third + 128)
             kz[m, 256 * third : 256 * third + 128] = high[rows]
@@ -82,41 +95,46 @@
         return jnp.where((at >= first) & (at < first + count), band, rest)
 
     for v in range(2):
-        row = taps[2 + v : 3 + v]
+        taps_x = row(v, 1, 2)
         for p in range(4):
             at = 32 * p
             none = jnp.zeros((32, 256), F32)
-            inner = between(toeplitz(row, 32, 256, at - HALF), at, 32, none)
-            outer = between(toeplitz(row, 32, 256, at + 1), at, 16, none)
-            outer = between(toeplitz(row, 32, 256, at - 2 * HALF - 1), at + 16, 16, outer)
+            inner = between(toeplitz(taps_x, 32, 256, at - HALF), at, 32, none)
+            outer = between(toeplitz(taps_x, 32, 256, at + 1), at, 16, none)
+            outer = between(toeplitz(taps_x, 32, 256, at - 2 * HALF - 1), at + 16, 16, outer)
             for m, band in ((IN + v, inner), (OUT + v, outer)):
                 mats[m, at : at + 32], mats[m, 128 + at : 160 + at] = split(band)
         rows = slice(128 * v, 128 * v + 128)
-        mats[0, rows], mats[1, rows] = split(toeplitz(taps[6 + v : 7 + v], 128, 256, -HALF))
-        mats[YT, :, rows], mats[YT + 1, :, rows] = split(toeplitz(taps[8 + v : 9 + v], 256, 256, -HALF)[:, :128])
+        mats[0, rows], mats[1, rows] = split(toeplitz(row(v, 2, 2), 128, 256, -HALF))
+        mats[YT, :, rows], mats[YT + 1, :, rows] = split(toeplitz(row(v, 2, 3), 256, 256, -HALF)[:, :128])
     for p in range(4):
         both = jnp.zeros((64, 256), F32)
         for v in range(2):
             at = 128 * v + 32 * p
-            both = between(toeplitz(taps[4 + v : 5 + v], 64, 256, at - 2 * HALF - 1), at, 32, both)
+            both = between(toeplitz(row(v, 1, 3), 64, 256, at - 2 * HALF - 1), at, 32, both)
         rims, at = jnp.concatenate([both[0:16], both[48:64]]), 32 * p
         mats[BT, at : at + 32], mats[BT, 128 + at : 160 + at] = split(rims)
         mats[BT + 1, at : at + 32], mats[BT + 1, 128 + at : 160 + at] = split(both[16:48])
 
 
-def placing(width, step, start):
-    place = np.zeros((TAPS, width), np.float32)
+def placing():
+    place = np.zeros((TAPS + 1, 4, 512), np.float32)
     for k in range(TAPS):
-        place[k, (step * (k - start)) % width] = 1
-    return place
-
-
-def bands(own, other, planes, psf, offsets):
+        for kind, at in enumerate((8 * (k - HALF), 8 * (HALF - k), k, TAPS - 1 - k)):
+            place[k, kind, at % 512] = 1
+    return jnp.asarray(place.reshape(TAPS + 1, 2048), BF16)
+
+
+def bands(taps, planes, psf, offsets):
     nz = 8 * planes
-    z_rows = jnp.dot(jnp.stack([own[0], own[0, ::-1]]), placing(512, 8, HALF), precision=highest)
-    rows = jnp.stack([own[1], other[1], own[1, ::-1], other[1, ::-1], own[2], other[2], own[2, ::-1], other[2, ::-1]])
-    taps = jnp.concatenate([z_rows, jnp.pad(rows, ((0, 0), (0, 512 - TAPS)))])
-    return call(bands_body, [((2, 2 * nz, nz), BF16), ((MATS, 256, 256), BF16)], [taps, psf, offsets], name="bands")
+    return call(
+        bands_body,
+        [((2, 2 * nz, nz), BF16), ((MATS, 256, 256), BF16)],
+        [taps, placing(), psf, offsets],
+        [pltpu.VMEM((16, 2048), F32)],
+        flops=BUSY,
+        name="bands",
+    )
 
 
 def pack_columns(value, at, width, scratch):
@@ -131,7 +149,7 @@
     return scratch[...].T
 
 
-def norm_body(shape, psf, offsets, norm, norm_ext):
+def norm_body(shape, psf, offsets, after, norm, norm_ext):
     nx, ny = shape
     views = offsets.shape[0]
     core = lax.axis_index("view") % 2
@@ -196,13 +214,11 @@
         out[first + t] = cols[:, 128 * t : 128 * t + 128]
 
 
-def begin_body(est, pack_out, cur, turned, sem):
-    tx = lax.axis_index("tx")
-    copy = pltpu.make_async_copy(est.at[pl.ds(24 * mesh_core(), 24)], cur, sem)
-    copy.start()
-    copy.wait()
+def begin_body(est, pack_out, turned):
+    tx = lax.axis_index("tx")
+    half = pl.ds(24 * mesh_core(), 24)
     for xh in range(2):
-        put_packs(cur[:, 16 * xh : 16 * xh + 16, :], 112 * (1 - tx), 16, turned, pack_out, 3 * xh)
+        put_packs(est[half, 16 * xh : 16 * xh + 16, :], 112 * (1 - tx), 16, turned, pack_out, 3 * xh)
 
 
 def raw_sides_body(raw, pack_out, turned):
@@ -228,7 +244,7 @@
     put_rims(pack[0:3], pack[3:6], even_out, odd_out, slice(24, 27))
 
 
-def raw_rims_body(raw, pack, odd_out, even_out):
+def raw_rims_body(raw, pack, after, odd_out, even_out):
     put_rims(raw[:, 0:8, :], raw[:, 24:32, :], even_out, odd_out, slice(0, 48))
     for t in range(3):
         put_rims(pack[t][None], pack[9 + t][None], even_out, odd_out, slice(48 + t, 49 + t))
@@ -258,8 +274,7 @@
         side = spread_columns([rim[48 + t] for t in range(3)], 120 * tx, 8, turned).reshape(48, 8, 128)
         both = jnp.concatenate([rim[0:48], side], axis=2)
         wide[:, rows, :] = pltpu.roll(both, lax.rem(256 - sy, 256), 2)[:, :, 0:128]
-    for z in range(0, 48, 8):
-        out[z : z + 8] = pltpu.roll(wide[z : z + 8], lax.rem(40 - sx, 48), 1)[:, 0:32, :]
+    out[...] = wide[:, pl.ds(8 + sx, 32), :]
 
 
 def put_columns(rows, main, rim, tx, x_h, x_l, turned):
@@ -375,7 +390,7 @@
     put_sides(sides, lax.axis_index("tx"), turned, put)
 
 
-def gather_body(mid, mid_ext, from_odd, from_even, sides_out, low_out, high_out, turned):
+def gather_body(mid, mid_ext, from_odd, from_even, after, sides_out, low_out, high_out, turned):
     tx = lax.axis_index("tx")
     odd = parity()
     above = jnp.where(odd, from_even[...], from_odd[...])
@@ -417,16 +432,16 @@
     put_rims(ext_out[0:3], ext_out[3:6], even_out, odd_out, slice(24, 27))
 
 
-def whole_body(mine, theirs, out, sems):
-    core = mesh_core()
-    copies = [
-        pltpu.make_async_copy(part, out.at[pl.ds(24 * half, 24)], sems.at[i])
-        for i, (part, half) in enumerate(((mine, core), (theirs, 1 - core)))
-    ]
-    for copy in copies:
-        copy.start()
-    for copy in copies:
-        copy.wait()
+def near_half_body(mine, out, sem):
+    copy = pltpu.make_async_copy(mine, out.at[pl.ds(24 * mesh_core(), 24)], sem)
+    copy.start()
+    copy.wait()
+
+
+def far_half_body(theirs, near, out, sem):
+    copy = pltpu.make_async_copy(theirs, out.at[pl.ds(24 * (1 - mesh_core()), 24)], sem)
+    copy.start()
+    copy.wait()
 
 
 def swap(value, axis, by, sizes):
@@ -446,7 +461,6 @@
 def shards(raw_views, psf_taps, offsets, estimate):
     depth, tile_x, tile_y = estimate.shape
     half = depth // 2
-    view = lax.axis_index("view")
     raw = raw_views[0]
 
     tile_half = ((half, tile_x, tile_y), F32)
@@ -456,15 +470,7 @@
     turned = pltpu.VMEM((128, 384), F32)
     two_sems = pltpu.SemaphoreType.DMA((2,))
 
-    (ext,) = call(
-        begin_body,
-        [pack],
-        [estimate],
-        [pltpu.VMEM((half, tile_x, tile_y), F32), turned, pltpu.SemaphoreType.DMA],
-        name="begin",
-        hbm=(0,),
-        limit=62,
-    )
+    (ext,) = call(begin_body, [pack], [estimate], [turned], name="begin")
     ext = swap(ext, ("view", "tx"), 5, (4, 2))
     (sides,) = call(raw_sides_body, [((12, OMAX, 128), F32)], [raw], [turned], flops=BUSY, name="raw_sides")
     sides = swap(sides, "tx", 1, (2,))
@@ -472,19 +478,13 @@
 
     odd, even = call(corners_body, [rim, rim], [ext, odd, even], name="corners", aliases={1: 0, 2: 1})
     late_taps, late_offsets, _ = lax.optimization_barrier((psf_taps, offsets, odd))
-    kernels = late_taps / jnp.sum(late_taps, axis=-1, keepdims=True)
-    own = lax.dynamic_index_in_dim(kernels, view, 0, keepdims=False)
-    other = lax.dynamic_index_in_dim(kernels, view ^ 1, 0, keepdims=False)
+    taps = jnp.pad(late_taps.reshape(-1, TAPS), ((0, 4), (0, 1)))
     flat_psf = late_taps.reshape(-1)
-    kz, mats = bands(own, other, depth, flat_psf, late_offsets)
+    kz, mats = bands(taps, depth, flat_psf, late_offsets)
     extents = (tile_x * lax.axis_size("ty"), tile_y * lax.axis_size("tx"))
-    norm, norm_ext = call(
-        functools.partial(norm_body, extents), [tile_half, pack], [flat_psf, late_offsets], name="norm"
-    )
-
     from_odd, from_even = rim_swap(odd, even)
     raw_rim = ((depth + 3, OMAX, 128), F32)
-    raw_odd, raw_even = call(raw_rims_body, [raw_rim, raw_rim], [raw, sides], name="raw_rims")
+    raw_odd, raw_even = call(raw_rims_body, [raw_rim, raw_rim], [raw, sides, taps], name="raw_rims")
     raw_from = rim_swap(raw_odd, raw_even)
     columns = [pltpu.VMEM((half, 32, 256), BF16), pltpu.VMEM((half, 32, 256), BF16), turned]
     seen = None
@@ -545,12 +545,16 @@
             flops=BUSY,
             name="mirror",
         )
+        if iteration == 0:
+            norm, norm_ext = call(
+                functools.partial(norm_body, extents), [tile_half, pack], [flat_psf, late_offsets, y_h], name="norm"
+            )
         from_odd, from_even = rim_swap(odd, even)
         last = iteration == ITERS - 1
         sides, low, high = call(
             gather_body,
             [pack if last else ((12, EDGE, 128), F32), tile_quarter, tile_quarter],
-            [mid, mid_ext, from_odd, from_even],
+            [mid, mid_ext, from_odd, from_even, norm],
             [turned],
             name="gather",
         )
@@ -571,7 +575,9 @@
         )
         from_odd, from_even = rim_swap(odd, even)
     far = swap(cur, "view", 1, (4,))
-    (out,) = call(whole_body, [((depth, tile_x, tile_y), F32)], [cur, far], [two_sems], name="whole", out_place=pl.ANY)
+    outs, sem = [((depth, tile_x, tile_y), F32)], [pltpu.SemaphoreType.DMA]
+    (near,) = call(near_half_body, outs, [cur], sem, flops=BUSY, name="near_half", out_place=pl.ANY)
+    (out,) = call(far_half_body, outs, [far, near], sem, name="far_half", hbm=(1,), aliases={1: 0}, out_place=pl.ANY)
     return out
 
 

time: 102 us -> 100 us (0.980)
  starting transfers between devices: 44.4 us -> 43.3 us
    ppermute x15, waiting for transfers between devices: 15.6 us -> 18.9 us  [swap(): return lax.ppermute(value, axis, [(i, i ^ by) for i in range(count)])]
    ppermute x5, waiting for transfers between devices: 17.3 us -> 14.3 us  [rim_swap(): from_odd = lax.ppermute(odd, 'ty', odd_pairs)]
    unnamed x12 -> x14, local copies, waits for them, and re-layouts: 1.36 us -> 2.5 us
    pallas_call x26 -> x27, Pallas kernels: 21 us -> 20.2 us  [call(): pl.pallas_call(body, out_shape=outs, in_specs=specs, out_specs=[pl.BlockS...]
  transfers between devices with their start and end apart: 25 -> 25, of which waited for: 12 -> 13; matrix products, arithmetic and copies ran while one was open for 1% -> 0% of each run, Pallas kernels for 12% -> 13%
where the time goes in v5:
time: 100 us; the launch traced here: 99.9 us
  starting transfers between devices  43.3 us (43%)
  waiting for transfers between devices  33.2 us (33%)
  Pallas kernels  20.2 us (20%)
  local copies, waits for them, and re-layouts  2.7 us (3%)
    ppermute x5, starting transfers between devices, rim_swap(): from_odd = lax.ppermute(odd, 'ty', odd_pairs)  22.2 us
    ppermute x15, starting transfers between devices, swap(): return lax.ppermute(value, axis, [(i, i ^ by) for i in range(count)])  20.7 us
    pallas_call x27, Pallas kernels, call(): pl.pallas_call(body, out_shape=outs, in_specs=specs, out_specs=[pl.BlockS...  20.2 us
    ppermute x15, waiting for transfers between devices, swap(): return lax.ppermute(value, axis, [(i, i ^ by) for i in range(count)])  18.9 us
    ppermute x5, waiting for transfers between devices, rim_swap(): from_odd = lax.ppermute(odd, 'ty', odd_pairs)  14.3 us
    unnamed x14, local copies, waits for them, and re-layouts  2.5 us
  transfers between devices with their start and end apart: 25, of which 13 were waited for; matrix products, arithmetic and copies ran while one was open for 0% of the time, Pallas kernels for 13%

profile of v5, /device:TPU:121, one launch (start us, length us, event | category | flops | bytes accessed | tf_op | source)
XLA Modules:
  0.0 99.9 jit_solution(3135694623723252384)
XLA Ops:
  0.0 1.1 %copy-done = f32[48,32,128]{2,1,0:T(8,128)S(1)} copy-done((f32[48,32,128]{2,1,0:T(8,128)S(1)}, f32[48,32,128]{2,1,0:T(8,128)}, u32[]{:S(2)}) %copy-start) | copy-done | bytes 786456
  1.1 0.2 begin.1
  1.3 2.6 %collective-permute-start = (f32[6,16,128]{2,1,0:T(8,128)S(1)}, f32[6,16,128]{2,1,0:T(8,128)S(1)}, u32[]{:S(2)}, u32[]{:S(2)}) collective-permute-start(f32[6,16,128]{2,1,0:T(8,128)S(1)} %begin.1), channel_id=1, source_target_pairs={{0,160},{32,128},{64,224},{96,192},{128,32},{160,0},{192,96},{224,... | collective-permute-start | bytes 147464 | tf_op jit(solution)/shard_map/ppermute | solution.py:449
  3.9 1.1 %copy-done.2 = f32[1,48,32,128]{3,2,1,0:T(8,128)S(1)} copy-done((f32[1,48,32,128]{3,2,1,0:T(8,128)S(1)}, f32[1,48,32,128]{3,2,1,0:T(8,128)}, u32[]{:S(2)}) %copy-start.2) | copy-done | bytes 786456
  5.0 0.3 raw_sides.1
  5.3 0.6 collective-permute-start.4
  5.9 0.2 copy-done.1
  6.1 0.1 rims.1
  6.3 0.1 reshape.7.psf
  6.4 4.4 %collective-permute-start.1 = (f32[27,16,128]{2,1,0:T(8,128)S(1)}, f32[27,16,128]{2,1,0:T(8,128)S(1)}, u32[]{:S(2)}, u32[]{:S(2)}) collective-permute-start(f32[27,16,128]{2,1,0:T(8,128)S(1)} %get-tuple-element.54), channel_id=1, source_target_pairs={{1,2},{3,4},{5,6},{7,8},{9,10},{11,12},{13,14},{15,16},{17,18},{19... | collective-permute-start | bytes 663560 | tf_op jit(solution)/shard_map/ppermute | solution.py:456
  10.8 0.1 copy.16.offsets
  11.0 4.5 %collective-permute-start.5 = (f32[51,8,128]{2,1,0:T(8,128)S(1)}, f32[51,8,128]{2,1,0:T(8,128)S(1)}, u32[]{:S(2)}, u32[]{:S(2)}) collective-permute-start(f32[51,8,128]{2,1,0:T(8,128)S(1)} %get-tuple-element.64), channel_id=1, source_target_pairs={{1,2},{3,4},{5,6},{7,8},{9,10},{11,12},{13,14},{15,16},{17,18},{19... | collective-permute-start | bytes 626696 | tf_op jit(solution)/shard_map/ppermute | solution.py:456
  15.5 0.1 collective-permute-start.6
  15.6 1.4 %bands.1 = (bf16[2,768,384]{2,1,0:T(8,128)(2,1)S(1)}, bf16[10,256,256]{2,1,0:T(8,128)(2,1)S(1)}) custom-call(f32[16,32]{1,0:T(8,128)S(1)} %pad.4.taps.after, bf16[32,2048]{1,0:T(8,128)(2,1)S(1)} %copy-done.4, f32[372]{0:T(512)S(1)} %reshape.7.psf, s32[4,2]{1,0:T(4,128)S(1)} %copy.16.offsets), custom_call_target="tpu_custom_call" | custom-call | flops 6000000000 | bytes 2625008 | tf_op jit(solution)/shard_map/bands/pallas_call | solution.py:49
  17.0 1.1 %inner.2 = (f32[24,32,128]{2,1,0:T(8,128)S(1)}, f32[24,32,128]{2,1,0:T(8,128)S(1)}) custom-call(f32[24,32,128]{2,1,0:T(8,128)S(1)} %get-tuple-element.59.cur, f32[6,16,128]{2,1,0:T(8,128)S(1)} %collective-permute-done.pack.ext, bf16[10,256,256]{2,1,0:T(8,128)(2,1)S(1)} %get-tuple-element.58.mats), custom_call_target="tpu_custom_call" | custom-call | flops 6000000000 | bytes 2539520 | tf_op jit(solution)/shard_map/inner/pallas_call | solution.py:49
  18.1 1.1 %outer.2 = (f32[24,32,128]{2,1,0:T(8,128)S(1)}, f32[24,32,128]{2,1,0:T(8,128)S(1)}) custom-call(f32[27,16,128]{2,1,0:T(8,128)S(1)} %collective-permute-done.1.from_odd, f32[27,16,128]{2,1,0:T(8,128)S(1)} %collective-permute-done.2.from_even, bf16[10,256,256]{2,1,0:T(8,128)(2,1)S(1)} %get-tuple-element.58.mats, f32[24,32,128]{2,1,0:T(8,128)S(1)} %get-tuple-element.60.in_own, ...), custom_call_target="tpu_custom_call" | custom-call | flops 6000000000 | bytes 3325952 | tf_op jit(solution)/shard_map/outer/pallas_call | solution.py:49
  19.2 2.1 %collective-permute-start.3 = (f32[24,32,128]{2,1,0:T(8,128)S(1)}, f32[24,32,128]{2,1,0:T(8,128)S(1)}, u32[]{:S(2)}, u32[]{:S(2)}) collective-permute-start(f32[24,32,128]{2,1,0:T(8,128)S(1)} %get-tuple-element.63), channel_id=1, source_target_pairs={{0,64},{64,0},{128,192},{192,128},{1,65},{65,1},{129,193},{193,129... | collective-permute-start | bytes 1179656 | tf_op jit(solution)/shard_map/ppermute | solution.py:449
  21.2 1.3 %register_columns.1.moved = f32[48,32,128]{2,1,0:T(8,128)S(1)} custom-call(s32[4,2]{1,0:T(4,128)S(1)} %copy.16.offsets, f32[48,32,128]{2,1,0:T(8,128)S(1)} %bitcast.3, f32[12,8,128]{2,1,0:T(8,128)S(1)} %collective-permute-done.4.pack, f32[24,32,128]{2,1,0:T(8,128)S(1)} %get-tuple-element.62.after.mine), custom_call_target="tpu_custom_call" | custom-call | flops 6000000000 | bytes 2015264 | tf_op jit(solution)/shard_map/register_columns/pallas_call | solution.py:49
  22.5 1.0 %register.1.seen = f32[48,32,128]{2,1,0:T(8,128)S(1)} custom-call(s32[4,2]{1,0:T(4,128)S(1)} %copy.16.offsets, f32[48,32,128]{2,1,0:T(8,128)S(1)} %register_columns.1.moved, f32[51,8,128]{2,1,0:T(8,128)S(1)} %collective-permute-done.5.from_odd, f32[51,8,128]{2,1,0:T(8,128)S(1)} %collective-permute-done.6.from_even), custom_call_target="tpu_custom_call" | custom-call | flops 6000000000 | bytes 1990688 | tf_op jit(solution)/shard_map/register/pallas_call | solution.py:49
  23.6 1.4 %ratio.2 = (f32[24,32,128]{2,1,0:T(8,128)S(1)}, f32[24,32,128]{2,1,0:T(8,128)S(1)}) custom-call(f32[24,32,128]{2,1,0:T(8,128)S(1)} %get-tuple-element.62.after.mine, f32[24,32,128]{2,1,0:T(8,128)S(1)} %collective-permute-done.3.theirs, f32[48,32,128]{2,1,0:T(8,128)S(1)} %register.1.seen, bf16[2,768,384]{2,1,0:T(8,128)(2,1)S(1)} %get-tuple-element.66.kz), custom_call_target="tpu_custom_call" | custom-call | flops 905969664 | bytes 3538944 | tf_op jit(solution)/shard_map/ratio/pallas_call | solution.py:49
  25.0 1.4 %collective-permute-start.7 = (f32[24,32,128]{2,1,0:T(8,128)S(1)}, f32[24,32,128]{2,1,0:T(8,128)S(1)}, u32[]{:S(2)}, u32[]{:S(2)}) collective-permute-start(f32[24,32,128]{2,1,0:T(8,128)S(1)} %get-tuple-element.68), channel_id=1, source_target_pairs={{0,64},{64,0},{128,192},{192,128},{1,65},{65,1},{129,193},{193,129... | collective-permute-start | bytes 1179656 | tf_op jit(solution)/shard_map/ppermute | solution.py:449
  26.5 1.3 %collective-permute-done.7.other = f32[24,32,128]{2,1,0:T(8,128)S(1)} collective-permute-done((f32[24,32,128]{2,1,0:T(8,128)S(1)}, f32[24,32,128]{2,1,0:T(8,128)S(1)}, u32[]{:S(2)}, u32[]{:S(2)}) %collective-permute-start.7) | collective-permute-done | bytes 393248 | tf_op jit(solution)/shard_map/ppermute | solution.py:449
  27.8 1.0 mirror_rims.2
  28.8 4.4 %collective-permute-start.8 = (f32[27,16,128]{2,1,0:T(8,128)S(1)}, f32[27,16,128]{2,1,0:T(8,128)S(1)}, u32[]{:S(2)}, u32[]{:S(2)}) collective-permute-start(f32[27,16,128]{2,1,0:T(8,128)S(1)} %get-tuple-element.73), channel_id=1, source_target_pairs={{1,2},{3,4},{5,6},{7,8},{9,10},{11,12},{13,14},{15,16},{17,18},{19... | collective-permute-start | bytes 663560 | tf_op jit(solution)/shard_map/ppermute | solution.py:456
  33.2 0.1 collective-permute-start.9
  33.3 0.6 mirror.2
  33.9 3.5 %norm.1 = (f32[24,32,128]{2,1,0:T(8,128)S(1)}, f32[6,16,128]{2,1,0:T(8,128)S(1)}) custom-call(f32[372]{0:T(512)S(1)} %reshape.7.psf, s32[4,2]{1,0:T(4,128)S(1)} %copy.16.offsets, bf16[2,768,256]{2,1,0:T(8,128)(2,1)S(1)} %get-tuple-element.69.y_h.after), custom_call_target="tpu_custom_call" | custom-call | bytes 1230320 | tf_op jit(solution)/shard_map/norm/pallas_call | solution.py:49
  37.4 3.2 %collective-permute-done.8.from_odd = f32[27,16,128]{2,1,0:T(8,128)S(1)} collective-permute-done((f32[27,16,128]{2,1,0:T(8,128)S(1)}, f32[27,16,128]{2,1,0:T(8,128)S(1)}, u32[]{:S(2)}, u32[]{:S(2)}) %collective-permute-start.8) | collective-permute-done | bytes 221216 | tf_op jit(solution)/shard_map/ppermute | solution.py:456
  40.7 0.2 gather.2
  40.9 0.2 collective-permute-start.10
  41.0 1.4 %collective-permute-start.12 = (f32[12,32,128]{2,1,0:T(8,128)S(1)}, f32[12,32,128]{2,1,0:T(8,128)S(1)}, u32[]{:S(2)}, u32[]{:S(2)}) collective-permute-start(f32[12,32,128]{2,1,0:T(8,128)S(1)} %get-tuple-element.77.low), channel_id=1, source_target_pairs={{0,128},{64,192},{128,0},{192,64},{1,129},{65,193},{129,1},{193,65... | collective-permute-start | bytes 589832 | tf_op jit(solution)/shard_map/ppermute | solution.py:449
  42.4 0.1 collective-permute-start.13
  42.5 1.9 %collective-permute-done.10.theirs = f32[12,16,128]{2,1,0:T(8,128)S(1)} collective-permute-done((f32[12,16,128]{2,1,0:T(8,128)S(1)}, f32[12,16,128]{2,1,0:T(8,128)S(1)}, u32[]{:S(2)}, u32[]{:S(2)}) %collective-permute-start.10) | collective-permute-done | bytes 98336 | tf_op jit(solution)/shard_map/ppermute | solution.py:449
  44.4 2.1 %collective-permute-start.11 = (f32[12,16,128]{2,1,0:T(8,128)S(1)}, f32[12,16,128]{2,1,0:T(8,128)S(1)}, u32[]{:S(2)}, u32[]{:S(2)}) collective-permute-start(f32[12,16,128]{2,1,0:T(8,128)S(1)} %join.2.joined), channel_id=1, source_target_pairs={{0,160},{32,128},{64,224},{96,192},{128,32},{160,0},{192,96},{224,... | collective-permute-start | bytes 294920 | tf_op jit(solution)/shard_map/ppermute | solution.py:449
  46.6 1.7 %collective-permute-done.12.p_low = f32[12,32,128]{2,1,0:T(8,128)S(1)} collective-permute-done((f32[12,32,128]{2,1,0:T(8,128)S(1)}, f32[12,32,128]{2,1,0:T(8,128)S(1)}, u32[]{:S(2)}, u32[]{:S(2)}) %collective-permute-start.12) | collective-permute-done | bytes 196640 | tf_op jit(solution)/shard_map/ppermute | solution.py:449
  48.2 4.2 %collective-permute-done.13.p_high = f32[12,32,128]{2,1,0:T(8,128)S(1)} collective-permute-done((f32[12,32,128]{2,1,0:T(8,128)S(1)}, f32[12,32,128]{2,1,0:T(8,128)S(1)}, u32[]{:S(2)}, u32[]{:S(2)}) %collective-permute-start.13) | collective-permute-done | bytes 196640 | tf_op jit(solution)/shard_map/ppermute | solution.py:449
  52.5 0.2 update.1
  52.7 4.5 %collective-permute-start.14 = (f32[27,16,128]{2,1,0:T(8,128)S(1)}, f32[27,16,128]{2,1,0:T(8,128)S(1)}, u32[]{:S(2)}, u32[]{:S(2)}) collective-permute-start(f32[27,16,128]{2,1,0:T(8,128)S(1)} %get-tuple-element.80), channel_id=1, source_target_pairs={{1,2},{3,4},{5,6},{7,8},{9,10},{11,12},{13,14},{15,16},{17,18},{19... | collective-permute-start | bytes 663560 | tf_op jit(solution)/shard_map/ppermute | solution.py:456
  57.1 0.1 collective-permute-start.15
  57.2 1.1 %inner.3 = (f32[24,32,128]{2,1,0:T(8,128)S(1)}, f32[24,32,128]{2,1,0:T(8,128)S(1)}) custom-call(f32[24,32,128]{2,1,0:T(8,128)S(1)} %get-tuple-element.82.cur, f32[6,16,128]{2,1,0:T(8,128)S(1)} %get-tuple-element.83.ext, bf16[10,256,256]{2,1,0:T(8,128)(2,1)S(1)} %get-tuple-element.58.mats), custom_call_target="tpu_custom_call" | custom-call | flops 6000000000 | bytes 2539520 | tf_op jit(solution)/shard_map/inner/pallas_call | solution.py:49
  58.3 4.4 %collective-permute-done.14.from_odd = f32[27,16,128]{2,1,0:T(8,128)S(1)} collective-permute-done((f32[27,16,128]{2,1,0:T(8,128)S(1)}, f32[27,16,128]{2,1,0:T(8,128)S(1)}, u32[]{:S(2)}, u32[]{:S(2)}) %collective-permute-start.14) | collective-permute-done | bytes 221216 | tf_op jit(solution)/shard_map/ppermute | solution.py:456
  62.7 1.1 %outer.3 = (f32[24,32,128]{2,1,0:T(8,128)S(1)}, f32[24,32,128]{2,1,0:T(8,128)S(1)}) custom-call(f32[27,16,128]{2,1,0:T(8,128)S(1)} %collective-permute-done.14.from_odd, f32[27,16,128]{2,1,0:T(8,128)S(1)} %collective-permute-done.15.from_even, bf16[10,256,256]{2,1,0:T(8,128)(2,1)S(1)} %get-tuple-element.58.mats, ...), custom_call_target="tpu_custom_call" | custom-call | flops 6000000000 | bytes 3325952 | tf_op jit(solution)/shard_map/outer/pallas_call | solution.py:49
  63.7 3.4 %collective-permute-start.16 = (f32[24,32,128]{2,1,0:T(8,128)S(1)}, f32[24,32,128]{2,1,0:T(8,128)S(1)}, u32[]{:S(2)}, u32[]{:S(2)}) collective-permute-start(f32[24,32,128]{2,1,0:T(8,128)S(1)} %get-tuple-element.87), channel_id=1, source_target_pairs={{0,64},{64,0},{128,192},{192,128},{1,65},{65,1},{129,193},{193,129... | collective-permute-start | bytes 1179656 | tf_op jit(solution)/shard_map/ppermute | solution.py:449
  67.1 1.3 %collective-permute-done.16.theirs = f32[24,32,128]{2,1,0:T(8,128)S(1)} collective-permute-done((f32[24,32,128]{2,1,0:T(8,128)S(1)}, f32[24,32,128]{2,1,0:T(8,128)S(1)}, u32[]{:S(2)}, u32[]{:S(2)}) %collective-permute-start.16) | collective-permute-done | bytes 393248 | tf_op jit(solution)/shard_map/ppermute | solution.py:449
  68.5 1.4 %ratio.3 = (f32[24,32,128]{2,1,0:T(8,128)S(1)}, f32[24,32,128]{2,1,0:T(8,128)S(1)}) custom-call(f32[24,32,128]{2,1,0:T(8,128)S(1)} %get-tuple-element.86.mine, f32[24,32,128]{2,1,0:T(8,128)S(1)} %collective-permute-done.16.theirs, f32[48,32,128]{2,1,0:T(8,128)S(1)} %register.1.seen, bf16[2,768,384]{2,1,0:T(8,128)(2,1)S(1)} %get-tuple-element.66.kz), custom_call_target="tpu_custom_call" | custom-call | flops 905969664 | bytes 3538944 | tf_op jit(solution)/shard_map/ratio/pallas_call | solution.py:49
  69.9 0.5 collective-permute-start.17
  70.4 1.3 %collective-permute-done.17.other = f32[24,32,128]{2,1,0:T(8,128)S(1)} collective-permute-done((f32[24,32,128]{2,1,0:T(8,128)S(1)}, f32[24,32,128]{2,1,0:T(8,128)S(1)}, u32[]{:S(2)}, u32[]{:S(2)}) %collective-permute-start.17) | collective-permute-done | bytes 393248 | tf_op jit(solution)/shard_map/ppermute | solution.py:449
  71.7 1.0 mirror_rims.3
  72.7 4.4 %collective-permute-start.18 = (f32[27,16,128]{2,1,0:T(8,128)S(1)}, f32[27,16,128]{2,1,0:T(8,128)S(1)}, u32[]{:S(2)}, u32[]{:S(2)}) collective-permute-start(f32[27,16,128]{2,1,0:T(8,128)S(1)} %get-tuple-element.94), channel_id=1, source_target_pairs={{1,2},{3,4},{5,6},{7,8},{9,10},{11,12},{13,14},{15,16},{17,18},{19... | collective-permute-start | bytes 663560 | tf_op jit(solution)/shard_map/ppermute | solution.py:456
  77.2 0.1 collective-permute-start.19
  77.3 0.6 mirror.3
  77.8 6.7 %collective-permute-done.18.from_odd = f32[27,16,128]{2,1,0:T(8,128)S(1)} collective-permute-done((f32[27,16,128]{2,1,0:T(8,128)S(1)}, f32[27,16,128]{2,1,0:T(8,128)S(1)}, u32[]{:S(2)}, u32[]{:S(2)}) %collective-permute-start.18) | collective-permute-done | bytes 221216 | tf_op jit(solution)/shard_map/ppermute | solution.py:456
  84.6 0.7 collective-permute-start.20
  85.3 0.8 collective-permute-start.22
  86.2 0.6 collective-permute-start.23
  86.8 0.9 collective-permute-done.20.theirs
  87.7 2.1 %collective-permute-start.21 = (f32[6,16,128]{2,1,0:T(8,128)S(1)}, f32[6,16,128]{2,1,0:T(8,128)S(1)}, u32[]{:S(2)}, u32[]{:S(2)}) collective-permute-start(f32[6,16,128]{2,1,0:T(8,128)S(1)} %join.3), channel_id=1, source_target_pairs={{0,160},{32,128},{64,224},{96,192},{128,32},{160,0},{192,96},{224,... | collective-permute-start | bytes 147464 | tf_op jit(solution)/shard_map/ppermute | solution.py:449
  89.8 2.1 %collective-permute-done.21.side = f32[6,16,128]{2,1,0:T(8,128)S(1)} collective-permute-done((f32[6,16,128]{2,1,0:T(8,128)S(1)}, f32[6,16,128]{2,1,0:T(8,128)S(1)}, u32[]{:S(2)}, u32[]{:S(2)}) %collective-permute-start.21) | collective-permute-done | bytes 49184 | tf_op jit(solution)/shard_map/ppermute | solution.py:449
  91.9 3.5 %collective-permute-done.23.p_high = f32[12,32,128]{2,1,0:T(8,128)S(1)} collective-permute-done((f32[12,32,128]{2,1,0:T(8,128)S(1)}, f32[12,32,128]{2,1,0:T(8,128)S(1)}, u32[]{:S(2)}, u32[]{:S(2)}) %collective-permute-start.23) | collective-permute-done | bytes 196640 | tf_op jit(solution)/shard_map/ppermute | solution.py:449
  95.4 0.2 last.1.mine
  95.6 2.1 %collective-permute-start.24 = (f32[24,32,128]{2,1,0:T(8,128)S(1)}, f32[24,32,128]{2,1,0:T(8,128)S(1)}, u32[]{:S(2)}, u32[]{:S(2)}) collective-permute-start(f32[24,32,128]{2,1,0:T(8,128)S(1)} %last.1.mine), channel_id=1, source_target_pairs={{0,64},{64,0},{128,192},{192,128},{1,65},{65,1},{129,193},{193,129... | collective-permute-start | bytes 1179656 | tf_op jit(solution)/shard_map/ppermute | solution.py:449
  97.7 0.8 near_half.1.near
  98.4 0.6 collective-permute-done.24.theirs
  99.0 0.8 far_half.1
  (32 shorter events, 0.2 us)
Async XLA Ops:
  0.0 1.1 %copy-start = (f32[48,32,128]{2,1,0:T(8,128)S(1)}, f32[48,32,128]{2,1,0:T(8,128)}, u32[]{:S(2)}) copy-start(f32[48,32,128]{2,1,0:T(8,128)} %est.3) | copy-start | bytes 2359300
  1.3 4.9 %collective-permute-start = (f32[6,16,128]{2,1,0:T(8,128)S(1)}, f32[6,16,128]{2,1,0:T(8,128)S(1)}, u32[]{:S(2)}, u32[]{:S(2)}) collective-permute-start(f32[6,16,128]{2,1,0:T(8,128)S(1)} %begin.1), channel_id=1, source_target_pairs={{0,160},{32,128},{64,224},{96,192},{128,32},{160,0},{192,96},{224,... | collective-permute-start | bytes 147464 | tf_op jit(solution)/shard_map/ppermute | solution.py:449
  3.9 1.1 %copy-start.2 = (f32[1,48,32,128]{3,2,1,0:T(8,128)S(1)}, f32[1,48,32,128]{3,2,1,0:T(8,128)}, u32[]{:S(2)}) copy-start(f32[1,48,32,128]{3,2,1,0:T(8,128)} %param.5) | copy-start | bytes 2359300
  5.0 1.1 %copy-start.1 = (f32[48,32,128]{2,1,0:T(8,128)S(1)}, f32[48,32,128]{2,1,0:T(8,128)}, u32[]{:S(2)}) copy-start(f32[48,32,128]{2,1,0:T(8,128)} %est.3) | copy-start | bytes 2359300
  5.0 1.2 %copy-start.5 = (f32[4,3,31]{2,0,1:T(4,128)S(1)}, f32[4,3,31]{2,0,1:T(4,128)}, u32[]{:S(2)}) copy-start(f32[4,3,31]{2,0,1:T(4,128)} %param.6) | copy-start | bytes 4468
  5.3 5.5 %copy-start.6 = (s32[4,2]{0,1:T(2,128)S(1)}, s32[4,2]{0,1:T(2,128)}, u32[]{:S(2)}) copy-start(s32[4,2]{0,1:T(2,128)} %param.7) | copy-start | bytes 100
  5.3 5.6 %copy-start.3 = (f32[1,48,32,128]{3,2,1,0:T(8,128)S(1)}, f32[1,48,32,128]{3,2,1,0:T(8,128)}, u32[]{:S(2)}) copy-start(f32[1,48,32,128]{3,2,1,0:T(8,128)} %param.5) | copy-start | bytes 2359300
  5.3 10.3 %copy-start.4 = (bf16[32,2048]{1,0:T(8,128)(2,1)S(1)}, bf16[32,2048]{1,0:T(8,128)(2,1)}, u32[]{:S(2)}) copy-start(bf16[32,2048]{1,0:T(8,128)(2,1)} %constant.5.clone.place) | copy-start | bytes 393220
  5.3 5.6 %collective-permute-start.4 = (f32[12,8,128]{2,1,0:T(8,128)S(1)}, f32[12,8,128]{2,1,0:T(8,128)S(1)}, u32[]{:S(2)}, u32[]{:S(2)}) collective-permute-start(f32[12,8,128]{2,1,0:T(8,128)S(1)} %raw_sides.1), channel_id=1, source_target_pairs={{0,32},{32,0},{1,33},{33,1},{2,34},{34,2},{3,35},{35,3},{4,36},{36... | collective-permute-start | bytes 147464 | tf_op jit(solution)/shard_map/ppermute | solution.py:449
  6.4 11.7 %collective-permute-start.1 = (f32[27,16,128]{2,1,0:T(8,128)S(1)}, f32[27,16,128]{2,1,0:T(8,128)S(1)}, u32[]{:S(2)}, u32[]{:S(2)}) collective-permute-start(f32[27,16,128]{2,1,0:T(8,128)S(1)} %get-tuple-element.54), channel_id=1, source_target_pairs={{1,2},{3,4},{5,6},{7,8},{9,10},{11,12},{13,14},{15,16},{17,18},{19... | collective-permute-start | bytes 663560 | tf_op jit(solution)/shard_map/ppermute | solution.py:456
  10.9 7.2 %collective-permute-start.2 = (f32[27,16,128]{2,1,0:T(8,128)S(1)}, f32[27,16,128]{2,1,0:T(8,128)S(1)}, u32[]{:S(2)}, u32[]{:S(2)}) collective-permute-start(f32[27,16,128]{2,1,0:T(8,128)S(1)} %get-tuple-element.55), channel_id=1, source_target_pairs={{0,1},{1,0},{2,3},{3,2},{4,5},{5,4},{6,7},{7,6},{8,9},{9,8},{10,11... | collective-permute-start | bytes 663560 | tf_op jit(solution)/shard_map/ppermute | solution.py:457
  11.0 11.5 %collective-permute-start.5 = (f32[51,8,128]{2,1,0:T(8,128)S(1)}, f32[51,8,128]{2,1,0:T(8,128)S(1)}, u32[]{:S(2)}, u32[]{:S(2)}) collective-permute-start(f32[51,8,128]{2,1,0:T(8,128)S(1)} %get-tuple-element.64), channel_id=1, source_target_pairs={{1,2},{3,4},{5,6},{7,8},{9,10},{11,12},{13,14},{15,16},{17,18},{19... | collective-permute-start | bytes 626696 | tf_op jit(solution)/shard_map/ppermute | solution.py:456
  15.5 7.0 %collective-permute-start.6 = (f32[51,8,128]{2,1,0:T(8,128)S(1)}, f32[51,8,128]{2,1,0:T(8,128)S(1)}, u32[]{:S(2)}, u32[]{:S(2)}) collective-permute-start(f32[51,8,128]{2,1,0:T(8,128)S(1)} %get-tuple-element.65), channel_id=1, source_target_pairs={{0,1},{1,0},{2,3},{3,2},{4,5},{5,4},{6,7},{7,6},{8,9},{9,8},{10,11... | collective-permute-start | bytes 626696 | tf_op jit(solution)/shard_map/ppermute | solution.py:457
  19.2 4.4 %collective-permute-start.3 = (f32[24,32,128]{2,1,0:T(8,128)S(1)}, f32[24,32,128]{2,1,0:T(8,128)S(1)}, u32[]{:S(2)}, u32[]{:S(2)}) collective-permute-start(f32[24,32,128]{2,1,0:T(8,128)S(1)} %get-tuple-element.63), channel_id=1, source_target_pairs={{0,64},{64,0},{128,192},{192,128},{1,65},{65,1},{129,193},{193,129... | collective-permute-start | bytes 1179656 | tf_op jit(solution)/shard_map/ppermute | solution.py:449
  25.0 2.8 %collective-permute-start.7 = (f32[24,32,128]{2,1,0:T(8,128)S(1)}, f32[24,32,128]{2,1,0:T(8,128)S(1)}, u32[]{:S(2)}, u32[]{:S(2)}) collective-permute-start(f32[24,32,128]{2,1,0:T(8,128)S(1)} %get-tuple-element.68), channel_id=1, source_target_pairs={{0,64},{64,0},{128,192},{192,128},{1,65},{65,1},{129,193},{193,129... | collective-permute-start | bytes 1179656 | tf_op jit(solution)/shard_map/ppermute | solution.py:449
  28.8 11.8 %collective-permute-start.8 = (f32[27,16,128]{2,1,0:T(8,128)S(1)}, f32[27,16,128]{2,1,0:T(8,128)S(1)}, u32[]{:S(2)}, u32[]{:S(2)}) collective-permute-start(f32[27,16,128]{2,1,0:T(8,128)S(1)} %get-tuple-element.73), channel_id=1, source_target_pairs={{1,2},{3,4},{5,6},{7,8},{9,10},{11,12},{13,14},{15,16},{17,18},{19... | collective-permute-start | bytes 663560 | tf_op jit(solution)/shard_map/ppermute | solution.py:456
  33.2 7.4 %collective-permute-start.9 = (f32[27,16,128]{2,1,0:T(8,128)S(1)}, f32[27,16,128]{2,1,0:T(8,128)S(1)}, u32[]{:S(2)}, u32[]{:S(2)}) collective-permute-start(f32[27,16,128]{2,1,0:T(8,128)S(1)} %get-tuple-element.74), channel_id=1, source_target_pairs={{0,1},{1,0},{2,3},{3,2},{4,5},{5,4},{6,7},{7,6},{8,9},{9,8},{10,11... | collective-permute-start | bytes 663560 | tf_op jit(solution)/shard_map/ppermute | solution.py:457
  40.9 3.6 %collective-permute-start.10 = (f32[12,16,128]{2,1,0:T(8,128)S(1)}, f32[12,16,128]{2,1,0:T(8,128)S(1)}, u32[]{:S(2)}, u32[]{:S(2)}) collective-permute-start(f32[12,16,128]{2,1,0:T(8,128)S(1)} %get-tuple-element.76.mine), channel_id=1, source_target_pairs={{0,128},{64,192},{128,0},{192,64},{1,129},{65,193},{129,1},{193,65... | collective-permute-start | bytes 294920 | tf_op jit(solution)/shard_map/ppermute | solution.py:449
  41.0 7.2 %collective-permute-start.12 = (f32[12,32,128]{2,1,0:T(8,128)S(1)}, f32[12,32,128]{2,1,0:T(8,128)S(1)}, u32[]{:S(2)}, u32[]{:S(2)}) collective-permute-start(f32[12,32,128]{2,1,0:T(8,128)S(1)} %get-tuple-element.77.low), channel_id=1, source_target_pairs={{0,128},{64,192},{128,0},{192,64},{1,129},{65,193},{129,1},{193,65... | collective-permute-start | bytes 589832 | tf_op jit(solution)/shard_map/ppermute | solution.py:449
  42.4 10.0 %collective-permute-start.13 = (f32[12,32,128]{2,1,0:T(8,128)S(1)}, f32[12,32,128]{2,1,0:T(8,128)S(1)}, u32[]{:S(2)}, u32[]{:S(2)}) collective-permute-start(f32[12,32,128]{2,1,0:T(8,128)S(1)} %get-tuple-element.78.high), channel_id=1, source_target_pairs={{0,128},{64,192},{128,0},{192,64},{1,129},{65,193},{129,1},{193,65... | collective-permute-start | bytes 589832 | tf_op jit(solution)/shard_map/ppermute | solution.py:449
  44.4 8.0 %collective-permute-start.11 = (f32[12,16,128]{2,1,0:T(8,128)S(1)}, f32[12,16,128]{2,1,0:T(8,128)S(1)}, u32[]{:S(2)}, u32[]{:S(2)}) collective-permute-start(f32[12,16,128]{2,1,0:T(8,128)S(1)} %join.2.joined), channel_id=1, source_target_pairs={{0,160},{32,128},{64,224},{96,192},{128,32},{160,0},{192,96},{224,... | collective-permute-start | bytes 294920 | tf_op jit(solution)/shard_map/ppermute | solution.py:449
  52.7 10.0 %collective-permute-start.14 = (f32[27,16,128]{2,1,0:T(8,128)S(1)}, f32[27,16,128]{2,1,0:T(8,128)S(1)}, u32[]{:S(2)}, u32[]{:S(2)}) collective-permute-start(f32[27,16,128]{2,1,0:T(8,128)S(1)} %get-tuple-element.80), channel_id=1, source_target_pairs={{1,2},{3,4},{5,6},{7,8},{9,10},{11,12},{13,14},{15,16},{17,18},{19... | collective-permute-start | bytes 663560 | tf_op jit(solution)/shard_map/ppermute | solution.py:456
  57.1 5.5 %collective-permute-start.15 = (f32[27,16,128]{2,1,0:T(8,128)S(1)}, f32[27,16,128]{2,1,0:T(8,128)S(1)}, u32[]{:S(2)}, u32[]{:S(2)}) collective-permute-start(f32[27,16,128]{2,1,0:T(8,128)S(1)} %get-tuple-element.81), channel_id=1, source_target_pairs={{0,1},{1,0},{2,3},{3,2},{4,5},{5,4},{6,7},{7,6},{8,9},{9,8},{10,11... | collective-permute-start | bytes 663560 | tf_op jit(solution)/shard_map/ppermute | solution.py:457
  63.7 4.7 %collective-permute-start.16 = (f32[24,32,128]{2,1,0:T(8,128)S(1)}, f32[24,32,128]{2,1,0:T(8,128)S(1)}, u32[]{:S(2)}, u32[]{:S(2)}) collective-permute-start(f32[24,32,128]{2,1,0:T(8,128)S(1)} %get-tuple-element.87), channel_id=1, source_target_pairs={{0,64},{64,0},{128,192},{192,128},{1,65},{65,1},{129,193},{193,129... | collective-permute-start | bytes 1179656 | tf_op jit(solution)/shard_map/ppermute | solution.py:449
  69.9 1.8 %collective-permute-start.17 = (f32[24,32,128]{2,1,0:T(8,128)S(1)}, f32[24,32,128]{2,1,0:T(8,128)S(1)}, u32[]{:S(2)}, u32[]{:S(2)}) collective-permute-start(f32[24,32,128]{2,1,0:T(8,128)S(1)} %get-tuple-element.89), channel_id=1, source_target_pairs={{0,64},{64,0},{128,192},{192,128},{1,65},{65,1},{129,193},{193,129... | collective-permute-start | bytes 1179656 | tf_op jit(solution)/shard_map/ppermute | solution.py:449
  72.7 11.9 %collective-permute-start.18 = (f32[27,16,128]{2,1,0:T(8,128)S(1)}, f32[27,16,128]{2,1,0:T(8,128)S(1)}, u32[]{:S(2)}, u32[]{:S(2)}) collective-permute-start(f32[27,16,128]{2,1,0:T(8,128)S(1)} %get-tuple-element.94), channel_id=1, source_target_pairs={{1,2},{3,4},{5,6},{7,8},{9,10},{11,12},{13,14},{15,16},{17,18},{19... | collective-permute-start | bytes 663560 | tf_op jit(solution)/shard_map/ppermute | solution.py:456
  77.2 7.4 %collective-permute-start.19 = (f32[27,16,128]{2,1,0:T(8,128)S(1)}, f32[27,16,128]{2,1,0:T(8,128)S(1)}, u32[]{:S(2)}, u32[]{:S(2)}) collective-permute-start(f32[27,16,128]{2,1,0:T(8,128)S(1)} %get-tuple-element.95), channel_id=1, source_target_pairs={{0,1},{1,0},{2,3},{3,2},{4,5},{5,4},{6,7},{7,6},{8,9},{9,8},{10,11... | collective-permute-start | bytes 663560 | tf_op jit(solution)/shard_map/ppermute | solution.py:457
  84.6 3.0 %collective-permute-start.20 = (f32[6,16,128]{2,1,0:T(8,128)S(1)}, f32[6,16,128]{2,1,0:T(8,128)S(1)}, u32[]{:S(2)}, u32[]{:S(2)}) collective-permute-start(f32[6,16,128]{2,1,0:T(8,128)S(1)} %get-tuple-element.96.mine), channel_id=1, source_target_pairs={{0,128},{64,192},{128,0},{192,64},{1,129},{65,193},{129,1},{193,65... | collective-permute-start | bytes 147464 | tf_op jit(solution)/shard_map/ppermute | solution.py:449
  85.3 6.6 %collective-permute-start.22 = (f32[12,32,128]{2,1,0:T(8,128)S(1)}, f32[12,32,128]{2,1,0:T(8,128)S(1)}, u32[]{:S(2)}, u32[]{:S(2)}) collective-permute-start(f32[12,32,128]{2,1,0:T(8,128)S(1)} %get-tuple-element.97.low), channel_id=1, source_target_pairs={{0,128},{64,192},{128,0},{192,64},{1,129},{65,193},{129,1},{193,65... | collective-permute-start | bytes 589832 | tf_op jit(solution)/shard_map/ppermute | solution.py:449
  86.2 9.2 %collective-permute-start.23 = (f32[12,32,128]{2,1,0:T(8,128)S(1)}, f32[12,32,128]{2,1,0:T(8,128)S(1)}, u32[]{:S(2)}, u32[]{:S(2)}) collective-permute-start(f32[12,32,128]{2,1,0:T(8,128)S(1)} %get-tuple-element.98.high), channel_id=1, source_target_pairs={{0,128},{64,192},{128,0},{192,64},{1,129},{65,193},{129,1},{193,65... | collective-permute-start | bytes 589832 | tf_op jit(solution)/shard_map/ppermute | solution.py:449
  87.7 4.2 %collective-permute-start.21 = (f32[6,16,128]{2,1,0:T(8,128)S(1)}, f32[6,16,128]{2,1,0:T(8,128)S(1)}, u32[]{:S(2)}, u32[]{:S(2)}) collective-permute-start(f32[6,16,128]{2,1,0:T(8,128)S(1)} %join.3), channel_id=1, source_target_pairs={{0,160},{32,128},{64,224},{96,192},{128,32},{160,0},{192,96},{224,... | collective-permute-start | bytes 147464 | tf_op jit(solution)/shard_map/ppermute | solution.py:449
  95.6 3.4 %collective-permute-start.24 = (f32[24,32,128]{2,1,0:T(8,128)S(1)}, f32[24,32,128]{2,1,0:T(8,128)S(1)}, u32[]{:S(2)}, u32[]{:S(2)}) collective-permute-start(f32[24,32,128]{2,1,0:T(8,128)S(1)} %last.1.mine), channel_id=1, source_target_pairs={{0,64},{64,0},{128,192},{192,128},{1,65},{65,1},{129,193},{193,129... | collective-permute-start | bytes 1179656 | tf_op jit(solution)/shard_map/ppermute | solution.py:449

commit v6 on v5

--- a/solution.py
+++ b/solution.py
@@ -262,7 +262,7 @@
         out[z : z + 4] = pltpu.roll(wide[z : z + 4], lax.rem(256 - sy, 256), 2)[:, :, 0:128]
 
 
-def register_body(offsets, moved, from_odd, from_even, out, wide, turned):
+def register_body(offsets, moved, from_odd, from_even, after, out, wide, turned):
     view, tx = lax.axis_index("view"), lax.axis_index("tx")
     sx, sy = offsets[view, 0], offsets[view, 1]
     odd = parity()
@@ -283,12 +283,14 @@
     x_h[:, rows, 128:256], x_l[:, rows, 128:256] = split(side)
 
 
-def blur_rows(x_h, x_l, yf, bx, g):
+def blur_rows(x_h, x_l, yf, bx, g, views=(0, 1)):
     z = slice(4 * g, 4 * g + 4)
     high, low = x_h[z].reshape(128, 256), x_l[z].reshape(128, 256)
+    first = 128 * views[0]
+    yf = [y[:, first : first + 128 * len(views)] for y in yf]
     along_y = split(dot(high, yf[0], NN) + (dot(high, yf[1], NN) + dot(low, yf[0], NN)))
-    for v in range(2):
-        cols = slice(128 * v, 128 * v + 128)
+    for i, v in enumerate(views):
+        cols = slice(128 * i, 128 * i + 128)
         yield v, z, rows3(bx[v][:, 0:128], (along_y[0][:, cols], along_y[1][:, cols])).reshape(4, 32, 128)
 
 
@@ -303,7 +305,7 @@
             (own, other)[v][z] = part
 
 
-def outer_body(from_odd, from_even, mats, in_own, in_other, own, other, x_h, x_l, turned):
+def fill_outer(from_odd, from_even, x_h, x_l, turned):
     tx = lax.axis_index("tx")
     odd = parity()
     above = jnp.where(odd, from_even[...], from_odd[...])
@@ -312,6 +314,17 @@
     for xh, rim in ((0, above), (1, below)):
         rows = slice(16 * xh, 16 * xh + 16)
         put_columns(rows, rim[0:24], [rim[24 + t] for t in range(3)], tx, x_h, x_l, turned)
+
+
+def outer_one_body(v, from_odd, from_even, mats, inner, out, x_h, x_l, turned):
+    fill_outer(from_odd, from_even, x_h, x_l, turned)
+    for g in range(6):
+        for _, z, part in blur_rows(x_h, x_l, (mats[YT], mats[YT + 1]), (mats[OUT], mats[OUT + 1]), g, (v,)):
+            out[z] = inner[z] + part
+
+
+def outer_body(from_odd, from_even, mats, in_own, in_other, own, other, x_h, x_l, turned):
+    fill_outer(from_odd, from_even, x_h, x_l, turned)
     for g in range(6):
         for v, z, part in blur_rows(x_h, x_l, (mats[YT], mats[YT + 1]), (mats[OUT], mats[OUT + 1]), g):
             (own, other)[v][z] = (in_own, in_other)[v][z] + part
@@ -324,23 +337,50 @@
     return jnp.concatenate(parts)
 
 
-def ratio_body(mine, theirs, seen, kz, keep, send, full):
+def plane_pair(ref, xp):
+    return jnp.concatenate(
+        [ref[:, 16 * xp + 8 * i : 16 * xp + 8 * i + 8, :].reshape(384, 128) for i in range(2)], axis=1
+    )
+
+
+def put_pair(ref, xp, value):
+    for i in range(2):
+        at = slice(16 * xp + 8 * i, 16 * xp + 8 * i + 8)
+        ref[:, at, :] = value[:, 128 * i : 128 * i + 128].reshape(48, 8, 128)
+
+
+def join_planes(mine, theirs, full):
     core = mesh_core()
     full[pl.ds(24 * core, 24)] = mine[...]
     full[pl.ds(24 * (1 - core), 24)] = theirs[...]
-    for xp in range(2):
-        def pair(ref):
-            return jnp.concatenate(
-                [ref[:, 16 * xp + 8 * i : 16 * xp + 8 * i + 8, :].reshape(384, 128) for i in range(2)], axis=1
-            )
-        blurred = along_z(kz, 0, *split(pair(full)))
-        ratio = pair(seen) / blurred
-        back = along_z(kz, 1, *split(ratio))
-        for i in range(2):
-            at = slice(16 * xp + 8 * i, 16 * xp + 8 * i + 8)
-            full[:, at, :] = back[:, 128 * i : 128 * i + 128].reshape(48, 8, 128)
+
+
+def part_planes(keep, send, full):
+    core = mesh_core()
     keep[...] = full[pl.ds(24 * core, 24)]
     send[...] = full[pl.ds(24 * (1 - core), 24)]
+
+
+def ratio_body(mine, theirs, seen, kz, keep, send, full):
+    join_planes(mine, theirs, full)
+    for xp in range(2):
+        blurred = along_z(kz, 0, *split(plane_pair(full, xp)))
+        ratio = plane_pair(seen, xp) / blurred
+        put_pair(full, xp, along_z(kz, 1, *split(ratio)))
+    part_planes(keep, send, full)
+
+
+def planes_body(mine, theirs, kz, out, full):
+    join_planes(mine, theirs, full)
+    for xp in range(2):
+        put_pair(out, xp, along_z(kz, 0, *split(plane_pair(full, xp))))
+
+
+def divide_body(blurred, seen, kz, keep, send, full):
+    for xp in range(2):
+        ratio = plane_pair(seen, xp) / plane_pair(blurred, xp)
+        put_pair(full, xp, along_z(kz, 1, *split(ratio)))
+    part_planes(keep, send, full)
 
 
 def put_sides(sides, tx, turned, put):
@@ -493,17 +533,38 @@
         inner = call(
             inner_body, [tile_half, tile_half], [cur, ext, mats], columns, flops=BUSY, name="inner"
         )
-        mine, theirs = call(
-            outer_body,
-            [tile_half, tile_half],
-            [from_odd, from_even, mats, *inner],
-            columns,
-            flops=BUSY,
-            name="outer",
-        )
+        if iteration == 0:
+            mine, theirs = call(
+                outer_body,
+                [tile_half, tile_half],
+                [from_odd, from_even, mats, *inner],
+                columns,
+                flops=BUSY,
+                name="outer",
+            )
+        else:
+            (theirs,), (mine,) = (
+                call(
+                    functools.partial(outer_one_body, v),
+                    [tile_half],
+                    [from_odd, from_even, mats, inner[v]],
+                    columns,
+                    flops=BUSY,
+                    name="outer_one",
+                )
+                for v in (1, 0)
+            )
         theirs = swap(theirs, "view", 1, (4,))
         if seen is None:
             whole = ((depth, tile_x, tile_y), F32)
+            (blurred,) = call(
+                planes_body,
+                [whole],
+                [mine, theirs, kz],
+                [pltpu.VMEM((depth, tile_x, tile_y), F32)],
+                flops=BUSY,
+                name="planes",
+            )
             (moved,) = call(
                 register_columns_body,
                 [whole],
@@ -515,15 +576,16 @@
             (seen,) = call(
                 register_body,
                 [whole],
-                [late_offsets, moved, *raw_from],
+                [late_offsets, moved, *raw_from, blurred],
                 [pltpu.VMEM((depth, tile_x + 2 * OMAX, 128), F32), turned],
                 flops=BUSY,
                 name="register",
             )
+        first = iteration == 0
         keep, send = call(
-            ratio_body,
+            divide_body if first else ratio_body,
             [tile_half, tile_half],
-            [mine, theirs, seen, kz],
+            [blurred, seen, kz] if first else [mine, theirs, seen, kz],
             [pltpu.VMEM((depth, tile_x, tile_y), F32)],
             flops=3 * 2 * 2 * 384 * 384 * 512,
             name="ratio",

time: 100 us -> 101 us (1.010)
  Pallas kernels: 20.2 us -> 22.1 us
    pallas_call x27 -> x29, Pallas kernels: 20.2 us -> 22.1 us  [call(): pl.pallas_call(body, out_shape=outs, in_specs=specs, out_specs=[pl.BlockS...]
    ppermute x15, waiting for transfers between devices: 18.9 us -> 17.8 us  [swap(): return lax.ppermute(value, axis, [(i, i ^ by) for i in range(count)])]
  transfers between devices with their start and end apart: 25 -> 25, of which waited for: 13 -> 13; matrix products, arithmetic and copies ran while one was open for 0% -> 0% of each run, Pallas kernels for 13% -> 14%
where the time goes in v6:
time: 101 us; the launch traced here: 100 us
  starting transfers between devices  42.3 us (42%)
  waiting for transfers between devices  32.5 us (32%)
  Pallas kernels  22.1 us (22%)
  local copies, waits for them, and re-layouts  2.7 us (3%)
    ppermute x5, starting transfers between devices, rim_swap(): from_odd = lax.ppermute(odd, 'ty', odd_pairs)  22.1 us
    pallas_call x29, Pallas kernels, call(): pl.pallas_call(body, out_shape=outs, in_specs=specs, out_specs=[pl.BlockS...  22.1 us
    ppermute x15, starting transfers between devices, swap(): return lax.ppermute(value, axis, [(i, i ^ by) for i in range(count)])  19.8 us
    ppermute x15, waiting for transfers between devices, swap(): return lax.ppermute(value, axis, [(i, i ^ by) for i in range(count)])  17.8 us
    ppermute x5, waiting for transfers between devices, rim_swap(): from_odd = lax.ppermute(odd, 'ty', odd_pairs)  14.6 us
    unnamed x14, local copies, waits for them, and re-layouts  2.5 us
  transfers between devices with their start and end apart: 25, of which 13 were waited for; matrix products, arithmetic and copies ran while one was open for 0% of the time, Pallas kernels for 14%

profile of v6, /device:TPU:121, one launch (start us, length us, event | category | flops | bytes accessed | tf_op | source)
XLA Modules:
  0.0 100.1 jit_solution(12687857576490300645)
XLA Ops:
  0.0 1.1 %copy-done = f32[48,32,128]{2,1,0:T(8,128)S(1)} copy-done((f32[48,32,128]{2,1,0:T(8,128)S(1)}, f32[48,32,128]{2,1,0:T(8,128)}, u32[]{:S(2)}) %copy-start) | copy-done | bytes 786456
  1.1 0.2 begin.1
  1.3 2.6 %collective-permute-start = (f32[6,16,128]{2,1,0:T(8,128)S(1)}, f32[6,16,128]{2,1,0:T(8,128)S(1)}, u32[]{:S(2)}, u32[]{:S(2)}) collective-permute-start(f32[6,16,128]{2,1,0:T(8,128)S(1)} %begin.1), channel_id=1, source_target_pairs={{0,160},{32,128},{64,224},{96,192},{128,32},{160,0},{192,96},{224,... | collective-permute-start | bytes 147464 | tf_op jit(solution)/shard_map/ppermute | solution.py:489
  3.9 1.1 %copy-done.2 = f32[1,48,32,128]{3,2,1,0:T(8,128)S(1)} copy-done((f32[1,48,32,128]{3,2,1,0:T(8,128)S(1)}, f32[1,48,32,128]{3,2,1,0:T(8,128)}, u32[]{:S(2)}) %copy-start.2) | copy-done | bytes 786456
  5.0 0.3 raw_sides.1
  5.3 0.6 collective-permute-start.4
  5.9 0.2 copy-done.1
  6.3 0.1 reshape.7.psf
  6.4 4.4 %collective-permute-start.1 = (f32[27,16,128]{2,1,0:T(8,128)S(1)}, f32[27,16,128]{2,1,0:T(8,128)S(1)}, u32[]{:S(2)}, u32[]{:S(2)}) collective-permute-start(f32[27,16,128]{2,1,0:T(8,128)S(1)} %get-tuple-element.52), channel_id=1, source_target_pairs={{1,2},{3,4},{5,6},{7,8},{9,10},{11,12},{13,14},{15,16},{17,18},{19... | collective-permute-start | bytes 663560 | tf_op jit(solution)/shard_map/ppermute | solution.py:496
  10.8 0.1 copy.16.offsets
  11.0 4.5 %collective-permute-start.5 = (f32[51,8,128]{2,1,0:T(8,128)S(1)}, f32[51,8,128]{2,1,0:T(8,128)S(1)}, u32[]{:S(2)}, u32[]{:S(2)}) collective-permute-start(f32[51,8,128]{2,1,0:T(8,128)S(1)} %get-tuple-element.63), channel_id=1, source_target_pairs={{1,2},{3,4},{5,6},{7,8},{9,10},{11,12},{13,14},{15,16},{17,18},{19... | collective-permute-start | bytes 626696 | tf_op jit(solution)/shard_map/ppermute | solution.py:496
  15.5 0.1 collective-permute-start.6
  15.6 1.4 %bands.1 = (bf16[2,768,384]{2,1,0:T(8,128)(2,1)S(1)}, bf16[10,256,256]{2,1,0:T(8,128)(2,1)S(1)}) custom-call(f32[16,32]{1,0:T(8,128)S(1)} %pad.4.taps.after, bf16[32,2048]{1,0:T(8,128)(2,1)S(1)} %copy-done.4, f32[372]{0:T(512)S(1)} %reshape.7.psf, s32[4,2]{1,0:T(4,128)S(1)} %copy.16.offsets), custom_call_target="tpu_custom_call" | custom-call | flops 6000000000 | bytes 2625008 | tf_op jit(solution)/shard_map/bands/pallas_call | solution.py:49
  17.0 1.1 %inner.2 = (f32[24,32,128]{2,1,0:T(8,128)S(1)}, f32[24,32,128]{2,1,0:T(8,128)S(1)}) custom-call(f32[24,32,128]{2,1,0:T(8,128)S(1)} %get-tuple-element.57.cur, f32[6,16,128]{2,1,0:T(8,128)S(1)} %collective-permute-done.pack.ext, bf16[10,256,256]{2,1,0:T(8,128)(2,1)S(1)} %get-tuple-element.56.mats), custom_call_target="tpu_custom_call" | custom-call | flops 6000000000 | bytes 2539520 | tf_op jit(solution)/shard_map/inner/pallas_call | solution.py:49
  18.1 1.1 %outer.1 = (f32[24,32,128]{2,1,0:T(8,128)S(1)}, f32[24,32,128]{2,1,0:T(8,128)S(1)}) custom-call(f32[27,16,128]{2,1,0:T(8,128)S(1)} %collective-permute-done.1.from_odd, f32[27,16,128]{2,1,0:T(8,128)S(1)} %collective-permute-done.2.from_even, bf16[10,256,256]{2,1,0:T(8,128)(2,1)S(1)} %get-tuple-element.56.mats, f32[24,32,128]{2,1,0:T(8,128)S(1)} %get-tuple-element.58.in_own, ...), custom_call_target="tpu_custom_call" | custom-call | flops 6000000000 | bytes 3325952 | tf_op jit(solution)/shard_map/outer/pallas_call | solution.py:49
  19.2 2.1 %collective-permute-start.3 = (f32[24,32,128]{2,1,0:T(8,128)S(1)}, f32[24,32,128]{2,1,0:T(8,128)S(1)}, u32[]{:S(2)}, u32[]{:S(2)}) collective-permute-start(f32[24,32,128]{2,1,0:T(8,128)S(1)} %get-tuple-element.61), channel_id=1, source_target_pairs={{0,64},{64,0},{128,192},{192,128},{1,65},{65,1},{129,193},{193,129... | collective-permute-start | bytes 1179656 | tf_op jit(solution)/shard_map/ppermute | solution.py:489
  21.2 1.3 %register_columns.1.moved = f32[48,32,128]{2,1,0:T(8,128)S(1)} custom-call(s32[4,2]{1,0:T(4,128)S(1)} %copy.16.offsets, f32[48,32,128]{2,1,0:T(8,128)S(1)} %bitcast.3, f32[12,8,128]{2,1,0:T(8,128)S(1)} %collective-permute-done.4.pack, f32[24,32,128]{2,1,0:T(8,128)S(1)} %get-tuple-element.60.mine.after), custom_call_target="tpu_custom_call" | custom-call | flops 6000000000 | bytes 2015264 | tf_op jit(solution)/shard_map/register_columns/pallas_call | solution.py:49
  22.6 0.6 planes.1.after.blurred
  23.3 1.0 %register.1.seen = f32[48,32,128]{2,1,0:T(8,128)S(1)} custom-call(s32[4,2]{1,0:T(4,128)S(1)} %copy.16.offsets, f32[48,32,128]{2,1,0:T(8,128)S(1)} %register_columns.1.moved, f32[51,8,128]{2,1,0:T(8,128)S(1)} %collective-permute-done.5.from_odd, f32[51,8,128]{2,1,0:T(8,128)S(1)} %collective-permute-done.6.from_even, f32[48,32,128]{2,1,0:T(8,128)S(1)} %planes.1.after.blurred), custom_call_target="tpu_custom_call" | custom-call | flops 6000000000 | bytes 2777120 | tf_op jit(solution)/shard_map/register/pallas_call | solution.py:49
  24.3 0.7 ratio.2
  25.0 0.7 collective-permute-start.7
  25.7 1.3 %collective-permute-done.7.other = f32[24,32,128]{2,1,0:T(8,128)S(1)} collective-permute-done((f32[24,32,128]{2,1,0:T(8,128)S(1)}, f32[24,32,128]{2,1,0:T(8,128)S(1)}, u32[]{:S(2)}, u32[]{:S(2)}) %collective-permute-start.7) | collective-permute-done | bytes 393248 | tf_op jit(solution)/shard_map/ppermute | solution.py:489
  27.1 1.0 mirror_rims.2
  28.1 4.4 %collective-permute-start.8 = (f32[27,16,128]{2,1,0:T(8,128)S(1)}, f32[27,16,128]{2,1,0:T(8,128)S(1)}, u32[]{:S(2)}, u32[]{:S(2)}) collective-permute-start(f32[27,16,128]{2,1,0:T(8,128)S(1)} %get-tuple-element.71), channel_id=1, source_target_pairs={{1,2},{3,4},{5,6},{7,8},{9,10},{11,12},{13,14},{15,16},{17,18},{19... | collective-permute-start | bytes 663560 | tf_op jit(solution)/shard_map/ppermute | solution.py:496
  32.5 0.1 collective-permute-start.9
  32.6 0.6 mirror.2
  33.2 3.5 %norm.1 = (f32[24,32,128]{2,1,0:T(8,128)S(1)}, f32[6,16,128]{2,1,0:T(8,128)S(1)}) custom-call(f32[372]{0:T(512)S(1)} %reshape.7.psf, s32[4,2]{1,0:T(4,128)S(1)} %copy.16.offsets, bf16[2,768,256]{2,1,0:T(8,128)(2,1)S(1)} %get-tuple-element.67.y_h.after), custom_call_target="tpu_custom_call" | custom-call | bytes 1230320 | tf_op jit(solution)/shard_map/norm/pallas_call | solution.py:49
  36.7 3.3 %collective-permute-done.8.from_odd = f32[27,16,128]{2,1,0:T(8,128)S(1)} collective-permute-done((f32[27,16,128]{2,1,0:T(8,128)S(1)}, f32[27,16,128]{2,1,0:T(8,128)S(1)}, u32[]{:S(2)}, u32[]{:S(2)}) %collective-permute-start.8) | collective-permute-done | bytes 221216 | tf_op jit(solution)/shard_map/ppermute | solution.py:496
  39.9 0.2 gather.2
  40.1 0.1 collective-permute-start.10
  40.3 1.4 %collective-permute-start.12 = (f32[12,32,128]{2,1,0:T(8,128)S(1)}, f32[12,32,128]{2,1,0:T(8,128)S(1)}, u32[]{:S(2)}, u32[]{:S(2)}) collective-permute-start(f32[12,32,128]{2,1,0:T(8,128)S(1)} %get-tuple-element.75.low), channel_id=1, source_target_pairs={{0,128},{64,192},{128,0},{192,64},{1,129},{65,193},{129,1},{193,65... | collective-permute-start | bytes 589832 | tf_op jit(solution)/shard_map/ppermute | solution.py:489
  41.7 0.1 collective-permute-start.13
  41.8 1.9 %collective-permute-done.10.theirs = f32[12,16,128]{2,1,0:T(8,128)S(1)} collective-permute-done((f32[12,16,128]{2,1,0:T(8,128)S(1)}, f32[12,16,128]{2,1,0:T(8,128)S(1)}, u32[]{:S(2)}, u32[]{:S(2)}) %collective-permute-start.10) | collective-permute-done | bytes 98336 | tf_op jit(solution)/shard_map/ppermute | solution.py:489
  43.7 2.3 %collective-permute-start.11 = (f32[12,16,128]{2,1,0:T(8,128)S(1)}, f32[12,16,128]{2,1,0:T(8,128)S(1)}, u32[]{:S(2)}, u32[]{:S(2)}) collective-permute-start(f32[12,16,128]{2,1,0:T(8,128)S(1)} %join.2.joined), channel_id=1, source_target_pairs={{0,160},{32,128},{64,224},{96,192},{128,32},{160,0},{192,96},{224,... | collective-permute-start | bytes 294920 | tf_op jit(solution)/shard_map/ppermute | solution.py:489
  46.0 1.5 %collective-permute-done.12.p_low = f32[12,32,128]{2,1,0:T(8,128)S(1)} collective-permute-done((f32[12,32,128]{2,1,0:T(8,128)S(1)}, f32[12,32,128]{2,1,0:T(8,128)S(1)}, u32[]{:S(2)}, u32[]{:S(2)}) %collective-permute-start.12) | collective-permute-done | bytes 196640 | tf_op jit(solution)/shard_map/ppermute | solution.py:489
  47.5 4.2 %collective-permute-done.13.p_high = f32[12,32,128]{2,1,0:T(8,128)S(1)} collective-permute-done((f32[12,32,128]{2,1,0:T(8,128)S(1)}, f32[12,32,128]{2,1,0:T(8,128)S(1)}, u32[]{:S(2)}, u32[]{:S(2)}) %collective-permute-start.13) | collective-permute-done | bytes 196640 | tf_op jit(solution)/shard_map/ppermute | solution.py:489
  51.7 0.2 update.1
  51.9 4.4 %collective-permute-start.14 = (f32[27,16,128]{2,1,0:T(8,128)S(1)}, f32[27,16,128]{2,1,0:T(8,128)S(1)}, u32[]{:S(2)}, u32[]{:S(2)}) collective-permute-start(f32[27,16,128]{2,1,0:T(8,128)S(1)} %get-tuple-element.78), channel_id=1, source_target_pairs={{1,2},{3,4},{5,6},{7,8},{9,10},{11,12},{13,14},{15,16},{17,18},{19... | collective-permute-start | bytes 663560 | tf_op jit(solution)/shard_map/ppermute | solution.py:496
  56.4 0.1 collective-permute-start.15
  56.5 1.1 %inner.3 = (f32[24,32,128]{2,1,0:T(8,128)S(1)}, f32[24,32,128]{2,1,0:T(8,128)S(1)}) custom-call(f32[24,32,128]{2,1,0:T(8,128)S(1)} %get-tuple-element.80.cur, f32[6,16,128]{2,1,0:T(8,128)S(1)} %get-tuple-element.81.ext, bf16[10,256,256]{2,1,0:T(8,128)(2,1)S(1)} %get-tuple-element.56.mats), custom_call_target="tpu_custom_call" | custom-call | flops 6000000000 | bytes 2539520 | tf_op jit(solution)/shard_map/inner/pallas_call | solution.py:49
  57.5 4.4 %collective-permute-done.14.from_odd = f32[27,16,128]{2,1,0:T(8,128)S(1)} collective-permute-done((f32[27,16,128]{2,1,0:T(8,128)S(1)}, f32[27,16,128]{2,1,0:T(8,128)S(1)}, u32[]{:S(2)}, u32[]{:S(2)}) %collective-permute-start.14) | collective-permute-done | bytes 221216 | tf_op jit(solution)/shard_map/ppermute | solution.py:496
  61.9 1.5 %outer_one.3 = f32[24,32,128]{2,1,0:T(8,128)S(1)} custom-call(f32[27,16,128]{2,1,0:T(8,128)S(1)} %collective-permute-done.14.from_odd, f32[27,16,128]{2,1,0:T(8,128)S(1)} %collective-permute-done.15.from_even, bf16[10,256,256]{2,1,0:T(8,128)(2,1)S(1)} %get-tuple-element.56.mats, f32[24,32,128]{2,1,0:T(8,128)S(1)} %get-tuple-element.83.inner), custom_call_target="tpu_custom_call" | custom-call | flops 6000000000 | bytes 2539520 | tf_op jit(solution)/shard_map/outer_one/pallas_call | solution.py:49
  63.5 3.4 %collective-permute-start.16 = (f32[24,32,128]{2,1,0:T(8,128)S(1)}, f32[24,32,128]{2,1,0:T(8,128)S(1)}, u32[]{:S(2)}, u32[]{:S(2)}) collective-permute-start(f32[24,32,128]{2,1,0:T(8,128)S(1)} %outer_one.3), channel_id=1, source_target_pairs={{0,64},{64,0},{128,192},{192,128},{1,65},{65,1},{129,193},{193,129... | collective-permute-start | bytes 1179656 | tf_op jit(solution)/shard_map/ppermute | solution.py:489
  66.9 1.5 %outer_one.2.mine = f32[24,32,128]{2,1,0:T(8,128)S(1)} custom-call(f32[27,16,128]{2,1,0:T(8,128)S(1)} %collective-permute-done.14.from_odd, f32[27,16,128]{2,1,0:T(8,128)S(1)} %collective-permute-done.15.from_even, bf16[10,256,256]{2,1,0:T(8,128)(2,1)S(1)} %get-tuple-element.56.mats, f32[24,32,128]{2,1,0:T(8,128)S(1)} %get-tuple-element.82.inner), custom_call_target="tpu_custom_call" | custom-call | flops 6000000000 | bytes 2539520 | tf_op jit(solution)/shard_map/outer_one/pallas_call | solution.py:49
  68.4 1.4 %ratio.3 = (f32[24,32,128]{2,1,0:T(8,128)S(1)}, f32[24,32,128]{2,1,0:T(8,128)S(1)}) custom-call(f32[24,32,128]{2,1,0:T(8,128)S(1)} %outer_one.2.mine, f32[24,32,128]{2,1,0:T(8,128)S(1)} %collective-permute-done.16.theirs, f32[48,32,128]{2,1,0:T(8,128)S(1)} %register.1.seen, bf16[2,768,384]{2,1,0:T(8,128)(2,1)S(1)} %get-tuple-element.62.kz), custom_call_target="tpu_custom_call" | custom-call | flops 905969664 | bytes 3538944 | tf_op jit(solution)/shard_map/ratio/pallas_call | solution.py:49
  69.9 0.3 collective-permute-start.17
  70.1 1.6 %collective-permute-done.17.other = f32[24,32,128]{2,1,0:T(8,128)S(1)} collective-permute-done((f32[24,32,128]{2,1,0:T(8,128)S(1)}, f32[24,32,128]{2,1,0:T(8,128)S(1)}, u32[]{:S(2)}, u32[]{:S(2)}) %collective-permute-start.17) | collective-permute-done | bytes 393248 | tf_op jit(solution)/shard_map/ppermute | solution.py:489
  71.7 1.0 mirror_rims.3
  72.7 4.4 %collective-permute-start.18 = (f32[27,16,128]{2,1,0:T(8,128)S(1)}, f32[27,16,128]{2,1,0:T(8,128)S(1)}, u32[]{:S(2)}, u32[]{:S(2)}) collective-permute-start(f32[27,16,128]{2,1,0:T(8,128)S(1)} %get-tuple-element.90), channel_id=1, source_target_pairs={{1,2},{3,4},{5,6},{7,8},{9,10},{11,12},{13,14},{15,16},{17,18},{19... | collective-permute-start | bytes 663560 | tf_op jit(solution)/shard_map/ppermute | solution.py:496
  77.1 0.1 collective-permute-start.19
  77.2 0.6 mirror.3
  77.8 7.0 %collective-permute-done.18.from_odd = f32[27,16,128]{2,1,0:T(8,128)S(1)} collective-permute-done((f32[27,16,128]{2,1,0:T(8,128)S(1)}, f32[27,16,128]{2,1,0:T(8,128)S(1)}, u32[]{:S(2)}, u32[]{:S(2)}) %collective-permute-start.18) | collective-permute-done | bytes 221216 | tf_op jit(solution)/shard_map/ppermute | solution.py:496
  84.8 0.7 collective-permute-start.20
  85.5 0.8 collective-permute-start.22
  86.4 0.6 collective-permute-start.23
  87.0 0.8 collective-permute-done.20.theirs
  87.9 2.3 %collective-permute-start.21 = (f32[6,16,128]{2,1,0:T(8,128)S(1)}, f32[6,16,128]{2,1,0:T(8,128)S(1)}, u32[]{:S(2)}, u32[]{:S(2)}) collective-permute-start(f32[6,16,128]{2,1,0:T(8,128)S(1)} %join.3), channel_id=1, source_target_pairs={{0,160},{32,128},{64,224},{96,192},{128,32},{160,0},{192,96},{224,... | collective-permute-start | bytes 147464 | tf_op jit(solution)/shard_map/ppermute | solution.py:489
  90.1 2.0 %collective-permute-done.21.side = f32[6,16,128]{2,1,0:T(8,128)S(1)} collective-permute-done((f32[6,16,128]{2,1,0:T(8,128)S(1)}, f32[6,16,128]{2,1,0:T(8,128)S(1)}, u32[]{:S(2)}, u32[]{:S(2)}) %collective-permute-start.21) | collective-permute-done | bytes 49184 | tf_op jit(solution)/shard_map/ppermute | solution.py:489
  92.1 3.8 %collective-permute-done.23.p_high = f32[12,32,128]{2,1,0:T(8,128)S(1)} collective-permute-done((f32[12,32,128]{2,1,0:T(8,128)S(1)}, f32[12,32,128]{2,1,0:T(8,128)S(1)}, u32[]{:S(2)}, u32[]{:S(2)}) %collective-permute-start.23) | collective-permute-done | bytes 196640 | tf_op jit(solution)/shard_map/ppermute | solution.py:489
  95.9 0.2 last.1.mine
  96.1 1.8 %collective-permute-start.24 = (f32[24,32,128]{2,1,0:T(8,128)S(1)}, f32[24,32,128]{2,1,0:T(8,128)S(1)}, u32[]{:S(2)}, u32[]{:S(2)}) collective-permute-start(f32[24,32,128]{2,1,0:T(8,128)S(1)} %last.1.mine), channel_id=1, source_target_pairs={{0,64},{64,0},{128,192},{192,128},{1,65},{65,1},{129,193},{193,129... | collective-permute-start | bytes 1179656 | tf_op jit(solution)/shard_map/ppermute | solution.py:489
  97.9 0.8 near_half.1.near
  98.6 0.6 collective-permute-done.24.theirs
  99.2 0.8 far_half.1
  (34 shorter events, 0.4 us)
Async XLA Ops:
  0.0 1.1 %copy-start = (f32[48,32,128]{2,1,0:T(8,128)S(1)}, f32[48,32,128]{2,1,0:T(8,128)}, u32[]{:S(2)}) copy-start(f32[48,32,128]{2,1,0:T(8,128)} %est.3) | copy-start | bytes 2359300
  1.3 4.9 %collective-permute-start = (f32[6,16,128]{2,1,0:T(8,128)S(1)}, f32[6,16,128]{2,1,0:T(8,128)S(1)}, u32[]{:S(2)}, u32[]{:S(2)}) collective-permute-start(f32[6,16,128]{2,1,0:T(8,128)S(1)} %begin.1), channel_id=1, source_target_pairs={{0,160},{32,128},{64,224},{96,192},{128,32},{160,0},{192,96},{224,... | collective-permute-start | bytes 147464 | tf_op jit(solution)/shard_map/ppermute | solution.py:489
  3.9 1.1 %copy-start.2 = (f32[1,48,32,128]{3,2,1,0:T(8,128)S(1)}, f32[1,48,32,128]{3,2,1,0:T(8,128)}, u32[]{:S(2)}) copy-start(f32[1,48,32,128]{3,2,1,0:T(8,128)} %param.5) | copy-start | bytes 2359300
  5.0 1.1 %copy-start.1 = (f32[48,32,128]{2,1,0:T(8,128)S(1)}, f32[48,32,128]{2,1,0:T(8,128)}, u32[]{:S(2)}) copy-start(f32[48,32,128]{2,1,0:T(8,128)} %est.3) | copy-start | bytes 2359300
  5.0 1.2 %copy-start.5 = (f32[4,3,31]{2,0,1:T(4,128)S(1)}, f32[4,3,31]{2,0,1:T(4,128)}, u32[]{:S(2)}) copy-start(f32[4,3,31]{2,0,1:T(4,128)} %param.6) | copy-start | bytes 4468
  5.3 5.5 %copy-start.6 = (s32[4,2]{0,1:T(2,128)S(1)}, s32[4,2]{0,1:T(2,128)}, u32[]{:S(2)}) copy-start(s32[4,2]{0,1:T(2,128)} %param.7) | copy-start | bytes 100
  5.3 5.6 %copy-start.3 = (f32[1,48,32,128]{3,2,1,0:T(8,128)S(1)}, f32[1,48,32,128]{3,2,1,0:T(8,128)}, u32[]{:S(2)}) copy-start(f32[1,48,32,128]{3,2,1,0:T(8,128)} %param.5) | copy-start | bytes 2359300
  5.3 10.3 %copy-start.4 = (bf16[32,2048]{1,0:T(8,128)(2,1)S(1)}, bf16[32,2048]{1,0:T(8,128)(2,1)}, u32[]{:S(2)}) copy-start(bf16[32,2048]{1,0:T(8,128)(2,1)} %constant.5.clone.place) | copy-start | bytes 393220
  5.3 5.6 %collective-permute-start.4 = (f32[12,8,128]{2,1,0:T(8,128)S(1)}, f32[12,8,128]{2,1,0:T(8,128)S(1)}, u32[]{:S(2)}, u32[]{:S(2)}) collective-permute-start(f32[12,8,128]{2,1,0:T(8,128)S(1)} %raw_sides.1), channel_id=1, source_target_pairs={{0,32},{32,0},{1,33},{33,1},{2,34},{34,2},{3,35},{35,3},{4,36},{36... | collective-permute-start | bytes 147464 | tf_op jit(solution)/shard_map/ppermute | solution.py:489
  6.4 11.7 %collective-permute-start.1 = (f32[27,16,128]{2,1,0:T(8,128)S(1)}, f32[27,16,128]{2,1,0:T(8,128)S(1)}, u32[]{:S(2)}, u32[]{:S(2)}) collective-permute-start(f32[27,16,128]{2,1,0:T(8,128)S(1)} %get-tuple-element.52), channel_id=1, source_target_pairs={{1,2},{3,4},{5,6},{7,8},{9,10},{11,12},{13,14},{15,16},{17,18},{19... | collective-permute-start | bytes 663560 | tf_op jit(solution)/shard_map/ppermute | solution.py:496
  10.9 7.2 %collective-permute-start.2 = (f32[27,16,128]{2,1,0:T(8,128)S(1)}, f32[27,16,128]{2,1,0:T(8,128)S(1)}, u32[]{:S(2)}, u32[]{:S(2)}) collective-permute-start(f32[27,16,128]{2,1,0:T(8,128)S(1)} %get-tuple-element.53), channel_id=1, source_target_pairs={{0,1},{1,0},{2,3},{3,2},{4,5},{5,4},{6,7},{7,6},{8,9},{9,8},{10,11... | collective-permute-start | bytes 663560 | tf_op jit(solution)/shard_map/ppermute | solution.py:497
  11.0 12.2 %collective-permute-start.5 = (f32[51,8,128]{2,1,0:T(8,128)S(1)}, f32[51,8,128]{2,1,0:T(8,128)S(1)}, u32[]{:S(2)}, u32[]{:S(2)}) collective-permute-start(f32[51,8,128]{2,1,0:T(8,128)S(1)} %get-tuple-element.63), channel_id=1, source_target_pairs={{1,2},{3,4},{5,6},{7,8},{9,10},{11,12},{13,14},{15,16},{17,18},{19... | collective-permute-start | bytes 626696 | tf_op jit(solution)/shard_map/ppermute | solution.py:496
  15.5 7.8 %collective-permute-start.6 = (f32[51,8,128]{2,1,0:T(8,128)S(1)}, f32[51,8,128]{2,1,0:T(8,128)S(1)}, u32[]{:S(2)}, u32[]{:S(2)}) collective-permute-start(f32[51,8,128]{2,1,0:T(8,128)S(1)} %get-tuple-element.64), channel_id=1, source_target_pairs={{0,1},{1,0},{2,3},{3,2},{4,5},{5,4},{6,7},{7,6},{8,9},{9,8},{10,11... | collective-permute-start | bytes 626696 | tf_op jit(solution)/shard_map/ppermute | solution.py:497
  19.2 3.4 %collective-permute-start.3 = (f32[24,32,128]{2,1,0:T(8,128)S(1)}, f32[24,32,128]{2,1,0:T(8,128)S(1)}, u32[]{:S(2)}, u32[]{:S(2)}) collective-permute-start(f32[24,32,128]{2,1,0:T(8,128)S(1)} %get-tuple-element.61), channel_id=1, source_target_pairs={{0,64},{64,0},{128,192},{192,128},{1,65},{65,1},{129,193},{193,129... | collective-permute-start | bytes 1179656 | tf_op jit(solution)/shard_map/ppermute | solution.py:489
  25.0 2.1 %collective-permute-start.7 = (f32[24,32,128]{2,1,0:T(8,128)S(1)}, f32[24,32,128]{2,1,0:T(8,128)S(1)}, u32[]{:S(2)}, u32[]{:S(2)}) collective-permute-start(f32[24,32,128]{2,1,0:T(8,128)S(1)} %get-tuple-element.66), channel_id=1, source_target_pairs={{0,64},{64,0},{128,192},{192,128},{1,65},{65,1},{129,193},{193,129... | collective-permute-start | bytes 1179656 | tf_op jit(solution)/shard_map/ppermute | solution.py:489
  28.1 11.9 %collective-permute-start.8 = (f32[27,16,128]{2,1,0:T(8,128)S(1)}, f32[27,16,128]{2,1,0:T(8,128)S(1)}, u32[]{:S(2)}, u32[]{:S(2)}) collective-permute-start(f32[27,16,128]{2,1,0:T(8,128)S(1)} %get-tuple-element.71), channel_id=1, source_target_pairs={{1,2},{3,4},{5,6},{7,8},{9,10},{11,12},{13,14},{15,16},{17,18},{19... | collective-permute-start | bytes 663560 | tf_op jit(solution)/shard_map/ppermute | solution.py:496
  32.5 7.4 %collective-permute-start.9 = (f32[27,16,128]{2,1,0:T(8,128)S(1)}, f32[27,16,128]{2,1,0:T(8,128)S(1)}, u32[]{:S(2)}, u32[]{:S(2)}) collective-permute-start(f32[27,16,128]{2,1,0:T(8,128)S(1)} %get-tuple-element.72), channel_id=1, source_target_pairs={{0,1},{1,0},{2,3},{3,2},{4,5},{5,4},{6,7},{7,6},{8,9},{9,8},{10,11... | collective-permute-start | bytes 663560 | tf_op jit(solution)/shard_map/ppermute | solution.py:497
  40.1 3.6 %collective-permute-start.10 = (f32[12,16,128]{2,1,0:T(8,128)S(1)}, f32[12,16,128]{2,1,0:T(8,128)S(1)}, u32[]{:S(2)}, u32[]{:S(2)}) collective-permute-start(f32[12,16,128]{2,1,0:T(8,128)S(1)} %get-tuple-element.74.mine), channel_id=1, source_target_pairs={{0,128},{64,192},{128,0},{192,64},{1,129},{65,193},{129,1},{193,65... | collective-permute-start | bytes 294920 | tf_op jit(solution)/shard_map/ppermute | solution.py:489
  40.3 7.2 %collective-permute-start.12 = (f32[12,32,128]{2,1,0:T(8,128)S(1)}, f32[12,32,128]{2,1,0:T(8,128)S(1)}, u32[]{:S(2)}, u32[]{:S(2)}) collective-permute-start(f32[12,32,128]{2,1,0:T(8,128)S(1)} %get-tuple-element.75.low), channel_id=1, source_target_pairs={{0,128},{64,192},{128,0},{192,64},{1,129},{65,193},{129,1},{193,65... | collective-permute-start | bytes 589832 | tf_op jit(solution)/shard_map/ppermute | solution.py:489
  41.7 10.0 %collective-permute-start.13 = (f32[12,32,128]{2,1,0:T(8,128)S(1)}, f32[12,32,128]{2,1,0:T(8,128)S(1)}, u32[]{:S(2)}, u32[]{:S(2)}) collective-permute-start(f32[12,32,128]{2,1,0:T(8,128)S(1)} %get-tuple-element.76.high), channel_id=1, source_target_pairs={{0,128},{64,192},{128,0},{192,64},{1,129},{65,193},{129,1},{193,65... | collective-permute-start | bytes 589832 | tf_op jit(solution)/shard_map/ppermute | solution.py:489
  43.7 8.0 %collective-permute-start.11 = (f32[12,16,128]{2,1,0:T(8,128)S(1)}, f32[12,16,128]{2,1,0:T(8,128)S(1)}, u32[]{:S(2)}, u32[]{:S(2)}) collective-permute-start(f32[12,16,128]{2,1,0:T(8,128)S(1)} %join.2.joined), channel_id=1, source_target_pairs={{0,160},{32,128},{64,224},{96,192},{128,32},{160,0},{192,96},{224,... | collective-permute-start | bytes 294920 | tf_op jit(solution)/shard_map/ppermute | solution.py:489
  51.9 10.0 %collective-permute-start.14 = (f32[27,16,128]{2,1,0:T(8,128)S(1)}, f32[27,16,128]{2,1,0:T(8,128)S(1)}, u32[]{:S(2)}, u32[]{:S(2)}) collective-permute-start(f32[27,16,128]{2,1,0:T(8,128)S(1)} %get-tuple-element.78), channel_id=1, source_target_pairs={{1,2},{3,4},{5,6},{7,8},{9,10},{11,12},{13,14},{15,16},{17,18},{19... | collective-permute-start | bytes 663560 | tf_op jit(solution)/shard_map/ppermute | solution.py:496
  56.4 5.6 %collective-permute-start.15 = (f32[27,16,128]{2,1,0:T(8,128)S(1)}, f32[27,16,128]{2,1,0:T(8,128)S(1)}, u32[]{:S(2)}, u32[]{:S(2)}) collective-permute-start(f32[27,16,128]{2,1,0:T(8,128)S(1)} %get-tuple-element.79), channel_id=1, source_target_pairs={{0,1},{1,0},{2,3},{3,2},{4,5},{5,4},{6,7},{7,6},{8,9},{9,8},{10,11... | collective-permute-start | bytes 663560 | tf_op jit(solution)/shard_map/ppermute | solution.py:497
  63.5 4.9 %collective-permute-start.16 = (f32[24,32,128]{2,1,0:T(8,128)S(1)}, f32[24,32,128]{2,1,0:T(8,128)S(1)}, u32[]{:S(2)}, u32[]{:S(2)}) collective-permute-start(f32[24,32,128]{2,1,0:T(8,128)S(1)} %outer_one.3), channel_id=1, source_target_pairs={{0,64},{64,0},{128,192},{192,128},{1,65},{65,1},{129,193},{193,129... | collective-permute-start | bytes 1179656 | tf_op jit(solution)/shard_map/ppermute | solution.py:489
  69.9 1.8 %collective-permute-start.17 = (f32[24,32,128]{2,1,0:T(8,128)S(1)}, f32[24,32,128]{2,1,0:T(8,128)S(1)}, u32[]{:S(2)}, u32[]{:S(2)}) collective-permute-start(f32[24,32,128]{2,1,0:T(8,128)S(1)} %get-tuple-element.85), channel_id=1, source_target_pairs={{0,64},{64,0},{128,192},{192,128},{1,65},{65,1},{129,193},{193,129... | collective-permute-start | bytes 1179656 | tf_op jit(solution)/shard_map/ppermute | solution.py:489
  72.7 12.1 %collective-permute-start.18 = (f32[27,16,128]{2,1,0:T(8,128)S(1)}, f32[27,16,128]{2,1,0:T(8,128)S(1)}, u32[]{:S(2)}, u32[]{:S(2)}) collective-permute-start(f32[27,16,128]{2,1,0:T(8,128)S(1)} %get-tuple-element.90), channel_id=1, source_target_pairs={{1,2},{3,4},{5,6},{7,8},{9,10},{11,12},{13,14},{15,16},{17,18},{19... | collective-permute-start | bytes 663560 | tf_op jit(solution)/shard_map/ppermute | solution.py:496
  77.1 7.7 %collective-permute-start.19 = (f32[27,16,128]{2,1,0:T(8,128)S(1)}, f32[27,16,128]{2,1,0:T(8,128)S(1)}, u32[]{:S(2)}, u32[]{:S(2)}) collective-permute-start(f32[27,16,128]{2,1,0:T(8,128)S(1)} %get-tuple-element.91), channel_id=1, source_target_pairs={{0,1},{1,0},{2,3},{3,2},{4,5},{5,4},{6,7},{7,6},{8,9},{9,8},{10,11... | collective-permute-start | bytes 663560 | tf_op jit(solution)/shard_map/ppermute | solution.py:497
  84.8 3.0 %collective-permute-start.20 = (f32[6,16,128]{2,1,0:T(8,128)S(1)}, f32[6,16,128]{2,1,0:T(8,128)S(1)}, u32[]{:S(2)}, u32[]{:S(2)}) collective-permute-start(f32[6,16,128]{2,1,0:T(8,128)S(1)} %get-tuple-element.92.mine), channel_id=1, source_target_pairs={{0,128},{64,192},{128,0},{192,64},{1,129},{65,193},{129,1},{193,65... | collective-permute-start | bytes 147464 | tf_op jit(solution)/shard_map/ppermute | solution.py:489
  85.5 6.6 %collective-permute-start.22 = (f32[12,32,128]{2,1,0:T(8,128)S(1)}, f32[12,32,128]{2,1,0:T(8,128)S(1)}, u32[]{:S(2)}, u32[]{:S(2)}) collective-permute-start(f32[12,32,128]{2,1,0:T(8,128)S(1)} %get-tuple-element.93.low), channel_id=1, source_target_pairs={{0,128},{64,192},{128,0},{192,64},{1,129},{65,193},{129,1},{193,65... | collective-permute-start | bytes 589832 | tf_op jit(solution)/shard_map/ppermute | solution.py:489
  86.4 9.5 %collective-permute-start.23 = (f32[12,32,128]{2,1,0:T(8,128)S(1)}, f32[12,32,128]{2,1,0:T(8,128)S(1)}, u32[]{:S(2)}, u32[]{:S(2)}) collective-permute-start(f32[12,32,128]{2,1,0:T(8,128)S(1)} %get-tuple-element.94.high), channel_id=1, source_target_pairs={{0,128},{64,192},{128,0},{192,64},{1,129},{65,193},{129,1},{193,65... | collective-permute-start | bytes 589832 | tf_op jit(solution)/shard_map/ppermute | solution.py:489
  87.9 4.2 %collective-permute-start.21 = (f32[6,16,128]{2,1,0:T(8,128)S(1)}, f32[6,16,128]{2,1,0:T(8,128)S(1)}, u32[]{:S(2)}, u32[]{:S(2)}) collective-permute-start(f32[6,16,128]{2,1,0:T(8,128)S(1)} %join.3), channel_id=1, source_target_pairs={{0,160},{32,128},{64,224},{96,192},{128,32},{160,0},{192,96},{224,... | collective-permute-start | bytes 147464 | tf_op jit(solution)/shard_map/ppermute | solution.py:489
  96.1 3.1 %collective-permute-start.24 = (f32[24,32,128]{2,1,0:T(8,128)S(1)}, f32[24,32,128]{2,1,0:T(8,128)S(1)}, u32[]{:S(2)}, u32[]{:S(2)}) collective-permute-start(f32[24,32,128]{2,1,0:T(8,128)S(1)} %last.1.mine), channel_id=1, source_target_pairs={{0,64},{64,0},{128,192},{192,128},{1,65},{65,1},{129,193},{193,129... | collective-permute-start | bytes 1179656 | tf_op jit(solution)/shard_map/ppermute | solution.py:489

commit v7 on v6

--- a/solution.py
+++ b/solution.py
@@ -250,16 +250,21 @@
         put_rims(pack[t][None], pack[9 + t][None], even_out, odd_out, slice(48 + t, 49 + t))
 
 
-def register_columns_body(offsets, raw, pack, after, out, wide, turned):
+def shift_columns(tile, side, sy):
+    lane = lax.broadcasted_iota(jnp.int32, tile.shape, 2)
+    inside = (lane >= sy) & (lane < 128 + sy)
+    return pltpu.roll(jnp.where(inside, tile, side), lax.rem(128 - sy, 128), 2)
+
+
+def register_columns_body(offsets, raw, pack, after, out, turned):
     view, tx = lax.axis_index("view"), lax.axis_index("tx")
     sy = offsets[view, 1]
-    wide[:, :, 0:128] = raw[...]
     turned[...] = jnp.zeros_like(turned)
     for b in range(4):
         parts = [pack[3 * b + t] for t in range(3)]
-        wide[:, 8 * b : 8 * b + 8, 128:256] = spread_columns(parts, 120 * tx, 8, turned).reshape(48, 8, 128)
-    for z in range(0, 48, 4):
-        out[z : z + 4] = pltpu.roll(wide[z : z + 4], lax.rem(256 - sy, 256), 2)[:, :, 0:128]
+        side = spread_columns(parts, 120 * tx, 8, turned).reshape(48, 8, 128)
+        rows = slice(8 * b, 8 * b + 8)
+        out[:, rows, :] = shift_columns(raw[:, rows, :], side, sy)
 
 
 def register_body(offsets, moved, from_odd, from_even, after, out, wide, turned):
@@ -272,8 +277,7 @@
     wide[:, 8:40, :] = moved[...]
     for rim, rows in ((above, slice(0, 8)), (below, slice(40, 48))):
         side = spread_columns([rim[48 + t] for t in range(3)], 120 * tx, 8, turned).reshape(48, 8, 128)
-        both = jnp.concatenate([rim[0:48], side], axis=2)
-        wide[:, rows, :] = pltpu.roll(both, lax.rem(256 - sy, 256), 2)[:, :, 0:128]
+        wide[:, rows, :] = shift_columns(rim[0:48], side, sy)
     out[...] = wide[:, pl.ds(8 + sx, 32), :]
 
 
@@ -283,14 +287,12 @@
     x_h[:, rows, 128:256], x_l[:, rows, 128:256] = split(side)
 
 
-def blur_rows(x_h, x_l, yf, bx, g, views=(0, 1)):
+def blur_rows(x_h, x_l, yf, bx, g):
     z = slice(4 * g, 4 * g + 4)
     high, low = x_h[z].reshape(128, 256), x_l[z].reshape(128, 256)
-    first = 128 * views[0]
-    yf = [y[:, first : first + 128 * len(views)] for y in yf]
     along_y = split(dot(high, yf[0], NN) + (dot(high, yf[1], NN) + dot(low, yf[0], NN)))
-    for i, v in enumerate(views):
-        cols = slice(128 * i, 128 * i + 128)
+    for v in range(2):
+        cols = slice(128 * v, 128 * v + 128)
         yield v, z, rows3(bx[v][:, 0:128], (along_y[0][:, cols], along_y[1][:, cols])).reshape(4, 32, 128)
 
 
@@ -314,13 +316,6 @@
     for xh, rim in ((0, above), (1, below)):
         rows = slice(16 * xh, 16 * xh + 16)
         put_columns(rows, rim[0:24], [rim[24 + t] for t in range(3)], tx, x_h, x_l, turned)
-
-
-def outer_one_body(v, from_odd, from_even, mats, inner, out, x_h, x_l, turned):
-    fill_outer(from_odd, from_even, x_h, x_l, turned)
-    for g in range(6):
-        for _, z, part in blur_rows(x_h, x_l, (mats[YT], mats[YT + 1]), (mats[OUT], mats[OUT + 1]), g, (v,)):
-            out[z] = inner[z] + part
 
 
 def outer_body(from_odd, from_even, mats, in_own, in_other, own, other, x_h, x_l, turned):
@@ -533,27 +528,14 @@
         inner = call(
             inner_body, [tile_half, tile_half], [cur, ext, mats], columns, flops=BUSY, name="inner"
         )
-        if iteration == 0:
-            mine, theirs = call(
-                outer_body,
-                [tile_half, tile_half],
-                [from_odd, from_even, mats, *inner],
-                columns,
-                flops=BUSY,
-                name="outer",
-            )
-        else:
-            (theirs,), (mine,) = (
-                call(
-                    functools.partial(outer_one_body, v),
-                    [tile_half],
-                    [from_odd, from_even, mats, inner[v]],
-                    columns,
-                    flops=BUSY,
-                    name="outer_one",
-                )
-                for v in (1, 0)
-            )
+        mine, theirs = call(
+            outer_body,
+            [tile_half, tile_half],
+            [from_odd, from_even, mats, *inner],
+            columns,
+            flops=BUSY,
+            name="outer",
+        )
         theirs = swap(theirs, "view", 1, (4,))
         if seen is None:
             whole = ((depth, tile_x, tile_y), F32)
@@ -569,7 +551,7 @@
                 register_columns_body,
                 [whole],
                 [late_offsets, raw, sides, mine],
-                [pltpu.VMEM((depth, tile_x, 256), F32), turned],
+                [turned],
                 flops=BUSY,
                 name="register_columns",
             )

time: 101 us -> 99.6 us (0.986)
  Pallas kernels: 22.1 us -> 19.8 us
    pallas_call x29 -> x28, Pallas kernels: 22.1 us -> 19.8 us  [call(): pl.pallas_call(body, out_shape=outs, in_specs=specs, out_specs=[pl.BlockS...]
  transfers between devices with their start and end apart: 25 -> 25, of which waited for: 13 -> 14; matrix products, arithmetic and copies ran while one was open for 0% -> 0% of each run, Pallas kernels for 14% -> 12%
where the time goes in v7:
time: 99.6 us; the launch traced here: 99.1 us
  starting transfers between devices  42.9 us (43%)
  waiting for transfers between devices  33.2 us (33%)
  Pallas kernels  19.8 us (20%)
  local copies, waits for them, and re-layouts  2.7 us (3%)
    ppermute x5, starting transfers between devices, rim_swap(): from_odd = lax.ppermute(odd, 'ty', odd_pairs)  22.1 us
    ppermute x15, starting transfers between devices, swap(): return lax.ppermute(value, axis, [(i, i ^ by) for i in range(count)])  20.4 us
    pallas_call x28, Pallas kernels, call(): pl.pallas_call(body, out_shape=outs, in_specs=specs, out_specs=[pl.BlockS...  19.8 us
    ppermute x15, waiting for transfers between devices, swap(): return lax.ppermute(value, axis, [(i, i ^ by) for i in range(count)])  18.8 us
    ppermute x5, waiting for transfers between devices, rim_swap(): from_odd = lax.ppermute(odd, 'ty', odd_pairs)  14.5 us
    unnamed x14, local copies, waits for them, and re-layouts  2.5 us
  transfers between devices with their start and end apart: 25, of which 14 were waited for; matrix products, arithmetic and copies ran while one was open for 0% of the time, Pallas kernels for 12%

profile of v7, /device:TPU:121, one launch (start us, length us, event | category | flops | bytes accessed | tf_op | source)
XLA Modules:
  0.0 99.1 jit_solution(5636201594537572185)
XLA Ops:
  0.0 1.1 %copy-done = f32[48,32,128]{2,1,0:T(8,128)S(1)} copy-done((f32[48,32,128]{2,1,0:T(8,128)S(1)}, f32[48,32,128]{2,1,0:T(8,128)}, u32[]{:S(2)}) %copy-start) | copy-done | bytes 786456
  1.1 0.2 begin.1
  1.3 2.6 %collective-permute-start = (f32[6,16,128]{2,1,0:T(8,128)S(1)}, f32[6,16,128]{2,1,0:T(8,128)S(1)}, u32[]{:S(2)}, u32[]{:S(2)}) collective-permute-start(f32[6,16,128]{2,1,0:T(8,128)S(1)} %begin.1), channel_id=1, source_target_pairs={{0,160},{32,128},{64,224},{96,192},{128,32},{160,0},{192,96},{224,... | collective-permute-start | bytes 147464 | tf_op jit(solution)/shard_map/ppermute | solution.py:484
  3.9 1.1 %copy-done.2 = f32[1,48,32,128]{3,2,1,0:T(8,128)S(1)} copy-done((f32[1,48,32,128]{3,2,1,0:T(8,128)S(1)}, f32[1,48,32,128]{3,2,1,0:T(8,128)}, u32[]{:S(2)}) %copy-start.2) | copy-done | bytes 786456
  5.0 0.3 raw_sides.1
  5.3 0.6 collective-permute-start.4
  5.9 0.2 copy-done.1
  6.4 4.4 %collective-permute-start.1 = (f32[27,16,128]{2,1,0:T(8,128)S(1)}, f32[27,16,128]{2,1,0:T(8,128)S(1)}, u32[]{:S(2)}, u32[]{:S(2)}) collective-permute-start(f32[27,16,128]{2,1,0:T(8,128)S(1)} %get-tuple-element.54), channel_id=1, source_target_pairs={{1,2},{3,4},{5,6},{7,8},{9,10},{11,12},{13,14},{15,16},{17,18},{19... | collective-permute-start | bytes 663560 | tf_op jit(solution)/shard_map/ppermute | solution.py:491
  10.8 0.1 copy.16.offsets
  11.0 4.5 %collective-permute-start.5 = (f32[51,8,128]{2,1,0:T(8,128)S(1)}, f32[51,8,128]{2,1,0:T(8,128)S(1)}, u32[]{:S(2)}, u32[]{:S(2)}) collective-permute-start(f32[51,8,128]{2,1,0:T(8,128)S(1)} %get-tuple-element.65), channel_id=1, source_target_pairs={{1,2},{3,4},{5,6},{7,8},{9,10},{11,12},{13,14},{15,16},{17,18},{19... | collective-permute-start | bytes 626696 | tf_op jit(solution)/shard_map/ppermute | solution.py:491
  15.5 0.1 collective-permute-start.6
  15.6 1.4 %bands.1 = (bf16[2,768,384]{2,1,0:T(8,128)(2,1)S(1)}, bf16[10,256,256]{2,1,0:T(8,128)(2,1)S(1)}) custom-call(f32[16,32]{1,0:T(8,128)S(1)} %pad.4.taps.after, bf16[32,2048]{1,0:T(8,128)(2,1)S(1)} %copy-done.4, f32[372]{0:T(512)S(1)} %reshape.7.psf, s32[4,2]{1,0:T(4,128)S(1)} %copy.16.offsets), custom_call_target="tpu_custom_call" | custom-call | flops 6000000000 | bytes 2625008 | tf_op jit(solution)/shard_map/bands/pallas_call | solution.py:49
  17.0 1.1 %inner.2 = (f32[24,32,128]{2,1,0:T(8,128)S(1)}, f32[24,32,128]{2,1,0:T(8,128)S(1)}) custom-call(f32[24,32,128]{2,1,0:T(8,128)S(1)} %get-tuple-element.59.cur, f32[6,16,128]{2,1,0:T(8,128)S(1)} %collective-permute-done.pack.ext, bf16[10,256,256]{2,1,0:T(8,128)(2,1)S(1)} %get-tuple-element.58.mats), custom_call_target="tpu_custom_call" | custom-call | flops 6000000000 | bytes 2539520 | tf_op jit(solution)/shard_map/inner/pallas_call | solution.py:49
  18.1 1.1 %outer.2 = (f32[24,32,128]{2,1,0:T(8,128)S(1)}, f32[24,32,128]{2,1,0:T(8,128)S(1)}) custom-call(f32[27,16,128]{2,1,0:T(8,128)S(1)} %collective-permute-done.1.from_odd, f32[27,16,128]{2,1,0:T(8,128)S(1)} %collective-permute-done.2.from_even, bf16[10,256,256]{2,1,0:T(8,128)(2,1)S(1)} %get-tuple-element.58.mats, f32[24,32,128]{2,1,0:T(8,128)S(1)} %get-tuple-element.60.in_own, ...), custom_call_target="tpu_custom_call" | custom-call | flops 6000000000 | bytes 3325952 | tf_op jit(solution)/shard_map/outer/pallas_call | solution.py:49
  19.2 2.1 %collective-permute-start.3 = (f32[24,32,128]{2,1,0:T(8,128)S(1)}, f32[24,32,128]{2,1,0:T(8,128)S(1)}, u32[]{:S(2)}, u32[]{:S(2)}) collective-permute-start(f32[24,32,128]{2,1,0:T(8,128)S(1)} %get-tuple-element.63), channel_id=1, source_target_pairs={{0,64},{64,0},{128,192},{192,128},{1,65},{65,1},{129,193},{193,129... | collective-permute-start | bytes 1179656 | tf_op jit(solution)/shard_map/ppermute | solution.py:484
  21.2 1.1 %register_columns.1.moved = f32[48,32,128]{2,1,0:T(8,128)S(1)} custom-call(s32[4,2]{1,0:T(4,128)S(1)} %copy.16.offsets, f32[48,32,128]{2,1,0:T(8,128)S(1)} %bitcast.3, f32[12,8,128]{2,1,0:T(8,128)S(1)} %collective-permute-done.4.pack, f32[24,32,128]{2,1,0:T(8,128)S(1)} %get-tuple-element.62.mine.after), custom_call_target="tpu_custom_call" | custom-call | flops 6000000000 | bytes 2015264 | tf_op jit(solution)/shard_map/register_columns/pallas_call | solution.py:49
  22.3 0.3 collective-permute-done.3.theirs
  22.6 0.6 planes.1.after.blurred
  23.3 0.9 register.1.seen
  24.2 0.7 ratio.2
  24.9 0.7 collective-permute-start.7
  25.6 1.3 %collective-permute-done.7.other = f32[24,32,128]{2,1,0:T(8,128)S(1)} collective-permute-done((f32[24,32,128]{2,1,0:T(8,128)S(1)}, f32[24,32,128]{2,1,0:T(8,128)S(1)}, u32[]{:S(2)}, u32[]{:S(2)}) %collective-permute-start.7) | collective-permute-done | bytes 393248 | tf_op jit(solution)/shard_map/ppermute | solution.py:484
  27.0 1.0 mirror_rims.2
  28.0 4.4 %collective-permute-start.8 = (f32[27,16,128]{2,1,0:T(8,128)S(1)}, f32[27,16,128]{2,1,0:T(8,128)S(1)}, u32[]{:S(2)}, u32[]{:S(2)}) collective-permute-start(f32[27,16,128]{2,1,0:T(8,128)S(1)} %get-tuple-element.73), channel_id=1, source_target_pairs={{1,2},{3,4},{5,6},{7,8},{9,10},{11,12},{13,14},{15,16},{17,18},{19... | collective-permute-start | bytes 663560 | tf_op jit(solution)/shard_map/ppermute | solution.py:491
  32.4 0.1 collective-permute-start.9
  32.5 0.6 mirror.2
  33.1 3.5 %norm.1 = (f32[24,32,128]{2,1,0:T(8,128)S(1)}, f32[6,16,128]{2,1,0:T(8,128)S(1)}) custom-call(f32[372]{0:T(512)S(1)} %reshape.7.psf, s32[4,2]{1,0:T(4,128)S(1)} %copy.16.offsets, bf16[2,768,256]{2,1,0:T(8,128)(2,1)S(1)} %get-tuple-element.69.y_h.after), custom_call_target="tpu_custom_call" | custom-call | bytes 1230320 | tf_op jit(solution)/shard_map/norm/pallas_call | solution.py:49
  36.6 3.3 %collective-permute-done.8.from_odd = f32[27,16,128]{2,1,0:T(8,128)S(1)} collective-permute-done((f32[27,16,128]{2,1,0:T(8,128)S(1)}, f32[27,16,128]{2,1,0:T(8,128)S(1)}, u32[]{:S(2)}, u32[]{:S(2)}) %collective-permute-start.8) | collective-permute-done | bytes 221216 | tf_op jit(solution)/shard_map/ppermute | solution.py:491
  39.8 0.2 gather.2
  40.0 0.1 collective-permute-start.10
  40.2 1.4 %collective-permute-start.12 = (f32[12,32,128]{2,1,0:T(8,128)S(1)}, f32[12,32,128]{2,1,0:T(8,128)S(1)}, u32[]{:S(2)}, u32[]{:S(2)}) collective-permute-start(f32[12,32,128]{2,1,0:T(8,128)S(1)} %get-tuple-element.77.low), channel_id=1, source_target_pairs={{0,128},{64,192},{128,0},{192,64},{1,129},{65,193},{129,1},{193,65... | collective-permute-start | bytes 589832 | tf_op jit(solution)/shard_map/ppermute | solution.py:484
  41.6 0.1 collective-permute-start.13
  41.7 1.9 %collective-permute-done.10.theirs = f32[12,16,128]{2,1,0:T(8,128)S(1)} collective-permute-done((f32[12,16,128]{2,1,0:T(8,128)S(1)}, f32[12,16,128]{2,1,0:T(8,128)S(1)}, u32[]{:S(2)}, u32[]{:S(2)}) %collective-permute-start.10) | collective-permute-done | bytes 98336 | tf_op jit(solution)/shard_map/ppermute | solution.py:484
  43.6 2.5 %collective-permute-start.11 = (f32[12,16,128]{2,1,0:T(8,128)S(1)}, f32[12,16,128]{2,1,0:T(8,128)S(1)}, u32[]{:S(2)}, u32[]{:S(2)}) collective-permute-start(f32[12,16,128]{2,1,0:T(8,128)S(1)} %join.2.joined), channel_id=1, source_target_pairs={{0,160},{32,128},{64,224},{96,192},{128,32},{160,0},{192,96},{224,... | collective-permute-start | bytes 294920 | tf_op jit(solution)/shard_map/ppermute | solution.py:484
  46.1 1.4 %collective-permute-done.12.p_low = f32[12,32,128]{2,1,0:T(8,128)S(1)} collective-permute-done((f32[12,32,128]{2,1,0:T(8,128)S(1)}, f32[12,32,128]{2,1,0:T(8,128)S(1)}, u32[]{:S(2)}, u32[]{:S(2)}) %collective-permute-start.12) | collective-permute-done | bytes 196640 | tf_op jit(solution)/shard_map/ppermute | solution.py:484
  47.4 4.2 %collective-permute-done.13.p_high = f32[12,32,128]{2,1,0:T(8,128)S(1)} collective-permute-done((f32[12,32,128]{2,1,0:T(8,128)S(1)}, f32[12,32,128]{2,1,0:T(8,128)S(1)}, u32[]{:S(2)}, u32[]{:S(2)}) %collective-permute-start.13) | collective-permute-done | bytes 196640 | tf_op jit(solution)/shard_map/ppermute | solution.py:484
  51.7 0.2 update.1
  51.9 4.4 %collective-permute-start.14 = (f32[27,16,128]{2,1,0:T(8,128)S(1)}, f32[27,16,128]{2,1,0:T(8,128)S(1)}, u32[]{:S(2)}, u32[]{:S(2)}) collective-permute-start(f32[27,16,128]{2,1,0:T(8,128)S(1)} %get-tuple-element.80), channel_id=1, source_target_pairs={{1,2},{3,4},{5,6},{7,8},{9,10},{11,12},{13,14},{15,16},{17,18},{19... | collective-permute-start | bytes 663560 | tf_op jit(solution)/shard_map/ppermute | solution.py:491
  56.3 0.1 collective-permute-start.15
  56.4 1.1 %inner.3 = (f32[24,32,128]{2,1,0:T(8,128)S(1)}, f32[24,32,128]{2,1,0:T(8,128)S(1)}) custom-call(f32[24,32,128]{2,1,0:T(8,128)S(1)} %get-tuple-element.82.cur, f32[6,16,128]{2,1,0:T(8,128)S(1)} %get-tuple-element.83.ext, bf16[10,256,256]{2,1,0:T(8,128)(2,1)S(1)} %get-tuple-element.58.mats), custom_call_target="tpu_custom_call" | custom-call | flops 6000000000 | bytes 2539520 | tf_op jit(solution)/shard_map/inner/pallas_call | solution.py:49
  57.4 4.4 %collective-permute-done.14.from_odd = f32[27,16,128]{2,1,0:T(8,128)S(1)} collective-permute-done((f32[27,16,128]{2,1,0:T(8,128)S(1)}, f32[27,16,128]{2,1,0:T(8,128)S(1)}, u32[]{:S(2)}, u32[]{:S(2)}) %collective-permute-start.14) | collective-permute-done | bytes 221216 | tf_op jit(solution)/shard_map/ppermute | solution.py:491
  61.9 1.1 %outer.3 = (f32[24,32,128]{2,1,0:T(8,128)S(1)}, f32[24,32,128]{2,1,0:T(8,128)S(1)}) custom-call(f32[27,16,128]{2,1,0:T(8,128)S(1)} %collective-permute-done.14.from_odd, f32[27,16,128]{2,1,0:T(8,128)S(1)} %collective-permute-done.15.from_even, bf16[10,256,256]{2,1,0:T(8,128)(2,1)S(1)} %get-tuple-element.58.mats, ...), custom_call_target="tpu_custom_call" | custom-call | flops 6000000000 | bytes 3325952 | tf_op jit(solution)/shard_map/outer/pallas_call | solution.py:49
  62.9 3.4 %collective-permute-start.16 = (f32[24,32,128]{2,1,0:T(8,128)S(1)}, f32[24,32,128]{2,1,0:T(8,128)S(1)}, u32[]{:S(2)}, u32[]{:S(2)}) collective-permute-start(f32[24,32,128]{2,1,0:T(8,128)S(1)} %get-tuple-element.87), channel_id=1, source_target_pairs={{0,64},{64,0},{128,192},{192,128},{1,65},{65,1},{129,193},{193,129... | collective-permute-start | bytes 1179656 | tf_op jit(solution)/shard_map/ppermute | solution.py:484
  66.3 1.3 %collective-permute-done.16.theirs = f32[24,32,128]{2,1,0:T(8,128)S(1)} collective-permute-done((f32[24,32,128]{2,1,0:T(8,128)S(1)}, f32[24,32,128]{2,1,0:T(8,128)S(1)}, u32[]{:S(2)}, u32[]{:S(2)}) %collective-permute-start.16) | collective-permute-done | bytes 393248 | tf_op jit(solution)/shard_map/ppermute | solution.py:484
  67.6 1.4 %ratio.3 = (f32[24,32,128]{2,1,0:T(8,128)S(1)}, f32[24,32,128]{2,1,0:T(8,128)S(1)}) custom-call(f32[24,32,128]{2,1,0:T(8,128)S(1)} %get-tuple-element.86.mine, f32[24,32,128]{2,1,0:T(8,128)S(1)} %collective-permute-done.16.theirs, f32[48,32,128]{2,1,0:T(8,128)S(1)} %register.1.seen, bf16[2,768,384]{2,1,0:T(8,128)(2,1)S(1)} %get-tuple-element.64.kz), custom_call_target="tpu_custom_call" | custom-call | flops 905969664 | bytes 3538944 | tf_op jit(solution)/shard_map/ratio/pallas_call | solution.py:49
  69.1 0.5 collective-permute-start.17
  69.6 1.3 %collective-permute-done.17.other = f32[24,32,128]{2,1,0:T(8,128)S(1)} collective-permute-done((f32[24,32,128]{2,1,0:T(8,128)S(1)}, f32[24,32,128]{2,1,0:T(8,128)S(1)}, u32[]{:S(2)}, u32[]{:S(2)}) %collective-permute-start.17) | collective-permute-done | bytes 393248 | tf_op jit(solution)/shard_map/ppermute | solution.py:484
  70.9 1.0 mirror_rims.3
  71.9 4.4 %collective-permute-start.18 = (f32[27,16,128]{2,1,0:T(8,128)S(1)}, f32[27,16,128]{2,1,0:T(8,128)S(1)}, u32[]{:S(2)}, u32[]{:S(2)}) collective-permute-start(f32[27,16,128]{2,1,0:T(8,128)S(1)} %get-tuple-element.94), channel_id=1, source_target_pairs={{1,2},{3,4},{5,6},{7,8},{9,10},{11,12},{13,14},{15,16},{17,18},{19... | collective-permute-start | bytes 663560 | tf_op jit(solution)/shard_map/ppermute | solution.py:491
  76.3 0.1 collective-permute-start.19
  76.4 0.6 mirror.3
  77.0 6.7 %collective-permute-done.18.from_odd = f32[27,16,128]{2,1,0:T(8,128)S(1)} collective-permute-done((f32[27,16,128]{2,1,0:T(8,128)S(1)}, f32[27,16,128]{2,1,0:T(8,128)S(1)}, u32[]{:S(2)}, u32[]{:S(2)}) %collective-permute-start.18) | collective-permute-done | bytes 221216 | tf_op jit(solution)/shard_map/ppermute | solution.py:491
  83.8 0.7 collective-permute-start.20
  84.5 0.8 collective-permute-start.22
  85.4 0.6 collective-permute-start.23
  86.0 0.8 collective-permute-done.20.theirs
  86.8 2.3 %collective-permute-start.21 = (f32[6,16,128]{2,1,0:T(8,128)S(1)}, f32[6,16,128]{2,1,0:T(8,128)S(1)}, u32[]{:S(2)}, u32[]{:S(2)}) collective-permute-start(f32[6,16,128]{2,1,0:T(8,128)S(1)} %join.3), channel_id=1, source_target_pairs={{0,160},{32,128},{64,224},{96,192},{128,32},{160,0},{192,96},{224,... | collective-permute-start | bytes 147464 | tf_op jit(solution)/shard_map/ppermute | solution.py:484
  89.1 2.0 %collective-permute-done.21.side = f32[6,16,128]{2,1,0:T(8,128)S(1)} collective-permute-done((f32[6,16,128]{2,1,0:T(8,128)S(1)}, f32[6,16,128]{2,1,0:T(8,128)S(1)}, u32[]{:S(2)}, u32[]{:S(2)}) %collective-permute-start.21) | collective-permute-done | bytes 49184 | tf_op jit(solution)/shard_map/ppermute | solution.py:484
  91.1 3.6 %collective-permute-done.23.p_high = f32[12,32,128]{2,1,0:T(8,128)S(1)} collective-permute-done((f32[12,32,128]{2,1,0:T(8,128)S(1)}, f32[12,32,128]{2,1,0:T(8,128)S(1)}, u32[]{:S(2)}, u32[]{:S(2)}) %collective-permute-start.23) | collective-permute-done | bytes 196640 | tf_op jit(solution)/shard_map/ppermute | solution.py:484
  94.6 0.2 last.1.mine
  94.8 2.0 %collective-permute-start.24 = (f32[24,32,128]{2,1,0:T(8,128)S(1)}, f32[24,32,128]{2,1,0:T(8,128)S(1)}, u32[]{:S(2)}, u32[]{:S(2)}) collective-permute-start(f32[24,32,128]{2,1,0:T(8,128)S(1)} %last.1.mine), channel_id=1, source_target_pairs={{0,64},{64,0},{128,192},{192,128},{1,65},{65,1},{129,193},{193,129... | collective-permute-start | bytes 1179656 | tf_op jit(solution)/shard_map/ppermute | solution.py:484
  96.9 0.8 near_half.1.near
  97.6 0.6 collective-permute-done.24.theirs
  98.2 0.8 far_half.1
  (33 shorter events, 0.4 us)
Async XLA Ops:
  0.0 1.1 %copy-start = (f32[48,32,128]{2,1,0:T(8,128)S(1)}, f32[48,32,128]{2,1,0:T(8,128)}, u32[]{:S(2)}) copy-start(f32[48,32,128]{2,1,0:T(8,128)} %est.3) | copy-start | bytes 2359300
  1.3 4.9 %collective-permute-start = (f32[6,16,128]{2,1,0:T(8,128)S(1)}, f32[6,16,128]{2,1,0:T(8,128)S(1)}, u32[]{:S(2)}, u32[]{:S(2)}) collective-permute-start(f32[6,16,128]{2,1,0:T(8,128)S(1)} %begin.1), channel_id=1, source_target_pairs={{0,160},{32,128},{64,224},{96,192},{128,32},{160,0},{192,96},{224,... | collective-permute-start | bytes 147464 | tf_op jit(solution)/shard_map/ppermute | solution.py:484
  3.9 1.1 %copy-start.2 = (f32[1,48,32,128]{3,2,1,0:T(8,128)S(1)}, f32[1,48,32,128]{3,2,1,0:T(8,128)}, u32[]{:S(2)}) copy-start(f32[1,48,32,128]{3,2,1,0:T(8,128)} %param.5) | copy-start | bytes 2359300
  5.0 1.1 %copy-start.1 = (f32[48,32,128]{2,1,0:T(8,128)S(1)}, f32[48,32,128]{2,1,0:T(8,128)}, u32[]{:S(2)}) copy-start(f32[48,32,128]{2,1,0:T(8,128)} %est.3) | copy-start | bytes 2359300
  5.0 1.2 %copy-start.5 = (f32[4,3,31]{2,0,1:T(4,128)S(1)}, f32[4,3,31]{2,0,1:T(4,128)}, u32[]{:S(2)}) copy-start(f32[4,3,31]{2,0,1:T(4,128)} %param.6) | copy-start | bytes 4468
  5.3 5.5 %copy-start.6 = (s32[4,2]{0,1:T(2,128)S(1)}, s32[4,2]{0,1:T(2,128)}, u32[]{:S(2)}) copy-start(s32[4,2]{0,1:T(2,128)} %param.7) | copy-start | bytes 100
  5.3 5.6 %copy-start.3 = (f32[1,48,32,128]{3,2,1,0:T(8,128)S(1)}, f32[1,48,32,128]{3,2,1,0:T(8,128)}, u32[]{:S(2)}) copy-start(f32[1,48,32,128]{3,2,1,0:T(8,128)} %param.5) | copy-start | bytes 2359300
  5.3 10.3 %copy-start.4 = (bf16[32,2048]{1,0:T(8,128)(2,1)S(1)}, bf16[32,2048]{1,0:T(8,128)(2,1)}, u32[]{:S(2)}) copy-start(bf16[32,2048]{1,0:T(8,128)(2,1)} %constant.5.clone.place) | copy-start | bytes 393220
  5.3 5.6 %collective-permute-start.4 = (f32[12,8,128]{2,1,0:T(8,128)S(1)}, f32[12,8,128]{2,1,0:T(8,128)S(1)}, u32[]{:S(2)}, u32[]{:S(2)}) collective-permute-start(f32[12,8,128]{2,1,0:T(8,128)S(1)} %raw_sides.1), channel_id=1, source_target_pairs={{0,32},{32,0},{1,33},{33,1},{2,34},{34,2},{3,35},{35,3},{4,36},{36... | collective-permute-start | bytes 147464 | tf_op jit(solution)/shard_map/ppermute | solution.py:484
  6.4 11.7 %collective-permute-start.1 = (f32[27,16,128]{2,1,0:T(8,128)S(1)}, f32[27,16,128]{2,1,0:T(8,128)S(1)}, u32[]{:S(2)}, u32[]{:S(2)}) collective-permute-start(f32[27,16,128]{2,1,0:T(8,128)S(1)} %get-tuple-element.54), channel_id=1, source_target_pairs={{1,2},{3,4},{5,6},{7,8},{9,10},{11,12},{13,14},{15,16},{17,18},{19... | collective-permute-start | bytes 663560 | tf_op jit(solution)/shard_map/ppermute | solution.py:491
  10.9 7.2 %collective-permute-start.2 = (f32[27,16,128]{2,1,0:T(8,128)S(1)}, f32[27,16,128]{2,1,0:T(8,128)S(1)}, u32[]{:S(2)}, u32[]{:S(2)}) collective-permute-start(f32[27,16,128]{2,1,0:T(8,128)S(1)} %get-tuple-element.55), channel_id=1, source_target_pairs={{0,1},{1,0},{2,3},{3,2},{4,5},{5,4},{6,7},{7,6},{8,9},{9,8},{10,11... | collective-permute-start | bytes 663560 | tf_op jit(solution)/shard_map/ppermute | solution.py:492
  11.0 12.2 %collective-permute-start.5 = (f32[51,8,128]{2,1,0:T(8,128)S(1)}, f32[51,8,128]{2,1,0:T(8,128)S(1)}, u32[]{:S(2)}, u32[]{:S(2)}) collective-permute-start(f32[51,8,128]{2,1,0:T(8,128)S(1)} %get-tuple-element.65), channel_id=1, source_target_pairs={{1,2},{3,4},{5,6},{7,8},{9,10},{11,12},{13,14},{15,16},{17,18},{19... | collective-permute-start | bytes 626696 | tf_op jit(solution)/shard_map/ppermute | solution.py:491
  15.5 7.8 %collective-permute-start.6 = (f32[51,8,128]{2,1,0:T(8,128)S(1)}, f32[51,8,128]{2,1,0:T(8,128)S(1)}, u32[]{:S(2)}, u32[]{:S(2)}) collective-permute-start(f32[51,8,128]{2,1,0:T(8,128)S(1)} %get-tuple-element.66), channel_id=1, source_target_pairs={{0,1},{1,0},{2,3},{3,2},{4,5},{5,4},{6,7},{7,6},{8,9},{9,8},{10,11... | collective-permute-start | bytes 626696 | tf_op jit(solution)/shard_map/ppermute | solution.py:492
  19.2 3.4 %collective-permute-start.3 = (f32[24,32,128]{2,1,0:T(8,128)S(1)}, f32[24,32,128]{2,1,0:T(8,128)S(1)}, u32[]{:S(2)}, u32[]{:S(2)}) collective-permute-start(f32[24,32,128]{2,1,0:T(8,128)S(1)} %get-tuple-element.63), channel_id=1, source_target_pairs={{0,64},{64,0},{128,192},{192,128},{1,65},{65,1},{129,193},{193,129... | collective-permute-start | bytes 1179656 | tf_op jit(solution)/shard_map/ppermute | solution.py:484
  24.9 2.1 %collective-permute-start.7 = (f32[24,32,128]{2,1,0:T(8,128)S(1)}, f32[24,32,128]{2,1,0:T(8,128)S(1)}, u32[]{:S(2)}, u32[]{:S(2)}) collective-permute-start(f32[24,32,128]{2,1,0:T(8,128)S(1)} %get-tuple-element.68), channel_id=1, source_target_pairs={{0,64},{64,0},{128,192},{192,128},{1,65},{65,1},{129,193},{193,129... | collective-permute-start | bytes 1179656 | tf_op jit(solution)/shard_map/ppermute | solution.py:484
  28.0 11.9 %collective-permute-start.8 = (f32[27,16,128]{2,1,0:T(8,128)S(1)}, f32[27,16,128]{2,1,0:T(8,128)S(1)}, u32[]{:S(2)}, u32[]{:S(2)}) collective-permute-start(f32[27,16,128]{2,1,0:T(8,128)S(1)} %get-tuple-element.73), channel_id=1, source_target_pairs={{1,2},{3,4},{5,6},{7,8},{9,10},{11,12},{13,14},{15,16},{17,18},{19... | collective-permute-start | bytes 663560 | tf_op jit(solution)/shard_map/ppermute | solution.py:491
  32.4 7.4 %collective-permute-start.9 = (f32[27,16,128]{2,1,0:T(8,128)S(1)}, f32[27,16,128]{2,1,0:T(8,128)S(1)}, u32[]{:S(2)}, u32[]{:S(2)}) collective-permute-start(f32[27,16,128]{2,1,0:T(8,128)S(1)} %get-tuple-element.74), channel_id=1, source_target_pairs={{0,1},{1,0},{2,3},{3,2},{4,5},{5,4},{6,7},{7,6},{8,9},{9,8},{10,11... | collective-permute-start | bytes 663560 | tf_op jit(solution)/shard_map/ppermute | solution.py:492
  40.0 3.6 %collective-permute-start.10 = (f32[12,16,128]{2,1,0:T(8,128)S(1)}, f32[12,16,128]{2,1,0:T(8,128)S(1)}, u32[]{:S(2)}, u32[]{:S(2)}) collective-permute-start(f32[12,16,128]{2,1,0:T(8,128)S(1)} %get-tuple-element.76.mine), channel_id=1, source_target_pairs={{0,128},{64,192},{128,0},{192,64},{1,129},{65,193},{129,1},{193,65... | collective-permute-start | bytes 294920 | tf_op jit(solution)/shard_map/ppermute | solution.py:484
  40.2 7.3 %collective-permute-start.12 = (f32[12,32,128]{2,1,0:T(8,128)S(1)}, f32[12,32,128]{2,1,0:T(8,128)S(1)}, u32[]{:S(2)}, u32[]{:S(2)}) collective-permute-start(f32[12,32,128]{2,1,0:T(8,128)S(1)} %get-tuple-element.77.low), channel_id=1, source_target_pairs={{0,128},{64,192},{128,0},{192,64},{1,129},{65,193},{129,1},{193,65... | collective-permute-start | bytes 589832 | tf_op jit(solution)/shard_map/ppermute | solution.py:484
  41.6 10.1 %collective-permute-start.13 = (f32[12,32,128]{2,1,0:T(8,128)S(1)}, f32[12,32,128]{2,1,0:T(8,128)S(1)}, u32[]{:S(2)}, u32[]{:S(2)}) collective-permute-start(f32[12,32,128]{2,1,0:T(8,128)S(1)} %get-tuple-element.78.high), channel_id=1, source_target_pairs={{0,128},{64,192},{128,0},{192,64},{1,129},{65,193},{129,1},{193,65... | collective-permute-start | bytes 589832 | tf_op jit(solution)/shard_map/ppermute | solution.py:484
  43.6 8.0 %collective-permute-start.11 = (f32[12,16,128]{2,1,0:T(8,128)S(1)}, f32[12,16,128]{2,1,0:T(8,128)S(1)}, u32[]{:S(2)}, u32[]{:S(2)}) collective-permute-start(f32[12,16,128]{2,1,0:T(8,128)S(1)} %join.2.joined), channel_id=1, source_target_pairs={{0,160},{32,128},{64,224},{96,192},{128,32},{160,0},{192,96},{224,... | collective-permute-start | bytes 294920 | tf_op jit(solution)/shard_map/ppermute | solution.py:484
  51.9 10.0 %collective-permute-start.14 = (f32[27,16,128]{2,1,0:T(8,128)S(1)}, f32[27,16,128]{2,1,0:T(8,128)S(1)}, u32[]{:S(2)}, u32[]{:S(2)}) collective-permute-start(f32[27,16,128]{2,1,0:T(8,128)S(1)} %get-tuple-element.80), channel_id=1, source_target_pairs={{1,2},{3,4},{5,6},{7,8},{9,10},{11,12},{13,14},{15,16},{17,18},{19... | collective-permute-start | bytes 663560 | tf_op jit(solution)/shard_map/ppermute | solution.py:491
  56.3 5.6 %collective-permute-start.15 = (f32[27,16,128]{2,1,0:T(8,128)S(1)}, f32[27,16,128]{2,1,0:T(8,128)S(1)}, u32[]{:S(2)}, u32[]{:S(2)}) collective-permute-start(f32[27,16,128]{2,1,0:T(8,128)S(1)} %get-tuple-element.81), channel_id=1, source_target_pairs={{0,1},{1,0},{2,3},{3,2},{4,5},{5,4},{6,7},{7,6},{8,9},{9,8},{10,11... | collective-permute-start | bytes 663560 | tf_op jit(solution)/shard_map/ppermute | solution.py:492
  62.9 4.7 %collective-permute-start.16 = (f32[24,32,128]{2,1,0:T(8,128)S(1)}, f32[24,32,128]{2,1,0:T(8,128)S(1)}, u32[]{:S(2)}, u32[]{:S(2)}) collective-permute-start(f32[24,32,128]{2,1,0:T(8,128)S(1)} %get-tuple-element.87), channel_id=1, source_target_pairs={{0,64},{64,0},{128,192},{192,128},{1,65},{65,1},{129,193},{193,129... | collective-permute-start | bytes 1179656 | tf_op jit(solution)/shard_map/ppermute | solution.py:484
  69.1 1.8 %collective-permute-start.17 = (f32[24,32,128]{2,1,0:T(8,128)S(1)}, f32[24,32,128]{2,1,0:T(8,128)S(1)}, u32[]{:S(2)}, u32[]{:S(2)}) collective-permute-start(f32[24,32,128]{2,1,0:T(8,128)S(1)} %get-tuple-element.89), channel_id=1, source_target_pairs={{0,64},{64,0},{128,192},{192,128},{1,65},{65,1},{129,193},{193,129... | collective-permute-start | bytes 1179656 | tf_op jit(solution)/shard_map/ppermute | solution.py:484
  71.9 11.9 %collective-permute-start.18 = (f32[27,16,128]{2,1,0:T(8,128)S(1)}, f32[27,16,128]{2,1,0:T(8,128)S(1)}, u32[]{:S(2)}, u32[]{:S(2)}) collective-permute-start(f32[27,16,128]{2,1,0:T(8,128)S(1)} %get-tuple-element.94), channel_id=1, source_target_pairs={{1,2},{3,4},{5,6},{7,8},{9,10},{11,12},{13,14},{15,16},{17,18},{19... | collective-permute-start | bytes 663560 | tf_op jit(solution)/shard_map/ppermute | solution.py:491
  76.3 7.4 %collective-permute-start.19 = (f32[27,16,128]{2,1,0:T(8,128)S(1)}, f32[27,16,128]{2,1,0:T(8,128)S(1)}, u32[]{:S(2)}, u32[]{:S(2)}) collective-permute-start(f32[27,16,128]{2,1,0:T(8,128)S(1)} %get-tuple-element.95), channel_id=1, source_target_pairs={{0,1},{1,0},{2,3},{3,2},{4,5},{5,4},{6,7},{7,6},{8,9},{9,8},{10,11... | collective-permute-start | bytes 663560 | tf_op jit(solution)/shard_map/ppermute | solution.py:492
  83.8 3.0 %collective-permute-start.20 = (f32[6,16,128]{2,1,0:T(8,128)S(1)}, f32[6,16,128]{2,1,0:T(8,128)S(1)}, u32[]{:S(2)}, u32[]{:S(2)}) collective-permute-start(f32[6,16,128]{2,1,0:T(8,128)S(1)} %get-tuple-element.96.mine), channel_id=1, source_target_pairs={{0,128},{64,192},{128,0},{192,64},{1,129},{65,193},{129,1},{193,65... | collective-permute-start | bytes 147464 | tf_op jit(solution)/shard_map/ppermute | solution.py:484
  84.5 6.5 %collective-permute-start.22 = (f32[12,32,128]{2,1,0:T(8,128)S(1)}, f32[12,32,128]{2,1,0:T(8,128)S(1)}, u32[]{:S(2)}, u32[]{:S(2)}) collective-permute-start(f32[12,32,128]{2,1,0:T(8,128)S(1)} %get-tuple-element.97.low), channel_id=1, source_target_pairs={{0,128},{64,192},{128,0},{192,64},{1,129},{65,193},{129,1},{193,65... | collective-permute-start | bytes 589832 | tf_op jit(solution)/shard_map/ppermute | solution.py:484
  85.4 9.3 %collective-permute-start.23 = (f32[12,32,128]{2,1,0:T(8,128)S(1)}, f32[12,32,128]{2,1,0:T(8,128)S(1)}, u32[]{:S(2)}, u32[]{:S(2)}) collective-permute-start(f32[12,32,128]{2,1,0:T(8,128)S(1)} %get-tuple-element.98.high), channel_id=1, source_target_pairs={{0,128},{64,192},{128,0},{192,64},{1,129},{65,193},{129,1},{193,65... | collective-permute-start | bytes 589832 | tf_op jit(solution)/shard_map/ppermute | solution.py:484
  86.8 4.2 %collective-permute-start.21 = (f32[6,16,128]{2,1,0:T(8,128)S(1)}, f32[6,16,128]{2,1,0:T(8,128)S(1)}, u32[]{:S(2)}, u32[]{:S(2)}) collective-permute-start(f32[6,16,128]{2,1,0:T(8,128)S(1)} %join.3), channel_id=1, source_target_pairs={{0,160},{32,128},{64,224},{96,192},{128,32},{160,0},{192,96},{224,... | collective-permute-start | bytes 147464 | tf_op jit(solution)/shard_map/ppermute | solution.py:484
  94.8 3.4 %collective-permute-start.24 = (f32[24,32,128]{2,1,0:T(8,128)S(1)}, f32[24,32,128]{2,1,0:T(8,128)S(1)}, u32[]{:S(2)}, u32[]{:S(2)}) collective-permute-start(f32[24,32,128]{2,1,0:T(8,128)S(1)} %last.1.mine), channel_id=1, source_target_pairs={{0,64},{64,0},{128,192},{192,128},{1,65},{65,1},{129,193},{193,129... | collective-permute-start | bytes 1179656 | tf_op jit(solution)/shard_map/ppermute | solution.py:484

commit v8 on v7

--- a/solution.py
+++ b/solution.py
@@ -214,17 +214,26 @@
         out[first + t] = cols[:, 128 * t : 128 * t + 128]
 
 
-def begin_body(est, pack_out, turned):
+def begin_body(est, raw, pack_out, raw_pack, cur, raw_here, turned, sems):
     tx = lax.axis_index("tx")
-    half = pl.ds(24 * mesh_core(), 24)
+    first = 24 * mesh_core()
+    copies = []
+    for i in range(2):
+        z = slice(12 * i, 12 * i + 12)
+        copies.append(pltpu.make_async_copy(est.at[pl.ds(first + 12 * i, 12)], cur.at[z], sems.at[i]))
+    for i in range(4):
+        z = slice(12 * i, 12 * i + 12)
+        copies.append(pltpu.make_async_copy(raw.at[z], raw_here.at[z], sems.at[2 + i]))
+    for copy in copies:
+        copy.start()
+    for copy in copies[:2]:
+        copy.wait()
     for xh in range(2):
-        put_packs(est[half, 16 * xh : 16 * xh + 16, :], 112 * (1 - tx), 16, turned, pack_out, 3 * xh)
-
-
-def raw_sides_body(raw, pack_out, turned):
-    tx = lax.axis_index("tx")
+        put_packs(cur[:, 16 * xh : 16 * xh + 16, :], 112 * (1 - tx), 16, turned, pack_out, 3 * xh)
+    for copy in copies[2:]:
+        copy.wait()
     for xb in range(4):
-        put_packs(raw[:, 8 * xb : 8 * xb + 8, :], 120 * (1 - tx), 8, turned, pack_out, 3 * xb)
+        put_packs(raw_here[:, 8 * xb : 8 * xb + 8, :], 120 * (1 - tx), 8, turned, raw_pack, 3 * xb)
 
 
 def put_rims(top, bottom, even_out, odd_out, planes):
@@ -505,9 +514,16 @@
     turned = pltpu.VMEM((128, 384), F32)
     two_sems = pltpu.SemaphoreType.DMA((2,))
 
-    (ext,) = call(begin_body, [pack], [estimate], [turned], name="begin")
+    ext, sides = call(
+        begin_body,
+        [pack, ((12, OMAX, 128), F32)],
+        [estimate, raw],
+        [pltpu.VMEM((half, tile_x, tile_y), F32), pltpu.VMEM(raw.shape, F32), turned, pltpu.SemaphoreType.DMA((6,))],
+        name="begin",
+        hbm=(0, 1),
+        limit=62,
+    )
     ext = swap(ext, ("view", "tx"), 5, (4, 2))
-    (sides,) = call(raw_sides_body, [((12, OMAX, 128), F32)], [raw], [turned], flops=BUSY, name="raw_sides")
     sides = swap(sides, "tx", 1, (2,))
     cur, odd, even = call(rims_body, [tile_half, rim, rim], [estimate], name="rims")
 

time: 99.6 us -> 101 us (1.014)
  local copies, waits for them, and re-layouts: 2.7 us -> 0.22 us
  Pallas kernels: 19.8 us -> 21.7 us
  starting transfers between devices: 42.9 us -> 44.3 us
    unnamed x14 -> x10, local copies, waits for them, and re-layouts: 2.5 us -> 0.02 us
    pallas_call x28 -> x27, Pallas kernels: 19.8 us -> 21.7 us  [call(): pl.pallas_call(body, out_shape=outs, in_specs=specs, out_specs=[pl.BlockS...]
  transfers between devices with their start and end apart: 25 -> 25, of which waited for: 14 -> 15; matrix products, arithmetic and copies ran while one was open for 0% -> 0% of each run, Pallas kernels for 12% -> 12%
where the time goes in v8:
time: 101 us; the launch traced here: 100 us
  starting transfers between devices  44.3 us (44%)
  waiting for transfers between devices  33.5 us (33%)
  Pallas kernels  21.7 us (21%)
    ppermute x5, starting transfers between devices, rim_swap(): from_odd = lax.ppermute(odd, 'ty', odd_pairs)  22.6 us
    pallas_call x27, Pallas kernels, call(): pl.pallas_call(body, out_shape=outs, in_specs=specs, out_specs=[pl.BlockS...  21.7 us
    ppermute x15, starting transfers between devices, swap(): return lax.ppermute(value, axis, [(i, i ^ by) for i in range(count)])  21.3 us
    ppermute x15, waiting for transfers between devices, swap(): return lax.ppermute(value, axis, [(i, i ^ by) for i in range(count)])  19.5 us
    ppermute x5, waiting for transfers between devices, rim_swap(): from_odd = lax.ppermute(odd, 'ty', odd_pairs)  13.9 us
  transfers between devices with their start and end apart: 25, of which 15 were waited for; matrix products, arithmetic and copies ran while one was open for 0% of the time, Pallas kernels for 12%

profile of v8, /device:TPU:121, one launch (start us, length us, event | category | flops | bytes accessed | tf_op | source)
XLA Modules:
  0.0 100.2 jit_solution(7986447923278177170)
XLA Ops:
  0.0 2.4 %begin.1 = (f32[6,16,128]{2,1,0:T(8,128)}, f32[12,8,128]{2,1,0:T(8,128)}) custom-call(f32[48,32,128]{2,1,0:T(8,128)} %est.3, f32[48,32,128]{2,1,0:T(8,128)} %bitcast.1), custom_call_target="tpu_custom_call" | custom-call | bytes 1671168 | tf_op jit(solution)/shard_map/begin/pallas_call | solution.py:49
  2.4 2.6 %collective-permute-start = (f32[6,16,128]{2,1,0:T(8,128)}, f32[6,16,128]{2,1,0:T(8,128)S(1)}, u32[]{:S(2)}, u32[]{:S(2)}) collective-permute-start(f32[6,16,128]{2,1,0:T(8,128)} %get-tuple-element.54), channel_id=1, source_target_pairs={{0,160},{32,128},{64,224},{96,192},{128,32},{160,0},{192,96},{224,... | collective-permute-start | bytes 147464 | tf_op jit(solution)/shard_map/ppermute | solution.py:493
  5.0 0.5 collective-permute-start.4
  5.5 0.1 rims.1
  5.6 1.3 %collective-permute-done.pack.ext = f32[6,16,128]{2,1,0:T(8,128)S(1)} collective-permute-done((f32[6,16,128]{2,1,0:T(8,128)}, f32[6,16,128]{2,1,0:T(8,128)S(1)}, u32[]{:S(2)}, u32[]{:S(2)}) %collective-permute-start) | collective-permute-done | bytes 49184 | tf_op jit(solution)/shard_map/ppermute | solution.py:493
  6.9 0.1 reshape.7.psf
  7.0 4.4 %collective-permute-start.1 = (f32[27,16,128]{2,1,0:T(8,128)S(1)}, f32[27,16,128]{2,1,0:T(8,128)S(1)}, u32[]{:S(2)}, u32[]{:S(2)}) collective-permute-start(f32[27,16,128]{2,1,0:T(8,128)S(1)} %get-tuple-element.57), channel_id=1, source_target_pairs={{1,2},{3,4},{5,6},{7,8},{9,10},{11,12},{13,14},{15,16},{17,18},{19... | collective-permute-start | bytes 663560 | tf_op jit(solution)/shard_map/ppermute | solution.py:500
  11.5 0.1 copy.16.offsets
  11.7 4.5 %collective-permute-start.5 = (f32[51,8,128]{2,1,0:T(8,128)S(1)}, f32[51,8,128]{2,1,0:T(8,128)S(1)}, u32[]{:S(2)}, u32[]{:S(2)}) collective-permute-start(f32[51,8,128]{2,1,0:T(8,128)S(1)} %get-tuple-element.69), channel_id=1, source_target_pairs={{1,2},{3,4},{5,6},{7,8},{9,10},{11,12},{13,14},{15,16},{17,18},{19... | collective-permute-start | bytes 626696 | tf_op jit(solution)/shard_map/ppermute | solution.py:500
  16.1 0.1 collective-permute-start.6
  16.2 1.4 %bands.1 = (bf16[2,768,384]{2,1,0:T(8,128)(2,1)S(1)}, bf16[10,256,256]{2,1,0:T(8,128)(2,1)S(1)}) custom-call(f32[16,32]{1,0:T(8,128)S(1)} %pad.4.taps.after, bf16[32,2048]{1,0:T(8,128)(2,1)S(1)} %copy-done.2, f32[372]{0:T(512)S(1)} %reshape.7.psf, s32[4,2]{1,0:T(4,128)S(1)} %copy.16.offsets), custom_call_target="tpu_custom_call" | custom-call | flops 6000000000 | bytes 2625008 | tf_op jit(solution)/shard_map/bands/pallas_call | solution.py:49
  17.7 1.1 %inner.2 = (f32[24,32,128]{2,1,0:T(8,128)S(1)}, f32[24,32,128]{2,1,0:T(8,128)S(1)}) custom-call(f32[24,32,128]{2,1,0:T(8,128)S(1)} %get-tuple-element.62.cur, f32[6,16,128]{2,1,0:T(8,128)S(1)} %collective-permute-done.pack.ext, bf16[10,256,256]{2,1,0:T(8,128)(2,1)S(1)} %get-tuple-element.61.mats), custom_call_target="tpu_custom_call" | custom-call | flops 6000000000 | bytes 2539520 | tf_op jit(solution)/shard_map/inner/pallas_call | solution.py:49
  18.7 1.1 %outer.2 = (f32[24,32,128]{2,1,0:T(8,128)S(1)}, f32[24,32,128]{2,1,0:T(8,128)S(1)}) custom-call(f32[27,16,128]{2,1,0:T(8,128)S(1)} %collective-permute-done.1.from_odd, f32[27,16,128]{2,1,0:T(8,128)S(1)} %collective-permute-done.2.from_even, bf16[10,256,256]{2,1,0:T(8,128)(2,1)S(1)} %get-tuple-element.61.mats, f32[24,32,128]{2,1,0:T(8,128)S(1)} %get-tuple-element.63.in_own, ...), custom_call_target="tpu_custom_call" | custom-call | flops 6000000000 | bytes 3325952 | tf_op jit(solution)/shard_map/outer/pallas_call | solution.py:49
  19.8 2.8 %collective-permute-start.3 = (f32[24,32,128]{2,1,0:T(8,128)S(1)}, f32[24,32,128]{2,1,0:T(8,128)S(1)}, u32[]{:S(2)}, u32[]{:S(2)}) collective-permute-start(f32[24,32,128]{2,1,0:T(8,128)S(1)} %get-tuple-element.66), channel_id=1, source_target_pairs={{0,64},{64,0},{128,192},{192,128},{1,65},{65,1},{129,193},{193,129... | collective-permute-start | bytes 1179656 | tf_op jit(solution)/shard_map/ppermute | solution.py:493
  22.6 1.1 %register_columns.1.moved = f32[48,32,128]{2,1,0:T(8,128)S(1)} custom-call(s32[4,2]{1,0:T(4,128)S(1)} %copy.16.offsets, f32[48,32,128]{2,1,0:T(8,128)S(1)} %bitcast.3, f32[12,8,128]{2,1,0:T(8,128)S(1)} %collective-permute-done.4.pack, f32[24,32,128]{2,1,0:T(8,128)S(1)} %get-tuple-element.65.mine.after), custom_call_target="tpu_custom_call" | custom-call | flops 6000000000 | bytes 2015264 | tf_op jit(solution)/shard_map/register_columns/pallas_call | solution.py:49
  23.6 0.3 collective-permute-done.3.theirs
  23.9 0.6 planes.1.after.blurred
  24.6 0.9 register.1.seen
  25.5 0.7 ratio.2
  26.2 0.5 collective-permute-start.7
  26.7 1.3 %collective-permute-done.7.other = f32[24,32,128]{2,1,0:T(8,128)S(1)} collective-permute-done((f32[24,32,128]{2,1,0:T(8,128)S(1)}, f32[24,32,128]{2,1,0:T(8,128)S(1)}, u32[]{:S(2)}, u32[]{:S(2)}) %collective-permute-start.7) | collective-permute-done | bytes 393248 | tf_op jit(solution)/shard_map/ppermute | solution.py:493
  28.0 1.0 mirror_rims.2
  29.0 4.6 %collective-permute-start.8 = (f32[27,16,128]{2,1,0:T(8,128)S(1)}, f32[27,16,128]{2,1,0:T(8,128)S(1)}, u32[]{:S(2)}, u32[]{:S(2)}) collective-permute-start(f32[27,16,128]{2,1,0:T(8,128)S(1)} %get-tuple-element.77), channel_id=1, source_target_pairs={{1,2},{3,4},{5,6},{7,8},{9,10},{11,12},{13,14},{15,16},{17,18},{19... | collective-permute-start | bytes 663560 | tf_op jit(solution)/shard_map/ppermute | solution.py:500
  33.6 0.1 collective-permute-start.9
  33.7 0.6 mirror.2
  34.3 3.5 %norm.1 = (f32[24,32,128]{2,1,0:T(8,128)S(1)}, f32[6,16,128]{2,1,0:T(8,128)S(1)}) custom-call(f32[372]{0:T(512)S(1)} %reshape.7.psf, s32[4,2]{1,0:T(4,128)S(1)} %copy.16.offsets, bf16[2,768,256]{2,1,0:T(8,128)(2,1)S(1)} %get-tuple-element.73.y_h.after), custom_call_target="tpu_custom_call" | custom-call | bytes 1230320 | tf_op jit(solution)/shard_map/norm/pallas_call | solution.py:49
  37.8 3.1 %collective-permute-done.8.from_odd = f32[27,16,128]{2,1,0:T(8,128)S(1)} collective-permute-done((f32[27,16,128]{2,1,0:T(8,128)S(1)}, f32[27,16,128]{2,1,0:T(8,128)S(1)}, u32[]{:S(2)}, u32[]{:S(2)}) %collective-permute-start.8) | collective-permute-done | bytes 221216 | tf_op jit(solution)/shard_map/ppermute | solution.py:500
  40.9 0.2 gather.2
  41.1 0.1 collective-permute-start.10
  41.2 1.5 %collective-permute-start.12 = (f32[12,32,128]{2,1,0:T(8,128)S(1)}, f32[12,32,128]{2,1,0:T(8,128)S(1)}, u32[]{:S(2)}, u32[]{:S(2)}) collective-permute-start(f32[12,32,128]{2,1,0:T(8,128)S(1)} %get-tuple-element.81.low), channel_id=1, source_target_pairs={{0,128},{64,192},{128,0},{192,64},{1,129},{65,193},{129,1},{193,65... | collective-permute-start | bytes 589832 | tf_op jit(solution)/shard_map/ppermute | solution.py:493
  42.7 0.1 collective-permute-start.13
  42.8 1.9 %collective-permute-done.10.theirs = f32[12,16,128]{2,1,0:T(8,128)S(1)} collective-permute-done((f32[12,16,128]{2,1,0:T(8,128)S(1)}, f32[12,16,128]{2,1,0:T(8,128)S(1)}, u32[]{:S(2)}, u32[]{:S(2)}) %collective-permute-start.10) | collective-permute-done | bytes 98336 | tf_op jit(solution)/shard_map/ppermute | solution.py:493
  44.7 2.7 %collective-permute-start.11 = (f32[12,16,128]{2,1,0:T(8,128)S(1)}, f32[12,16,128]{2,1,0:T(8,128)S(1)}, u32[]{:S(2)}, u32[]{:S(2)}) collective-permute-start(f32[12,16,128]{2,1,0:T(8,128)S(1)} %join.2.joined), channel_id=1, source_target_pairs={{0,160},{32,128},{64,224},{96,192},{128,32},{160,0},{192,96},{224,... | collective-permute-start | bytes 294920 | tf_op jit(solution)/shard_map/ppermute | solution.py:493
  47.4 1.1 %collective-permute-done.12.p_low = f32[12,32,128]{2,1,0:T(8,128)S(1)} collective-permute-done((f32[12,32,128]{2,1,0:T(8,128)S(1)}, f32[12,32,128]{2,1,0:T(8,128)S(1)}, u32[]{:S(2)}, u32[]{:S(2)}) %collective-permute-start.12) | collective-permute-done | bytes 196640 | tf_op jit(solution)/shard_map/ppermute | solution.py:493
  48.5 4.2 %collective-permute-done.13.p_high = f32[12,32,128]{2,1,0:T(8,128)S(1)} collective-permute-done((f32[12,32,128]{2,1,0:T(8,128)S(1)}, f32[12,32,128]{2,1,0:T(8,128)S(1)}, u32[]{:S(2)}, u32[]{:S(2)}) %collective-permute-start.13) | collective-permute-done | bytes 196640 | tf_op jit(solution)/shard_map/ppermute | solution.py:493
  52.7 0.2 update.1
  52.9 4.6 %collective-permute-start.14 = (f32[27,16,128]{2,1,0:T(8,128)S(1)}, f32[27,16,128]{2,1,0:T(8,128)S(1)}, u32[]{:S(2)}, u32[]{:S(2)}) collective-permute-start(f32[27,16,128]{2,1,0:T(8,128)S(1)} %get-tuple-element.84), channel_id=1, source_target_pairs={{1,2},{3,4},{5,6},{7,8},{9,10},{11,12},{13,14},{15,16},{17,18},{19... | collective-permute-start | bytes 663560 | tf_op jit(solution)/shard_map/ppermute | solution.py:500
  57.5 0.1 collective-permute-start.15
  57.6 1.1 %inner.3 = (f32[24,32,128]{2,1,0:T(8,128)S(1)}, f32[24,32,128]{2,1,0:T(8,128)S(1)}) custom-call(f32[24,32,128]{2,1,0:T(8,128)S(1)} %get-tuple-element.86.cur, f32[6,16,128]{2,1,0:T(8,128)S(1)} %get-tuple-element.87.ext, bf16[10,256,256]{2,1,0:T(8,128)(2,1)S(1)} %get-tuple-element.61.mats), custom_call_target="tpu_custom_call" | custom-call | flops 6000000000 | bytes 2539520 | tf_op jit(solution)/shard_map/inner/pallas_call | solution.py:49
  58.7 4.2 %collective-permute-done.14.from_odd = f32[27,16,128]{2,1,0:T(8,128)S(1)} collective-permute-done((f32[27,16,128]{2,1,0:T(8,128)S(1)}, f32[27,16,128]{2,1,0:T(8,128)S(1)}, u32[]{:S(2)}, u32[]{:S(2)}) %collective-permute-start.14) | collective-permute-done | bytes 221216 | tf_op jit(solution)/shard_map/ppermute | solution.py:500
  62.9 1.1 %outer.3 = (f32[24,32,128]{2,1,0:T(8,128)S(1)}, f32[24,32,128]{2,1,0:T(8,128)S(1)}) custom-call(f32[27,16,128]{2,1,0:T(8,128)S(1)} %collective-permute-done.14.from_odd, f32[27,16,128]{2,1,0:T(8,128)S(1)} %collective-permute-done.15.from_even, bf16[10,256,256]{2,1,0:T(8,128)(2,1)S(1)} %get-tuple-element.61.mats, ...), custom_call_target="tpu_custom_call" | custom-call | flops 6000000000 | bytes 3325952 | tf_op jit(solution)/shard_map/outer/pallas_call | solution.py:49
  64.0 3.4 %collective-permute-start.16 = (f32[24,32,128]{2,1,0:T(8,128)S(1)}, f32[24,32,128]{2,1,0:T(8,128)S(1)}, u32[]{:S(2)}, u32[]{:S(2)}) collective-permute-start(f32[24,32,128]{2,1,0:T(8,128)S(1)} %get-tuple-element.91), channel_id=1, source_target_pairs={{0,64},{64,0},{128,192},{192,128},{1,65},{65,1},{129,193},{193,129... | collective-permute-start | bytes 1179656 | tf_op jit(solution)/shard_map/ppermute | solution.py:493
  67.3 1.3 %collective-permute-done.16.theirs = f32[24,32,128]{2,1,0:T(8,128)S(1)} collective-permute-done((f32[24,32,128]{2,1,0:T(8,128)S(1)}, f32[24,32,128]{2,1,0:T(8,128)S(1)}, u32[]{:S(2)}, u32[]{:S(2)}) %collective-permute-start.16) | collective-permute-done | bytes 393248 | tf_op jit(solution)/shard_map/ppermute | solution.py:493
  68.7 1.4 %ratio.3 = (f32[24,32,128]{2,1,0:T(8,128)S(1)}, f32[24,32,128]{2,1,0:T(8,128)S(1)}) custom-call(f32[24,32,128]{2,1,0:T(8,128)S(1)} %get-tuple-element.90.mine, f32[24,32,128]{2,1,0:T(8,128)S(1)} %collective-permute-done.16.theirs, f32[48,32,128]{2,1,0:T(8,128)S(1)} %register.1.seen, bf16[2,768,384]{2,1,0:T(8,128)(2,1)S(1)} %get-tuple-element.67.kz), custom_call_target="tpu_custom_call" | custom-call | flops 905969664 | bytes 3538944 | tf_op jit(solution)/shard_map/ratio/pallas_call | solution.py:49
  70.1 0.5 collective-permute-start.17
  70.6 1.4 %collective-permute-done.17.other = f32[24,32,128]{2,1,0:T(8,128)S(1)} collective-permute-done((f32[24,32,128]{2,1,0:T(8,128)S(1)}, f32[24,32,128]{2,1,0:T(8,128)S(1)}, u32[]{:S(2)}, u32[]{:S(2)}) %collective-permute-start.17) | collective-permute-done | bytes 393248 | tf_op jit(solution)/shard_map/ppermute | solution.py:493
  72.0 1.0 mirror_rims.3
  72.9 4.6 %collective-permute-start.18 = (f32[27,16,128]{2,1,0:T(8,128)S(1)}, f32[27,16,128]{2,1,0:T(8,128)S(1)}, u32[]{:S(2)}, u32[]{:S(2)}) collective-permute-start(f32[27,16,128]{2,1,0:T(8,128)S(1)} %get-tuple-element.98), channel_id=1, source_target_pairs={{1,2},{3,4},{5,6},{7,8},{9,10},{11,12},{13,14},{15,16},{17,18},{19... | collective-permute-start | bytes 663560 | tf_op jit(solution)/shard_map/ppermute | solution.py:500
  77.5 0.1 collective-permute-start.19
  77.6 0.6 mirror.3
  78.2 6.6 %collective-permute-done.18.from_odd = f32[27,16,128]{2,1,0:T(8,128)S(1)} collective-permute-done((f32[27,16,128]{2,1,0:T(8,128)S(1)}, f32[27,16,128]{2,1,0:T(8,128)S(1)}, u32[]{:S(2)}, u32[]{:S(2)}) %collective-permute-start.18) | collective-permute-done | bytes 221216 | tf_op jit(solution)/shard_map/ppermute | solution.py:500
  84.8 0.1 gather.3
  84.9 0.8 collective-permute-start.20
  85.6 0.8 collective-permute-start.22
  86.4 0.7 collective-permute-start.23
  87.1 0.8 collective-permute-done.20.theirs
  87.9 2.6 %collective-permute-start.21 = (f32[6,16,128]{2,1,0:T(8,128)S(1)}, f32[6,16,128]{2,1,0:T(8,128)S(1)}, u32[]{:S(2)}, u32[]{:S(2)}) collective-permute-start(f32[6,16,128]{2,1,0:T(8,128)S(1)} %join.3), channel_id=1, source_target_pairs={{0,160},{32,128},{64,224},{96,192},{128,32},{160,0},{192,96},{224,... | collective-permute-start | bytes 147464 | tf_op jit(solution)/shard_map/ppermute | solution.py:493
  90.5 1.7 %collective-permute-done.21.side = f32[6,16,128]{2,1,0:T(8,128)S(1)} collective-permute-done((f32[6,16,128]{2,1,0:T(8,128)S(1)}, f32[6,16,128]{2,1,0:T(8,128)S(1)}, u32[]{:S(2)}, u32[]{:S(2)}) %collective-permute-start.21) | collective-permute-done | bytes 49184 | tf_op jit(solution)/shard_map/ppermute | solution.py:493
  92.1 3.6 %collective-permute-done.23.p_high = f32[12,32,128]{2,1,0:T(8,128)S(1)} collective-permute-done((f32[12,32,128]{2,1,0:T(8,128)S(1)}, f32[12,32,128]{2,1,0:T(8,128)S(1)}, u32[]{:S(2)}, u32[]{:S(2)}) %collective-permute-start.23) | collective-permute-done | bytes 196640 | tf_op jit(solution)/shard_map/ppermute | solution.py:493
  95.8 0.2 last.1.mine
  96.0 2.0 %collective-permute-start.24 = (f32[24,32,128]{2,1,0:T(8,128)S(1)}, f32[24,32,128]{2,1,0:T(8,128)S(1)}, u32[]{:S(2)}, u32[]{:S(2)}) collective-permute-start(f32[24,32,128]{2,1,0:T(8,128)S(1)} %last.1.mine), channel_id=1, source_target_pairs={{0,64},{64,0},{128,192},{192,128},{1,65},{65,1},{129,193},{193,129... | collective-permute-start | bytes 1179656 | tf_op jit(solution)/shard_map/ppermute | solution.py:493
  98.0 0.8 near_half.1.near
  98.7 0.6 collective-permute-done.24.theirs
  99.3 0.8 far_half.1
  (28 shorter events, 0.2 us)
Async XLA Ops:
  0.0 5.5 %copy-start = (f32[48,32,128]{2,1,0:T(8,128)S(1)}, f32[48,32,128]{2,1,0:T(8,128)}, u32[]{:S(2)}) copy-start(f32[48,32,128]{2,1,0:T(8,128)} %est.3) | copy-start | bytes 2359300
  0.0 6.9 %copy-start.3 = (f32[4,3,31]{2,0,1:T(4,128)S(1)}, f32[4,3,31]{2,0,1:T(4,128)}, u32[]{:S(2)}) copy-start(f32[4,3,31]{2,0,1:T(4,128)} %param.6) | copy-start | bytes 4468
  0.0 11.4 %copy-start.4 = (s32[4,2]{0,1:T(2,128)S(1)}, s32[4,2]{0,1:T(2,128)}, u32[]{:S(2)}) copy-start(s32[4,2]{0,1:T(2,128)} %param.7) | copy-start | bytes 100
  0.0 11.6 %copy-start.1 = (f32[1,48,32,128]{3,2,1,0:T(8,128)S(1)}, f32[1,48,32,128]{3,2,1,0:T(8,128)}, u32[]{:S(2)}) copy-start(f32[1,48,32,128]{3,2,1,0:T(8,128)} %param.5) | copy-start | bytes 2359300
  2.4 13.8 %copy-start.2 = (bf16[32,2048]{1,0:T(8,128)(2,1)S(1)}, bf16[32,2048]{1,0:T(8,128)(2,1)}, u32[]{:S(2)}) copy-start(bf16[32,2048]{1,0:T(8,128)(2,1)} %constant.5.clone.place) | copy-start | bytes 393220
  2.4 4.4 %collective-permute-start = (f32[6,16,128]{2,1,0:T(8,128)}, f32[6,16,128]{2,1,0:T(8,128)S(1)}, u32[]{:S(2)}, u32[]{:S(2)}) collective-permute-start(f32[6,16,128]{2,1,0:T(8,128)} %get-tuple-element.54), channel_id=1, source_target_pairs={{0,160},{32,128},{64,224},{96,192},{128,32},{160,0},{192,96},{224,... | collective-permute-start | bytes 147464 | tf_op jit(solution)/shard_map/ppermute | solution.py:493
  5.0 6.6 %collective-permute-start.4 = (f32[12,8,128]{2,1,0:T(8,128)}, f32[12,8,128]{2,1,0:T(8,128)S(1)}, u32[]{:S(2)}, u32[]{:S(2)}) collective-permute-start(f32[12,8,128]{2,1,0:T(8,128)} %get-tuple-element.68), channel_id=1, source_target_pairs={{0,32},{32,0},{1,33},{33,1},{2,34},{34,2},{3,35},{35,3},{4,36},{36... | collective-permute-start | bytes 147464 | tf_op jit(solution)/shard_map/ppermute | solution.py:493
  7.0 11.7 %collective-permute-start.1 = (f32[27,16,128]{2,1,0:T(8,128)S(1)}, f32[27,16,128]{2,1,0:T(8,128)S(1)}, u32[]{:S(2)}, u32[]{:S(2)}) collective-permute-start(f32[27,16,128]{2,1,0:T(8,128)S(1)} %get-tuple-element.57), channel_id=1, source_target_pairs={{1,2},{3,4},{5,6},{7,8},{9,10},{11,12},{13,14},{15,16},{17,18},{19... | collective-permute-start | bytes 663560 | tf_op jit(solution)/shard_map/ppermute | solution.py:500
  11.5 7.2 %collective-permute-start.2 = (f32[27,16,128]{2,1,0:T(8,128)S(1)}, f32[27,16,128]{2,1,0:T(8,128)S(1)}, u32[]{:S(2)}, u32[]{:S(2)}) collective-permute-start(f32[27,16,128]{2,1,0:T(8,128)S(1)} %get-tuple-element.58), channel_id=1, source_target_pairs={{0,1},{1,0},{2,3},{3,2},{4,5},{5,4},{6,7},{7,6},{8,9},{9,8},{10,11... | collective-permute-start | bytes 663560 | tf_op jit(solution)/shard_map/ppermute | solution.py:501
  11.7 12.9 %collective-permute-start.5 = (f32[51,8,128]{2,1,0:T(8,128)S(1)}, f32[51,8,128]{2,1,0:T(8,128)S(1)}, u32[]{:S(2)}, u32[]{:S(2)}) collective-permute-start(f32[51,8,128]{2,1,0:T(8,128)S(1)} %get-tuple-element.69), channel_id=1, source_target_pairs={{1,2},{3,4},{5,6},{7,8},{9,10},{11,12},{13,14},{15,16},{17,18},{19... | collective-permute-start | bytes 626696 | tf_op jit(solution)/shard_map/ppermute | solution.py:500
  16.1 8.4 %collective-permute-start.6 = (f32[51,8,128]{2,1,0:T(8,128)S(1)}, f32[51,8,128]{2,1,0:T(8,128)S(1)}, u32[]{:S(2)}, u32[]{:S(2)}) collective-permute-start(f32[51,8,128]{2,1,0:T(8,128)S(1)} %get-tuple-element.70), channel_id=1, source_target_pairs={{0,1},{1,0},{2,3},{3,2},{4,5},{5,4},{6,7},{7,6},{8,9},{9,8},{10,11... | collective-permute-start | bytes 626696 | tf_op jit(solution)/shard_map/ppermute | solution.py:501
  19.8 4.1 %collective-permute-start.3 = (f32[24,32,128]{2,1,0:T(8,128)S(1)}, f32[24,32,128]{2,1,0:T(8,128)S(1)}, u32[]{:S(2)}, u32[]{:S(2)}) collective-permute-start(f32[24,32,128]{2,1,0:T(8,128)S(1)} %get-tuple-element.66), channel_id=1, source_target_pairs={{0,64},{64,0},{128,192},{192,128},{1,65},{65,1},{129,193},{193,129... | collective-permute-start | bytes 1179656 | tf_op jit(solution)/shard_map/ppermute | solution.py:493
  26.2 1.8 %collective-permute-start.7 = (f32[24,32,128]{2,1,0:T(8,128)S(1)}, f32[24,32,128]{2,1,0:T(8,128)S(1)}, u32[]{:S(2)}, u32[]{:S(2)}) collective-permute-start(f32[24,32,128]{2,1,0:T(8,128)S(1)} %get-tuple-element.72), channel_id=1, source_target_pairs={{0,64},{64,0},{128,192},{192,128},{1,65},{65,1},{129,193},{193,129... | collective-permute-start | bytes 1179656 | tf_op jit(solution)/shard_map/ppermute | solution.py:493
  29.0 11.9 %collective-permute-start.8 = (f32[27,16,128]{2,1,0:T(8,128)S(1)}, f32[27,16,128]{2,1,0:T(8,128)S(1)}, u32[]{:S(2)}, u32[]{:S(2)}) collective-permute-start(f32[27,16,128]{2,1,0:T(8,128)S(1)} %get-tuple-element.77), channel_id=1, source_target_pairs={{1,2},{3,4},{5,6},{7,8},{9,10},{11,12},{13,14},{15,16},{17,18},{19... | collective-permute-start | bytes 663560 | tf_op jit(solution)/shard_map/ppermute | solution.py:500
  33.6 7.3 %collective-permute-start.9 = (f32[27,16,128]{2,1,0:T(8,128)S(1)}, f32[27,16,128]{2,1,0:T(8,128)S(1)}, u32[]{:S(2)}, u32[]{:S(2)}) collective-permute-start(f32[27,16,128]{2,1,0:T(8,128)S(1)} %get-tuple-element.78), channel_id=1, source_target_pairs={{0,1},{1,0},{2,3},{3,2},{4,5},{5,4},{6,7},{7,6},{8,9},{9,8},{10,11... | collective-permute-start | bytes 663560 | tf_op jit(solution)/shard_map/ppermute | solution.py:501
  41.1 3.6 %collective-permute-start.10 = (f32[12,16,128]{2,1,0:T(8,128)S(1)}, f32[12,16,128]{2,1,0:T(8,128)S(1)}, u32[]{:S(2)}, u32[]{:S(2)}) collective-permute-start(f32[12,16,128]{2,1,0:T(8,128)S(1)} %get-tuple-element.80.mine), channel_id=1, source_target_pairs={{0,128},{64,192},{128,0},{192,64},{1,129},{65,193},{129,1},{193,65... | collective-permute-start | bytes 294920 | tf_op jit(solution)/shard_map/ppermute | solution.py:493
  41.2 7.3 %collective-permute-start.12 = (f32[12,32,128]{2,1,0:T(8,128)S(1)}, f32[12,32,128]{2,1,0:T(8,128)S(1)}, u32[]{:S(2)}, u32[]{:S(2)}) collective-permute-start(f32[12,32,128]{2,1,0:T(8,128)S(1)} %get-tuple-element.81.low), channel_id=1, source_target_pairs={{0,128},{64,192},{128,0},{192,64},{1,129},{65,193},{129,1},{193,65... | collective-permute-start | bytes 589832 | tf_op jit(solution)/shard_map/ppermute | solution.py:493
  42.7 10.0 %collective-permute-start.13 = (f32[12,32,128]{2,1,0:T(8,128)S(1)}, f32[12,32,128]{2,1,0:T(8,128)S(1)}, u32[]{:S(2)}, u32[]{:S(2)}) collective-permute-start(f32[12,32,128]{2,1,0:T(8,128)S(1)} %get-tuple-element.82.high), channel_id=1, source_target_pairs={{0,128},{64,192},{128,0},{192,64},{1,129},{65,193},{129,1},{193,65... | collective-permute-start | bytes 589832 | tf_op jit(solution)/shard_map/ppermute | solution.py:493
  44.7 8.0 %collective-permute-start.11 = (f32[12,16,128]{2,1,0:T(8,128)S(1)}, f32[12,16,128]{2,1,0:T(8,128)S(1)}, u32[]{:S(2)}, u32[]{:S(2)}) collective-permute-start(f32[12,16,128]{2,1,0:T(8,128)S(1)} %join.2.joined), channel_id=1, source_target_pairs={{0,160},{32,128},{64,224},{96,192},{128,32},{160,0},{192,96},{224,... | collective-permute-start | bytes 294920 | tf_op jit(solution)/shard_map/ppermute | solution.py:493
  52.9 10.0 %collective-permute-start.14 = (f32[27,16,128]{2,1,0:T(8,128)S(1)}, f32[27,16,128]{2,1,0:T(8,128)S(1)}, u32[]{:S(2)}, u32[]{:S(2)}) collective-permute-start(f32[27,16,128]{2,1,0:T(8,128)S(1)} %get-tuple-element.84), channel_id=1, source_target_pairs={{1,2},{3,4},{5,6},{7,8},{9,10},{11,12},{13,14},{15,16},{17,18},{19... | collective-permute-start | bytes 663560 | tf_op jit(solution)/shard_map/ppermute | solution.py:500
  57.5 5.4 %collective-permute-start.15 = (f32[27,16,128]{2,1,0:T(8,128)S(1)}, f32[27,16,128]{2,1,0:T(8,128)S(1)}, u32[]{:S(2)}, u32[]{:S(2)}) collective-permute-start(f32[27,16,128]{2,1,0:T(8,128)S(1)} %get-tuple-element.85), channel_id=1, source_target_pairs={{0,1},{1,0},{2,3},{3,2},{4,5},{5,4},{6,7},{7,6},{8,9},{9,8},{10,11... | collective-permute-start | bytes 663560 | tf_op jit(solution)/shard_map/ppermute | solution.py:501
  64.0 4.7 %collective-permute-start.16 = (f32[24,32,128]{2,1,0:T(8,128)S(1)}, f32[24,32,128]{2,1,0:T(8,128)S(1)}, u32[]{:S(2)}, u32[]{:S(2)}) collective-permute-start(f32[24,32,128]{2,1,0:T(8,128)S(1)} %get-tuple-element.91), channel_id=1, source_target_pairs={{0,64},{64,0},{128,192},{192,128},{1,65},{65,1},{129,193},{193,129... | collective-permute-start | bytes 1179656 | tf_op jit(solution)/shard_map/ppermute | solution.py:493
  70.1 1.8 %collective-permute-start.17 = (f32[24,32,128]{2,1,0:T(8,128)S(1)}, f32[24,32,128]{2,1,0:T(8,128)S(1)}, u32[]{:S(2)}, u32[]{:S(2)}) collective-permute-start(f32[24,32,128]{2,1,0:T(8,128)S(1)} %get-tuple-element.93), channel_id=1, source_target_pairs={{0,64},{64,0},{128,192},{192,128},{1,65},{65,1},{129,193},{193,129... | collective-permute-start | bytes 1179656 | tf_op jit(solution)/shard_map/ppermute | solution.py:493
  72.9 11.9 %collective-permute-start.18 = (f32[27,16,128]{2,1,0:T(8,128)S(1)}, f32[27,16,128]{2,1,0:T(8,128)S(1)}, u32[]{:S(2)}, u32[]{:S(2)}) collective-permute-start(f32[27,16,128]{2,1,0:T(8,128)S(1)} %get-tuple-element.98), channel_id=1, source_target_pairs={{1,2},{3,4},{5,6},{7,8},{9,10},{11,12},{13,14},{15,16},{17,18},{19... | collective-permute-start | bytes 663560 | tf_op jit(solution)/shard_map/ppermute | solution.py:500
  77.5 7.3 %collective-permute-start.19 = (f32[27,16,128]{2,1,0:T(8,128)S(1)}, f32[27,16,128]{2,1,0:T(8,128)S(1)}, u32[]{:S(2)}, u32[]{:S(2)}) collective-permute-start(f32[27,16,128]{2,1,0:T(8,128)S(1)} %get-tuple-element.99), channel_id=1, source_target_pairs={{0,1},{1,0},{2,3},{3,2},{4,5},{5,4},{6,7},{7,6},{8,9},{9,8},{10,11... | collective-permute-start | bytes 663560 | tf_op jit(solution)/shard_map/ppermute | solution.py:501
  84.9 3.0 %collective-permute-start.20 = (f32[6,16,128]{2,1,0:T(8,128)S(1)}, f32[6,16,128]{2,1,0:T(8,128)S(1)}, u32[]{:S(2)}, u32[]{:S(2)}) collective-permute-start(f32[6,16,128]{2,1,0:T(8,128)S(1)} %get-tuple-element.100.mine), channel_id=1, source_target_pairs={{0,128},{64,192},{128,0},{192,64},{1,129},{65,193},{129,1},{193,65... | collective-permute-start | bytes 147464 | tf_op jit(solution)/shard_map/ppermute | solution.py:493
  85.6 6.5 %collective-permute-start.22 = (f32[12,32,128]{2,1,0:T(8,128)S(1)}, f32[12,32,128]{2,1,0:T(8,128)S(1)}, u32[]{:S(2)}, u32[]{:S(2)}) collective-permute-start(f32[12,32,128]{2,1,0:T(8,128)S(1)} %get-tuple-element.101.low), channel_id=1, source_target_pairs={{0,128},{64,192},{128,0},{192,64},{1,129},{65,193},{129,1},{193,65... | collective-permute-start | bytes 589832 | tf_op jit(solution)/shard_map/ppermute | solution.py:493
  86.4 9.4 %collective-permute-start.23 = (f32[12,32,128]{2,1,0:T(8,128)S(1)}, f32[12,32,128]{2,1,0:T(8,128)S(1)}, u32[]{:S(2)}, u32[]{:S(2)}) collective-permute-start(f32[12,32,128]{2,1,0:T(8,128)S(1)} %get-tuple-element.102.high), channel_id=1, source_target_pairs={{0,128},{64,192},{128,0},{192,64},{1,129},{65,193},{129,1},{193,65... | collective-permute-start | bytes 589832 | tf_op jit(solution)/shard_map/ppermute | solution.py:493
  87.9 4.2 %collective-permute-start.21 = (f32[6,16,128]{2,1,0:T(8,128)S(1)}, f32[6,16,128]{2,1,0:T(8,128)S(1)}, u32[]{:S(2)}, u32[]{:S(2)}) collective-permute-start(f32[6,16,128]{2,1,0:T(8,128)S(1)} %join.3), channel_id=1, source_target_pairs={{0,160},{32,128},{64,224},{96,192},{128,32},{160,0},{192,96},{224,... | collective-permute-start | bytes 147464 | tf_op jit(solution)/shard_map/ppermute | solution.py:493
  96.0 3.3 %collective-permute-start.24 = (f32[24,32,128]{2,1,0:T(8,128)S(1)}, f32[24,32,128]{2,1,0:T(8,128)S(1)}, u32[]{:S(2)}, u32[]{:S(2)}) collective-permute-start(f32[24,32,128]{2,1,0:T(8,128)S(1)} %last.1.mine), channel_id=1, source_target_pairs={{0,64},{64,0},{128,192},{192,128},{1,65},{65,1},{129,193},{193,129... | collective-permute-start | bytes 1179656 | tf_op jit(solution)/shard_map/ppermute | solution.py:493

commit v9 on v7

--- a/solution.py
+++ b/solution.py
@@ -425,43 +425,40 @@
     put_sides(sides, lax.axis_index("tx"), turned, put)
 
 
-def gather_body(mid, mid_ext, from_odd, from_even, after, sides_out, low_out, high_out, turned):
+def gather_body(mid, mid_ext, from_odd, from_even, after, sides_out, out, turned):
     tx = lax.axis_index("tx")
     odd = parity()
     above = jnp.where(odd, from_even[...], from_odd[...])
     below = jnp.where(odd, from_odd[...], from_even[...])
-    for out, z in ((low_out, slice(0, 12)), (high_out, slice(12, 24))):
-        out[:, 0:16, :] = mid[z, 0:16, :] + above[z]
-        out[:, 16:32, :] = mid[z, 16:32, :] + below[z]
+    out[:, 0:16, :] = mid[:, 0:16, :] + above[0:24]
+    out[:, 16:32, :] = mid[:, 16:32, :] + below[0:24]
     sides_out[0:3] = mid_ext[0:3] + above[24:27]
     sides_out[3:6] = mid_ext[3:6] + below[24:27]
     if sides_out.shape[0] == 12:
         for xh in range(2):
             at = slice(16 * xh, 16 * xh + 16)
-            both = jnp.concatenate([low_out[:, at, :], high_out[:, at, :]])
-            put_packs(both, 112 * (1 - tx), 16, turned, sides_out, 6 + 3 * xh)
+            put_packs(out[:, at, :], 112 * (1 - tx), 16, turned, sides_out, 6 + 3 * xh)
 
 
 def join_body(mine, theirs, out):
     out[...] = mine[...] + theirs[...]
 
 
-def new_estimate(side, low, high, p_low, p_high, cur, norm, cur_out, turned):
+def new_estimate(side, mine, theirs, cur, norm, cur_out, turned):
     tx = lax.axis_index("tx")
     turned[...] = jnp.zeros_like(turned)
     for xh in range(2):
         at = slice(16 * xh, 16 * xh + 16)
         parts = [side[3 * xh + t] for t in range(3)]
         edge = spread_columns(parts, 112 * (1 - tx), 16, turned).reshape(24, 16, 128)
-        for mine, theirs, z in ((low, p_low, slice(0, 12)), (high, p_high, slice(12, 24))):
-            total = mine[:, at, :] + theirs[:, at, :] + edge[z]
-            cur_out[z, at, :] = cur[z, at, :] * total / norm[z, at, :]
+        total = mine[:, at, :] + theirs[:, at, :] + edge
+        cur_out[:, at, :] = cur[:, at, :] * total / norm[:, at, :]
 
 
 def update_body(
-    side, low, high, p_low, p_high, cur, norm, joined, ext, norm_ext, cur_out, ext_out, odd_out, even_out, turned
+    side, mine, theirs, cur, norm, joined, ext, norm_ext, cur_out, ext_out, odd_out, even_out, turned
 ):
-    new_estimate(side, low, high, p_low, p_high, cur, norm, cur_out, turned)
+    new_estimate(side, mine, theirs, cur, norm, cur_out, turned)
     ext_out[...] = ext[0:6] * (side[6:12] + joined[0:6]) / norm_ext[...]
     put_rims(cur_out[:, 0:16, :], cur_out[:, 16:32, :], even_out, odd_out, slice(0, 24))
     put_rims(ext_out[0:3], ext_out[3:6], even_out, odd_out, slice(24, 27))
@@ -499,7 +496,6 @@
     raw = raw_views[0]
 
     tile_half = ((half, tile_x, tile_y), F32)
-    tile_quarter = ((half // 2, tile_x, tile_y), F32)
     pack = ((6, EDGE, 128), F32)
     rim = ((half + 3, EDGE, 128), F32)
     turned = pltpu.VMEM((128, 384), F32)
@@ -595,25 +591,24 @@
             )
         from_odd, from_even = rim_swap(odd, even)
         last = iteration == ITERS - 1
-        sides, low, high = call(
+        sides, summed = call(
             gather_body,
-            [pack if last else ((12, EDGE, 128), F32), tile_quarter, tile_quarter],
+            [pack if last else ((12, EDGE, 128), F32), tile_half],
             [mid, mid_ext, from_odd, from_even, norm],
             [turned],
             name="gather",
         )
         theirs = swap(sides, "view", 2, (4,))
-        p_low = swap(low, "view", 2, (4,))
-        p_high = swap(high, "view", 2, (4,))
+        partner = swap(summed, "view", 2, (4,))
         (joined,) = call(join_body, [(sides.shape, F32)], [sides, theirs], flops=BUSY, name="join")
         side = swap(joined, ("view", "tx"), 5, (4, 2))
         if last:
-            (cur,) = call(new_estimate, [tile_half], [side, low, high, p_low, p_high, cur, norm], [turned], name="last")
+            (cur,) = call(new_estimate, [tile_half], [side, summed, partner, cur, norm], [turned], name="last")
             break
         cur, ext, odd, even = call(
             update_body,
             [tile_half, pack, rim, rim],
-            [side, low, high, p_low, p_high, cur, norm, joined, ext, norm_ext],
+            [side, summed, partner, cur, norm, joined, ext, norm_ext],
             [turned],
             name="update",
         )

time: 99.6 us -> 99.8 us (level)
  waiting for transfers between devices: 33.2 us -> 34.2 us
    ppermute x15 -> x13, waiting for transfers between devices: 18.8 us -> 19.7 us  [swap(): return lax.ppermute(value, axis, [(i, i ^ by) for i in range(count)])]
    ppermute x15 -> x13, starting transfers between devices: 20.4 us -> 19.5 us  [swap(): return lax.ppermute(value, axis, [(i, i ^ by) for i in range(count)])]
  transfers between devices with their start and end apart: 25 -> 23, of which waited for: 14 -> 14; matrix products, arithmetic and copies ran while one was open for 0% -> 0% of each run, Pallas kernels for 12% -> 12%
where the time goes in v9:
time: 99.8 us; the launch traced here: 99.3 us
  starting transfers between devices  42.1 us (42%)
  waiting for transfers between devices  34.2 us (34%)
  Pallas kernels  19.8 us (20%)
  local copies, waits for them, and re-layouts  2.7 us (3%)
    ppermute x5, starting transfers between devices, rim_swap(): from_odd = lax.ppermute(odd, 'ty', odd_pairs)  22.3 us
    pallas_call x28, Pallas kernels, call(): pl.pallas_call(body, out_shape=outs, in_specs=specs, out_specs=[pl.BlockS...  19.8 us
    ppermute x13, waiting for transfers between devices, swap(): return lax.ppermute(value, axis, [(i, i ^ by) for i in range(count)])  19.7 us
    ppermute x13, starting transfers between devices, swap(): return lax.ppermute(value, axis, [(i, i ^ by) for i in range(count)])  19.5 us
    ppermute x5, waiting for transfers between devices, rim_swap(): from_odd = lax.ppermute(odd, 'ty', odd_pairs)  14.4 us
    unnamed x14, local copies, waits for them, and re-layouts  2.5 us
  transfers between devices with their start and end apart: 23, of which 14 were waited for; matrix products, arithmetic and copies ran while one was open for 0% of the time, Pallas kernels for 12%

profile of v9, /device:TPU:121, one launch (start us, length us, event | category | flops | bytes accessed | tf_op | source)
XLA Modules:
  0.0 99.3 jit_solution(13476750737885874579)
XLA Ops:
  0.0 1.1 %copy-done = f32[48,32,128]{2,1,0:T(8,128)S(1)} copy-done((f32[48,32,128]{2,1,0:T(8,128)S(1)}, f32[48,32,128]{2,1,0:T(8,128)}, u32[]{:S(2)}) %copy-start) | copy-done | bytes 786456
  1.1 0.2 begin.1
  1.3 2.6 %collective-permute-start = (f32[6,16,128]{2,1,0:T(8,128)S(1)}, f32[6,16,128]{2,1,0:T(8,128)S(1)}, u32[]{:S(2)}, u32[]{:S(2)}) collective-permute-start(f32[6,16,128]{2,1,0:T(8,128)S(1)} %begin.1), channel_id=1, source_target_pairs={{0,160},{32,128},{64,224},{96,192},{128,32},{160,0},{192,96},{224,... | collective-permute-start | bytes 147464 | tf_op jit(solution)/shard_map/ppermute | solution.py:481
  3.9 1.1 %copy-done.2 = f32[1,48,32,128]{3,2,1,0:T(8,128)S(1)} copy-done((f32[1,48,32,128]{3,2,1,0:T(8,128)S(1)}, f32[1,48,32,128]{3,2,1,0:T(8,128)}, u32[]{:S(2)}) %copy-start.2) | copy-done | bytes 786456
  5.0 0.3 raw_sides.1
  5.3 0.6 collective-permute-start.4
  5.9 0.2 copy-done.1
  6.3 0.1 reshape.7.psf
  6.4 4.4 %collective-permute-start.1 = (f32[27,16,128]{2,1,0:T(8,128)S(1)}, f32[27,16,128]{2,1,0:T(8,128)S(1)}, u32[]{:S(2)}, u32[]{:S(2)}) collective-permute-start(f32[27,16,128]{2,1,0:T(8,128)S(1)} %get-tuple-element.52), channel_id=1, source_target_pairs={{1,2},{3,4},{5,6},{7,8},{9,10},{11,12},{13,14},{15,16},{17,18},{19... | collective-permute-start | bytes 663560 | tf_op jit(solution)/shard_map/ppermute | solution.py:488
  10.8 0.1 copy.16.offsets
  11.0 4.5 %collective-permute-start.5 = (f32[51,8,128]{2,1,0:T(8,128)S(1)}, f32[51,8,128]{2,1,0:T(8,128)S(1)}, u32[]{:S(2)}, u32[]{:S(2)}) collective-permute-start(f32[51,8,128]{2,1,0:T(8,128)S(1)} %get-tuple-element.63), channel_id=1, source_target_pairs={{1,2},{3,4},{5,6},{7,8},{9,10},{11,12},{13,14},{15,16},{17,18},{19... | collective-permute-start | bytes 626696 | tf_op jit(solution)/shard_map/ppermute | solution.py:488
  15.5 0.1 collective-permute-start.6
  15.6 1.4 %bands.1 = (bf16[2,768,384]{2,1,0:T(8,128)(2,1)S(1)}, bf16[10,256,256]{2,1,0:T(8,128)(2,1)S(1)}) custom-call(f32[16,32]{1,0:T(8,128)S(1)} %pad.4.taps.after, bf16[32,2048]{1,0:T(8,128)(2,1)S(1)} %copy-done.4, f32[372]{0:T(512)S(1)} %reshape.7.psf, s32[4,2]{1,0:T(4,128)S(1)} %copy.16.offsets), custom_call_target="tpu_custom_call" | custom-call | flops 6000000000 | bytes 2625008 | tf_op jit(solution)/shard_map/bands/pallas_call | solution.py:49
  17.0 1.1 %inner.2 = (f32[24,32,128]{2,1,0:T(8,128)S(1)}, f32[24,32,128]{2,1,0:T(8,128)S(1)}) custom-call(f32[24,32,128]{2,1,0:T(8,128)S(1)} %get-tuple-element.57.cur, f32[6,16,128]{2,1,0:T(8,128)S(1)} %collective-permute-done.pack.ext, bf16[10,256,256]{2,1,0:T(8,128)(2,1)S(1)} %get-tuple-element.56.mats), custom_call_target="tpu_custom_call" | custom-call | flops 6000000000 | bytes 2539520 | tf_op jit(solution)/shard_map/inner/pallas_call | solution.py:49
  18.1 1.1 %outer.2 = (f32[24,32,128]{2,1,0:T(8,128)S(1)}, f32[24,32,128]{2,1,0:T(8,128)S(1)}) custom-call(f32[27,16,128]{2,1,0:T(8,128)S(1)} %collective-permute-done.1.from_odd, f32[27,16,128]{2,1,0:T(8,128)S(1)} %collective-permute-done.2.from_even, bf16[10,256,256]{2,1,0:T(8,128)(2,1)S(1)} %get-tuple-element.56.mats, f32[24,32,128]{2,1,0:T(8,128)S(1)} %get-tuple-element.58.in_own, ...), custom_call_target="tpu_custom_call" | custom-call | flops 6000000000 | bytes 3325952 | tf_op jit(solution)/shard_map/outer/pallas_call | solution.py:49
  19.2 2.1 %collective-permute-start.3 = (f32[24,32,128]{2,1,0:T(8,128)S(1)}, f32[24,32,128]{2,1,0:T(8,128)S(1)}, u32[]{:S(2)}, u32[]{:S(2)}) collective-permute-start(f32[24,32,128]{2,1,0:T(8,128)S(1)} %get-tuple-element.61), channel_id=1, source_target_pairs={{0,64},{64,0},{128,192},{192,128},{1,65},{65,1},{129,193},{193,129... | collective-permute-start | bytes 1179656 | tf_op jit(solution)/shard_map/ppermute | solution.py:481
  21.2 1.1 %register_columns.1.moved = f32[48,32,128]{2,1,0:T(8,128)S(1)} custom-call(s32[4,2]{1,0:T(4,128)S(1)} %copy.16.offsets, f32[48,32,128]{2,1,0:T(8,128)S(1)} %bitcast.3, f32[12,8,128]{2,1,0:T(8,128)S(1)} %collective-permute-done.4.pack, f32[24,32,128]{2,1,0:T(8,128)S(1)} %get-tuple-element.60.mine.after), custom_call_target="tpu_custom_call" | custom-call | flops 6000000000 | bytes 2015264 | tf_op jit(solution)/shard_map/register_columns/pallas_call | solution.py:49
  22.3 0.3 collective-permute-done.3.theirs
  22.6 0.6 planes.1.after.blurred
  23.3 0.9 register.1.seen
  24.2 0.7 ratio.2
  24.9 0.7 collective-permute-start.7
  25.6 1.3 %collective-permute-done.7.other = f32[24,32,128]{2,1,0:T(8,128)S(1)} collective-permute-done((f32[24,32,128]{2,1,0:T(8,128)S(1)}, f32[24,32,128]{2,1,0:T(8,128)S(1)}, u32[]{:S(2)}, u32[]{:S(2)}) %collective-permute-start.7) | collective-permute-done | bytes 393248 | tf_op jit(solution)/shard_map/ppermute | solution.py:481
  27.0 1.0 mirror_rims.2
  28.0 4.4 %collective-permute-start.8 = (f32[27,16,128]{2,1,0:T(8,128)S(1)}, f32[27,16,128]{2,1,0:T(8,128)S(1)}, u32[]{:S(2)}, u32[]{:S(2)}) collective-permute-start(f32[27,16,128]{2,1,0:T(8,128)S(1)} %get-tuple-element.71), channel_id=1, source_target_pairs={{1,2},{3,4},{5,6},{7,8},{9,10},{11,12},{13,14},{15,16},{17,18},{19... | collective-permute-start | bytes 663560 | tf_op jit(solution)/shard_map/ppermute | solution.py:488
  32.4 0.1 collective-permute-start.9
  32.5 0.6 mirror.2
  33.1 3.5 %norm.1 = (f32[24,32,128]{2,1,0:T(8,128)S(1)}, f32[6,16,128]{2,1,0:T(8,128)S(1)}) custom-call(f32[372]{0:T(512)S(1)} %reshape.7.psf, s32[4,2]{1,0:T(4,128)S(1)} %copy.16.offsets, bf16[2,768,256]{2,1,0:T(8,128)(2,1)S(1)} %get-tuple-element.67.y_h.after), custom_call_target="tpu_custom_call" | custom-call | bytes 1230320 | tf_op jit(solution)/shard_map/norm/pallas_call | solution.py:49
  36.6 3.3 %collective-permute-done.8.from_odd = f32[27,16,128]{2,1,0:T(8,128)S(1)} collective-permute-done((f32[27,16,128]{2,1,0:T(8,128)S(1)}, f32[27,16,128]{2,1,0:T(8,128)S(1)}, u32[]{:S(2)}, u32[]{:S(2)}) %collective-permute-start.8) | collective-permute-done | bytes 221216 | tf_op jit(solution)/shard_map/ppermute | solution.py:488
  39.8 0.2 gather.2
  40.1 0.1 collective-permute-start.10
  40.2 1.4 %collective-permute-start.12 = (f32[24,32,128]{2,1,0:T(8,128)S(1)}, f32[24,32,128]{2,1,0:T(8,128)S(1)}, u32[]{:S(2)}, u32[]{:S(2)}) collective-permute-start(f32[24,32,128]{2,1,0:T(8,128)S(1)} %get-tuple-element.75.mine), channel_id=1, source_target_pairs={{0,128},{64,192},{128,0},{192,64},{1,129},{65,193},{129,1},{193,65... | collective-permute-start | bytes 1179656 | tf_op jit(solution)/shard_map/ppermute | solution.py:481
  41.6 2.0 %collective-permute-done.10.theirs = f32[12,16,128]{2,1,0:T(8,128)S(1)} collective-permute-done((f32[12,16,128]{2,1,0:T(8,128)S(1)}, f32[12,16,128]{2,1,0:T(8,128)S(1)}, u32[]{:S(2)}, u32[]{:S(2)}) %collective-permute-start.10) | collective-permute-done | bytes 98336 | tf_op jit(solution)/shard_map/ppermute | solution.py:481
  43.6 2.3 %collective-permute-start.11 = (f32[12,16,128]{2,1,0:T(8,128)S(1)}, f32[12,16,128]{2,1,0:T(8,128)S(1)}, u32[]{:S(2)}, u32[]{:S(2)}) collective-permute-start(f32[12,16,128]{2,1,0:T(8,128)S(1)} %join.2.joined), channel_id=1, source_target_pairs={{0,160},{32,128},{64,224},{96,192},{128,32},{160,0},{192,96},{224,... | collective-permute-start | bytes 294920 | tf_op jit(solution)/shard_map/ppermute | solution.py:481
  45.9 2.5 %collective-permute-done.11.side = f32[12,16,128]{2,1,0:T(8,128)S(1)} collective-permute-done((f32[12,16,128]{2,1,0:T(8,128)S(1)}, f32[12,16,128]{2,1,0:T(8,128)S(1)}, u32[]{:S(2)}, u32[]{:S(2)}) %collective-permute-start.11) | collective-permute-done | bytes 98336 | tf_op jit(solution)/shard_map/ppermute | solution.py:481
  48.4 3.3 %collective-permute-done.12.theirs = f32[24,32,128]{2,1,0:T(8,128)S(1)} collective-permute-done((f32[24,32,128]{2,1,0:T(8,128)S(1)}, f32[24,32,128]{2,1,0:T(8,128)S(1)}, u32[]{:S(2)}, u32[]{:S(2)}) %collective-permute-start.12) | collective-permute-done | bytes 393248 | tf_op jit(solution)/shard_map/ppermute | solution.py:481
  51.7 0.2 update.1
  51.9 4.6 %collective-permute-start.13 = (f32[27,16,128]{2,1,0:T(8,128)S(1)}, f32[27,16,128]{2,1,0:T(8,128)S(1)}, u32[]{:S(2)}, u32[]{:S(2)}) collective-permute-start(f32[27,16,128]{2,1,0:T(8,128)S(1)} %get-tuple-element.77), channel_id=1, source_target_pairs={{1,2},{3,4},{5,6},{7,8},{9,10},{11,12},{13,14},{15,16},{17,18},{19... | collective-permute-start | bytes 663560 | tf_op jit(solution)/shard_map/ppermute | solution.py:488
  56.4 0.1 collective-permute-start.14
  56.5 1.1 %inner.3 = (f32[24,32,128]{2,1,0:T(8,128)S(1)}, f32[24,32,128]{2,1,0:T(8,128)S(1)}) custom-call(f32[24,32,128]{2,1,0:T(8,128)S(1)} %get-tuple-element.79.cur, f32[6,16,128]{2,1,0:T(8,128)S(1)} %get-tuple-element.80.ext, bf16[10,256,256]{2,1,0:T(8,128)(2,1)S(1)} %get-tuple-element.56.mats), custom_call_target="tpu_custom_call" | custom-call | flops 6000000000 | bytes 2539520 | tf_op jit(solution)/shard_map/inner/pallas_call | solution.py:49
  57.6 4.4 %collective-permute-done.13.from_odd = f32[27,16,128]{2,1,0:T(8,128)S(1)} collective-permute-done((f32[27,16,128]{2,1,0:T(8,128)S(1)}, f32[27,16,128]{2,1,0:T(8,128)S(1)}, u32[]{:S(2)}, u32[]{:S(2)}) %collective-permute-start.13) | collective-permute-done | bytes 221216 | tf_op jit(solution)/shard_map/ppermute | solution.py:488
  62.0 1.1 %outer.3 = (f32[24,32,128]{2,1,0:T(8,128)S(1)}, f32[24,32,128]{2,1,0:T(8,128)S(1)}) custom-call(f32[27,16,128]{2,1,0:T(8,128)S(1)} %collective-permute-done.13.from_odd, f32[27,16,128]{2,1,0:T(8,128)S(1)} %collective-permute-done.14.from_even, bf16[10,256,256]{2,1,0:T(8,128)(2,1)S(1)} %get-tuple-element.56.mats, ...), custom_call_target="tpu_custom_call" | custom-call | flops 6000000000 | bytes 3325952 | tf_op jit(solution)/shard_map/outer/pallas_call | solution.py:49
  63.1 3.4 %collective-permute-start.15 = (f32[24,32,128]{2,1,0:T(8,128)S(1)}, f32[24,32,128]{2,1,0:T(8,128)S(1)}, u32[]{:S(2)}, u32[]{:S(2)}) collective-permute-start(f32[24,32,128]{2,1,0:T(8,128)S(1)} %get-tuple-element.84), channel_id=1, source_target_pairs={{0,64},{64,0},{128,192},{192,128},{1,65},{65,1},{129,193},{193,129... | collective-permute-start | bytes 1179656 | tf_op jit(solution)/shard_map/ppermute | solution.py:481
  66.5 1.3 %collective-permute-done.15.theirs = f32[24,32,128]{2,1,0:T(8,128)S(1)} collective-permute-done((f32[24,32,128]{2,1,0:T(8,128)S(1)}, f32[24,32,128]{2,1,0:T(8,128)S(1)}, u32[]{:S(2)}, u32[]{:S(2)}) %collective-permute-start.15) | collective-permute-done | bytes 393248 | tf_op jit(solution)/shard_map/ppermute | solution.py:481
  67.8 1.4 %ratio.3 = (f32[24,32,128]{2,1,0:T(8,128)S(1)}, f32[24,32,128]{2,1,0:T(8,128)S(1)}) custom-call(f32[24,32,128]{2,1,0:T(8,128)S(1)} %get-tuple-element.83.mine, f32[24,32,128]{2,1,0:T(8,128)S(1)} %collective-permute-done.15.theirs, f32[48,32,128]{2,1,0:T(8,128)S(1)} %register.1.seen, bf16[2,768,384]{2,1,0:T(8,128)(2,1)S(1)} %get-tuple-element.62.kz), custom_call_target="tpu_custom_call" | custom-call | flops 905969664 | bytes 3538944 | tf_op jit(solution)/shard_map/ratio/pallas_call | solution.py:49
  69.3 0.5 collective-permute-start.16
  69.7 1.3 %collective-permute-done.16.other = f32[24,32,128]{2,1,0:T(8,128)S(1)} collective-permute-done((f32[24,32,128]{2,1,0:T(8,128)S(1)}, f32[24,32,128]{2,1,0:T(8,128)S(1)}, u32[]{:S(2)}, u32[]{:S(2)}) %collective-permute-start.16) | collective-permute-done | bytes 393248 | tf_op jit(solution)/shard_map/ppermute | solution.py:481
  71.1 1.0 mirror_rims.3
  72.1 4.4 %collective-permute-start.17 = (f32[27,16,128]{2,1,0:T(8,128)S(1)}, f32[27,16,128]{2,1,0:T(8,128)S(1)}, u32[]{:S(2)}, u32[]{:S(2)}) collective-permute-start(f32[27,16,128]{2,1,0:T(8,128)S(1)} %get-tuple-element.91), channel_id=1, source_target_pairs={{1,2},{3,4},{5,6},{7,8},{9,10},{11,12},{13,14},{15,16},{17,18},{19... | collective-permute-start | bytes 663560 | tf_op jit(solution)/shard_map/ppermute | solution.py:488
  76.5 0.1 collective-permute-start.18
  76.6 0.6 mirror.3
  77.2 6.7 %collective-permute-done.17.from_odd = f32[27,16,128]{2,1,0:T(8,128)S(1)} collective-permute-done((f32[27,16,128]{2,1,0:T(8,128)S(1)}, f32[27,16,128]{2,1,0:T(8,128)S(1)}, u32[]{:S(2)}, u32[]{:S(2)}) %collective-permute-start.17) | collective-permute-done | bytes 221216 | tf_op jit(solution)/shard_map/ppermute | solution.py:488
  83.9 0.1 gather.3
  84.0 0.7 collective-permute-start.19
  84.7 0.8 collective-permute-start.21
  85.5 1.5 %collective-permute-done.19.theirs = f32[6,16,128]{2,1,0:T(8,128)S(1)} collective-permute-done((f32[6,16,128]{2,1,0:T(8,128)S(1)}, f32[6,16,128]{2,1,0:T(8,128)S(1)}, u32[]{:S(2)}, u32[]{:S(2)}) %collective-permute-start.19) | collective-permute-done | bytes 49184 | tf_op jit(solution)/shard_map/ppermute | solution.py:481
  87.0 2.3 %collective-permute-start.20 = (f32[6,16,128]{2,1,0:T(8,128)S(1)}, f32[6,16,128]{2,1,0:T(8,128)S(1)}, u32[]{:S(2)}, u32[]{:S(2)}) collective-permute-start(f32[6,16,128]{2,1,0:T(8,128)S(1)} %join.3), channel_id=1, source_target_pairs={{0,160},{32,128},{64,224},{96,192},{128,32},{160,0},{192,96},{224,... | collective-permute-start | bytes 147464 | tf_op jit(solution)/shard_map/ppermute | solution.py:481
  89.3 2.0 %collective-permute-done.20.side = f32[6,16,128]{2,1,0:T(8,128)S(1)} collective-permute-done((f32[6,16,128]{2,1,0:T(8,128)S(1)}, f32[6,16,128]{2,1,0:T(8,128)S(1)}, u32[]{:S(2)}, u32[]{:S(2)}) %collective-permute-start.20) | collective-permute-done | bytes 49184 | tf_op jit(solution)/shard_map/ppermute | solution.py:481
  91.3 3.6 %collective-permute-done.21.theirs = f32[24,32,128]{2,1,0:T(8,128)S(1)} collective-permute-done((f32[24,32,128]{2,1,0:T(8,128)S(1)}, f32[24,32,128]{2,1,0:T(8,128)S(1)}, u32[]{:S(2)}, u32[]{:S(2)}) %collective-permute-start.21) | collective-permute-done | bytes 393248 | tf_op jit(solution)/shard_map/ppermute | solution.py:481
  94.8 0.2 last.1.mine
  95.0 2.0 %collective-permute-start.22 = (f32[24,32,128]{2,1,0:T(8,128)S(1)}, f32[24,32,128]{2,1,0:T(8,128)S(1)}, u32[]{:S(2)}, u32[]{:S(2)}) collective-permute-start(f32[24,32,128]{2,1,0:T(8,128)S(1)} %last.1.mine), channel_id=1, source_target_pairs={{0,64},{64,0},{128,192},{192,128},{1,65},{65,1},{129,193},{193,129... | collective-permute-start | bytes 1179656 | tf_op jit(solution)/shard_map/ppermute | solution.py:481
  97.1 0.8 near_half.1.near
  97.8 0.6 collective-permute-done.22.theirs
  98.4 0.8 far_half.1
  (29 shorter events, 0.2 us)
Async XLA Ops:
  0.0 1.1 %copy-start = (f32[48,32,128]{2,1,0:T(8,128)S(1)}, f32[48,32,128]{2,1,0:T(8,128)}, u32[]{:S(2)}) copy-start(f32[48,32,128]{2,1,0:T(8,128)} %est.3) | copy-start | bytes 2359300
  1.3 4.9 %collective-permute-start = (f32[6,16,128]{2,1,0:T(8,128)S(1)}, f32[6,16,128]{2,1,0:T(8,128)S(1)}, u32[]{:S(2)}, u32[]{:S(2)}) collective-permute-start(f32[6,16,128]{2,1,0:T(8,128)S(1)} %begin.1), channel_id=1, source_target_pairs={{0,160},{32,128},{64,224},{96,192},{128,32},{160,0},{192,96},{224,... | collective-permute-start | bytes 147464 | tf_op jit(solution)/shard_map/ppermute | solution.py:481
  3.9 1.1 %copy-start.2 = (f32[1,48,32,128]{3,2,1,0:T(8,128)S(1)}, f32[1,48,32,128]{3,2,1,0:T(8,128)}, u32[]{:S(2)}) copy-start(f32[1,48,32,128]{3,2,1,0:T(8,128)} %param.5) | copy-start | bytes 2359300
  5.0 1.1 %copy-start.1 = (f32[48,32,128]{2,1,0:T(8,128)S(1)}, f32[48,32,128]{2,1,0:T(8,128)}, u32[]{:S(2)}) copy-start(f32[48,32,128]{2,1,0:T(8,128)} %est.3) | copy-start | bytes 2359300
  5.0 1.2 %copy-start.5 = (f32[4,3,31]{2,0,1:T(4,128)S(1)}, f32[4,3,31]{2,0,1:T(4,128)}, u32[]{:S(2)}) copy-start(f32[4,3,31]{2,0,1:T(4,128)} %param.6) | copy-start | bytes 4468
  5.3 5.5 %copy-start.6 = (s32[4,2]{0,1:T(2,128)S(1)}, s32[4,2]{0,1:T(2,128)}, u32[]{:S(2)}) copy-start(s32[4,2]{0,1:T(2,128)} %param.7) | copy-start | bytes 100
  5.3 5.6 %copy-start.3 = (f32[1,48,32,128]{3,2,1,0:T(8,128)S(1)}, f32[1,48,32,128]{3,2,1,0:T(8,128)}, u32[]{:S(2)}) copy-start(f32[1,48,32,128]{3,2,1,0:T(8,128)} %param.5) | copy-start | bytes 2359300
  5.3 10.3 %copy-start.4 = (bf16[32,2048]{1,0:T(8,128)(2,1)S(1)}, bf16[32,2048]{1,0:T(8,128)(2,1)}, u32[]{:S(2)}) copy-start(bf16[32,2048]{1,0:T(8,128)(2,1)} %constant.5.clone.place) | copy-start | bytes 393220
  5.3 5.6 %collective-permute-start.4 = (f32[12,8,128]{2,1,0:T(8,128)S(1)}, f32[12,8,128]{2,1,0:T(8,128)S(1)}, u32[]{:S(2)}, u32[]{:S(2)}) collective-permute-start(f32[12,8,128]{2,1,0:T(8,128)S(1)} %raw_sides.1), channel_id=1, source_target_pairs={{0,32},{32,0},{1,33},{33,1},{2,34},{34,2},{3,35},{35,3},{4,36},{36... | collective-permute-start | bytes 147464 | tf_op jit(solution)/shard_map/ppermute | solution.py:481
  6.4 11.7 %collective-permute-start.1 = (f32[27,16,128]{2,1,0:T(8,128)S(1)}, f32[27,16,128]{2,1,0:T(8,128)S(1)}, u32[]{:S(2)}, u32[]{:S(2)}) collective-permute-start(f32[27,16,128]{2,1,0:T(8,128)S(1)} %get-tuple-element.52), channel_id=1, source_target_pairs={{1,2},{3,4},{5,6},{7,8},{9,10},{11,12},{13,14},{15,16},{17,18},{19... | collective-permute-start | bytes 663560 | tf_op jit(solution)/shard_map/ppermute | solution.py:488
  10.9 7.2 %collective-permute-start.2 = (f32[27,16,128]{2,1,0:T(8,128)S(1)}, f32[27,16,128]{2,1,0:T(8,128)S(1)}, u32[]{:S(2)}, u32[]{:S(2)}) collective-permute-start(f32[27,16,128]{2,1,0:T(8,128)S(1)} %get-tuple-element.53), channel_id=1, source_target_pairs={{0,1},{1,0},{2,3},{3,2},{4,5},{5,4},{6,7},{7,6},{8,9},{9,8},{10,11... | collective-permute-start | bytes 663560 | tf_op jit(solution)/shard_map/ppermute | solution.py:489
  11.0 12.2 %collective-permute-start.5 = (f32[51,8,128]{2,1,0:T(8,128)S(1)}, f32[51,8,128]{2,1,0:T(8,128)S(1)}, u32[]{:S(2)}, u32[]{:S(2)}) collective-permute-start(f32[51,8,128]{2,1,0:T(8,128)S(1)} %get-tuple-element.63), channel_id=1, source_target_pairs={{1,2},{3,4},{5,6},{7,8},{9,10},{11,12},{13,14},{15,16},{17,18},{19... | collective-permute-start | bytes 626696 | tf_op jit(solution)/shard_map/ppermute | solution.py:488
  15.5 7.8 %collective-permute-start.6 = (f32[51,8,128]{2,1,0:T(8,128)S(1)}, f32[51,8,128]{2,1,0:T(8,128)S(1)}, u32[]{:S(2)}, u32[]{:S(2)}) collective-permute-start(f32[51,8,128]{2,1,0:T(8,128)S(1)} %get-tuple-element.64), channel_id=1, source_target_pairs={{0,1},{1,0},{2,3},{3,2},{4,5},{5,4},{6,7},{7,6},{8,9},{9,8},{10,11... | collective-permute-start | bytes 626696 | tf_op jit(solution)/shard_map/ppermute | solution.py:489
  19.2 3.4 %collective-permute-start.3 = (f32[24,32,128]{2,1,0:T(8,128)S(1)}, f32[24,32,128]{2,1,0:T(8,128)S(1)}, u32[]{:S(2)}, u32[]{:S(2)}) collective-permute-start(f32[24,32,128]{2,1,0:T(8,128)S(1)} %get-tuple-element.61), channel_id=1, source_target_pairs={{0,64},{64,0},{128,192},{192,128},{1,65},{65,1},{129,193},{193,129... | collective-permute-start | bytes 1179656 | tf_op jit(solution)/shard_map/ppermute | solution.py:481
  24.9 2.1 %collective-permute-start.7 = (f32[24,32,128]{2,1,0:T(8,128)S(1)}, f32[24,32,128]{2,1,0:T(8,128)S(1)}, u32[]{:S(2)}, u32[]{:S(2)}) collective-permute-start(f32[24,32,128]{2,1,0:T(8,128)S(1)} %get-tuple-element.66), channel_id=1, source_target_pairs={{0,64},{64,0},{128,192},{192,128},{1,65},{65,1},{129,193},{193,129... | collective-permute-start | bytes 1179656 | tf_op jit(solution)/shard_map/ppermute | solution.py:481
  28.0 11.9 %collective-permute-start.8 = (f32[27,16,128]{2,1,0:T(8,128)S(1)}, f32[27,16,128]{2,1,0:T(8,128)S(1)}, u32[]{:S(2)}, u32[]{:S(2)}) collective-permute-start(f32[27,16,128]{2,1,0:T(8,128)S(1)} %get-tuple-element.71), channel_id=1, source_target_pairs={{1,2},{3,4},{5,6},{7,8},{9,10},{11,12},{13,14},{15,16},{17,18},{19... | collective-permute-start | bytes 663560 | tf_op jit(solution)/shard_map/ppermute | solution.py:488
  32.4 7.4 %collective-permute-start.9 = (f32[27,16,128]{2,1,0:T(8,128)S(1)}, f32[27,16,128]{2,1,0:T(8,128)S(1)}, u32[]{:S(2)}, u32[]{:S(2)}) collective-permute-start(f32[27,16,128]{2,1,0:T(8,128)S(1)} %get-tuple-element.72), channel_id=1, source_target_pairs={{0,1},{1,0},{2,3},{3,2},{4,5},{5,4},{6,7},{7,6},{8,9},{9,8},{10,11... | collective-permute-start | bytes 663560 | tf_op jit(solution)/shard_map/ppermute | solution.py:489
  40.1 3.6 %collective-permute-start.10 = (f32[12,16,128]{2,1,0:T(8,128)S(1)}, f32[12,16,128]{2,1,0:T(8,128)S(1)}, u32[]{:S(2)}, u32[]{:S(2)}) collective-permute-start(f32[12,16,128]{2,1,0:T(8,128)S(1)} %get-tuple-element.74.mine), channel_id=1, source_target_pairs={{0,128},{64,192},{128,0},{192,64},{1,129},{65,193},{129,1},{193,65... | collective-permute-start | bytes 294920 | tf_op jit(solution)/shard_map/ppermute | solution.py:481
  40.2 11.5 %collective-permute-start.12 = (f32[24,32,128]{2,1,0:T(8,128)S(1)}, f32[24,32,128]{2,1,0:T(8,128)S(1)}, u32[]{:S(2)}, u32[]{:S(2)}) collective-permute-start(f32[24,32,128]{2,1,0:T(8,128)S(1)} %get-tuple-element.75.mine), channel_id=1, source_target_pairs={{0,128},{64,192},{128,0},{192,64},{1,129},{65,193},{129,1},{193,65... | collective-permute-start | bytes 1179656 | tf_op jit(solution)/shard_map/ppermute | solution.py:481
  43.6 4.8 %collective-permute-start.11 = (f32[12,16,128]{2,1,0:T(8,128)S(1)}, f32[12,16,128]{2,1,0:T(8,128)S(1)}, u32[]{:S(2)}, u32[]{:S(2)}) collective-permute-start(f32[12,16,128]{2,1,0:T(8,128)S(1)} %join.2.joined), channel_id=1, source_target_pairs={{0,160},{32,128},{64,224},{96,192},{128,32},{160,0},{192,96},{224,... | collective-permute-start | bytes 294920 | tf_op jit(solution)/shard_map/ppermute | solution.py:481
  51.9 10.2 %collective-permute-start.13 = (f32[27,16,128]{2,1,0:T(8,128)S(1)}, f32[27,16,128]{2,1,0:T(8,128)S(1)}, u32[]{:S(2)}, u32[]{:S(2)}) collective-permute-start(f32[27,16,128]{2,1,0:T(8,128)S(1)} %get-tuple-element.77), channel_id=1, source_target_pairs={{1,2},{3,4},{5,6},{7,8},{9,10},{11,12},{13,14},{15,16},{17,18},{19... | collective-permute-start | bytes 663560 | tf_op jit(solution)/shard_map/ppermute | solution.py:488
  56.4 5.6 %collective-permute-start.14 = (f32[27,16,128]{2,1,0:T(8,128)S(1)}, f32[27,16,128]{2,1,0:T(8,128)S(1)}, u32[]{:S(2)}, u32[]{:S(2)}) collective-permute-start(f32[27,16,128]{2,1,0:T(8,128)S(1)} %get-tuple-element.78), channel_id=1, source_target_pairs={{0,1},{1,0},{2,3},{3,2},{4,5},{5,4},{6,7},{7,6},{8,9},{9,8},{10,11... | collective-permute-start | bytes 663560 | tf_op jit(solution)/shard_map/ppermute | solution.py:489
  63.1 4.7 %collective-permute-start.15 = (f32[24,32,128]{2,1,0:T(8,128)S(1)}, f32[24,32,128]{2,1,0:T(8,128)S(1)}, u32[]{:S(2)}, u32[]{:S(2)}) collective-permute-start(f32[24,32,128]{2,1,0:T(8,128)S(1)} %get-tuple-element.84), channel_id=1, source_target_pairs={{0,64},{64,0},{128,192},{192,128},{1,65},{65,1},{129,193},{193,129... | collective-permute-start | bytes 1179656 | tf_op jit(solution)/shard_map/ppermute | solution.py:481
  69.3 1.8 %collective-permute-start.16 = (f32[24,32,128]{2,1,0:T(8,128)S(1)}, f32[24,32,128]{2,1,0:T(8,128)S(1)}, u32[]{:S(2)}, u32[]{:S(2)}) collective-permute-start(f32[24,32,128]{2,1,0:T(8,128)S(1)} %get-tuple-element.86), channel_id=1, source_target_pairs={{0,64},{64,0},{128,192},{192,128},{1,65},{65,1},{129,193},{193,129... | collective-permute-start | bytes 1179656 | tf_op jit(solution)/shard_map/ppermute | solution.py:481
  72.1 11.9 %collective-permute-start.17 = (f32[27,16,128]{2,1,0:T(8,128)S(1)}, f32[27,16,128]{2,1,0:T(8,128)S(1)}, u32[]{:S(2)}, u32[]{:S(2)}) collective-permute-start(f32[27,16,128]{2,1,0:T(8,128)S(1)} %get-tuple-element.91), channel_id=1, source_target_pairs={{1,2},{3,4},{5,6},{7,8},{9,10},{11,12},{13,14},{15,16},{17,18},{19... | collective-permute-start | bytes 663560 | tf_op jit(solution)/shard_map/ppermute | solution.py:488
  76.5 7.4 %collective-permute-start.18 = (f32[27,16,128]{2,1,0:T(8,128)S(1)}, f32[27,16,128]{2,1,0:T(8,128)S(1)}, u32[]{:S(2)}, u32[]{:S(2)}) collective-permute-start(f32[27,16,128]{2,1,0:T(8,128)S(1)} %get-tuple-element.92), channel_id=1, source_target_pairs={{0,1},{1,0},{2,3},{3,2},{4,5},{5,4},{6,7},{7,6},{8,9},{9,8},{10,11... | collective-permute-start | bytes 663560 | tf_op jit(solution)/shard_map/ppermute | solution.py:489
  84.0 3.0 %collective-permute-start.19 = (f32[6,16,128]{2,1,0:T(8,128)S(1)}, f32[6,16,128]{2,1,0:T(8,128)S(1)}, u32[]{:S(2)}, u32[]{:S(2)}) collective-permute-start(f32[6,16,128]{2,1,0:T(8,128)S(1)} %get-tuple-element.93.mine), channel_id=1, source_target_pairs={{0,128},{64,192},{128,0},{192,64},{1,129},{65,193},{129,1},{193,65... | collective-permute-start | bytes 147464 | tf_op jit(solution)/shard_map/ppermute | solution.py:481
  84.7 10.1 %collective-permute-start.21 = (f32[24,32,128]{2,1,0:T(8,128)S(1)}, f32[24,32,128]{2,1,0:T(8,128)S(1)}, u32[]{:S(2)}, u32[]{:S(2)}) collective-permute-start(f32[24,32,128]{2,1,0:T(8,128)S(1)} %get-tuple-element.94.mine), channel_id=1, source_target_pairs={{0,128},{64,192},{128,0},{192,64},{1,129},{65,193},{129,1},{193,65... | collective-permute-start | bytes 1179656 | tf_op jit(solution)/shard_map/ppermute | solution.py:481
  87.0 4.2 %collective-permute-start.20 = (f32[6,16,128]{2,1,0:T(8,128)S(1)}, f32[6,16,128]{2,1,0:T(8,128)S(1)}, u32[]{:S(2)}, u32[]{:S(2)}) collective-permute-start(f32[6,16,128]{2,1,0:T(8,128)S(1)} %join.3), channel_id=1, source_target_pairs={{0,160},{32,128},{64,224},{96,192},{128,32},{160,0},{192,96},{224,... | collective-permute-start | bytes 147464 | tf_op jit(solution)/shard_map/ppermute | solution.py:481
  95.0 3.4 %collective-permute-start.22 = (f32[24,32,128]{2,1,0:T(8,128)S(1)}, f32[24,32,128]{2,1,0:T(8,128)S(1)}, u32[]{:S(2)}, u32[]{:S(2)}) collective-permute-start(f32[24,32,128]{2,1,0:T(8,128)S(1)} %last.1.mine), channel_id=1, source_target_pairs={{0,64},{64,0},{128,192},{192,128},{1,65},{65,1},{129,193},{193,129... | collective-permute-start | bytes 1179656 | tf_op jit(solution)/shard_map/ppermute | solution.py:481
